TPU v7x, 32 devices: a whole 2x2x4 slice. The times are simulated.
32 devices in a mesh: ctx: 4 (over y, core), exp: 8 (over z, x).
Axes of the slice: x: 2, y: 2, z: 4, core: 2. Of those that a mesh axis runs over, the one named last changes fastest.
Arguments:
- layer_input: bfloat16 [8, 1024, 1536], P('exp', 'ctx'), may hold values from -6 to 6
- attn_gain: float32 [1536], replicated, may hold values from 0.1 to 1.9
- w_query: bfloat16 [1536, 1536], replicated, may hold values from -0.3125 to 0.3125
- w_key: bfloat16 [1536, 512], replicated, may hold values from -0.15625 to 0.15625
- w_value: bfloat16 [1536, 512], replicated, may hold values from -0.15625 to 0.15625
- w_out: bfloat16 [1536, 1536], replicated, may hold values from -1.25 to 1.25
- ffn_gain: float32 [1536], replicated, may hold values from 0.1 to 1.9
- shared_gate: bfloat16 [1536, 1024], replicated, may hold values from -0.15625 to 0.15625
- shared_up: bfloat16 [1536, 1024], replicated, may hold values from -0.15625 to 0.15625
- shared_down: bfloat16 [1024, 1536], replicated, may hold values from -0.1875 to 0.1875
- expert_gate: bfloat16 [16, 1536, 512], P('exp'), may hold values from -0.15625 to 0.15625
- expert_up: bfloat16 [16, 1536, 512], P('exp'), may hold values from -0.15625 to 0.15625
- expert_down: bfloat16 [16, 512, 1536], P('exp'), may hold values from -0.5 to 0.5
- routes: int32 [8, 1024, 6], P('exp', 'ctx'), may hold values from 0 to 15, all different within a row; in each aligned block of 256 rows (0 to 255, 256 to 511, ..., all dimensions but the last counted through in order) at most 192 rows name the same one
- gate_logits: float32 [8, 1024, 6], P('exp', 'ctx'), may hold values from -3 to 3
- span_order: int32 [8], replicated, may hold values from 0 to 7, each once
- cotangent: bfloat16 [8, 1024, 1536], P('exp', 'ctx'), may hold values from -6 to 6
Outputs:
- layer_output: bfloat16 [8, 1024, 1536], P('exp', 'ctx')
- input_grad: float32 [8, 1024, 1536], P('exp', 'ctx')
- attn_gain_grad: float32 [1536], P(('ctx', 'exp'))
- w_query_grad: float32 [1536, 1536], P(('ctx', 'exp'))
- w_key_grad: float32 [1536, 512], P(('ctx', 'exp'))
- w_value_grad: float32 [1536, 512], P(('ctx', 'exp'))
- w_out_grad: float32 [1536, 1536], P(('ctx', 'exp'))
- ffn_gain_grad: float32 [1536], P(('ctx', 'exp'))
- shared_gate_grad: float32 [1536, 1024], P(('ctx', 'exp'))
- shared_up_grad: float32 [1536, 1024], P(('ctx', 'exp'))
- shared_down_grad: float32 [1024, 1536], P(('ctx', 'exp'))
- expert_gate_grad: float32 [16, 1536, 512], P('exp', 'ctx')
- expert_up_grad: float32 [16, 1536, 512], P('exp', 'ctx')
- expert_down_grad: float32 [16, 512, 1536], P('exp', None, 'ctx')
Inputs may be any that keep to these rules, and one draw needn't show every extreme that they name: `routes`: each row names 6 different experts. In each aligned block of 256 rows (the rows of one device) no expert is named by more than 192 rows, a bound that some block reaches. `span_order`: each number appears once; entry c gives which block of 128 consecutive positions the c-th block of stored rows holds.
All inputs are finite; a program needn't handle non-finite values.
Results may differ from a plain program's by a relative error of at most 0.02.
Values may be sent and summed in bfloat16 or wider, within the bound.
No kernel may reach another device: no remote copies, remote signals or barrier semaphores. Data moves between devices by JAX's collectives and lax.ppermute only.
A program may use at most 320 MiB of HBM per device.

v0:
```python
import jax
import jax.numpy as jnp
from jax import lax
from jax.sharding import PartitionSpec as P

H = 12
HD = 128
KVH = 4
KB = 512


EPSILON = 1e-06
NEGATIVE = -1e30


def positions(stored, span_order, span_rows):
    span_ids = stored // span_rows
    matches = span_ids[:, None] == jnp.arange(span_order.shape[0], dtype=jnp.int32)[None, :]
    return (
        jnp.sum(jnp.where(matches, span_order[None, :], 0), axis=1) * span_rows + stored % span_rows
    )


def norm_forward(values, gain_vec):
    factor = lax.rsqrt(jnp.mean(values * values, axis=-1, keepdims=True) + EPSILON)
    return (values * factor * gain_vec, factor)


def norm_backward(values, factor, gain_vec, upstream):
    scaled = upstream * gain_vec
    inner_mean = jnp.mean(scaled * values, axis=-1, keepdims=True)
    value_grad = factor * scaled - values * factor * factor * factor * inner_mean
    return (value_grad, jnp.sum(upstream * values * factor, axis=0))


def silu_slope(values):
    sigmoid_v = jax.nn.sigmoid(values)
    return sigmoid_v * (1.0 + values * (1.0 - sigmoid_v))


def matmul(left_op, right_op):
    return jnp.dot(left_op, right_op, preferred_element_type=jnp.float32)


def matmul_right_t(left_op, right_op):
    return lax.dot_general(
        left_op, right_op, (((1,), (1,)), ((), ())), preferred_element_type=jnp.float32
    )


def matmul_left_t(left_op, right_op):
    return lax.dot_general(
        left_op, right_op, (((0,), (0,)), ((), ())), preferred_element_type=jnp.float32
    )


def shards(
    layer_input,
    attn_gain,
    w_query,
    w_key,
    w_value,
    w_out,
    ffn_gain,
    shared_gate,
    shared_up,
    shared_down,
    expert_gate,
    expert_up,
    expert_down,
    routes,
    gate_logits,
    span_order,
    cotangent,
):
    tokens = layer_input.shape[1]
    model_width = layer_input.shape[2]
    span_rows = tokens // 2
    groups = H // KVH
    kv_width = KVH * HD
    score_scale = HD ** (-0.5)
    resid_in = layer_input[0].astype(jnp.float32)
    own_rows = lax.axis_index("ctx") * tokens + jnp.arange(tokens, dtype=jnp.int32)
    query_places = positions(own_rows, span_order, span_rows)
    normed, factor_one = norm_forward(resid_in, attn_gain)
    normed_low = normed.astype(jnp.bfloat16)
    query_low = matmul(normed_low, w_query).astype(jnp.bfloat16)
    query_heads = query_low.reshape(tokens, KVH, groups, HD)
    key_value = jnp.concatenate(
        [matmul(normed_low, w_key), matmul(normed_low, w_value)], axis=1
    ).astype(jnp.bfloat16)

    def block_scores(kv_piece, first_row):
        piece_rows = kv_piece.shape[0]
        key_places = positions(
            first_row + jnp.arange(piece_rows, dtype=jnp.int32), span_order, span_rows
        )
        key_heads = kv_piece[:, :kv_width].reshape(piece_rows, KVH, HD)
        value_heads = kv_piece[:, kv_width:].reshape(piece_rows, KVH, HD)
        scores = (
            jnp.einsum("tgrd,jgd->tgrj", query_heads, key_heads, preferred_element_type=jnp.float32)
            * score_scale
        )
        visible = (key_places[None, :] <= query_places[:, None])[:, None, None, :]
        return (jnp.where(visible, scores, NEGATIVE), visible, key_heads, value_heads)

    running = jnp.full((tokens, KVH, groups), NEGATIVE, jnp.float32)
    scores, visible, key_heads, value_heads = block_scores(
        lax.all_gather(key_value, "ctx", axis=0, tiled=True), jnp.int32(0)
    )
    newest = jnp.maximum(running, jnp.max(scores, axis=-1))
    weights = jnp.where(visible, jnp.exp(scores - newest[..., None]), 0.0)
    row_sum = jnp.sum(weights, axis=-1)
    summed = jnp.einsum(
        "tgrj,jgd->tgrd",
        weights.astype(jnp.bfloat16),
        value_heads,
        preferred_element_type=jnp.float32,
    )
    running, row_sum, summed = (newest, row_sum, summed)
    log_total = running + jnp.log(row_sum)
    attended = (summed / row_sum[..., None]).reshape(tokens, H * HD)
    attended_low = attended.astype(jnp.bfloat16)
    middle = resid_in + matmul(attended_low, w_out)
    mixed_in, factor_two = norm_forward(middle, ffn_gain)
    rows_low = mixed_in.astype(jnp.bfloat16)
    shared_g = matmul(rows_low, shared_gate)
    shared_u = matmul(rows_low, shared_up)
    shared_act = jax.nn.silu(shared_g)
    shared_hidden = (shared_act * shared_u).astype(jnp.bfloat16)
    shared_out = matmul(shared_hidden, shared_down)
    route_ids = routes[0]
    top_count = route_ids.shape[1]
    gate_vals = jax.nn.softmax(gate_logits[0], axis=-1)
    local_experts = expert_gate.shape[0]
    expert_count = local_experts * lax.axis_size("exp")
    capacity = 2 * tokens * top_count // expert_count
    assigned = tokens * top_count
    flat_route = route_ids.reshape(assigned)
    one_hot = (flat_route[:, None] == jnp.arange(expert_count, dtype=jnp.int32)[None, :]).astype(
        jnp.int32
    )
    earlier = jnp.cumsum(one_hot, axis=0) - one_hot
    slot_ids = flat_route * capacity + jnp.sum(earlier * one_hot, axis=1)
    owners = jnp.arange(assigned, dtype=jnp.int32) // top_count
    slot_owner = jnp.full((expert_count * capacity,), tokens, jnp.int32).at[slot_ids].set(owners)
    padded_rows = jnp.concatenate([rows_low, jnp.zeros((1, model_width), jnp.bfloat16)], axis=0)
    outgoing = padded_rows[slot_owner].reshape(expert_count, 1, capacity, model_width)
    arrived = lax.all_to_all(outgoing, "exp", split_axis=0, concat_axis=1, tiled=True)
    flat_rows = arrived.reshape(local_experts, -1, model_width)
    gate_act = jnp.einsum(
        "esd,edf->esf", flat_rows, expert_gate, preferred_element_type=jnp.float32
    )
    up_act = jnp.einsum("esd,edf->esf", flat_rows, expert_up, preferred_element_type=jnp.float32)
    hidden_low = (jax.nn.silu(gate_act) * up_act).astype(jnp.bfloat16)
    produced = jnp.einsum(
        "esf,efd->esd", hidden_low, expert_down, preferred_element_type=jnp.float32
    )
    produced = produced.astype(jnp.bfloat16).reshape(arrived.shape)
    returned_rows = lax.all_to_all(produced, "exp", split_axis=1, concat_axis=0, tiled=True)
    returned_flat = returned_rows.reshape(expert_count * capacity, model_width)
    picked = returned_flat[slot_ids].reshape(tokens, top_count, model_width).astype(jnp.float32)
    routed = jnp.sum(gate_vals[..., None] * picked, axis=1)
    layer_out = middle + shared_out + routed
    upstream_low = cotangent[0]
    upstream = upstream_low.astype(jnp.float32)
    grad_shared_down = matmul_left_t(shared_hidden, upstream_low)
    hidden_grad = matmul_right_t(upstream_low, shared_down)
    shared_g_grad = (hidden_grad * shared_u * silu_slope(shared_g)).astype(jnp.bfloat16)
    shared_u_grad = (hidden_grad * shared_act).astype(jnp.bfloat16)
    grad_shared_gate = matmul_left_t(rows_low, shared_g_grad)
    grad_shared_up = matmul_left_t(rows_low, shared_u_grad)
    rows_grad = matmul_right_t(shared_g_grad, shared_gate) + matmul_right_t(
        shared_u_grad, shared_up
    )
    slot_grads = (
        (gate_vals[..., None] * upstream[:, None, :])
        .reshape(assigned, model_width)
        .astype(jnp.bfloat16)
    )
    grad_slots = (
        jnp.zeros((expert_count * capacity, model_width), jnp.bfloat16).at[slot_ids].set(slot_grads)
    )
    grad_slots = grad_slots.reshape(expert_count, 1, capacity, model_width)
    arrived_grad = lax.all_to_all(grad_slots, "exp", split_axis=0, concat_axis=1, tiled=True)
    flat_rows = arrived.reshape(local_experts, -1, model_width)
    flat_grad = arrived_grad.reshape(local_experts, -1, model_width)
    gate_act = jnp.einsum(
        "esd,edf->esf", flat_rows, expert_gate, preferred_element_type=jnp.float32
    )
    up_act = jnp.einsum("esd,edf->esf", flat_rows, expert_up, preferred_element_type=jnp.float32)
    gate_silu = jax.nn.silu(gate_act)
    hidden_low = (gate_silu * up_act).astype(jnp.bfloat16)
    grad_expert_down = jnp.einsum(
        "esf,esd->efd", hidden_low, flat_grad, preferred_element_type=jnp.float32
    )
    expert_hidden_grad = jnp.einsum(
        "esd,efd->esf", flat_grad, expert_down, preferred_element_type=jnp.float32
    )
    gate_grad_e = (expert_hidden_grad * up_act * silu_slope(gate_act)).astype(jnp.bfloat16)
    up_grad_e = (expert_hidden_grad * gate_silu).astype(jnp.bfloat16)
    grad_expert_gate = jnp.einsum(
        "esd,esf->edf", flat_rows, gate_grad_e, preferred_element_type=jnp.float32
    )
    grad_expert_up = jnp.einsum(
        "esd,esf->edf", flat_rows, up_grad_e, preferred_element_type=jnp.float32
    )
    sent_grad = jnp.einsum(
        "esf,edf->esd", gate_grad_e, expert_gate, preferred_element_type=jnp.float32
    )
    sent_grad = sent_grad + jnp.einsum(
        "esf,edf->esd", up_grad_e, expert_up, preferred_element_type=jnp.float32
    )
    sent_grad = sent_grad.astype(jnp.bfloat16).reshape(arrived.shape)
    back_grad = lax.all_to_all(sent_grad, "exp", split_axis=1, concat_axis=0, tiled=True).reshape(
        expert_count * capacity, model_width
    )
    rows_grad = rows_grad + jnp.sum(
        back_grad[slot_ids].reshape(tokens, top_count, model_width).astype(jnp.float32), axis=1
    )
    expert_sums = (
        lax.psum_scatter(
            grad_expert_gate.astype(jnp.bfloat16), "ctx", scatter_dimension=1, tiled=True
        ).astype(jnp.float32),
        lax.psum_scatter(
            grad_expert_up.astype(jnp.bfloat16), "ctx", scatter_dimension=1, tiled=True
        ).astype(jnp.float32),
        lax.psum_scatter(
            grad_expert_down.astype(jnp.bfloat16), "ctx", scatter_dimension=2, tiled=True
        ).astype(jnp.float32),
    )
    middle_grad_norm, grad_ffn_gain = norm_backward(middle, factor_two, ffn_gain, rows_grad)
    middle_grad = upstream + middle_grad_norm
    attn_grad_low = middle_grad.astype(jnp.bfloat16)
    grad_w_out = matmul_left_t(attended_low, attn_grad_low)
    out_heads_grad = (
        matmul_right_t(attn_grad_low, w_out).astype(jnp.bfloat16).reshape(tokens, KVH, groups, HD)
    )
    row_delta = jnp.sum(
        out_heads_grad.astype(jnp.float32) * attended.reshape(tokens, KVH, groups, HD), axis=-1
    )
    key_value_all = lax.all_gather(key_value, "ctx", axis=0, tiled=True)
    length = key_value_all.shape[0]

    def back_block(query_grad, block_index):
        kv_piece = lax.dynamic_slice_in_dim(key_value_all, block_index * KB, KB, 0)
        scores, visible, key_heads, value_heads = block_scores(kv_piece, block_index * KB)
        probabilities = jnp.where(visible, jnp.exp(scores - log_total[..., None]), 0.0)
        prob_grad = jnp.einsum(
            "tgrd,jgd->tgrj", out_heads_grad, value_heads, preferred_element_type=jnp.float32
        )
        score_grad = (probabilities * (prob_grad - row_delta[..., None]) * score_scale).astype(
            jnp.bfloat16
        )
        query_grad = query_grad + jnp.einsum(
            "tgrj,jgd->tgrd", score_grad, key_heads, preferred_element_type=jnp.float32
        )
        key_grad = jnp.einsum(
            "tgrj,tgrd->jgd", score_grad, query_heads, preferred_element_type=jnp.float32
        )
        value_grad = jnp.einsum(
            "tgrj,tgrd->jgd",
            probabilities.astype(jnp.bfloat16),
            out_heads_grad,
            preferred_element_type=jnp.float32,
        )
        return (
            query_grad,
            jnp.concatenate(
                [key_grad.reshape(KB, kv_width), value_grad.reshape(KB, kv_width)], axis=1
            ),
        )

    query_grad, kv_terms = lax.scan(
        back_block,
        jnp.zeros((tokens, KVH, groups, HD), jnp.float32),
        jnp.arange(length // KB, dtype=jnp.int32),
    )
    kv_grad = lax.psum_scatter(
        kv_terms.reshape(length, 2 * kv_width).astype(jnp.bfloat16),
        "ctx",
        scatter_dimension=0,
        tiled=True,
    ).astype(jnp.float32)
    query_grad_low = query_grad.reshape(tokens, H * HD).astype(jnp.bfloat16)
    key_grad_low = kv_grad[:, :kv_width].astype(jnp.bfloat16)
    value_grad_low = kv_grad[:, kv_width:].astype(jnp.bfloat16)
    normed_grad = matmul_right_t(query_grad_low, w_query) + matmul_right_t(key_grad_low, w_key)
    normed_grad = normed_grad + matmul_right_t(value_grad_low, w_value)
    grad_w_query = matmul_left_t(normed_low, query_grad_low)
    grad_w_key = matmul_left_t(normed_low, key_grad_low)
    grad_w_value = matmul_left_t(normed_low, value_grad_low)
    input_grad_norm, grad_attn_gain = norm_backward(resid_in, factor_one, attn_gain, normed_grad)
    input_grad = middle_grad + input_grad_norm
    dense_sums = (
        lax.psum_scatter(grad_attn_gain, ("ctx", "exp"), scatter_dimension=0, tiled=True),
        lax.psum_scatter(grad_w_query, ("ctx", "exp"), scatter_dimension=0, tiled=True),
        lax.psum_scatter(grad_w_key, ("ctx", "exp"), scatter_dimension=0, tiled=True),
        lax.psum_scatter(grad_w_value, ("ctx", "exp"), scatter_dimension=0, tiled=True),
        lax.psum_scatter(grad_w_out, ("ctx", "exp"), scatter_dimension=0, tiled=True),
        lax.psum_scatter(grad_ffn_gain, ("ctx", "exp"), scatter_dimension=0, tiled=True),
        lax.psum_scatter(grad_shared_gate, ("ctx", "exp"), scatter_dimension=0, tiled=True),
        lax.psum_scatter(grad_shared_up, ("ctx", "exp"), scatter_dimension=0, tiled=True),
        lax.psum_scatter(grad_shared_down, ("ctx", "exp"), scatter_dimension=0, tiled=True),
    )
    return (
        layer_out.astype(jnp.bfloat16)[None],
        input_grad[None],
        dense_sums[0],
        dense_sums[1],
        dense_sums[2],
        dense_sums[3],
        dense_sums[4],
        dense_sums[5],
        dense_sums[6],
        dense_sums[7],
        dense_sums[8],
        expert_sums[0],
        expert_sums[1],
        expert_sums[2],
    )


def solution(mesh):
    return jax.shard_map(
        shards,
        mesh=mesh,
        in_specs=(
            P("exp", "ctx", None),
            P(),
            P(),
            P(),
            P(),
            P(),
            P(),
            P(),
            P(),
            P(),
            P("exp", None, None),
            P("exp", None, None),
            P("exp", None, None),
            P("exp", "ctx", None),
            P("exp", "ctx", None),
            P(),
            P("exp", "ctx", None),
        ),
        out_specs=(
            P("exp", "ctx", None),
            P("exp", "ctx", None),
            P(("ctx", "exp")),
            P(("ctx", "exp"), None),
            P(("ctx", "exp"), None),
            P(("ctx", "exp"), None),
            P(("ctx", "exp"), None),
            P(("ctx", "exp")),
            P(("ctx", "exp"), None),
            P(("ctx", "exp"), None),
            P(("ctx", "exp"), None),
            P("exp", "ctx", None),
            P("exp", "ctx", None),
            P("exp", None, "ctx"),
        ),
        check_vma=False,
    )
```

profile of v0, /device:TPU:0, one launch (start us, length us, event | category | flops | bytes accessed | tf_op | source)
XLA Modules:
  0.0 1954.9 jit_solution(10747921747378810908)
XLA Ops:
  20.8 6.1 mul.337
  27.0 11.8 mul.338
  38.9 14.8 scatter_custom_fusion.1
  53.7 7.4 all-to-all-start.2
  66.8 6.2 scatter_custom_fusion
  73.0 5.2 convolution_convert_fusion.5
  81.5 9.4 all-gather.2.cloned.1.call-done
  114.5 20.6 %gather_fusion = bf16[3072,1536]{1,0:T(8,128)(2,1)} fusion(bf16[257,1536]{1,0:T(8,128)(2,1)} %concatenate.14, s32[3072]{0:T(1024)S(1)} %fusion.76), kind=kCustom, calls=%fused_computation | custom fusion | bytes 18886656 | tf_op jit(solution)/shard_map/gather | solution.py:148
  135.1 131.6 %all-to-all-done.2 = bf16[16,1,192,1536]{3,2,1,0:T(8,128)(2,1)} async-done(((bf16[16,1,192,1536]{3,2,1,0:T(8,128)(2,1)}), bf16[16,1,192,1536]{3,2,1,0:T(8,128)(2,1)}, u32[]{:S(2)}, u32[]{:S(2)}) %all-to-all-start.2) | async-done | bytes 9437216 | tf_op jit(solution)/shard_map/all_to_all | solution.py:185
  266.7 5.5 all-to-all-start
  272.2 8.2 copy.130
  280.3 196.5 %all-to-all-done = bf16[16,1,192,1536]{3,2,1,0:T(8,128)(2,1)} async-done(((bf16[16,1,192,1536]{3,2,1,0:T(8,128)(2,1)}), bf16[16,1,192,1536]{3,2,1,0:T(8,128)(2,1)}, u32[]{:S(2)}, u32[]{:S(2)}) %all-to-all-start) | async-done | bytes 9437216 | tf_op jit(solution)/shard_map/all_to_all | solution.py:149
  476.8 8.2 copy.125
  485.1 11.6 fusion.112
  496.7 7.0 fusion.111
  503.7 15.5 multiply_convert_fusion.1
  519.2 11.2 fusion.114
  530.3 12.3 add_convert_fusion
  542.7 8.2 copy.131
  550.9 5.2 all-to-all-start.3
  566.9 193.5 %all-to-all-done.3 = bf16[2,8,192,1536]{3,2,0,1:T(8,128)(2,1)} async-done(((bf16[2,8,192,1536]{3,2,0,1:T(8,128)(2,1)}), bf16[2,8,192,1536]{3,2,0,1:T(8,128)(2,1)}, u32[]{:S(2)}, u32[]{:S(2)}) %all-to-all-start.3) | async-done | bytes 9437216 | tf_op jit(solution)/shard_map/all_to_all | solution.py:215
  760.4 15.5 gather_fusion.2
  775.9 8.9 reshape.409
  784.8 9.6 reduce_sum.149
  794.4 5.6 multiply_reduce_fusion.1
  808.1 48.6 %while.15 = (s32[]{:T(128)}, f32[256,4,3,128]{0,3,2,1:T(8,128)}, bf16[2,512,1024]{2,1,0:T(8,128)(2,1)}, s32[2]{0:T(128)S(1)}, bf16[1024,1024]{1,0:T(8,128)(2,1)}...) while((s32[]{:T(128)}, f32[256,4,3,128]{0,3,2,1:T(8,128)}, ...), condition=%wide.region_19.20_spmd.clone, body=%wide.region_17.19_spmd.clone.sunk | while | flops 2036754944 | bytes 71222728 | solution.py:274
  856.8 10.7 convolution_convert_fusion.1
  867.4 8.7 copy.162
  880.6 13.1 convolution_convert_fusion.2
  893.9 13.7 convolution_convert_fusion.3
  907.6 5.3 fusion.116
  931.1 6.9 fusion.63
  938.0 10.1 convolution_convert_fusion
  948.1 8.4 copy.126
  964.0 6.3 fusion.55
  982.5 26.8 %reduce-scatter.30.cloned.1.call-done = bf16[2,384,512]{2,1,0:T(8,128)(2,1)} async-done(((bf16[2,1536,512]{2,1,0:T(8,128)(2,1)}), bf16[2,384,512]{2,1,0:T(8,128)(2,1)}) %reduce-scatter.30.cloned.1.call-update) | async-done | bytes 786448 | tf_op jit(solution)/shard_map/reduce_scatter | solution.py:222
  1011.8 178.3 %all-to-all-done.1 = bf16[2,8,192,1536]{3,2,0,1:T(8,128)(2,1)} async-done(((bf16[2,8,192,1536]{3,2,0,1:T(8,128)(2,1)}), bf16[2,8,192,1536]{3,2,0,1:T(8,128)(2,1)}, u32[]{:S(2)}, u32[]{:S(2)}) %all-to-all-start.1) | async-done | bytes 9437216 | tf_op jit(solution)/shard_map/all_to_all | solution.py:160
  1190.2 15.3 gather_fusion.1
  1205.4 9.1 reshape.408
  1214.6 10.6 multiply_reduce_fusion
  1225.2 5.1 fusion.30
  1238.1 38.5 %all-reduce.3 = (f32[1536]{0:T(1024)S(1)}, f32[1536]{0:T(1024)S(1)}) all-reduce(f32[1536]{0:T(1024)S(1)} %get-tuple-element.239, f32[1536]{0:T(1024)S(1)} %copy-done.44), channel_id=3, replica_groups=mesh['ctx'=4,'exp'=8] {'ctx','exp'}, use_global_device_ids=true, to_apply=%region_23.24.clone | all-reduce | flops 3072 | bytes 24576
  1281.6 48.4 %reduce-scatter.26.cloned.1.call-done = f32[48,1024]{1,0:T(8,128)} async-done(((f32[1536,1024]{1,0:T(8,128)}), f32[48,1024]{1,0:T(8,128)}) %reduce-scatter.26.cloned.1.call-update) | async-done | bytes 196624 | tf_op jit(solution)/shard_map/reduce_scatter | solution.py:303
  1329.9 119.8 %reduce-scatter.28.cloned.1.call-done = f32[32,1536]{1,0:T(8,128)} async-done(((f32[1024,1536]{1,0:T(8,128)}), f32[32,1536]{1,0:T(8,128)}) %reduce-scatter.28.cloned.1.call-update) | async-done | bytes 196624 | tf_op jit(solution)/shard_map/reduce_scatter | solution.py:304
  1449.7 107.8 %reduce-scatter.18.cloned.1.call-done = f32[48,512]{1,0:T(8,128)} async-done(((f32[1536,512]{1,0:T(8,128)}), f32[48,512]{1,0:T(8,128)}) %reduce-scatter.18.cloned.1.call-update) | async-done | bytes 98320 | tf_op jit(solution)/shard_map/reduce_scatter | solution.py:298
  1557.5 107.2 %reduce-scatter.20.cloned.1.call-done = f32[48,512]{1,0:T(8,128)} async-done(((f32[1536,512]{1,0:T(8,128)}), f32[48,512]{1,0:T(8,128)}) %reduce-scatter.20.cloned.1.call-update) | async-done | bytes 98320 | tf_op jit(solution)/shard_map/reduce_scatter | solution.py:299
  1664.6 142.1 %reduce-scatter.22.cloned.1.call-done = f32[48,1536]{1,0:T(8,128)} async-done(((f32[1536,1536]{1,0:T(8,128)}), f32[48,1536]{1,0:T(8,128)}) %reduce-scatter.22.cloned.1.call-update) | async-done | bytes 294928 | tf_op jit(solution)/shard_map/reduce_scatter | solution.py:300
  1806.7 140.8 %reduce-scatter.16.cloned.1.call-done = f32[48,1536]{1,0:T(8,128)} async-done(((f32[1536,1536]{1,0:T(8,128)}), f32[48,1536]{1,0:T(8,128)}) %reduce-scatter.16.cloned.1.call-update) | async-done | bytes 294928 | tf_op jit(solution)/shard_map/reduce_scatter | solution.py:297
  (278 shorter events, 168.8 us)
Async XLA Ops:
  7.2 496.5 %copy-start = (bf16[2,512,1536]{2,1,0:T(8,128)(2,1)S(1)}, bf16[2,512,1536]{2,1,0:T(8,128)(2,1)}, u32[]{:S(2)}) copy-start(bf16[2,512,1536]{2,1,0:T(8,128)(2,1)} %param.31) | copy-start | bytes 9437188
  27.0 11.9 copy-start.47
  27.0 11.9 copy-start.40
  27.0 11.9 copy-start.41
  38.9 27.9 %copy-start.42 = (s32[1536]{0:T(1024)}, s32[1536]{0:T(1024)S(1)}, u32[]{:S(2)}) copy-start(s32[1536]{0:T(1024)S(1)} %fusion.87) | copy-start | bytes 18436
  53.7 9.2 copy-start.29
  53.7 213.0 %all-to-all-start.2 = ((bf16[16,1,192,1536]{3,2,1,0:T(8,128)(2,1)}), bf16[16,1,192,1536]{3,2,1,0:T(8,128)(2,1)}, u32[]{:S(2)}, u32[]{:S(2)}) async-start(bf16[16,1,192,1536]{3,2,1,0:T(8,128)(2,1)} %bitcast.292), calls=%async_computation.2 | async-start | bytes 18874368 | tf_op jit(solution)/shard_map/all_to_all | solution.py:185
  61.1 29.8 %all-gather.2.cloned.1.call-start = ((), (), s32[]{:S(2)}) async-start(), calls=%async_computation.15 | async-start | bytes 2621440 | tf_op jit(solution)/shard_map/all_gather | solution.py:109
  61.3 3.9 copy-start.5
  61.3 3.9 copy-start.25
  62.9 10.1 copy-start.38
  73.0 7.5 copy-start.45
  101.9 7.8 slice-start
  105.1 4.7 copy-start.6
  105.1 4.7 slice-start.1
  266.7 210.1 %all-to-all-start = ((bf16[16,1,192,1536]{3,2,1,0:T(8,128)(2,1)}), bf16[16,1,192,1536]{3,2,1,0:T(8,128)(2,1)}, u32[]{:S(2)}, u32[]{:S(2)}) async-start(bf16[16,1,192,1536]{3,2,1,0:T(8,128)(2,1)} %bitcast.293), calls=%async_computation | async-start | bytes 18874368 | tf_op jit(solution)/shard_map/all_to_all | solution.py:149
  485.1 11.6 copy-start.14
  485.1 11.6 copy-start.54
  519.2 11.2 copy-start.55
  550.8 5.3 copy-start.43
  550.9 209.5 %all-to-all-start.3 = ((bf16[2,8,192,1536]{3,2,0,1:T(8,128)(2,1)}), bf16[2,8,192,1536]{3,2,0,1:T(8,128)(2,1)}, u32[]{:S(2)}, u32[]{:S(2)}) async-start(bf16[2,8,192,1536]{3,2,0,1:T(8,128)(2,1)} %copy.131), calls=%async_computation.3 | async-start | bytes 18874368 | tf_op jit(solution)/shard_map/all_to_all | solution.py:215
  556.0 367.0 %reduce-scatter.14.cloned.1.call-start = ((), (), s32[]{:S(2)}) async-start(), calls=%async_computation.16 | async-start | bytes 2621440 | tf_op jit(solution)/shard_map/reduce_scatter | solution.py:279
  556.1 3.3 copy-start.11
  556.1 3.3 copy-start.18
  556.2 204.2 %copy-start.32 = (s32[2048]{0:T(1024)}, s32[2048]{0:T(1024)S(1)}, u32[]{:S(2)}) copy-start(s32[2048]{0:T(1024)S(1)} %pad_clamp_fusion) | copy-start | bytes 24580
  784.8 9.6 copy-start.35
  784.8 9.6 copy-start.51
  794.4 7.3 slice-start.2
  794.4 5.6 copy-start.9
  794.4 5.6 copy-start.17
  794.4 7.3 slice-start.3
  804.0 4.1 copy-start.37
  804.0 4.1 copy-start.46
  856.7 114.5 %reduce-scatter.34.cloned.1.call-start = ((), (), s32[]{:S(2)}) async-start(), calls=%async_computation.26 | async-start | bytes 3932160
  880.6 99.4 %reduce-scatter.32.cloned.1.call-start = ((), (), s32[]{:S(2)}) async-start(), calls=%async_computation.25 | async-start | bytes 3932160 | tf_op jit(solution)/shard_map/reduce_scatter | solution.py:225
  893.8 115.5 %reduce-scatter.30.cloned.1.call-start = ((), (), s32[]{:S(2)}) async-start(), calls=%async_computation.24 | async-start | bytes 3932160 | tf_op jit(solution)/shard_map/reduce_scatter | solution.py:222
  907.6 374.0 %reduce-scatter.24.cloned.1.call-start = ((), (), s32[]{:S(2)}) async-start(), calls=%async_computation.21 | async-start | bytes 6488064 | tf_op jit(solution)/shard_map/reduce_scatter | solution.py:302
  912.9 417.0 %reduce-scatter.26.cloned.1.call-start = ((), (), s32[]{:S(2)}) async-start(), calls=%async_computation.22 | async-start | bytes 6488064 | tf_op jit(solution)/shard_map/reduce_scatter | solution.py:303
  917.9 531.8 %reduce-scatter.28.cloned.1.call-start = ((), (), s32[]{:S(2)}) async-start(), calls=%async_computation.23 | async-start | bytes 6488064 | tf_op jit(solution)/shard_map/reduce_scatter | solution.py:304
  922.9 634.5 %reduce-scatter.18.cloned.1.call-start = ((), (), s32[]{:S(2)}) async-start(), calls=%async_computation.18 | async-start | bytes 3244032 | tf_op jit(solution)/shard_map/reduce_scatter | solution.py:298
  927.2 737.5 %reduce-scatter.20.cloned.1.call-start = ((), (), s32[]{:S(2)}) async-start(), calls=%async_computation.19 | async-start | bytes 3244032 | tf_op jit(solution)/shard_map/reduce_scatter | solution.py:299
  930.8 875.9 %reduce-scatter.22.cloned.1.call-start = ((), (), s32[]{:S(2)}) async-start(), calls=%async_computation.20 | async-start | bytes 9732096 | tf_op jit(solution)/shard_map/reduce_scatter | solution.py:300
  956.5 233.6 %all-to-all-start.1 = ((bf16[2,8,192,1536]{3,2,0,1:T(8,128)(2,1)}), bf16[2,8,192,1536]{3,2,0,1:T(8,128)(2,1)}, u32[]{:S(2)}, u32[]{:S(2)}) async-start(bf16[2,8,192,1536]{3,2,0,1:T(8,128)(2,1)} %copy.126), calls=%async_computation.1 | async-start | bytes 18874368 | tf_op jit(solution)/shard_map/all_to_all | solution.py:160
  961.6 986.0 %reduce-scatter.16.cloned.1.call-start = ((), (), s32[]{:S(2)}) async-start(), calls=%async_computation.17 | async-start | bytes 9732096 | tf_op jit(solution)/shard_map/reduce_scatter | solution.py:297
  977.6 212.6 %copy-start.33 = (s32[2048]{0:T(1024)S(1)}, s32[2048]{0:T(1024)}, u32[]{:S(2)}) copy-start(s32[2048]{0:T(1024)} %copy-done.32) | copy-start | bytes 24580
  1225.2 5.1 copy-start.20
  1230.4 4.1 copy-start.24
  1230.4 4.1 copy-start.26
  (34 other events, 52.2 us)
Sparse Core Ops, SparseCore 0:
  66.8 23.9 all-gather.1
  856.9 30.8 reduce-scatter.13
  890.5 37.9 reduce-scatter.33
  930.8 37.9 reduce-scatter.31
  971.4 37.9 reduce-scatter.29
  1015.4 193.1 reduce-scatter.23
  1215.8 114.1 reduce-scatter.25
  1336.1 113.5 reduce-scatter.27
  1456.6 100.8 reduce-scatter.17
  1564.2 100.4 reduce-scatter.19
  1672.1 134.5 reduce-scatter.21
  1813.1 134.4 reduce-scatter.15
where the time goes:
time: 1970 us; the launch traced here: 1950 us
  waiting for transfers between devices  1400 us (71%)
  matrix products  205 us (10%)
  local copies, waits for them, and re-layouts  200 us (10%)
  other arithmetic  67.3 us (3%)
  blocking collectives  38.5 us (2%)
  starting transfers between devices  24 us (1%)
    all_to_all x1, waiting for transfers between devices, shards(): lax.all_to_all(outgoing, 'exp', split_axis=0, concat_axis=1, tiled=True)  196 us
    all_to_all x1, waiting for transfers between devices, shards(): lax.all_to_all(sent_grad, 'exp', split_axis=1, concat_axis=0, tiled=True)  193 us
    all_to_all x1, waiting for transfers between devices, shards(): lax.all_to_all(produced, 'exp', split_axis=1, concat_axis=0, tiled=True)  178 us
    reduce_scatter x1, waiting for transfers between devices, shards(): lax.psum_scatter(grad_w_out, ('ctx', 'exp'), scatter_dimension=0, tiled=T...  142 us
    reduce_scatter x1, waiting for transfers between devices, shards(): lax.psum_scatter(grad_w_query, ('ctx', 'exp'), scatter_dimension=0, tiled...  141 us
    all_to_all x1, waiting for transfers between devices, shards(): lax.all_to_all(grad_slots, 'exp', split_axis=0, concat_axis=1, tiled=True)  132 us
    reduce_scatter x1, waiting for transfers between devices, shards(): lax.psum_scatter(grad_shared_down, ('ctx', 'exp'), scatter_dimension=0, t...  120 us
    reduce_scatter x1, waiting for transfers between devices, shards(): lax.psum_scatter(grad_w_key, ('ctx', 'exp'), scatter_dimension=0, tiled=T...  108 us
  transfers between devices with their start and end apart: 16, of which 12 were waited for; matrix products, arithmetic and copies ran while one was open for 13% of the time, Pallas kernels for 0%

commit v1 on v0

v1 whole, which is shorter than its diff:
```python
import functools

import jax
import jax.numpy as jnp
from jax import lax
from jax.experimental import pallas as pl
from jax.experimental.pallas import tpu as pltpu
from jax.sharding import PartitionSpec as P

H = 12
HD = 128
KVH = 4
GROUPS = H // KVH
EPSILON = 1e-06
NEGATIVE = -1e30
SCALE = HD ** (-0.5)
BOTH = ("ctx", "exp")
GATE_LANES = 128
LOW_LANE = 64
VMEM_LIMIT = 60 * 2**20
bf16 = jnp.bfloat16
f32 = jnp.float32


def dot(left_op, right_op):
    return jnp.dot(left_op, right_op, preferred_element_type=f32)


def dot_nt(left_op, right_op):
    return lax.dot_general(left_op, right_op, (((1,), (1,)), ((), ())), preferred_element_type=f32)


def dot_tn(left_op, right_op):
    return lax.dot_general(left_op, right_op, (((0,), (0,)), ((), ())), preferred_element_type=f32)


def whole(shape):
    return pl.BlockSpec(shape, lambda *_: (0,) * len(shape))


def params():
    return pltpu.CompilerParams(vmem_limit_bytes=VMEM_LIMIT)


def cost(flops, nbytes):
    return pl.CostEstimate(flops=flops, bytes_accessed=nbytes, transcendentals=0)


def keyvalue_kernel(x_ref, gain_ref, wk_ref, wv_ref, normed_ref, kv_ref):
    @pl.when(pl.program_id(0) == 0)
    def _():
        x = x_ref[...].astype(f32)
        factor = lax.rsqrt(jnp.mean(x * x, axis=-1, keepdims=True) + EPSILON)
        normed_ref[...] = (x * factor * gain_ref[...]).astype(bf16)

    both = jnp.concatenate([wk_ref[...], wv_ref[...]], axis=1)
    kv_ref[...] = dot(normed_ref[...], both).astype(bf16)


def keyvalue(x, gain, wk, wv):
    rows, width = x.shape
    return pl.pallas_call(
        keyvalue_kernel,
        grid=(KVH,),
        in_specs=[
            whole((rows, width)),
            whole((1, width)),
            pl.BlockSpec((width, HD), lambda g: (0, g)),
            pl.BlockSpec((width, HD), lambda g: (0, g)),
        ],
        out_specs=[whole((rows, width)), pl.BlockSpec((rows, 2 * HD), lambda g: (0, g))],
        out_shape=[
            jax.ShapeDtypeStruct((rows, width), bf16),
            jax.ShapeDtypeStruct((rows, 2 * KVH * HD), bf16),
        ],
        compiler_params=params(),
        cost_estimate=cost(4 * rows * width * KVH * HD, 5 * 2**20),
    )(x, gain.reshape(1, width), wk, wv)


def stack_heads(ref):
    return jnp.concatenate([ref[:, r * HD : (r + 1) * HD] for r in range(GROUPS)], axis=0)


def place_column(bases, at, rows):
    row = lax.broadcasted_iota(jnp.int32, (rows, 1), 0)
    half = rows // 2
    return jnp.where(row < half, bases[at] + row, bases[at + 1] + row - half)


def place_row(bases, rows):
    row = lax.broadcasted_iota(jnp.int32, (1, GROUPS * rows), 1) % rows
    half = rows // 2
    return jnp.where(row < half, bases[0] + row, bases[1] + row - half)


def attend_kernel(blocks, bases, q_ref, *refs):
    kv_refs = refs[:blocks]
    out_ref, lse_ref, score_ref = refs[blocks:]
    rows = q_ref.shape[0]
    queries = stack_heads(q_ref)
    wanted = place_row(bases, rows)
    peak = jnp.full((1, GROUPS * rows), NEGATIVE, f32)
    for b in range(blocks):
        scores = dot_nt(kv_refs[b][:, :HD], queries) * SCALE
        visible = place_column(bases, 2 + 2 * b, rows) <= wanted
        scores = jnp.where(visible, scores, NEGATIVE)
        score_ref[b * rows : (b + 1) * rows, :] = scores
        peak = jnp.maximum(peak, jnp.max(scores, axis=0, keepdims=True))
    total = jnp.zeros_like(peak)
    mixed = jnp.zeros((HD, GROUPS * rows), f32)
    for b in range(blocks):
        weights = jnp.exp(score_ref[b * rows : (b + 1) * rows, :] - peak)
        total = total + jnp.sum(weights, axis=0, keepdims=True)
        mixed = mixed + dot_tn(kv_refs[b][:, HD:], weights.astype(bf16))
    lse_ref[0] = peak + jnp.log(total)
    mixed = jnp.transpose(mixed / total)
    for r in range(GROUPS):
        out_ref[:, r * HD : (r + 1) * HD] = mixed[r * rows : (r + 1) * rows].astype(bf16)


def attend(bases, queries, kv_blocks):
    rows = queries.shape[0]
    blocks = len(kv_blocks)
    wide = GROUPS * HD
    return pl.pallas_call(
        functools.partial(attend_kernel, blocks),
        grid_spec=pltpu.PrefetchScalarGridSpec(
            num_scalar_prefetch=1,
            grid=(KVH,),
            in_specs=[pl.BlockSpec((rows, wide), lambda g, _: (0, g))]
            + [pl.BlockSpec((rows, 2 * HD), lambda g, _: (0, g))] * blocks,
            out_specs=[
                pl.BlockSpec((rows, wide), lambda g, _: (0, g)),
                pl.BlockSpec((1, 1, GROUPS * rows), lambda g, _: (g, 0, 0)),
            ],
            scratch_shapes=[pltpu.VMEM((blocks * rows, GROUPS * rows), f32)],
        ),
        out_shape=[
            jax.ShapeDtypeStruct((rows, H * HD), bf16),
            jax.ShapeDtypeStruct((KVH, 1, GROUPS * rows), f32),
        ],
        compiler_params=params(),
        cost_estimate=cost(8 * rows * rows * blocks * H * HD, 4 * 2**20),
    )(bases, queries, *kv_blocks)


def attend_back_kernel(blocks, bases, q_ref, grad_ref, lse_ref, *refs):
    kv_refs = refs[:blocks]
    dq_ref = refs[blocks]
    dkv_refs = refs[blocks + 1 : 2 * blocks + 1]
    prob_ref, slope_ref = refs[2 * blocks + 1 :]
    rows = q_ref.shape[0]
    queries = stack_heads(q_ref)
    grads = stack_heads(grad_ref)
    wanted = place_row(bases, rows)
    lse = lse_ref[0]
    delta = jnp.zeros((1, GROUPS * rows), f32)
    for b in range(blocks):
        part = slice(b * rows, (b + 1) * rows)
        scores = dot_nt(kv_refs[b][:, :HD], queries) * SCALE - lse
        visible = place_column(bases, 2 + 2 * b, rows) <= wanted
        prob = jnp.exp(jnp.where(visible, scores, NEGATIVE))
        slope = dot_nt(kv_refs[b][:, HD:], grads)
        delta = delta + jnp.sum(prob * slope, axis=0, keepdims=True)
        prob_ref[part, :] = prob
        slope_ref[part, :] = slope
        dkv_refs[b][:, HD:] = dot(prob.astype(bf16), grads).astype(bf16)
    query_grad = jnp.zeros((HD, GROUPS * rows), f32)
    for b in range(blocks):
        part = slice(b * rows, (b + 1) * rows)
        dscore = (prob_ref[part, :] * (slope_ref[part, :] - delta) * SCALE).astype(bf16)
        dkv_refs[b][:, :HD] = dot(dscore, queries).astype(bf16)
        query_grad = query_grad + dot_tn(kv_refs[b][:, :HD], dscore)
    query_grad = jnp.transpose(query_grad)
    for r in range(GROUPS):
        dq_ref[:, r * HD : (r + 1) * HD] = query_grad[r * rows : (r + 1) * rows].astype(bf16)


def attend_back(bases, queries, grads, lse, kv_blocks):
    rows = queries.shape[0]
    blocks = len(kv_blocks)
    wide = GROUPS * HD
    by_group = pl.BlockSpec((rows, wide), lambda g, _: (0, g))
    kv_spec = pl.BlockSpec((rows, 2 * HD), lambda g, _: (0, g))
    return pl.pallas_call(
        functools.partial(attend_back_kernel, blocks),
        grid_spec=pltpu.PrefetchScalarGridSpec(
            num_scalar_prefetch=1,
            grid=(KVH,),
            in_specs=[
                by_group,
                by_group,
                pl.BlockSpec((1, 1, GROUPS * rows), lambda g, _: (g, 0, 0)),
            ]
            + [kv_spec] * blocks,
            out_specs=[by_group] + [kv_spec] * blocks,
            scratch_shapes=[pltpu.VMEM((blocks * rows, GROUPS * rows), f32)] * 2,
        ),
        out_shape=[jax.ShapeDtypeStruct((rows, H * HD), bf16)]
        + [jax.ShapeDtypeStruct((rows, 2 * KVH * HD), bf16)] * blocks,
        compiler_params=params(),
        cost_estimate=cost(20 * rows * rows * blocks * H * HD, 8 * 2**20),
    )(bases, queries, grads, lse, *kv_blocks)


def middle_kernel(x_ref, att_ref, w_ref, gain_ref, middle_ref, rows_ref):
    step = pl.program_id(0)
    tile = w_ref.shape[1]
    columns = pl.ds(pl.multiple_of(step * tile, tile), tile)
    middle_ref[:, columns] = x_ref[...].astype(f32) + dot(att_ref[...], w_ref[...])

    @pl.when(step == pl.num_programs(0) - 1)
    def _():
        middle = middle_ref[...]
        factor = lax.rsqrt(jnp.mean(middle * middle, axis=-1, keepdims=True) + EPSILON)
        rows_ref[...] = (middle * factor * gain_ref[...]).astype(bf16)


def middle_forward(x, attended, w_out, gain, tile=512):
    rows, width = x.shape
    return pl.pallas_call(
        middle_kernel,
        grid=(width // tile,),
        in_specs=[
            pl.BlockSpec((rows, tile), lambda n: (0, n)),
            whole(attended.shape),
            pl.BlockSpec((w_out.shape[0], tile), lambda n: (0, n)),
            whole((1, width)),
        ],
        out_specs=[whole((rows, width))] * 2,
        out_shape=[
            jax.ShapeDtypeStruct((rows, width), f32),
            jax.ShapeDtypeStruct((rows, width), bf16),
        ],
        compiler_params=params(),
        cost_estimate=cost(2 * rows * width * width, 8 * 2**20),
    )(x, attended, w_out, gain.reshape(1, width))


def middle_back_kernel(parts, *refs):
    grad_refs = refs[:parts]
    middle_ref, cot_ref, gain_ref, w_ref = refs[parts : parts + 4]
    mgrad_ref, low_ref, dgain_ref, out_ref = refs[parts + 4 :]

    @pl.when(pl.program_id(0) == 0)
    def _():
        upstream = grad_refs[0][...].astype(f32)
        for ref in grad_refs[1:]:
            upstream = upstream + ref[...].astype(f32)
        middle = middle_ref[...]
        factor = lax.rsqrt(jnp.mean(middle * middle, axis=-1, keepdims=True) + EPSILON)
        scaled = upstream * gain_ref[...]
        inner = jnp.mean(scaled * middle, axis=-1, keepdims=True)
        grad = factor * scaled - middle * (factor * factor * factor * inner)
        grad = cot_ref[...].astype(f32) + grad
        mgrad_ref[...] = grad
        low_ref[...] = grad.astype(bf16)
        dgain_ref[...] = jnp.sum(upstream * middle * factor, axis=0, keepdims=True)

    out_ref[...] = dot_nt(low_ref[...], w_ref[...]).astype(bf16)


def middle_back(grads, middle, cotangent, gain, w_out, tile=512):
    rows, width = middle.shape
    inner = w_out.shape[0]
    return pl.pallas_call(
        functools.partial(middle_back_kernel, len(grads)),
        grid=(inner // tile,),
        in_specs=[whole((rows, width))] * (len(grads) + 2)
        + [whole((1, width)), pl.BlockSpec((tile, width), lambda n: (n, 0))],
        out_specs=[
            whole((rows, width)),
            whole((rows, width)),
            whole((1, width)),
            pl.BlockSpec((rows, tile), lambda n: (0, n)),
        ],
        out_shape=[
            jax.ShapeDtypeStruct((rows, width), f32),
            jax.ShapeDtypeStruct((rows, width), bf16),
            jax.ShapeDtypeStruct((1, width), f32),
            jax.ShapeDtypeStruct((rows, inner), bf16),
        ],
        compiler_params=params(),
        cost_estimate=cost(2 * rows * width * inner, 16 * 2**20),
    )(*grads, middle, cotangent, gain.reshape(1, width), w_out)


def input_back_kernel(dq_ref, dkv_ref, wq_ref, wk_ref, wv_ref, x_ref, gain_ref, mgrad_ref, out_ref, dgain_ref):
    step = pl.program_id(0)
    term = dot_nt(dq_ref[...], wq_ref[...])
    term = term + dot_nt(dkv_ref[:, :HD], wk_ref[...]) + dot_nt(dkv_ref[:, HD:], wv_ref[...])

    @pl.when(step == 0)
    def _():
        out_ref[...] = term

    @pl.when(step > 0)
    def _():
        out_ref[...] += term

    @pl.when(step == pl.num_programs(0) - 1)
    def _():
        upstream = out_ref[...]
        x = x_ref[...].astype(f32)
        factor = lax.rsqrt(jnp.mean(x * x, axis=-1, keepdims=True) + EPSILON)
        scaled = upstream * gain_ref[...]
        inner = jnp.mean(scaled * x, axis=-1, keepdims=True)
        out_ref[...] = mgrad_ref[...] + factor * scaled - x * (factor * factor * factor * inner)
        dgain_ref[...] = jnp.sum(upstream * x * factor, axis=0, keepdims=True)


def input_back(dq, dkv, wq, wk, wv, x, gain, mgrad):
    rows, width = x.shape
    wide = GROUPS * HD
    return pl.pallas_call(
        input_back_kernel,
        grid=(KVH,),
        in_specs=[
            pl.BlockSpec((rows, wide), lambda g: (0, g)),
            pl.BlockSpec((rows, 2 * HD), lambda g: (0, g)),
            pl.BlockSpec((width, wide), lambda g: (0, g)),
            pl.BlockSpec((width, HD), lambda g: (0, g)),
            pl.BlockSpec((width, HD), lambda g: (0, g)),
            whole((rows, width)),
            whole((1, width)),
            whole((rows, width)),
        ],
        out_specs=[whole((rows, width)), whole((1, width))],
        out_shape=[
            jax.ShapeDtypeStruct((rows, width), f32),
            jax.ShapeDtypeStruct((1, width), f32),
        ],
        compiler_params=params(),
        cost_estimate=cost(2 * rows * width * (H + 2 * KVH) * HD, 14 * 2**20),
    )(dq, dkv, wq, wk, wv, x, gain.reshape(1, width), mgrad)


def experts_kernel(count, per, weighted, ids_ref, *refs):
    x_refs, c_refs = refs[:count], refs[count : 2 * count]
    wg_ref, wu_ref, wd_ref = refs[2 * count : 2 * count + 3]
    outs = refs[-(2 * count + 6) :]
    o_refs, g_refs = outs[:count], outs[count : 2 * count]
    x_all, c_all, hid_ref, dgu_ref, acc_o, acc_g = outs[2 * count :]
    step = pl.program_id(0)
    rows, width = x_refs[0].shape
    chunk = wg_ref.shape[2]

    @pl.when(step == 0)
    def _():
        for i in range(count):
            x_all[i * rows : (i + 1) * rows, :] = x_refs[i][...]
            c_all[i * rows : (i + 1) * rows, :] = c_refs[i][:, :width]

    x = x_all[...]
    gate = dot(x, wg_ref[0])
    up = dot(x, wu_ref[0])
    slope = dot_nt(c_all[...], wd_ref[0])
    sigmoid = 1.0 / (1.0 + jnp.exp(-gate))
    act = gate * sigmoid
    hidden = act * up
    if weighted:
        lane = ids_ref[0] + step // per
        lanes = lax.broadcasted_iota(jnp.int32, (rows, GATE_LANES), 1)
        chosen = (lanes == lane) | (lanes == lane + LOW_LANE)
        weight = jnp.concatenate(
            [
                jnp.sum(
                    jnp.where(chosen, c_refs[i][:, width:].astype(f32), 0.0),
                    axis=1,
                    keepdims=True,
                )
                for i in range(count)
            ],
            axis=0,
        )
        hidden = hidden * weight
        slope = slope * weight
    hidden = hidden.astype(bf16)
    dg = (slope * up * (sigmoid * (1.0 + gate * (1.0 - sigmoid)))).astype(bf16)
    du = (slope * act).astype(bf16)
    hid_ref[...] = hidden
    dgu_ref[:, :chunk] = dg
    dgu_ref[:, chunk:] = du
    out_term = dot(hidden, wd_ref[0])
    grad_term = dot_nt(dg, wg_ref[0]) + dot_nt(du, wu_ref[0])

    @pl.when(step == 0)
    def _():
        acc_o[...] = out_term
        acc_g[...] = grad_term

    @pl.when((step > 0) & (step < pl.num_programs(0) - 1))
    def _():
        acc_o[...] += out_term
        acc_g[...] += grad_term

    @pl.when(step == pl.num_programs(0) - 1)
    def _():
        out = acc_o[...] + out_term
        grad = acc_g[...] + grad_term
        for i in range(count):
            o_refs[i][...] = out[i * rows : (i + 1) * rows].astype(o_refs[i].dtype)
            g_refs[i][...] = grad[i * rows : (i + 1) * rows].astype(g_refs[i].dtype)


def experts(lane, xs, cs, wg, wu, wd, part, parts, kept, weighted, kind, chunk=256):
    count = len(xs)
    rows, width = xs[0].shape
    held, _, inner = wg.shape
    per = inner // chunk
    steps = held * per
    taken = count * rows
    collected = [
        jax.ShapeDtypeStruct((parts * taken, width), bf16),
        jax.ShapeDtypeStruct((parts * taken, width), bf16),
        jax.ShapeDtypeStruct((parts * taken, held * inner), bf16),
        jax.ShapeDtypeStruct((parts * taken, 2 * held * inner), bf16),
    ]
    in_specs = [whole((rows, width))] * count + [whole(cs[0].shape)] * count
    in_specs += [
        pl.BlockSpec((1, width, chunk), lambda i, _: (i // per, 0, i % per)),
        pl.BlockSpec((1, width, chunk), lambda i, _: (i // per, 0, i % per)),
        pl.BlockSpec((1, chunk, width), lambda i, _: (i // per, i % per, 0)),
    ]
    operands = [lane, *xs, *cs, wg, wu, wd]
    aliases = {}
    if kept is not None:
        aliases = {len(operands) + j: 2 * count + j for j in range(4)}
        operands += list(kept)
        in_specs += [pl.BlockSpec(memory_space=pl.ANY)] * 4
    result = pl.pallas_call(
        functools.partial(experts_kernel, count, per, weighted),
        grid_spec=pltpu.PrefetchScalarGridSpec(
            num_scalar_prefetch=1,
            grid=(steps,),
            in_specs=in_specs,
            out_specs=[whole((rows, width))] * (2 * count)
            + [
                pl.BlockSpec((taken, width), lambda i, _: (part, 0)),
                pl.BlockSpec((taken, width), lambda i, _: (part, 0)),
                pl.BlockSpec((taken, chunk), lambda i, _: (part, i)),
                pl.BlockSpec((taken, 2 * chunk), lambda i, _: (part, i)),
            ],
            scratch_shapes=[pltpu.VMEM((taken, width), f32)] * 2,
        ),
        out_shape=[jax.ShapeDtypeStruct((rows, width), kind)] * (2 * count) + collected,
        input_output_aliases=aliases,
        compiler_params=params(),
        cost_estimate=cost(12 * taken * width * held * inner, 24 * 2**20),
    )(*operands)
    return result[:count], result[count : 2 * count], result[2 * count :]


def swap_inner(value, axis):
    size = lax.axis_size(axis)
    return lax.ppermute(value, axis, [(i, i ^ 1) for i in range(size)])


def shift_outer(value, axis, by):
    outer = lax.axis_size(axis) // 2
    perm = [(o * 2 + i, ((o + by) % outer) * 2 + i) for o in range(outer) for i in range(2)]
    return lax.ppermute(value, axis, perm)


def ring_step(value, by):
    n_ctx, n_exp = lax.axis_size("ctx"), lax.axis_size("exp")
    outer = n_exp // 2
    perm = []
    for c in range(n_ctx):
        way = by if c % 2 == 0 else -by
        for o in range(outer):
            for i in range(2):
                perm.append((c * n_exp + o * 2 + i, c * n_exp + ((o + way) % outer) * 2 + i))
    return lax.ppermute(value, BOTH, perm)


def ring_gather(block):
    own = [block]
    for _ in range(lax.axis_size("exp") // 2 - 1):
        own.append(ring_step(own[-1], 1))
    return [(b, swap_inner(b, "exp")) for b in own]


def ring_reduce(pieces):
    pairs = [(a, swap_inner(b, "exp")) for a, b in pieces]
    moved = None
    for a, b in reversed(pairs[1:]):
        total = a.astype(f32) + b.astype(f32)
        if moved is not None:
            total = total + moved.astype(f32)
        moved = ring_step(total.astype(bf16), -1)
    return [pairs[0][0], pairs[0][1], moved]


def pick(value, index, dim):
    return lax.dynamic_index_in_dim(value, index, dim, keepdims=False)


def stages(total, dims, order, kind):
    c, e = lax.axis_index("ctx"), lax.axis_index("exp")
    at = {"y": c // 2, "core": c % 2, "z": e // 2, "x": e % 2}
    axis = {"y": "ctx", "core": "ctx", "z": "exp", "x": "exp"}
    dims = list(dims)
    for name in order:
        dim = dims.index(name)
        dims.remove(name)
        size = total.shape[dim]
        kept = pick(total, at[name], dim).astype(f32)
        for d in range(1, size):
            sent = pick(total, (at[name] + d) % size, dim).astype(kind)
            if name in ("core", "x"):
                got = swap_inner(sent, axis[name])
            else:
                got = shift_outer(sent, axis[name], d)
            kept = kept + got.astype(f32)
        total = kept
    return total


def weight_sum(left_op, right_op, order):
    n_ctx, n_exp = lax.axis_size("ctx"), lax.axis_size("exp")
    core = lax.axis_index("ctx") % 2
    tokens, height = left_op.shape
    outer = n_ctx // 2
    rows = height // (n_ctx * n_exp)
    split = left_op.reshape(tokens, outer, 2, height // n_ctx)
    halves = []
    for side in (1 - core, core):
        mine = pick(split, side, 2).reshape(tokens, height // 2)
        halves.append(dot_tn(mine, right_op).astype(bf16))
    total = halves[1].astype(f32) + swap_inner(halves[0], "ctx").astype(f32)
    total = total.reshape(outer, n_exp // 2, 2, rows, right_op.shape[1])
    return stages(total, ("y", "z", "x"), order, bf16)


def shards(
    layer_input,
    attn_gain,
    w_query,
    w_key,
    w_value,
    w_out,
    ffn_gain,
    shared_gate,
    shared_up,
    shared_down,
    expert_gate,
    expert_up,
    expert_down,
    routes,
    gate_logits,
    span_order,
    cotangent,
):
    x = layer_input[0]
    cot = cotangent[0]
    tokens, width = x.shape
    span_rows = tokens // 2
    n_ctx, n_exp = lax.axis_size("ctx"), lax.axis_size("exp")
    ctx_id, exp_id = lax.axis_index("ctx"), lax.axis_index("exp")
    local_experts, _, inner = expert_gate.shape
    expert_count = local_experts * n_exp

    normed, kv = keyvalue(x, attn_gain, w_key, w_value)
    kv_blocks, kv_ids = [], []
    moved = kv
    for k in range(n_ctx // 2):
        if k:
            moved = shift_outer(moved, "ctx", 1)
        source = ((ctx_id // 2 - k) % (n_ctx // 2)) * 2 + ctx_id % 2
        kv_blocks += [moved, swap_inner(moved, "ctx")]
        kv_ids += [source, source ^ 1]
    queries = dot(normed, w_query).astype(bf16)
    spans = jnp.stack([2 * i + s for i in [ctx_id] + kv_ids for s in range(2)])
    bases = span_order[spans] * span_rows

    gate_vals = jax.nn.softmax(gate_logits[0], axis=-1)
    named = routes[0][:, None, :] == jnp.arange(expert_count, dtype=jnp.int32)[None, :, None]
    row_gates = jnp.sum(jnp.where(named, gate_vals[:, None, :], 0.0), axis=-1)
    high = row_gates.astype(bf16)
    low = (row_gates - high.astype(f32)).astype(bf16)
    fill = ((0, 0), (0, LOW_LANE - expert_count))
    cot_ext = jnp.concatenate([cot, jnp.pad(high, fill), jnp.pad(low, fill)], axis=1)
    cot_blocks = ring_gather(cot_ext)

    attended, lse = attend(bases, queries, kv_blocks)
    middle, rows_low = middle_forward(x, attended, w_out, ffn_gain)

    row_blocks = ring_gather(rows_low)
    lane = (exp_id * local_experts).astype(jnp.int32).reshape(1)
    (shared_out,), (shared_grad,), (_, _, shared_hidden, shared_dgu) = experts(
        lane,
        [rows_low],
        [cot],
        shared_gate[None],
        shared_up[None],
        shared_down[None],
        0,
        1,
        None,
        False,
        f32,
    )
    levels = n_exp // 2
    out_terms, grad_terms, kept = [], [], None
    for k in range(levels):
        out_k, grad_k, kept = experts(
            lane,
            list(row_blocks[k]),
            list(cot_blocks[k]),
            expert_gate,
            expert_up,
            expert_down,
            k,
            levels,
            kept,
            True,
            bf16,
        )
        out_terms.append(out_k)
        grad_terms.append(grad_k)
    row_grads = ring_reduce(grad_terms)
    routed = ring_reduce(out_terms)
    rows_all, cot_all, hid_all, dgu_all = kept

    sum_gate_up = weight_sum(rows_low, shared_dgu, ("y", "x", "z"))
    sum_down = weight_sum(shared_hidden, cot, ("y", "x", "z"))
    grad_gate_up = dot_tn(rows_all, dgu_all).astype(bf16)
    grad_down = dot_tn(cot_all, hid_all).astype(bf16)
    expert_gate_up = lax.psum_scatter(grad_gate_up, "ctx", scatter_dimension=0, tiled=True)
    expert_down_t = lax.psum_scatter(grad_down, "ctx", scatter_dimension=0, tiled=True)

    mgrad, mgrad_low, ffn_gain_grad, att_grad = middle_back(
        [shared_grad] + row_grads, middle, cot, ffn_gain, w_out
    )
    dq, *dkv_blocks = attend_back(bases, queries, att_grad, lse, kv_blocks)
    kv_grad = None
    for k in reversed(range(n_ctx // 2)):
        term = dkv_blocks[2 * k].astype(f32) + swap_inner(dkv_blocks[2 * k + 1], "ctx").astype(f32)
        if kv_grad is not None:
            term = term + shift_outer(kv_grad.astype(bf16), "ctx", -1).astype(f32)
        kv_grad = term
    dkv = kv_grad.astype(bf16)
    sum_out = weight_sum(attended, mgrad_low, ("y", "x", "z"))
    middle_column = w_query.shape[1] // 2
    sum_query_a = weight_sum(normed, dq[:, :middle_column], ("x", "z", "y"))
    sum_query_b = weight_sum(normed, dq[:, middle_column:], ("z", "x", "y"))
    sum_kv = weight_sum(normed, dkv, ("y", "x", "z"))
    input_grad, attn_gain_grad = input_back(
        dq, dkv, w_query, w_key, w_value, x, attn_gain, mgrad
    )
    gains = jnp.stack(
        [
            attn_gain_grad.reshape(n_ctx // 2, 2, n_exp // 2, 2, -1),
            ffn_gain_grad.reshape(n_ctx // 2, 2, n_exp // 2, 2, -1),
        ],
        axis=4,
    )
    gains = stages(gains, ("y", "core", "z", "x"), ("core", "y", "x", "z"), f32)

    layer_out = middle + shared_out + sum(r.astype(f32) for r in routed)
    out_rows = width // n_ctx
    per = inner // 256
    expert_gate_up = expert_gate_up.reshape(out_rows, local_experts, per, 2, 256).astype(f32)
    expert_grads = [
        jnp.moveaxis(expert_gate_up[:, :, :, i], 1, 0).reshape(local_experts, out_rows, inner)
        for i in range(2)
    ]
    expert_down_grad = jnp.transpose(
        expert_down_t.reshape(out_rows, local_experts, inner), (1, 2, 0)
    ).astype(f32)
    shared_rows = sum_gate_up.reshape(sum_gate_up.shape[0], -1, 2, 256)
    kv_rows = sum_kv.reshape(sum_kv.shape[0], KVH, 2, HD)
    return (
        layer_out.astype(bf16)[None],
        input_grad[None],
        gains[0],
        jnp.concatenate([sum_query_a, sum_query_b], axis=1),
        kv_rows[:, :, 0].reshape(sum_kv.shape[0], -1),
        kv_rows[:, :, 1].reshape(sum_kv.shape[0], -1),
        sum_out,
        gains[1],
        shared_rows[:, :, 0].reshape(sum_gate_up.shape[0], -1),
        shared_rows[:, :, 1].reshape(sum_gate_up.shape[0], -1),
        sum_down,
        expert_grads[0],
        expert_grads[1],
        expert_down_grad,
    )


def solution(mesh):
    return jax.shard_map(
        shards,
        mesh=mesh,
        in_specs=(
            P("exp", "ctx", None),
            P(),
            P(),
            P(),
            P(),
            P(),
            P(),
            P(),
            P(),
            P(),
            P("exp", None, None),
            P("exp", None, None),
            P("exp", None, None),
            P("exp", "ctx", None),
            P("exp", "ctx", None),
            P(),
            P("exp", "ctx", None),
        ),
        out_specs=(
            P("exp", "ctx", None),
            P("exp", "ctx", None),
            P(("ctx", "exp")),
            P(("ctx", "exp"), None),
            P(("ctx", "exp"), None),
            P(("ctx", "exp"), None),
            P(("ctx", "exp"), None),
            P(("ctx", "exp")),
            P(("ctx", "exp"), None),
            P(("ctx", "exp"), None),
            P(("ctx", "exp"), None),
            P("exp", "ctx", None),
            P("exp", "ctx", None),
            P("exp", None, "ctx"),
        ),
        check_vma=False,
    )
```

time: 1970 us -> 678 us (0.34)
  waiting for transfers between devices: 1400 us -> 266 us
  matrix products: 205 us -> 53.8 us
  Pallas kernels: 0 us -> 144 us
  local copies, waits for them, and re-layouts: 200 us -> 77.4 us
  starting transfers between devices: 24 us -> 85.1 us
  blocking collectives: 38.5 us -> 0 us
  other arithmetic: 67.3 us -> 30.8 us
    all_to_all x4 -> x0, waiting for transfers between devices: 700 us -> none  [the longest x1 196 us: shards(): lax.all_to_all(outgoing, 'exp', split_axis=0, concat_axis=1, tiled=True)]
    reduce_scatter x10 -> x2, waiting for transfers between devices: 693 us -> 0.01 us  [the longest x1 0.01 us: shards(): lax.psum_scatter(grad_down, 'ctx', scatter_dimension=0, tiled=True)]
    ppermute x0 -> x76, waiting for transfers between devices: none -> 266 us  [the longest x34 109 us: swap_inner(): return lax.ppermute(value, axis, [(i, i ^ 1) for i in range(size)])]
    dot_general x42 -> x15, matrix products: 205 us -> 53.8 us  [the longest x14 49.2 us: dot_tn(): lax.dot_general(left_op, right_op, (((0,), (0,)), ((), ())), preferred_el...]
    pallas_call x0 -> x11, Pallas kernels: none -> 144 us  [the longest x5 90.2 us: experts(): pl.pallas_call(functools.partial(experts_kernel, count, per, weighted), g...]
    ppermute x0 -> x76, starting transfers between devices: none -> 85 us  [the longest x30 51.9 us: shift_outer(): return lax.ppermute(value, axis, perm)]
    gather x3 -> x1, local copies, waits for them, and re-layouts: 51.4 us -> 0.66 us  [shards(): bases = span_order[spans] * span_rows]
    unnamed x1 -> x0, blocking collectives: 38.5 us -> none
  transfers between devices with their start and end apart: 16 -> 78, of which waited for: 12 -> 27; matrix products, arithmetic and copies ran while one was open for 13% -> 20% of each run, Pallas kernels for 0% -> 21%
where the time goes in v1:
time: 678 us; the launch traced here: 672 us
  waiting for transfers between devices  266 us (39%)
  Pallas kernels  144 us (21%)
  starting transfers between devices  85.1 us (13%)
  local copies, waits for them, and re-layouts  77.4 us (11%)
  matrix products  53.8 us (8%)
  other arithmetic  30.8 us (5%)
  between operations  15.7 us (2%)
    ppermute x34, waiting for transfers between devices, swap_inner(): return lax.ppermute(value, axis, [(i, i ^ 1) for i in range(size)])  109 us
    ppermute x30, waiting for transfers between devices, shift_outer(): return lax.ppermute(value, axis, perm)  94 us
    pallas_call x5, Pallas kernels, experts(): pl.pallas_call(functools.partial(experts_kernel, count, per, weighted), g...  90.2 us
    ppermute x12, waiting for transfers between devices, ring_step(): return lax.ppermute(value, BOTH, perm)  63 us
    ppermute x30, starting transfers between devices, shift_outer(): return lax.ppermute(value, axis, perm)  51.9 us
    dot_general x14, matrix products, dot_tn(): lax.dot_general(left_op, right_op, (((0,), (0,)), ((), ())), preferred_el...  49.2 us
    unnamed x111, local copies, waits for them, and re-layouts  28 us
    ppermute x34, starting transfers between devices, swap_inner(): return lax.ppermute(value, axis, [(i, i ^ 1) for i in range(size)])  22.8 us
  transfers between devices with their start and end apart: 78, of which 27 were waited for; matrix products, arithmetic and copies ran while one was open for 20% of the time, Pallas kernels for 21%

profile of v1, /device:TPU:0, one launch (start us, length us, event | category | flops | bytes accessed | tf_op | source)
XLA Modules:
  0.0 671.9 jit_solution(8849798208638686844)
XLA Ops:
  8.5 5.0 shard_map.272
  13.6 3.0 collective-permute-start.1
  22.1 6.6 collective-permute-done.1.refs_2_
  29.8 4.6 convolution_convert_fusion.8.q_ref
  34.5 8.7 %collective-permute-done.8.refs_2_ = bf16[256,1664]{1,0:T(8,128)(2,1)} collective-permute-done((bf16[256,1664]{1,0:T(8,128)(2,1)}, bf16[256,1664]{1,0:T(8,128)(2,1)}, u32[]{:S(2)}, u32[]{:S(2)}) %collective-permute-start.8) | collective-permute-done | bytes 852000 | tf_op jit(solution)/shard_map/ppermute | solution.py:475
  44.8 9.6 %shard_map.273 = (bf16[256,1536]{1,0:T(8,128)(2,1)}, f32[4,1,768]{2,1,0:T(1,128)}) custom-call(s32[10]{0:T(128)} %broadcast_multiply_fusion.bases, bf16[256,1536]{1,0:T(8,128)(2,1)} %convolution_convert_fusion.8.q_ref, bf16[256,1024]{1,0:T(8,128)(2,1)} %get-tuple-element.68.refs_0_, bf16[256,1024]{1,0:T(8,128)(2,1)} %copy-done.44, ...), custom_call_target="tpu_custom_call" | custom-call | flops 3221225472 | bytes 4194304 | tf_op jit(solution)/shard_map/pallas_call | solution.py:126
  54.4 6.1 shard_map.274
  63.1 12.0 %shard_map.275 = (f32[256,1536]{1,0:T(8,128)}, f32[256,1536]{1,0:T(8,128)}, bf16[256,1536]{1,0:T(8,128)(2,1)}, bf16[256,1536]{1,0:T(8,128)(2,1)}, bf16[256,1024]{1,0:T(8,128)(2,1)}, /*index=5*/bf16[256,2048]{1,0:T(8,128)(2,1)}) custom-call(s32[1]{0:T(128)} %bitcast.12.ids_ref, bf16[256,1536]{1,0:T(8,128)(2,1)} %get-tuple-element.71.refs_0_, ...), custom_call_target="tpu_custom_call" | custom-call | flops 4831838208 | bytes 25165824 | tf_op jit(solution)/shard_map/pallas_call | solution.py:432
  95.6 19.5 %shard_map.276 = (bf16[256,1536]{1,0:T(8,128)(2,1)}, bf16[256,1536]{1,0:T(8,128)(2,1)}, bf16[256,1536]{1,0:T(8,128)(2,1)}, bf16[256,1536]{1,0:T(8,128)(2,1)}, bf...) custom-call(s32[1]{0:T(128)} %bitcast.12.ids_ref, ...), custom_call_target="tpu_custom_call" | custom-call | flops 9663676416 | bytes 25165824 | tf_op jit(solution)/shard_map/pallas_call | solution.py:432
  122.0 9.9 %collective-permute-done.11.refs_0_ = bf16[256,1536]{1,0:T(8,128)(2,1)} collective-permute-done((bf16[256,1536]{1,0:T(8,128)(2,1)}, bf16[256,1536]{1,0:T(8,128)(2,1)}, u32[]{:S(2)}, u32[]{:S(2)}) %collective-permute-start.11) | collective-permute-done | bytes 786464 | tf_op jit(solution)/shard_map/ppermute | solution.py:475
  133.0 19.6 %shard_map.277 = (bf16[256,1536]{1,0:T(8,128)(2,1)}, bf16[256,1536]{1,0:T(8,128)(2,1)}, bf16[256,1536]{1,0:T(8,128)(2,1)}, bf16[256,1536]{1,0:T(8,128)(2,1)}, bf...) custom-call(s32[1]{0:T(128)} %bitcast.12.ids_ref, ...), custom_call_target="tpu_custom_call", output_to_operand_aliasing={{4}: (8, {}), {5}: (9, {}), {6}: (10, {}), {7}: (11, {})} | custom-call | flops 9663676416 | bytes 25165824 | tf_op jit(solution)/shard_map/pallas_call | solution.py:432
  154.6 27.9 %collective-permute-done.12.refs_1_ = bf16[256,1536]{1,0:T(8,128)(2,1)} collective-permute-done((bf16[256,1536]{1,0:T(8,128)(2,1)}, bf16[256,1536]{1,0:T(8,128)(2,1)}, u32[]{:S(2)}, u32[]{:S(2)}) %collective-permute-start.12) | collective-permute-done | bytes 786464 | tf_op jit(solution)/shard_map/ppermute | solution.py:457
  182.5 19.5 %shard_map.278 = (bf16[256,1536]{1,0:T(8,128)(2,1)}, bf16[256,1536]{1,0:T(8,128)(2,1)}, bf16[256,1536]{1,0:T(8,128)(2,1)}, bf16[256,1536]{1,0:T(8,128)(2,1)}, bf...) custom-call(s32[1]{0:T(128)} %bitcast.12.ids_ref, ...), custom_call_target="tpu_custom_call", output_to_operand_aliasing={{4}: (8, {}), {5}: (9, {}), {6}: (10, {}), {7}: (11, {})} | custom-call | flops 9663676416 | bytes 25165824 | tf_op jit(solution)/shard_map/pallas_call | solution.py:432
  203.2 19.6 %shard_map.279 = (bf16[256,1536]{1,0:T(8,128)(2,1)}, bf16[256,1536]{1,0:T(8,128)(2,1)}, bf16[256,1536]{1,0:T(8,128)(2,1)}, bf16[256,1536]{1,0:T(8,128)(2,1)}, bf...) custom-call(s32[1]{0:T(128)} %bitcast.12.ids_ref, ...), custom_call_target="tpu_custom_call", output_to_operand_aliasing={{4}: (8, {}), {5}: (9, {}), {6}: (10, {}), {7}: (11, {})} | custom-call | flops 9663676416 | bytes 25165824 | tf_op jit(solution)/shard_map/pallas_call | solution.py:432
  222.8 11.3 %convolution_convert_fusion.1 = bf16[1536,1024]{1,0:T(8,128)(2,1)} fusion(bf16[2048,1536]{1,0:T(8,128)(2,1)} %get-tuple-element.118, bf16[2048,1024]{1,0:T(8,128)(2,1)} %get-tuple-element.119), kind=kOutput, calls=%fused_computation.4 | convolution fusion | flops 6444023808 | bytes 13631488 | tf_op jit(solution)/shard_map/dot_general | solution.py:34
  248.0 3.0 copy.170
  255.4 3.3 collective-permute-start.75
  263.2 3.0 copy.167
  270.0 3.2 convert_add_fusion
  279.5 17.9 %convolution_convert_fusion = bf16[1536,2048]{1,0:T(8,128)(2,1)} fusion(bf16[2048,1536]{1,0:T(8,128)(2,1)S(1)} %bitcast.264, bf16[2048,2048]{1,0:T(8,128)(2,1)} %get-tuple-element.117), kind=kOutput, calls=%fused_computation.1 | convolution fusion | flops 12888047616 | bytes 20971520 | tf_op jit(solution)/shard_map/dot_general | solution.py:34
  297.5 23.2 %collective-permute-done.27 = bf16[256,1536]{1,0:T(8,128)(2,1)} collective-permute-done((bf16[256,1536]{1,0:T(8,128)(2,1)}, bf16[256,1536]{1,0:T(8,128)(2,1)}, u32[]{:S(2)}, u32[]{:S(2)}) %collective-permute-start.27) | collective-permute-done | bytes 786464 | tf_op jit(solution)/shard_map/ppermute | solution.py:457
  322.5 14.9 %collective-permute-done.20 = bf16[256,1536]{1,0:T(8,128)(2,1)S(1)} collective-permute-done((bf16[256,1536]{1,0:T(8,128)(2,1)}, bf16[256,1536]{1,0:T(8,128)(2,1)S(1)}, u32[]{:S(2)}, u32[]{:S(2)}) %collective-permute-start.20) | collective-permute-done | bytes 786464 | tf_op jit(solution)/shard_map/ppermute | solution.py:457
  339.6 2.9 bitcast_add_fusion
  344.0 14.0 %collective-permute-done.28 = bf16[256,1536]{1,0:T(8,128)(2,1)S(1)} collective-permute-done((bf16[256,1536]{1,0:T(8,128)(2,1)S(1)}, bf16[256,1536]{1,0:T(8,128)(2,1)S(1)}, u32[]{:S(2)}, u32[]{:S(2)}) %collective-permute-start.28) | collective-permute-done | bytes 786464 | tf_op jit(solution)/shard_map/ppermute | solution.py:475
  361.7 8.7 %collective-permute-done.21 = bf16[256,1536]{1,0:T(8,128)(2,1)S(1)} collective-permute-done((bf16[256,1536]{1,0:T(8,128)(2,1)S(1)}, bf16[256,1536]{1,0:T(8,128)(2,1)S(1)}, u32[]{:S(2)}, u32[]{:S(2)}) %collective-permute-start.21) | collective-permute-done | bytes 786464 | tf_op jit(solution)/shard_map/ppermute | solution.py:475
  371.1 16.9 %collective-permute-done.66 = bf16[4,48,2048]{2,1,0:T(8,128)(2,1)S(1)} collective-permute-done((bf16[4,48,2048]{2,1,0:T(8,128)(2,1)S(1)}, bf16[4,48,2048]{2,1,0:T(8,128)(2,1)S(1)}, u32[]{:S(2)}, u32[]{:S(2)}) %collective-permute-start.66) | collective-permute-done | bytes 786464 | tf_op jit(solution)/shard_map/ppermute | solution.py:457
  392.0 9.8 %collective-permute-done.10 = bf16[256,1536]{1,0:T(8,128)(2,1)S(1)} collective-permute-done((bf16[256,1536]{1,0:T(8,128)(2,1)S(1)}, bf16[256,1536]{1,0:T(8,128)(2,1)S(1)}, u32[]{:S(2)}, u32[]{:S(2)}) %collective-permute-start.10) | collective-permute-done | bytes 786464 | tf_op jit(solution)/shard_map/ppermute | solution.py:457
  402.3 9.0 %collective-permute-done.22 = bf16[256,1536]{1,0:T(8,128)(2,1)S(1)} collective-permute-done((bf16[256,1536]{1,0:T(8,128)(2,1)S(1)}, bf16[256,1536]{1,0:T(8,128)(2,1)S(1)}, u32[]{:S(2)}, u32[]{:S(2)}) %collective-permute-start.22) | collective-permute-done | bytes 786464 | tf_op jit(solution)/shard_map/ppermute | solution.py:475
  413.3 14.5 %collective-permute-done.68 = bf16[48,2048]{1,0:T(8,128)(2,1)S(1)} collective-permute-done((bf16[48,2048]{1,0:T(8,128)(2,1)S(1)}, bf16[48,2048]{1,0:T(8,128)(2,1)S(1)}, u32[]{:S(2)}, u32[]{:S(2)}) %collective-permute-start.68) | collective-permute-done | bytes 196640 | tf_op jit(solution)/shard_map/ppermute | solution.py:463
  430.8 12.7 %collective-permute-done.30.refs_3_ = bf16[256,1536]{1,0:T(8,128)(2,1)S(1)} collective-permute-done((bf16[256,1536]{1,0:T(8,128)(2,1)}, bf16[256,1536]{1,0:T(8,128)(2,1)S(1)}, u32[]{:S(2)}, u32[]{:S(2)}) %collective-permute-start.30) | collective-permute-done | bytes 786464 | tf_op jit(solution)/shard_map/ppermute | solution.py:475
  444.4 8.4 %shard_map.280 = (f32[256,1536]{1,0:T(8,128)}, bf16[256,1536]{1,0:T(8,128)(2,1)}, f32[1,1536]{1,0:T(1,128)}, bf16[256,1536]{1,0:T(8,128)(2,1)}) custom-call(f32[256,1536]{1,0:T(8,128)} %get-tuple-element.93.refs_0_, bf16[256,1536]{1,0:T(8,128)(2,1)} %get-tuple-element.94.refs_1_, bf16[256,1536]{1,0:T(8,128)(2,1)} %collective-permute-done.24.refs_2_, ...), custom_call_target="tpu_custom_call" | custom-call | flops 1207959552 | bytes 16777216 | tf_op jit(solution)/shard_map/pallas_call | solution.py:267
  452.9 3.4 convolution_convert_fusion.4
  457.1 14.6 %shard_map.281 = (bf16[256,1536]{1,0:T(8,128)(2,1)}, bf16[256,1024]{1,0:T(8,128)(2,1)}, bf16[256,1024]{1,0:T(8,128)(2,1)}, bf16[256,1024]{1,0:T(8,128)(2,1)}, bf16[256,1024]{1,0:T(8,128)(2,1)}) custom-call(s32[10]{0:T(128)} %broadcast_multiply_fusion.bases, bf16[256,1536]{1,0:T(8,128)(2,1)} %convolution_convert_fusion.8.q_ref, ...), custom_call_target="tpu_custom_call" | custom-call | flops 8053063680 | bytes 8388608 | tf_op jit(solution)/shard_map/pallas_call | solution.py:186
  479.7 3.5 fusion.2
  483.3 9.7 %collective-permute-done.33 = bf16[256,1024]{1,0:T(8,128)(2,1)S(1)} collective-permute-done((bf16[256,1024]{1,0:T(8,128)(2,1)S(1)}, bf16[256,1024]{1,0:T(8,128)(2,1)S(1)}, u32[]{:S(2)}, u32[]{:S(2)}) %collective-permute-start.33) | collective-permute-done | bytes 524320 | tf_op jit(solution)/shard_map/ppermute | solution.py:463
  495.0 9.7 %shard_map.282 = (f32[256,1536]{1,0:T(8,128)}, f32[1,1536]{1,0:T(1,128)}) custom-call(bf16[256,1536]{1,0:T(8,128)(2,1)} %get-tuple-element.104.dq_ref, bf16[256,1024]{1,0:T(8,128)(2,1)} %add_convert_fusion.7.dkv_ref, bf16[1536,1536]{1,0:T(8,128)(2,1)} %wq_ref.1, bf16[1536,512]{1,0:T(8,128)(2,1)} %wk_ref.3, bf16[1536,512]{1,0:T(8,128)(2,1)} %wv_ref.3, ...), custom_call_target="tpu_custom_call" | custom-call | flops 2013265920 | bytes 14680064 | tf_op jit(solution)/shard_map/pallas_call | solution.py:316
  526.1 3.2 collective-permute-start.48
  532.0 4.9 collective-permute-done.47
  537.4 11.7 %collective-permute-done.48 = bf16[2,2,48,768]{3,2,0,1:T(8,128)(2,1)S(1)} collective-permute-done((bf16[2,2,48,768]{3,2,0,1:T(8,128)(2,1)S(1)}, bf16[2,2,48,768]{3,2,0,1:T(8,128)(2,1)S(1)}, u32[]{:S(2)}, u32[]{:S(2)}) %collective-permute-start.48) | collective-permute-done | bytes 294944 | tf_op jit(solution)/shard_map/ppermute | solution.py:463
  550.5 4.0 collective-permute-done.50
  555.6 6.5 collective-permute-start.42
  564.1 2.8 collective-permute-start.44
  572.8 37.1 %collective-permute-done.45 = bf16[48,768]{1,0:T(8,128)(2,1)S(1)} collective-permute-done((bf16[48,768]{1,0:T(8,128)(2,1)S(1)}, bf16[48,768]{1,0:T(8,128)(2,1)S(1)}, u32[]{:S(2)}, u32[]{:S(2)}) %collective-permute-start.45) | collective-permute-done | bytes 73760 | tf_op jit(solution)/shard_map/ppermute | solution.py:463
  613.7 8.8 %collective-permute-done.54 = bf16[4,48,1024]{2,1,0:T(8,128)(2,1)S(1)} collective-permute-done((bf16[4,48,1024]{2,1,0:T(8,128)(2,1)S(1)}, bf16[4,48,1024]{2,1,0:T(8,128)(2,1)S(1)}, u32[]{:S(2)}, u32[]{:S(2)}) %collective-permute-start.54) | collective-permute-done | bytes 393248 | tf_op jit(solution)/shard_map/ppermute | solution.py:457
  634.5 5.0 collective-permute-start.61
  642.9 3.8 collective-permute-done.62
  647.5 4.2 reshape.599
  656.9 3.1 reshape.609
  (353 shorter events, 172.2 us)
Async XLA Ops:
  7.2 620.9 %reduce-scatter.5.cloned.1.call-start = ((), (), s32[]{:S(2)}) async-start(), calls=%async_computation.3 | async-start | bytes 3932160 | tf_op jit(solution)/shard_map/reduce_scatter | solution.py:632
  16.6 26.6 %collective-permute-start = (bf16[256,1024]{1,0:T(8,128)(2,1)}, bf16[256,1024]{1,0:T(8,128)(2,1)S(1)}, u32[]{:S(2)}, u32[]{:S(2)}) collective-permute-start(bf16[256,1024]{1,0:T(8,128)(2,1)} %get-tuple-element.68.refs_0_), channel_id=1, source_target_pairs={{0,8},{8,0},{16,24},{24,16},{1,9},{9,1},{17,25},{25,17},{2,10},{10... | collective-permute-start | bytes 1572872 | tf_op jit(solution)/shard_map/ppermute | solution.py:457
  18.3 71.9 %collective-permute-start.4 = (bf16[256,1664]{1,0:T(8,128)(2,1)}, bf16[256,1664]{1,0:T(8,128)(2,1)}, u32[]{:S(2)}, u32[]{:S(2)}) collective-permute-start(bf16[256,1664]{1,0:T(8,128)(2,1)} %concatenate.25.refs_2_), channel_id=1, source_target_pairs={{0,1},{1,0},{2,3},{3,2},{4,5},{5,4},{6,7},{7,6},{8,9},{9,8},{10,11... | collective-permute-start | bytes 2555912 | tf_op jit(solution)/shard_map/ppermute | solution.py:457
  19.8 23.4 %collective-permute-start.8 = (bf16[256,1664]{1,0:T(8,128)(2,1)}, bf16[256,1664]{1,0:T(8,128)(2,1)}, u32[]{:S(2)}, u32[]{:S(2)}) collective-permute-start(bf16[256,1664]{1,0:T(8,128)(2,1)} %concatenate.25.refs_2_), channel_id=1, source_target_pairs={{0,2},{1,3},{2,4},{3,5},{4,6},{5,7},{6,0},{7,1},{8,14},{9,15},{10,... | collective-permute-start | bytes 2555912 | tf_op jit(solution)/shard_map/ppermute | solution.py:475
  43.2 48.5 %collective-permute-start.13 = (bf16[256,1664]{1,0:T(8,128)(2,1)}, bf16[256,1664]{1,0:T(8,128)(2,1)}, u32[]{:S(2)}, u32[]{:S(2)}) collective-permute-start(bf16[256,1664]{1,0:T(8,128)(2,1)} %collective-permute-done.8.refs_2_), channel_id=1, source_target_pairs={{0,2},{1,3},{2,4},{3,5},{4,6},{5,7},{6,0},{7,1},{8,14},{9,15},{10,... | collective-permute-start | bytes 2555912 | tf_op jit(solution)/shard_map/ppermute | solution.py:475
  60.5 33.4 %collective-permute-start.3 = (bf16[256,1536]{1,0:T(8,128)(2,1)}, bf16[256,1536]{1,0:T(8,128)(2,1)}, u32[]{:S(2)}, u32[]{:S(2)}) collective-permute-start(bf16[256,1536]{1,0:T(8,128)(2,1)} %get-tuple-element.71.refs_0_), channel_id=1, source_target_pairs={{0,1},{1,0},{2,3},{3,2},{4,5},{5,4},{6,7},{7,6},{8,9},{9,8},{10,11... | collective-permute-start | bytes 2359304 | tf_op jit(solution)/shard_map/ppermute | solution.py:457
  61.0 32.3 %collective-permute-start.6 = (bf16[256,1536]{1,0:T(8,128)(2,1)}, bf16[256,1536]{1,0:T(8,128)(2,1)}, u32[]{:S(2)}, u32[]{:S(2)}) collective-permute-start(bf16[256,1536]{1,0:T(8,128)(2,1)} %get-tuple-element.71.refs_0_), channel_id=1, source_target_pairs={{0,2},{1,3},{2,4},{3,5},{4,6},{5,7},{6,0},{7,1},{8,14},{9,15},{10,... | collective-permute-start | bytes 2359304 | tf_op jit(solution)/shard_map/ppermute | solution.py:475
  79.8 35.2 %collective-permute-start.70 = (bf16[512,1536]{1,0:T(8,128)(2,1)}, bf16[512,1536]{1,0:T(8,128)(2,1)}, u32[]{:S(2)}, u32[]{:S(2)}) collective-permute-start(bf16[512,1536]{1,0:T(8,128)(2,1)} %convolution_convert_fusion.6), channel_id=1, source_target_pairs={{0,8},{8,0},{16,24},{24,16},{1,9},{9,1},{17,25},{25,17},{2,10},{10... | collective-permute-start | bytes 4718600 | tf_op jit(solution)/shard_map/ppermute | solution.py:457
  90.2 29.8 %collective-permute-start.9 = (bf16[256,1664]{1,0:T(8,128)(2,1)}, bf16[256,1664]{1,0:T(8,128)(2,1)S(1)}, u32[]{:S(2)}, u32[]{:S(2)}) collective-permute-start(bf16[256,1664]{1,0:T(8,128)(2,1)} %collective-permute-done.8.refs_2_), channel_id=1, source_target_pairs={{0,1},{1,0},{2,3},{3,2},{4,5},{5,4},{6,7},{7,6},{8,9},{9,8},{10,11... | collective-permute-start | bytes 2555912 | tf_op jit(solution)/shard_map/ppermute | solution.py:457
  91.7 29.8 %collective-permute-start.18 = (bf16[256,1664]{1,0:T(8,128)(2,1)}, bf16[256,1664]{1,0:T(8,128)(2,1)S(1)}, u32[]{:S(2)}, u32[]{:S(2)}) collective-permute-start(bf16[256,1664]{1,0:T(8,128)(2,1)} %collective-permute-done.13.refs_2_), channel_id=1, source_target_pairs={{0,2},{1,3},{2,4},{3,5},{4,6},{5,7},{6,0},{7,1},{8,14},{9,15},{10,... | collective-permute-start | bytes 2555912 | tf_op jit(solution)/shard_map/ppermute | solution.py:475
  93.3 39.2 %collective-permute-start.7 = (bf16[256,1536]{1,0:T(8,128)(2,1)}, bf16[256,1536]{1,0:T(8,128)(2,1)}, u32[]{:S(2)}, u32[]{:S(2)}) collective-permute-start(bf16[256,1536]{1,0:T(8,128)(2,1)} %collective-permute-done.6.refs_0_), channel_id=1, source_target_pairs={{0,1},{1,0},{2,3},{3,2},{4,5},{5,4},{6,7},{7,6},{8,9},{9,8},{10,11... | collective-permute-start | bytes 2359304 | tf_op jit(solution)/shard_map/ppermute | solution.py:457
  93.9 38.1 %collective-permute-start.11 = (bf16[256,1536]{1,0:T(8,128)(2,1)}, bf16[256,1536]{1,0:T(8,128)(2,1)}, u32[]{:S(2)}, u32[]{:S(2)}) collective-permute-start(bf16[256,1536]{1,0:T(8,128)(2,1)} %collective-permute-done.6.refs_0_), channel_id=1, source_target_pairs={{0,2},{1,3},{2,4},{3,5},{4,6},{5,7},{6,0},{7,1},{8,14},{9,15},{10,... | collective-permute-start | bytes 2359304 | tf_op jit(solution)/shard_map/ppermute | solution.py:475
  115.1 154.9 %collective-permute-start.64 = (bf16[768,2048]{1,0:T(8,128)(2,1)}, bf16[768,2048]{1,0:T(8,128)(2,1)}, u32[]{:S(2)}, u32[]{:S(2)}) collective-permute-start(bf16[768,2048]{1,0:T(8,128)(2,1)} %convolution_convert_fusion.2), channel_id=1, source_target_pairs={{0,8},{8,0},{16,24},{24,16},{1,9},{9,1},{17,25},{25,17},{2,10},{10... | collective-permute-start | bytes 9437192 | tf_op jit(solution)/shard_map/ppermute | solution.py:457
  120.0 32.5 %collective-permute-start.14 = (bf16[256,1664]{1,0:T(8,128)(2,1)}, bf16[256,1664]{1,0:T(8,128)(2,1)S(1)}, u32[]{:S(2)}, u32[]{:S(2)}) collective-permute-start(bf16[256,1664]{1,0:T(8,128)(2,1)} %collective-permute-done.13.refs_2_), channel_id=1, source_target_pairs={{0,1},{1,0},{2,3},{3,2},{4,5},{5,4},{6,7},{7,6},{8,9},{9,8},{10,11... | collective-permute-start | bytes 2555912 | tf_op jit(solution)/shard_map/ppermute | solution.py:457
  121.5 80.5 %collective-permute-start.19 = (bf16[256,1664]{1,0:T(8,128)(2,1)S(1)}, bf16[256,1664]{1,0:T(8,128)(2,1)S(1)}, u32[]{:S(2)}, u32[]{:S(2)}) collective-permute-start(bf16[256,1664]{1,0:T(8,128)(2,1)S(1)} %collective-permute-done.18.refs_2_), channel_id=1, source_target_pairs={{0,1},{1,0},{2,3},{3,2},{4,5},{5,4},{6,7},{7,6},{8,9},{9,8},{10,11... | collective-permute-start | bytes 2555912 | tf_op jit(solution)/shard_map/ppermute | solution.py:457
  131.9 50.6 %collective-permute-start.12 = (bf16[256,1536]{1,0:T(8,128)(2,1)}, bf16[256,1536]{1,0:T(8,128)(2,1)}, u32[]{:S(2)}, u32[]{:S(2)}) collective-permute-start(bf16[256,1536]{1,0:T(8,128)(2,1)} %collective-permute-done.11.refs_0_), channel_id=1, source_target_pairs={{0,1},{1,0},{2,3},{3,2},{4,5},{5,4},{6,7},{7,6},{8,9},{9,8},{10,11... | collective-permute-start | bytes 2359304 | tf_op jit(solution)/shard_map/ppermute | solution.py:457
  132.5 20.6 %collective-permute-start.16 = (bf16[256,1536]{1,0:T(8,128)(2,1)}, bf16[256,1536]{1,0:T(8,128)(2,1)}, u32[]{:S(2)}, u32[]{:S(2)}) collective-permute-start(bf16[256,1536]{1,0:T(8,128)(2,1)} %collective-permute-done.11.refs_0_), channel_id=1, source_target_pairs={{0,2},{1,3},{2,4},{3,5},{4,6},{5,7},{6,0},{7,1},{8,14},{9,15},{10,... | collective-permute-start | bytes 2359304 | tf_op jit(solution)/shard_map/ppermute | solution.py:475
  152.5 81.7 %collective-permute-start.71 = (bf16[4,2,32,1536]{3,2,0,1:T(8,128)(2,1)}, bf16[4,2,32,1536]{3,2,0,1:T(8,128)(2,1)}, u32[]{:S(2)}, u32[]{:S(2)}) collective-permute-start(bf16[4,2,32,1536]{3,2,0,1:T(8,128)(2,1)} %fusion.5), channel_id=1, source_target_pairs={{0,16},{8,24},{16,0},{24,8},{1,17},{9,25},{17,1},{25,9},{2,18},{10... | collective-permute-start | bytes 2359304 | tf_op jit(solution)/shard_map/ppermute | solution.py:463
  153.1 48.9 %collective-permute-start.17 = (bf16[256,1536]{1,0:T(8,128)(2,1)}, bf16[256,1536]{1,0:T(8,128)(2,1)S(1)}, u32[]{:S(2)}, u32[]{:S(2)}) collective-permute-start(bf16[256,1536]{1,0:T(8,128)(2,1)} %collective-permute-done.16.refs_0_), channel_id=1, source_target_pairs={{0,1},{1,0},{2,3},{3,2},{4,5},{5,4},{6,7},{7,6},{8,9},{9,8},{10,11... | collective-permute-start | bytes 2359304 | tf_op jit(solution)/shard_map/ppermute | solution.py:457
  234.2 413.3 %reduce-scatter.3.cloned.1.call-start = ((), (), s32[]{:S(2)}) async-start(), calls=%async_computation.2 | async-start | bytes 7864320 | tf_op jit(solution)/shard_map/reduce_scatter | solution.py:631
  266.2 164.6 %collective-permute-start.24 = (bf16[256,1536]{1,0:T(8,128)(2,1)}, bf16[256,1536]{1,0:T(8,128)(2,1)}, u32[]{:S(2)}, u32[]{:S(2)}) collective-permute-start(bf16[256,1536]{1,0:T(8,128)(2,1)} %get-tuple-element.95), channel_id=1, source_target_pairs={{0,1},{1,0},{2,3},{3,2},{4,5},{5,4},{6,7},{7,6},{8,9},{9,8},{10,11... | collective-permute-start | bytes 2359304 | tf_op jit(solution)/shard_map/ppermute | solution.py:457
  266.7 76.0 %collective-permute-start.26 = (bf16[256,1536]{1,0:T(8,128)(2,1)}, bf16[256,1536]{1,0:T(8,128)(2,1)}, u32[]{:S(2)}, u32[]{:S(2)}) collective-permute-start(bf16[256,1536]{1,0:T(8,128)(2,1)} %get-tuple-element.99), channel_id=1, source_target_pairs={{0,1},{1,0},{2,3},{3,2},{4,5},{5,4},{6,7},{7,6},{8,9},{9,8},{10,11... | collective-permute-start | bytes 2359304 | tf_op jit(solution)/shard_map/ppermute | solution.py:457
  277.2 61.0 %collective-permute-start.65 = (bf16[4,2,48,2048]{3,2,1,0:T(8,128)(2,1)}, bf16[4,2,48,2048]{3,2,1,0:T(8,128)(2,1)}, u32[]{:S(2)}, u32[]{:S(2)}) collective-permute-start(bf16[4,2,48,2048]{3,2,1,0:T(8,128)(2,1)} %fusion), channel_id=1, source_target_pairs={{0,16},{8,24},{16,0},{24,8},{1,17},{9,25},{17,1},{25,9},{2,18},{10... | collective-permute-start | bytes 4718600 | tf_op jit(solution)/shard_map/ppermute | solution.py:463
  277.5 43.2 %collective-permute-start.27 = (bf16[256,1536]{1,0:T(8,128)(2,1)}, bf16[256,1536]{1,0:T(8,128)(2,1)}, u32[]{:S(2)}, u32[]{:S(2)}) collective-permute-start(bf16[256,1536]{1,0:T(8,128)(2,1)} %get-tuple-element.101), channel_id=1, source_target_pairs={{0,1},{1,0},{2,3},{3,2},{4,5},{5,4},{6,7},{7,6},{8,9},{9,8},{10,11... | collective-permute-start | bytes 2359304 | tf_op jit(solution)/shard_map/ppermute | solution.py:457
  278.1 59.3 %collective-permute-start.20 = (bf16[256,1536]{1,0:T(8,128)(2,1)}, bf16[256,1536]{1,0:T(8,128)(2,1)S(1)}, u32[]{:S(2)}, u32[]{:S(2)}) collective-permute-start(bf16[256,1536]{1,0:T(8,128)(2,1)} %get-tuple-element.92), channel_id=1, source_target_pairs={{0,1},{1,0},{2,3},{3,2},{4,5},{5,4},{6,7},{7,6},{8,9},{9,8},{10,11... | collective-permute-start | bytes 2359304 | tf_op jit(solution)/shard_map/ppermute | solution.py:457
  320.7 39.3 %collective-permute-start.15 = (bf16[256,1536]{1,0:T(8,128)(2,1)}, bf16[256,1536]{1,0:T(8,128)(2,1)S(1)}, u32[]{:S(2)}, u32[]{:S(2)}) collective-permute-start(bf16[256,1536]{1,0:T(8,128)(2,1)} %get-tuple-element.86), channel_id=1, source_target_pairs={{0,1},{1,0},{2,3},{3,2},{4,5},{5,4},{6,7},{7,6},{8,9},{9,8},{10,11... | collective-permute-start | bytes 2359304 | tf_op jit(solution)/shard_map/ppermute | solution.py:457
  337.4 20.6 %collective-permute-start.28 = (bf16[256,1536]{1,0:T(8,128)(2,1)S(1)}, bf16[256,1536]{1,0:T(8,128)(2,1)S(1)}, u32[]{:S(2)}, u32[]{:S(2)}) collective-permute-start(bf16[256,1536]{1,0:T(8,128)(2,1)S(1)} %add_convert_fusion.2), channel_id=1, source_target_pairs={{0,6},{1,7},{2,0},{3,1},{4,2},{5,3},{6,4},{7,5},{8,10},{9,11},{10,... | collective-permute-start | bytes 2359304 | tf_op jit(solution)/shard_map/ppermute | solution.py:475
  338.1 32.2 %collective-permute-start.21 = (bf16[256,1536]{1,0:T(8,128)(2,1)S(1)}, bf16[256,1536]{1,0:T(8,128)(2,1)S(1)}, u32[]{:S(2)}, u32[]{:S(2)}) collective-permute-start(bf16[256,1536]{1,0:T(8,128)(2,1)S(1)} %add_convert_fusion.6), channel_id=1, source_target_pairs={{0,6},{1,7},{2,0},{3,1},{4,2},{5,3},{6,4},{7,5},{8,10},{9,11},{10,... | collective-permute-start | bytes 2359304 | tf_op jit(solution)/shard_map/ppermute | solution.py:475
  343.6 45.1 %collective-permute-start.25 = (bf16[256,1536]{1,0:T(8,128)(2,1)S(1)}, bf16[256,1536]{1,0:T(8,128)(2,1)S(1)}, u32[]{:S(2)}, u32[]{:S(2)}) collective-permute-start(bf16[256,1536]{1,0:T(8,128)(2,1)S(1)} %copy-done.42), channel_id=1, source_target_pairs={{0,1},{1,0},{2,3},{3,2},{4,5},{5,4},{6,7},{7,6},{8,9},{9,8},{10,11... | collective-permute-start | bytes 2359304 | tf_op jit(solution)/shard_map/ppermute | solution.py:457
  358.0 29.9 %collective-permute-start.66 = (bf16[4,48,2048]{2,1,0:T(8,128)(2,1)S(1)}, bf16[4,48,2048]{2,1,0:T(8,128)(2,1)S(1)}, u32[]{:S(2)}, u32[]{:S(2)}) collective-permute-start(bf16[4,48,2048]{2,1,0:T(8,128)(2,1)S(1)} %fusion.4), channel_id=1, source_target_pairs={{0,1},{1,0},{2,3},{3,2},{4,5},{5,4},{6,7},{7,6},{8,9},{9,8},{10,11... | collective-permute-start | bytes 2359304 | tf_op jit(solution)/shard_map/ppermute | solution.py:457
  360.0 41.9 %collective-permute-start.10 = (bf16[256,1536]{1,0:T(8,128)(2,1)S(1)}, bf16[256,1536]{1,0:T(8,128)(2,1)S(1)}, u32[]{:S(2)}, u32[]{:S(2)}) collective-permute-start(bf16[256,1536]{1,0:T(8,128)(2,1)S(1)} %copy-done.41), channel_id=1, source_target_pairs={{0,1},{1,0},{2,3},{3,2},{4,5},{5,4},{6,7},{7,6},{8,9},{9,8},{10,11... | collective-permute-start | bytes 2359304 | tf_op jit(solution)/shard_map/ppermute | solution.py:457
  370.4 20.0 %collective-permute-start.29 = (bf16[256,1536]{1,0:T(8,128)(2,1)S(1)}, bf16[256,1536]{1,0:T(8,128)(2,1)S(1)}, u32[]{:S(2)}, u32[]{:S(2)}) collective-permute-start(bf16[256,1536]{1,0:T(8,128)(2,1)S(1)} %add_convert_fusion.1), channel_id=1, source_target_pairs={{0,6},{1,7},{2,0},{3,1},{4,2},{5,3},{6,4},{7,5},{8,10},{9,11},{10,... | collective-permute-start | bytes 2359304 | tf_op jit(solution)/shard_map/ppermute | solution.py:475
  388.0 23.4 %collective-permute-start.22 = (bf16[256,1536]{1,0:T(8,128)(2,1)S(1)}, bf16[256,1536]{1,0:T(8,128)(2,1)S(1)}, u32[]{:S(2)}, u32[]{:S(2)}) collective-permute-start(bf16[256,1536]{1,0:T(8,128)(2,1)S(1)} %add_convert_fusion.5), channel_id=1, source_target_pairs={{0,6},{1,7},{2,0},{3,1},{4,2},{5,3},{6,4},{7,5},{8,10},{9,11},{10,... | collective-permute-start | bytes 2359304 | tf_op jit(solution)/shard_map/ppermute | solution.py:475
  388.8 24.0 %collective-permute-start.67 = (bf16[48,2048]{1,0:T(8,128)(2,1)S(1)}, bf16[48,2048]{1,0:T(8,128)(2,1)S(1)}, u32[]{:S(2)}, u32[]{:S(2)}) collective-permute-start(bf16[48,2048]{1,0:T(8,128)(2,1)S(1)} %get-tuple-element.127), channel_id=1, source_target_pairs={{0,2},{1,3},{2,4},{3,5},{4,6},{5,7},{6,0},{7,1},{8,10},{9,11},{10,... | collective-permute-start | bytes 589832 | tf_op jit(solution)/shard_map/ppermute | solution.py:463
  390.4 37.5 %collective-permute-start.68 = (bf16[48,2048]{1,0:T(8,128)(2,1)S(1)}, bf16[48,2048]{1,0:T(8,128)(2,1)S(1)}, u32[]{:S(2)}, u32[]{:S(2)}) collective-permute-start(bf16[48,2048]{1,0:T(8,128)(2,1)S(1)} %get-tuple-element.129), channel_id=1, source_target_pairs={{0,4},{1,5},{2,6},{3,7},{4,0},{5,1},{6,2},{7,3},{8,12},{9,13},{10,... | collective-permute-start | bytes 589832 | tf_op jit(solution)/shard_map/ppermute | solution.py:463
  401.8 26.0 %collective-permute-start.69 = (bf16[48,2048]{1,0:T(8,128)(2,1)S(1)}, bf16[48,2048]{1,0:T(8,128)(2,1)S(1)}, u32[]{:S(2)}, u32[]{:S(2)}) collective-permute-start(bf16[48,2048]{1,0:T(8,128)(2,1)S(1)} %get-tuple-element.128), channel_id=1, source_target_pairs={{0,6},{1,7},{2,0},{3,1},{4,2},{5,3},{6,4},{7,5},{8,14},{9,15},{10,... | collective-permute-start | bytes 589832 | tf_op jit(solution)/shard_map/ppermute | solution.py:463
  411.3 32.2 %collective-permute-start.30 = (bf16[256,1536]{1,0:T(8,128)(2,1)}, bf16[256,1536]{1,0:T(8,128)(2,1)S(1)}, u32[]{:S(2)}, u32[]{:S(2)}) collective-permute-start(bf16[256,1536]{1,0:T(8,128)(2,1)} %add_convert_fusion), channel_id=1, source_target_pairs={{0,6},{1,7},{2,0},{3,1},{4,2},{5,3},{6,4},{7,5},{8,10},{9,11},{10,... | collective-permute-start | bytes 2359304 | tf_op jit(solution)/shard_map/ppermute | solution.py:475
  412.8 66.1 %collective-permute-start.5 = (bf16[256,1536]{1,0:T(8,128)(2,1)}, bf16[256,1536]{1,0:T(8,128)(2,1)}, u32[]{:S(2)}, u32[]{:S(2)}) collective-permute-start(bf16[256,1536]{1,0:T(8,128)(2,1)} %get-tuple-element.74), channel_id=1, source_target_pairs={{0,1},{1,0},{2,3},{3,2},{4,5},{5,4},{6,7},{7,6},{8,9},{9,8},{10,11... | collective-permute-start | bytes 2359304 | tf_op jit(solution)/shard_map/ppermute | solution.py:457
  427.8 51.9 %collective-permute-start.23 = (bf16[256,1536]{1,0:T(8,128)(2,1)}, bf16[256,1536]{1,0:T(8,128)(2,1)}, u32[]{:S(2)}, u32[]{:S(2)}) collective-permute-start(bf16[256,1536]{1,0:T(8,128)(2,1)} %add_convert_fusion.4), channel_id=1, source_target_pairs={{0,6},{1,7},{2,0},{3,1},{4,2},{5,3},{6,4},{7,5},{8,10},{9,11},{10,... | collective-permute-start | bytes 2359304 | tf_op jit(solution)/shard_map/ppermute | solution.py:475
  476.2 53.1 %collective-permute-start.40 = (bf16[768,768]{1,0:T(8,128)(2,1)}, bf16[768,768]{1,0:T(8,128)(2,1)}, u32[]{:S(2)}, u32[]{:S(2)}) collective-permute-start(bf16[768,768]{1,0:T(8,128)(2,1)} %convolution_convert_fusion.13), channel_id=1, source_target_pairs={{0,8},{8,0},{16,24},{24,16},{1,9},{9,1},{17,25},{25,17},{2,10},{10... | collective-permute-start | bytes 3538952 | tf_op jit(solution)/shard_map/ppermute | solution.py:457
  477.0 46.4 %collective-permute-start.46 = (bf16[768,768]{1,0:T(8,128)(2,1)}, bf16[768,768]{1,0:T(8,128)(2,1)}, u32[]{:S(2)}, u32[]{:S(2)}) collective-permute-start(bf16[768,768]{1,0:T(8,128)(2,1)} %convolution_convert_fusion.11), channel_id=1, source_target_pairs={{0,8},{8,0},{16,24},{24,16},{1,9},{9,1},{17,25},{25,17},{2,10},{10... | collective-permute-start | bytes 3538952 | tf_op jit(solution)/shard_map/ppermute | solution.py:457
  522.1 42.0 %collective-permute-start.58 = (bf16[768,1536]{1,0:T(8,128)(2,1)S(1)}, bf16[768,1536]{1,0:T(8,128)(2,1)S(1)}, u32[]{:S(2)}, u32[]{:S(2)}) collective-permute-start(bf16[768,1536]{1,0:T(8,128)(2,1)S(1)} %copy-done.19), channel_id=1, source_target_pairs={{0,8},{8,0},{16,24},{24,16},{1,9},{9,1},{17,25},{25,17},{2,10},{10... | collective-permute-start | bytes 7077896 | tf_op jit(solution)/shard_map/ppermute | solution.py:457
  523.4 44.4 %collective-permute-start.52 = (bf16[768,1024]{1,0:T(8,128)(2,1)S(1)}, bf16[768,1024]{1,0:T(8,128)(2,1)S(1)}, u32[]{:S(2)}, u32[]{:S(2)}) collective-permute-start(bf16[768,1024]{1,0:T(8,128)(2,1)S(1)} %convolution_convert_fusion.9), channel_id=1, source_target_pairs={{0,8},{8,0},{16,24},{24,16},{1,9},{9,1},{17,25},{25,17},{2,10},{10... | collective-permute-start | bytes 4718600 | tf_op jit(solution)/shard_map/ppermute | solution.py:457
  526.1 23.0 %collective-permute-start.48 = (bf16[2,2,48,768]{3,2,0,1:T(8,128)(2,1)S(1)}, bf16[2,2,48,768]{3,2,0,1:T(8,128)(2,1)S(1)}, u32[]{:S(2)}, u32[]{:S(2)}) collective-permute-start(bf16[2,2,48,768]{3,2,0,1:T(8,128)(2,1)S(1)} %bitcast.300), channel_id=1, source_target_pairs={{0,4},{1,5},{2,6},{3,7},{4,0},{5,1},{6,2},{7,3},{8,12},{9,13},{10,... | collective-permute-start | bytes 884744 | tf_op jit(solution)/shard_map/ppermute | solution.py:463
  567.8 42.9 %collective-permute-start.59 = (bf16[4,2,48,1536]{3,2,0,1:T(8,128)(2,1)S(1)}, bf16[4,2,48,1536]{3,2,0,1:T(8,128)(2,1)S(1)}, u32[]{:S(2)}, u32[]{:S(2)}) collective-permute-start(bf16[4,2,48,1536]{3,2,0,1:T(8,128)(2,1)S(1)} %fusion.1), channel_id=1, source_target_pairs={{0,16},{8,24},{16,0},{24,8},{1,17},{9,25},{17,1},{25,9},{2,18},{10... | collective-permute-start | bytes 3538952 | tf_op jit(solution)/shard_map/ppermute | solution.py:463
  569.9 40.0 %collective-permute-start.53 = (bf16[4,2,48,1024]{3,2,1,0:T(8,128)(2,1)S(1)}, bf16[4,2,48,1024]{3,2,1,0:T(8,128)(2,1)S(1)}, u32[]{:S(2)}, u32[]{:S(2)}) collective-permute-start(bf16[4,2,48,1024]{3,2,1,0:T(8,128)(2,1)S(1)} %fusion.3), channel_id=1, source_target_pairs={{0,16},{8,24},{16,0},{24,8},{1,17},{9,25},{17,1},{25,9},{2,18},{10... | collective-permute-start | bytes 2359304 | tf_op jit(solution)/shard_map/ppermute | solution.py:463
  571.5 38.4 %collective-permute-start.45 = (bf16[48,768]{1,0:T(8,128)(2,1)S(1)}, bf16[48,768]{1,0:T(8,128)(2,1)S(1)}, u32[]{:S(2)}, u32[]{:S(2)}) collective-permute-start(bf16[48,768]{1,0:T(8,128)(2,1)S(1)} %fusion.45), channel_id=1, source_target_pairs={{0,16},{8,24},{16,0},{24,8},{1,17},{9,25},{17,1},{25,9},{2,18},{10... | collective-permute-start | bytes 221192 | tf_op jit(solution)/shard_map/ppermute | solution.py:463
  611.9 21.3 %collective-permute-start.60 = (bf16[4,48,1536]{2,1,0:T(8,128)(2,1)}, bf16[4,48,1536]{2,1,0:T(8,128)(2,1)}, u32[]{:S(2)}, u32[]{:S(2)}) collective-permute-start(bf16[4,48,1536]{2,1,0:T(8,128)(2,1)} %fusion.6), channel_id=1, source_target_pairs={{0,1},{1,0},{2,3},{3,2},{4,5},{5,4},{6,7},{7,6},{8,9},{9,8},{10,11... | collective-permute-start | bytes 1769480 | tf_op jit(solution)/shard_map/ppermute | solution.py:457
  (78 other events, 708.1 us)
Sparse Core Ops, SparseCore 0:
  234.3 37.1 reduce-scatter.4
  297.6 55.8 reduce-scatter.2

commit v2 on v1

v2 whole, which is shorter than its diff:
```python
import functools

import jax
import jax.numpy as jnp
from jax import lax
from jax.experimental import pallas as pl
from jax.experimental.pallas import tpu as pltpu
from jax.sharding import PartitionSpec as P

H = 12
HD = 128
KVH = 4
GROUPS = H // KVH
EPSILON = 1e-06
GATE_LANES = 128
LOW_LANE = 64
NEGATIVE = -1e30
SCALE = HD ** (-0.5)
BOTH = ("ctx", "exp")
VMEM_LIMIT = 60 * 2**20
bf16 = jnp.bfloat16
f32 = jnp.float32


def dot(left_op, right_op):
    return jnp.dot(left_op, right_op, preferred_element_type=f32)


def dot_nt(left_op, right_op):
    return lax.dot_general(left_op, right_op, (((1,), (1,)), ((), ())), preferred_element_type=f32)


def dot_tn(left_op, right_op):
    return lax.dot_general(left_op, right_op, (((0,), (0,)), ((), ())), preferred_element_type=f32)


def whole(shape):
    return pl.BlockSpec(shape, lambda *_: (0,) * len(shape))


def params():
    return pltpu.CompilerParams(vmem_limit_bytes=VMEM_LIMIT)


def anywhere(count):
    return [pl.BlockSpec(memory_space=pl.ANY)] * count


def cost(flops, nbytes):
    return pl.CostEstimate(flops=flops // 4, bytes_accessed=nbytes // 4, transcendentals=0)


def keyvalue_kernel(x_ref, gain_ref, wk_ref, wv_ref, normed_ref, kv_ref):
    @pl.when(pl.program_id(0) == 0)
    def _():
        x = x_ref[...].astype(f32)
        factor = lax.rsqrt(jnp.mean(x * x, axis=-1, keepdims=True) + EPSILON)
        normed_ref[...] = (x * factor * gain_ref[...]).astype(bf16)

    both = jnp.concatenate([wk_ref[...], wv_ref[...]], axis=1)
    kv_ref[...] = dot(normed_ref[...], both).astype(bf16)


def keyvalue(x, gain, wk, wv):
    rows, width = x.shape
    return pl.pallas_call(
        keyvalue_kernel,
        grid=(KVH,),
        in_specs=[
            whole((rows, width)),
            whole((1, width)),
            pl.BlockSpec((width, HD), lambda g: (0, g)),
            pl.BlockSpec((width, HD), lambda g: (0, g)),
        ],
        out_specs=[whole((rows, width)), pl.BlockSpec((rows, 2 * HD), lambda g: (0, g))],
        out_shape=[
            jax.ShapeDtypeStruct((rows, width), bf16),
            jax.ShapeDtypeStruct((rows, 2 * KVH * HD), bf16),
        ],
        compiler_params=params(),
        cost_estimate=cost(4 * rows * width * KVH * HD, 5 * 2**20),
    )(x, gain.reshape(1, width), wk, wv)


def stack_heads(ref):
    return jnp.concatenate([ref[:, r * HD : (r + 1) * HD] for r in range(GROUPS)], axis=0)


def places(pos, spans, block, shape, dim, rows):
    outer, side = (0, 0) if block is None else (block // 2, block % 2)
    ring = spans.shape[0] // 4
    owner = 2 * lax.rem(pos[0] + ring - outer, ring) + lax.rem(pos[1] + side, 2)
    row = lax.broadcasted_iota(jnp.int32, shape, dim) % rows
    half = rows // 2
    first, second = spans[2 * owner] * half, spans[2 * owner + 1] * half
    return jnp.where(row < half, first + row, second + row - half)


def attend_kernel(blocks, extra, pos, spans, q_ref, *refs):
    kv_refs = refs[:blocks]
    out_ref, lse_ref, score_ref = refs[blocks + extra :]
    rows = q_ref.shape[0]
    queries = stack_heads(q_ref)
    wanted = places(pos, spans, None, (1, GROUPS * rows), 1, rows)
    peak = jnp.full((1, GROUPS * rows), NEGATIVE, f32)
    for b in range(blocks):
        scores = dot_nt(kv_refs[b][:, :HD], queries) * SCALE
        visible = places(pos, spans, b, (rows, 1), 0, rows) <= wanted
        scores = jnp.where(visible, scores, NEGATIVE)
        score_ref[b * rows : (b + 1) * rows, :] = scores
        peak = jnp.maximum(peak, jnp.max(scores, axis=0, keepdims=True))
    total = jnp.zeros_like(peak)
    mixed = jnp.zeros((HD, GROUPS * rows), f32)
    for b in range(blocks):
        weights = jnp.exp(score_ref[b * rows : (b + 1) * rows, :] - peak)
        total = total + jnp.sum(weights, axis=0, keepdims=True)
        mixed = mixed + dot_tn(kv_refs[b][:, HD:], weights.astype(bf16))
    lse_ref[0] = peak + jnp.log(total)
    mixed = jnp.transpose(mixed / total)
    for r in range(GROUPS):
        out_ref[:, r * HD : (r + 1) * HD] = mixed[r * rows : (r + 1) * rows].astype(bf16)


def attend(pos, spans, queries, kv_blocks, after=()):
    rows = queries.shape[0]
    blocks = len(kv_blocks)
    wide = GROUPS * HD
    return pl.pallas_call(
        functools.partial(attend_kernel, blocks, len(after)),
        grid_spec=pltpu.PrefetchScalarGridSpec(
            num_scalar_prefetch=2,
            grid=(KVH,),
            in_specs=[pl.BlockSpec((rows, wide), lambda g, *_: (0, g))]
            + [pl.BlockSpec((rows, 2 * HD), lambda g, *_: (0, g))] * blocks
            + anywhere(len(after)),
            out_specs=[
                pl.BlockSpec((rows, wide), lambda g, *_: (0, g)),
                pl.BlockSpec((1, 1, GROUPS * rows), lambda g, *_: (g, 0, 0)),
            ],
            scratch_shapes=[pltpu.VMEM((blocks * rows, GROUPS * rows), f32)],
        ),
        out_shape=[
            jax.ShapeDtypeStruct((rows, H * HD), bf16),
            jax.ShapeDtypeStruct((KVH, 1, GROUPS * rows), f32),
        ],
        compiler_params=params(),
        cost_estimate=cost(8 * rows * rows * blocks * H * HD, 4 * 2**20),
    )(pos, spans, queries, *kv_blocks, *after)


def attend_back_kernel(blocks, extra, pos, spans, q_ref, grad_ref, lse_ref, *refs):
    kv_refs = refs[:blocks]
    dq_ref, same_ref, other_ref = refs[blocks + extra : -2]
    prob_ref, slope_ref = refs[-2:]
    rows = q_ref.shape[0]
    queries = stack_heads(q_ref)
    grads = stack_heads(grad_ref)
    wanted = places(pos, spans, None, (1, GROUPS * rows), 1, rows)
    lse = lse_ref[0]
    delta = jnp.zeros((1, GROUPS * rows), f32)
    for b in range(blocks):
        part = slice(b * rows, (b + 1) * rows)
        scores = dot_nt(kv_refs[b][:, :HD], queries) * SCALE - lse
        visible = places(pos, spans, b, (rows, 1), 0, rows) <= wanted
        prob = jnp.exp(jnp.where(visible, scores, NEGATIVE))
        slope = dot_nt(kv_refs[b][:, HD:], grads)
        delta = delta + jnp.sum(prob * slope, axis=0, keepdims=True)
        prob_ref[part, :] = prob
        slope_ref[part, :] = slope
        dkv_ref = other_ref if b % 2 else same_ref
        dkv_ref[rows * (b // 2) : rows * (b // 2 + 1), HD:] = dot(prob.astype(bf16), grads).astype(bf16)
    query_grad = jnp.zeros((HD, GROUPS * rows), f32)
    for b in range(blocks):
        part = slice(b * rows, (b + 1) * rows)
        dscore = (prob_ref[part, :] * (slope_ref[part, :] - delta) * SCALE).astype(bf16)
        dkv_ref = other_ref if b % 2 else same_ref
        dkv_ref[rows * (b // 2) : rows * (b // 2 + 1), :HD] = dot(dscore, queries).astype(bf16)
        query_grad = query_grad + dot_tn(kv_refs[b][:, :HD], dscore)
    query_grad = jnp.transpose(query_grad)
    for r in range(GROUPS):
        dq_ref[:, r * HD : (r + 1) * HD] = query_grad[r * rows : (r + 1) * rows].astype(bf16)


def attend_back(pos, spans, queries, grads, lse, kv_blocks, after=()):
    rows = queries.shape[0]
    blocks = len(kv_blocks)
    wide = GROUPS * HD
    by_group = pl.BlockSpec((rows, wide), lambda g, *_: (0, g))
    kv_spec = pl.BlockSpec((rows, 2 * HD), lambda g, *_: (0, g))
    return pl.pallas_call(
        functools.partial(attend_back_kernel, blocks, len(after)),
        grid_spec=pltpu.PrefetchScalarGridSpec(
            num_scalar_prefetch=2,
            grid=(KVH,),
            in_specs=[
                by_group,
                by_group,
                pl.BlockSpec((1, 1, GROUPS * rows), lambda g, *_: (g, 0, 0)),
            ]
            + [kv_spec] * blocks
            + anywhere(len(after)),
            out_specs=[by_group]
            + [pl.BlockSpec((blocks // 2 * rows, 2 * HD), lambda g, *_: (0, g))] * 2,
            scratch_shapes=[pltpu.VMEM((blocks * rows, GROUPS * rows), f32)] * 2,
        ),
        out_shape=[jax.ShapeDtypeStruct((rows, H * HD), bf16)]
        + [jax.ShapeDtypeStruct((blocks // 2 * rows, 2 * KVH * HD), bf16)] * 2,
        compiler_params=params(),
        cost_estimate=cost(20 * rows * rows * blocks * H * HD, 8 * 2**20),
    )(pos, spans, queries, grads, lse, *kv_blocks, *after)


def middle_kernel(x_ref, att_ref, w_ref, gain_ref, middle_ref, rows_ref):
    step = pl.program_id(0)
    tile = w_ref.shape[1]
    columns = pl.ds(pl.multiple_of(step * tile, tile), tile)
    middle_ref[:, columns] = x_ref[...].astype(f32) + dot(att_ref[...], w_ref[...])

    @pl.when(step == pl.num_programs(0) - 1)
    def _():
        middle = middle_ref[...]
        factor = lax.rsqrt(jnp.mean(middle * middle, axis=-1, keepdims=True) + EPSILON)
        rows_ref[...] = (middle * factor * gain_ref[...]).astype(bf16)


def middle_forward(x, attended, w_out, gain, tile=512):
    rows, width = x.shape
    return pl.pallas_call(
        middle_kernel,
        grid=(width // tile,),
        in_specs=[
            pl.BlockSpec((rows, tile), lambda n: (0, n)),
            whole(attended.shape),
            pl.BlockSpec((w_out.shape[0], tile), lambda n: (0, n)),
            whole((1, width)),
        ],
        out_specs=[whole((rows, width))] * 2,
        out_shape=[
            jax.ShapeDtypeStruct((rows, width), f32),
            jax.ShapeDtypeStruct((rows, width), bf16),
        ],
        compiler_params=params(),
        cost_estimate=cost(2 * rows * width * width, 8 * 2**20),
    )(x, attended, w_out, gain.reshape(1, width))


def middle_back_kernel(parts, *refs):
    grad_refs = refs[:parts]
    middle_ref, cot_ref, gain_ref, w_ref = refs[parts : parts + 4]
    mgrad_ref, low_ref, dgain_ref, out_ref = refs[-4:]

    @pl.when(pl.program_id(0) == 0)
    def _():
        upstream = grad_refs[0][...].astype(f32)
        for ref in grad_refs[1:]:
            upstream = upstream + ref[...].astype(f32)
        middle = middle_ref[...]
        factor = lax.rsqrt(jnp.mean(middle * middle, axis=-1, keepdims=True) + EPSILON)
        scaled = upstream * gain_ref[...]
        inner = jnp.mean(scaled * middle, axis=-1, keepdims=True)
        grad = factor * scaled - middle * (factor * factor * factor * inner)
        grad = cot_ref[...].astype(f32) + grad
        mgrad_ref[...] = grad
        low_ref[...] = grad.astype(bf16)
        dgain_ref[...] = jnp.sum(upstream * middle * factor, axis=0, keepdims=True)

    out_ref[...] = dot_nt(low_ref[...], w_ref[...]).astype(bf16)


def middle_back(grads, middle, cotangent, gain, w_out, after=(), tile=512):
    rows, width = middle.shape
    inner = w_out.shape[0]
    return pl.pallas_call(
        functools.partial(middle_back_kernel, len(grads)),
        grid=(inner // tile,),
        in_specs=[whole((rows, width))] * (len(grads) + 2)
        + [whole((1, width)), pl.BlockSpec((tile, width), lambda n: (n, 0))]
        + anywhere(len(after)),
        out_specs=[
            whole((rows, width)),
            whole((rows, width)),
            whole((1, width)),
            pl.BlockSpec((rows, tile), lambda n: (0, n)),
        ],
        out_shape=[
            jax.ShapeDtypeStruct((rows, width), f32),
            jax.ShapeDtypeStruct((rows, width), bf16),
            jax.ShapeDtypeStruct((1, width), f32),
            jax.ShapeDtypeStruct((rows, inner), bf16),
        ],
        compiler_params=params(),
        cost_estimate=cost(2 * rows * width * inner, 16 * 2**20),
    )(*grads, middle, cotangent, gain.reshape(1, width), w_out, *after)


def input_back_kernel(dq_ref, dkv_ref, wq_ref, wk_ref, wv_ref, x_ref, gain_ref, mgrad_ref, *refs):
    out_ref, dgain_ref = refs[-2:]
    step = pl.program_id(0)
    term = dot_nt(dq_ref[...], wq_ref[...])
    term = term + dot_nt(dkv_ref[:, :HD], wk_ref[...]) + dot_nt(dkv_ref[:, HD:], wv_ref[...])

    @pl.when(step == 0)
    def _():
        out_ref[...] = term

    @pl.when(step > 0)
    def _():
        out_ref[...] += term

    @pl.when(step == pl.num_programs(0) - 1)
    def _():
        upstream = out_ref[...]
        x = x_ref[...].astype(f32)
        factor = lax.rsqrt(jnp.mean(x * x, axis=-1, keepdims=True) + EPSILON)
        scaled = upstream * gain_ref[...]
        inner = jnp.mean(scaled * x, axis=-1, keepdims=True)
        out_ref[...] = mgrad_ref[...] + factor * scaled - x * (factor * factor * factor * inner)
        dgain_ref[...] = jnp.sum(upstream * x * factor, axis=0, keepdims=True)


def input_back(dq, dkv, wq, wk, wv, x, gain, mgrad, after=()):
    rows, width = x.shape
    wide = GROUPS * HD
    return pl.pallas_call(
        input_back_kernel,
        grid=(KVH,),
        in_specs=[
            pl.BlockSpec((rows, wide), lambda g: (0, g)),
            pl.BlockSpec((rows, 2 * HD), lambda g: (0, g)),
            pl.BlockSpec((width, wide), lambda g: (0, g)),
            pl.BlockSpec((width, HD), lambda g: (0, g)),
            pl.BlockSpec((width, HD), lambda g: (0, g)),
            whole((rows, width)),
            whole((1, width)),
            whole((rows, width)),
        ]
        + anywhere(len(after)),
        out_specs=[whole((rows, width)), whole((1, width))],
        out_shape=[
            jax.ShapeDtypeStruct((rows, width), f32),
            jax.ShapeDtypeStruct((1, width), f32),
        ],
        compiler_params=params(),
        cost_estimate=cost(2 * rows * width * (H + 2 * KVH) * HD, 14 * 2**20),
    )(dq, dkv, wq, wk, wv, x, gain.reshape(1, width), mgrad, *after)


def gate_column(expert, gates):
    lanes = lax.broadcasted_iota(jnp.int32, gates.shape, 1)
    chosen = (lanes == expert) | (lanes == expert + LOW_LANE)
    return jnp.sum(jnp.where(chosen, gates.astype(f32), 0.0), axis=1, keepdims=True)


def experts_kernel(per, gated, extra, keeps, pos, x_ref, c_ref, *refs):
    weights = refs[:3]
    out_ref, grad_ref, *kept_refs, acc_o, acc_g = refs[3 + extra :]
    step = pl.program_id(0)
    last = pl.num_programs(0) - 1
    width = x_ref.shape[1]
    if keeps:

        @pl.when(step == 0)
        def _():
            kept_refs[0][...] = x_ref[...]
            kept_refs[1][...] = c_ref[...]
            kept_refs[2][...] = jnp.transpose(x_ref[...])
            kept_refs[3][...] = jnp.transpose(c_ref[:, :width])

    hid_ref, dgu_ref = kept_refs[-2:]

    def work(wg_ref, wu_ref, wd_ref):
        chunk = wg_ref.shape[1]
        x = x_ref[...]
        gate = dot(x, wg_ref[...])
        up = dot(x, wu_ref[...])
        slope = dot_nt(c_ref[:, :width], wd_ref[...])
        sigmoid = 1.0 / (1.0 + jnp.exp(-gate))
        act = gate * sigmoid
        hidden = act * up
        if gated:
            held = pl.num_programs(0) // per
            expert = (2 * pos[2] + pos[3]) * held + step // per
            weight = gate_column(expert, c_ref[:, width:])
            hidden = hidden * weight
            slope = slope * weight
        hidden = hidden.astype(bf16)
        dg = (slope * up * (sigmoid * (1.0 + gate * (1.0 - sigmoid)))).astype(bf16)
        du = (slope * act).astype(bf16)
        hid_ref[...] = hidden
        dgu_ref[:, :chunk] = dg
        dgu_ref[:, chunk:] = du
        out_term = dot(hidden, wd_ref[...])
        grad_term = dot_nt(dg, wg_ref[...]) + dot_nt(du, wu_ref[...])

        @pl.when(step == 0)
        def _():
            acc_o[...] = out_term
            acc_g[...] = grad_term

        @pl.when(step > 0)
        def _():
            acc_o[...] += out_term
            acc_g[...] += grad_term

    work(*weights)

    @pl.when(step == last)
    def _():
        out_ref[...] = acc_o[...].astype(out_ref.dtype)
        grad_ref[...] = acc_g[...].astype(grad_ref.dtype)


def experts(pos, x, c, weights, part, parts, kept, gated, kind, after=(), chunk=256):
    rows, width = x.shape
    inner = weights[2].shape[1]
    per = inner // chunk
    steps = weights[0].shape[0] * per
    specs = [
        pl.BlockSpec((None, width, chunk), lambda i, _: (i // per, 0, i % per)),
        pl.BlockSpec((None, width, chunk), lambda i, _: (i // per, 0, i % per)),
        pl.BlockSpec((None, chunk, width), lambda i, _: (i // per, i % per, 0)),
    ]
    collected = [
        jax.ShapeDtypeStruct((parts * rows, steps * chunk), bf16),
        jax.ShapeDtypeStruct((parts * rows, 2 * steps * chunk), bf16),
    ]
    collected_specs = [
        pl.BlockSpec((rows, chunk), lambda i, _: (part, i)),
        pl.BlockSpec((rows, 2 * chunk), lambda i, _: (part, i)),
    ]
    if gated:
        collected = [
            jax.ShapeDtypeStruct((parts * rows, width), bf16),
            jax.ShapeDtypeStruct((parts * rows, c.shape[1]), bf16),
            jax.ShapeDtypeStruct((width, parts * rows), bf16),
            jax.ShapeDtypeStruct((width, parts * rows), bf16),
        ] + collected
        collected_specs = [
            pl.BlockSpec((rows, width), lambda i, _: (part, 0)),
            pl.BlockSpec((rows, c.shape[1]), lambda i, _: (part, 0)),
            pl.BlockSpec((width, rows), lambda i, _: (0, part)),
            pl.BlockSpec((width, rows), lambda i, _: (0, part)),
        ] + collected_specs
    operands = [pos, x, c, *weights]
    aliases = {}
    if kept is not None:
        aliases = {len(operands) + j: 2 + j for j in range(len(collected))}
        operands += list(kept)
    extra = len(after) + (0 if kept is None else len(collected))
    operands += list(after)
    result = pl.pallas_call(
        functools.partial(experts_kernel, per, gated, extra, gated),
        grid_spec=pltpu.PrefetchScalarGridSpec(
            num_scalar_prefetch=1,
            grid=(steps,),
            in_specs=[whole((rows, width)), whole(c.shape)] + specs + anywhere(extra),
            out_specs=[whole((rows, width))] * 2 + collected_specs,
            scratch_shapes=[pltpu.VMEM((rows, width), f32)] * 2,
        ),
        out_shape=[jax.ShapeDtypeStruct((rows, width), kind)] * 2 + collected,
        input_output_aliases=aliases,
        compiler_params=params(),
        cost_estimate=cost(26 * rows * width * steps * chunk, 12 * 2**20),
    )(*operands)
    return result[0], result[1], result[2:]


def others_kernel(sets, per, extra, pos, x_ref, c_ref, *refs):
    weights = refs[: 3 * sets * per]
    out_ref, grad_ref, hid_ref, dgu_ref = refs[3 * sets * per + extra :]
    step = pl.program_id(0)
    chunk = weights[0].shape[1]
    width = x_ref.shape[1]
    tile = out_ref.shape[1]

    def places(t, n):
        at = (lax.rem(pos[1] + t, 2) * per + n) * chunk
        cut = lambda first: pl.ds(pl.multiple_of(first, chunk), chunk)
        return cut(at), cut(2 * at), cut(2 * at + chunk)

    def hidden_chunk(t, n, wg_ref, wu_ref, wd_ref):
        at_hidden, at_gate, at_up = places(t, n)
        expert = (2 * pos[2] + 1 - pos[3]) * sets + lax.rem(pos[1] + t, 2)
        for p in range(2):
            half = x_ref.shape[0] // 2
            part = slice(p * half, (p + 1) * half)
            x = x_ref[part, :]
            gate = dot(x, wg_ref[...])
            up = dot(x, wu_ref[...])
            slope = dot_nt(c_ref[part, :width], wd_ref[...])
            sigmoid = 1.0 / (1.0 + jnp.exp(-gate))
            act = gate * sigmoid
            weight = gate_column(expert, c_ref[part, width:])
            slope = slope * weight
            hid_ref[part, at_hidden] = (act * up * weight).astype(bf16)
            dgu_ref[part, at_gate] = (
                slope * up * (sigmoid * (1.0 + gate * (1.0 - sigmoid)))
            ).astype(bf16)
            dgu_ref[part, at_up] = (slope * act).astype(bf16)

    for t in range(sets):
        for n in range(per):
            at = t * per + n
            pl.when(step == at)(functools.partial(hidden_chunk, t, n, *weights[3 * at : 3 * at + 3]))

    @pl.when(step >= sets * per)
    def _():
        out = grad = 0.0
        first = pl.multiple_of((step - sets * per) * tile, tile)
        for t in range(sets):
            for n in range(per):
                at = t * per + n
                wg_ref, wu_ref, wd_ref = weights[3 * at : 3 * at + 3]
                at_hidden, at_gate, at_up = places(t, n)
                out = out + dot(hid_ref[:, at_hidden], wd_ref[:, pl.ds(first, tile)])
                grad = grad + dot_nt(dgu_ref[:, at_gate], wg_ref[pl.ds(first, tile), :])
                grad = grad + dot_nt(dgu_ref[:, at_up], wu_ref[pl.ds(first, tile), :])
        out_ref[...] = out.astype(bf16)
        grad_ref[...] = grad.astype(bf16)


def others(pos, x, c, weights, after=(), tile=512):
    taken, width = x.shape
    sets, per = len(weights), len(weights[0])
    inner = per * weights[0][0][0].shape[1]
    flat = [v for one in weights for triple in one for v in triple]
    resident = lambda v: pl.BlockSpec(v.shape, lambda *_: (0, 0), pipeline_mode=pl.Buffered(1))
    late = lambda i: jnp.maximum(i - sets * per, 0)
    return pl.pallas_call(
        functools.partial(others_kernel, sets, per, len(after)),
        grid_spec=pltpu.PrefetchScalarGridSpec(
            num_scalar_prefetch=1,
            grid=(sets * per + width // tile,),
            in_specs=[resident(v) for v in [x, c] + flat] + anywhere(len(after)),
            out_specs=[pl.BlockSpec((taken, tile), lambda i, _: (0, late(i)))] * 2
            + [whole((taken, sets * inner)), whole((taken, 2 * sets * inner))],
        ),
        out_shape=[jax.ShapeDtypeStruct((taken, width), bf16)] * 2
        + [
            jax.ShapeDtypeStruct((taken, sets * inner), bf16),
            jax.ShapeDtypeStruct((taken, 2 * sets * inner), bf16),
        ],
        compiler_params=params(),
        cost_estimate=cost(26 * taken * width * sets * inner, 12 * 2**20),
    )(pos, x, c, *flat, *after)


def side_of(outer, s, pos):
    return 2 * lax.rem(s, outer) + lax.rem(pos[1] + 1 - s // outer, 2)


def halves_kernel(shape, outer, pos, *refs):
    sent_ref, kept_ref = refs[-2:]

    def write(out_ref):
        out_ref[...] = jnp.zeros_like(out_ref)
        first = 0
        for i, rows in enumerate(shape):
            total = dot_tn(refs[2 * i][...], refs[2 * i + 1][...]).astype(bf16)
            for e in range(out_ref.shape[0]):
                part = total[e * rows : (e + 1) * rows]
                out_ref[e, first : first + rows, : total.shape[1]] = part
            first += rows

    pl.when(pl.program_id(0) < outer)(lambda: write(sent_ref))
    pl.when(pl.program_id(0) >= outer)(lambda: write(kept_ref))


def halves(pos, pairs, after=()):
    n_ctx, n_exp = lax.axis_size("ctx"), lax.axis_size("exp")
    outer = n_ctx // 2
    shape = [left.shape[1] // (n_ctx * n_exp) for left, _ in pairs]
    wide = max(right.shape[1] for _, right in pairs)
    full = (outer * n_exp, sum(shape), wide)
    if any((left.shape[1] // n_ctx) % 128 for left, _ in pairs):
        out = []
        for side in (1, 0):
            parts = []
            for left, right in pairs:
                split = left.reshape(left.shape[0], outer, 2, -1)
                mine = lax.dynamic_index_in_dim(split, (pos[1] + side) % 2, 2, keepdims=False)
                total = dot_tn(mine.reshape(left.shape[0], -1), right).astype(bf16)
                total = total.reshape(outer * n_exp, -1, right.shape[1])
                parts.append(jnp.pad(total, ((0, 0), (0, 0), (0, wide - right.shape[1]))))
            out.append(jnp.concatenate(parts, axis=1))
        return out
    in_specs, operands = [], []
    for left, right in pairs:
        columns = left.shape[1] // n_ctx
        in_specs.append(
            pl.BlockSpec((left.shape[0], columns), lambda s, pos: (0, side_of(outer, s, pos)))
        )
        in_specs.append(whole(right.shape))
        operands += [left, right]
    block = (n_exp,) + full[1:]
    flops = sum(2 * left.size * right.shape[1] for left, right in pairs)
    return pl.pallas_call(
        functools.partial(halves_kernel, shape, outer),
        grid_spec=pltpu.PrefetchScalarGridSpec(
            num_scalar_prefetch=1,
            grid=(2 * outer,),
            in_specs=in_specs + anywhere(len(after)),
            out_specs=[
                pl.BlockSpec(block, lambda s, pos: (jnp.minimum(s, outer - 1), 0, 0)),
                pl.BlockSpec(block, lambda s, pos: (jnp.maximum(s - outer, 0), 0, 0)),
            ],
        ),
        out_shape=[jax.ShapeDtypeStruct(full, bf16)] * 2,
        compiler_params=params(),
        cost_estimate=cost(2 * flops, 8 * 2**20),
    )(pos, *operands, *after)


def rows_product_kernel(blocks, pos, *refs):
    total = dot_tn(refs[0][...], refs[blocks][...])
    for b in range(1, blocks):
        total = total + dot_tn(refs[b][...], refs[blocks + b][...])
    refs[-1][...] = total.astype(bf16)


def rows_product(pos, lefts, rights, tile=512):
    n_ctx, n_exp = lax.axis_size("ctx"), lax.axis_size("exp")
    depth, height = lefts[0].shape
    high, wide = height // n_ctx, rights[0].shape[1]
    if high % 128:
        place = lax.axis_index("ctx") * high
        total = sum(
            dot_tn(lax.dynamic_slice_in_dim(a, place, high, 1), b) for a, b in zip(lefts, rights)
        )
        return total.astype(bf16).reshape(n_exp, -1, wide)
    blocks = len(lefts)
    left_spec = pl.BlockSpec((depth, high), lambda n, pos: (0, 2 * pos[0] + pos[1]))
    total = pl.pallas_call(
        functools.partial(rows_product_kernel, blocks),
        grid_spec=pltpu.PrefetchScalarGridSpec(
            num_scalar_prefetch=1,
            grid=(wide // tile,),
            in_specs=[left_spec] * blocks
            + [pl.BlockSpec((depth, tile), lambda n, pos: (0, n))] * blocks,
            out_specs=pl.BlockSpec((high, tile), lambda n, pos: (0, n)),
        ),
        out_shape=jax.ShapeDtypeStruct((high, wide), bf16),
        compiler_params=params(),
        cost_estimate=cost(4 * blocks * depth * high * wide, 4 * 2**20),
    )(pos, *lefts, *rights)
    return total.reshape(n_exp, -1, wide)


def expert_halves_kernel(outer, tiles, pos, rows_ref, cot_ref, dgu_ref, hid_ref, *refs):
    sent_ref, kept_ref = refs[-2:]
    s, n = pl.program_id(0), pl.program_id(1)

    def write(left_ref, right_ref):
        total = dot(left_ref[...], right_ref[...]).astype(bf16)

        def put(out_ref):
            for i in range(out_ref.shape[0]):
                out_ref[i] = total[i * out_ref.shape[1] : (i + 1) * out_ref.shape[1]]

        pl.when(s < outer)(lambda: put(sent_ref))
        pl.when(s >= outer)(lambda: put(kept_ref))

    pl.when(n < tiles)(lambda: write(rows_ref, dgu_ref))
    pl.when(n >= tiles)(lambda: write(cot_ref, hid_ref))


def expert_steps(width):
    high = width // lax.axis_size("ctx")
    return high // 128 if high % 128 == 0 else 1


def expert_halves(pos, rows_t, cot_t, dgu, hid, after=(), tile=1024):
    n_ctx = lax.axis_size("ctx")
    outer = n_ctx // 2
    width, depth = rows_t.shape
    high = width // n_ctx
    wide = dgu.shape[1] + hid.shape[1]
    tiles, down = dgu.shape[1] // tile, hid.shape[1] // tile
    steps = expert_steps(width)
    left_spec = pl.BlockSpec((high, depth), lambda s, n, pos: (side_of(outer, s, pos), 0))
    last = tiles + down - 1
    return pl.pallas_call(
        functools.partial(expert_halves_kernel, outer, tiles),
        grid_spec=pltpu.PrefetchScalarGridSpec(
            num_scalar_prefetch=1,
            grid=(2 * outer, tiles + down),
            in_specs=[
                left_spec,
                left_spec,
                pl.BlockSpec((depth, tile), lambda s, n, pos: (0, jnp.minimum(n, tiles - 1))),
                pl.BlockSpec((depth, tile), lambda s, n, pos: (0, jnp.maximum(n - tiles, 0))),
            ]
            + anywhere(len(after)),
            out_specs=[
                pl.BlockSpec(
                    (steps, high // steps, tile),
                    lambda s, n, pos: (jnp.minimum(s, outer - 1), 0, jnp.where(s < outer, n, last)),
                ),
                pl.BlockSpec(
                    (steps, high // steps, tile),
                    lambda s, n, pos: (jnp.maximum(s - outer, 0), 0, jnp.where(s < outer, 0, n)),
                ),
            ],
        ),
        out_shape=[jax.ShapeDtypeStruct((outer * steps, high // steps, wide), bf16)] * 2,
        compiler_params=params(),
        cost_estimate=cost(4 * depth * width * wide, 16 * 2**20),
    )(pos, rows_t, cot_t, dgu, hid, *after)


def sums_kernel(shape, extra, pos, *refs):
    ins, outs = refs[: sum(shape)], refs[sum(shape) + extra :]
    at = 0
    for count, out in zip(shape, outs):
        total = ins[at][...].astype(f32)
        for ref in ins[at + 1 : at + count]:
            total = total + ref[...].astype(f32)
        out[...] = total.astype(out.dtype)
        at += count


def sums(pos, steps, outputs, after=()):
    operands, in_specs, out_specs, out_shape = [], [], [], []
    for kind, block, terms in outputs:
        block = (1,) + tuple(block)
        for array, index in terms:
            operands.append(array)
            in_specs.append(pl.BlockSpec(block, functools.partial(place_of, index)))
        out_specs.append(pl.BlockSpec(block, lambda i, pos: (i, 0, 0)))
        out_shape.append(jax.ShapeDtypeStruct((steps,) + block[1:], kind))
    return pl.pallas_call(
        functools.partial(sums_kernel, [len(terms) for _, _, terms in outputs], len(after)),
        grid_spec=pltpu.PrefetchScalarGridSpec(
            num_scalar_prefetch=1,
            grid=(steps,),
            in_specs=in_specs + anywhere(len(after)),
            out_specs=out_specs,
        ),
        out_shape=out_shape,
        compiler_params=params(),
        cost_estimate=cost(0, 8 * 2**20),
    )(pos, *operands, *after)


def place_of(index, i, pos):
    at = index(i, pos)
    return at if isinstance(at, tuple) else (at, 0, 0)


def straight(i, pos):
    return i


def row_sum(terms, kind=bf16):
    total = terms[0].astype(f32)
    for term in terms[1:]:
        total = total + term.astype(f32)
    return total.astype(kind)


def expert_out_kernel(gates, each, *refs):
    in_refs, (gate_ref, up_ref, down_ref) = refs[:4], refs[4:]
    n = pl.program_id(0)

    def write(ref):
        @pl.when((n < gates) & (lax.rem(n, 2) == 0))
        def _():
            gate_ref[0] = ref[...].astype(f32)

        @pl.when((n < gates) & (lax.rem(n, 2) == 1))
        def _():
            up_ref[0] = ref[...].astype(f32)

        @pl.when(n >= gates)
        def _():
            down_ref[0] = jnp.transpose(ref[...].astype(f32))

    for q in range(4):
        pl.when(n // each == q)(functools.partial(write, in_refs[q]))


def expert_out(quarters, inner, chunk=256):
    rows, wide = quarters[0].shape
    each = wide // chunk
    held = 4 * wide // (3 * inner)
    per = inner // chunk
    gates = 2 * held * per
    tile = lambda n: jnp.minimum(n, gates - 1) // 2
    spec = pl.BlockSpec((1, rows, chunk), lambda n: (tile(n) // per, 0, lax.rem(tile(n), per)))
    at = lambda n: jnp.maximum(n - gates, 0)
    return pl.pallas_call(
        functools.partial(expert_out_kernel, gates, each),
        grid=(4 * each,),
        in_specs=[
            pl.BlockSpec(
                (rows, chunk),
                functools.partial(lambda q, n: (0, jnp.clip(n - q * each, 0, each - 1)), q),
            )
            for q in range(4)
        ],
        out_specs=[
            spec,
            spec,
            pl.BlockSpec((1, chunk, rows), lambda n: (at(n) // per, lax.rem(at(n), per), 0)),
        ],
        out_shape=[jax.ShapeDtypeStruct((held, rows, inner), f32)] * 2
        + [jax.ShapeDtypeStruct((held, inner, rows), f32)],
        compiler_params=params(),
        cost_estimate=cost(0, 8 * 2**20),
    )(*quarters)


def hold(values, after):
    count = len(values)
    return pl.pallas_call(
        lambda *_: None,
        in_specs=[pl.BlockSpec(memory_space=pl.ANY)] * (count + len(after)),
        out_specs=[pl.BlockSpec(memory_space=pl.ANY)] * count,
        out_shape=[jax.ShapeDtypeStruct(v.shape, v.dtype) for v in values],
        input_output_aliases={i: i for i in range(count)},
        compiler_params=params(),
        cost_estimate=cost(0, 0),
    )(*values, *after)


def swap_inner(value, axis):
    size = lax.axis_size(axis)
    return lax.ppermute(value, axis, [(i, i ^ 1) for i in range(size)])


def shift_outer(value, axis, by):
    outer = lax.axis_size(axis) // 2
    perm = [(o * 2 + i, ((o + by) % outer) * 2 + i) for o in range(outer) for i in range(2)]
    return lax.ppermute(value, axis, perm)


def ring_step(value, by):
    n_ctx, n_exp = lax.axis_size("ctx"), lax.axis_size("exp")
    outer = n_exp // 2
    perm = []
    for c in range(n_ctx):
        way = by if c % 2 == 0 else -by
        for o in range(outer):
            for i in range(2):
                perm.append((c * n_exp + o * 2 + i, c * n_exp + ((o + way) % outer) * 2 + i))
    return lax.ppermute(value, BOTH, perm)


def by_blocks(value, together):
    return value.reshape(-1, together * value.shape[1], value.shape[2])


def spread_outer(value):
    moved, out = value, []
    for _ in range(1, lax.axis_size("ctx") // 2):
        moved = shift_outer(moved, "ctx", 1)
        out.append(moved)
    return out, swap_inner(value, "ctx")


def spread_inner(moved):
    return [swap_inner(v, "ctx") for v in moved]


def spread_all(value, moved, across, moved_across):
    blocks = [value, across]
    for a, b in zip(moved, moved_across):
        blocks += [a, b]
    return blocks


def shared_x_send(pos, kept, got):
    outer, levels = lax.axis_size("ctx") // 2, lax.axis_size("exp") // 2
    outputs = []
    for y in range(outer):
        index = functools.partial(
            lambda y, i, pos: (y * levels + i) * 2 + 1 - pos[3], y
        )
        outputs.append((bf16, kept.shape[1:], [(v, index) for v in (kept, got)]))
    return sums(pos, levels, outputs)


def shared_terms(kept, got, arrived, d):
    outer, levels = lax.axis_size("ctx") // 2, lax.axis_size("exp") // 2
    place = lambda pos: lax.rem(pos[0] + d, outer) * levels
    terms = [(v, lambda i, pos: (place(pos) + i) * 2 + pos[3]) for v in (kept, got)]
    return terms + [(arrived, lambda i, pos: place(pos) + i)]


def shared_y(pos, kept, got, arrived):
    outer, levels = lax.axis_size("ctx") // 2, lax.axis_size("exp") // 2
    out = []
    for d in range(1, outer):
        terms = shared_terms(kept, got, arrived, d)
        (sent,) = sums(pos, levels, [(bf16, kept.shape[1:], terms)])
        out.append(shift_outer(sent, "ctx", d))
    return out


def shared_total(pos, kept, got, arrived, moved):
    levels = lax.axis_size("exp") // 2
    terms = shared_terms(kept, got, arrived, 0) + [(v, straight) for v in moved]
    (total,) = sums(pos, levels, [(bf16, kept.shape[1:], terms)])
    return total


def z_take(total, d):
    levels = total.shape[0]
    return lax.dynamic_index_in_dim(total, (lax.axis_index("exp") // 2 + d) % levels, 0, False)


def z_send(total, d):
    return shift_outer(z_take(total, d), "exp", d)


def over_x(total):
    pairs = total.reshape((-1, 2) + total.shape[1:])
    return swap_inner(lax.dynamic_index_in_dim(pairs, 1 - lax.axis_index("exp") % 2, 1, False), "exp")


def over_z(total, arrived):
    pairs = total.reshape((-1, 2) + total.shape[1:])
    mine = lax.dynamic_index_in_dim(pairs, lax.axis_index("exp") % 2, 1, False)
    mine = mine.astype(f32) + arrived.astype(f32)
    levels, level = mine.shape[0], lax.axis_index("exp") // 2
    take = lambda d: lax.dynamic_index_in_dim(mine, (level + d) % levels, 0, False)
    return [take(0)] + [shift_outer(take(d).astype(bf16), "exp", d) for d in range(1, levels)]


def dense_result(pairs, terms):
    devices = lax.axis_size("ctx") * lax.axis_size("exp")
    out, first = [], 0
    for left, right in pairs:
        rows = left.shape[1] // devices
        out.append(sum(t[first : first + rows, : right.shape[1]].astype(f32) for t in terms))
        first += rows
    return out


def expert_quarter(kept, got, q, row):
    block = (kept.shape[1], kept.shape[2] // 4)
    return block, [(v, lambda i, pos: (row(i, pos), 0, q)) for v in (kept, got)]


def expert_pieces(pos, kept, got, quarters):
    outputs = []
    for q in quarters:
        block, terms = expert_quarter(kept, got, q, straight)
        outputs.append((bf16, block, terms))
    return sums(pos, kept.shape[0], outputs)


def expert_rows(kept, d):
    outer = lax.axis_size("ctx") // 2
    steps = kept.shape[0] // outer
    return steps, lambda i, pos: lax.rem(pos[0] + d, outer) * steps + i


def expert_send(pos, kept, got, pieces, quarters):
    sent = []
    for d in range(1, lax.axis_size("ctx") // 2):
        steps, row = expert_rows(kept, d)
        outputs = []
        for q in quarters:
            block, terms = expert_quarter(kept, got, q, row)
            outputs.append((bf16, block, terms + [(pieces[q], row)]))
        sent.append(sums(pos, steps, outputs))
    return sent


def expert_move(sent):
    return [[shift_outer(v, "ctx", d + 1) for v in part] for d, part in enumerate(sent)]


def expert_total(pos, kept, got, pieces, arrived):
    steps, row = expert_rows(kept, 0)
    outputs = []
    for q in range(4):
        block, terms = expert_quarter(kept, got, q, row)
        terms = terms + [(pieces[q], row)] + [(v, straight) for v in arrived[q]]
        outputs.append((bf16, block, terms))
    return [v.reshape(-1, v.shape[2]) for v in sums(pos, steps, outputs)]


def shards(
    layer_input,
    attn_gain,
    w_query,
    w_key,
    w_value,
    w_out,
    ffn_gain,
    shared_gate,
    shared_up,
    shared_down,
    expert_gate,
    expert_up,
    expert_down,
    routes,
    gate_logits,
    span_order,
    cotangent,
):
    x = layer_input[0]
    cot = cotangent[0]
    tokens, width = x.shape
    span_rows = tokens // 2
    n_ctx, n_exp = lax.axis_size("ctx"), lax.axis_size("exp")
    ctx_id, exp_id = lax.axis_index("ctx"), lax.axis_index("exp")
    local_experts, _, inner = expert_gate.shape
    expert_count = local_experts * n_exp

    levels = n_exp // 2
    pos = jnp.stack([ctx_id // 2, ctx_id % 2, exp_id // 2, exp_id % 2]).astype(jnp.int32)

    always = pos[0] < n_ctx
    ring = n_ctx // 2

    def region(work):
        made = jax.eval_shape(work)
        return lax.cond(always, work, lambda: jax.tree.map(lambda v: jnp.zeros(v.shape, v.dtype), made))

    gate_vals = jax.nn.softmax(gate_logits[0], axis=-1)
    named = routes[0][:, None, :] == jnp.arange(expert_count, dtype=jnp.int32)[None, :, None]
    row_gates = jnp.sum(jnp.where(named, gate_vals[:, None, :], 0.0), axis=-1)
    high = row_gates.astype(bf16)
    low = (row_gates - high.astype(f32)).astype(bf16)
    fill = lambda width: ((0, 0), (0, width - expert_count))
    cot_ring = [
        jnp.concatenate(
            [cot, jnp.pad(high, fill(LOW_LANE)), jnp.pad(low, fill(GATE_LANES - LOW_LANE))], axis=1
        )
    ]

    normed, kv = keyvalue(x, attn_gain, w_key, w_value)
    chunk = 256
    per = inner // chunk

    def fetch(part):
        which, n = part % 3, part // 3
        array = (expert_gate, expert_up, expert_down)[which]
        mine = lax.dynamic_index_in_dim(array, pos[1], 0, keepdims=False)
        dim = 0 if which == 2 else 1
        return swap_inner(lax.slice_in_dim(mine, n * chunk, (n + 1) * chunk, axis=dim), "exp")

    fetches = [range(0, 1), range(1, 2), range(2, 4), range(4, 5), range(5, 3 * per)]

    def fetch_some(k):
        return [fetch(p) for p in fetches[k]]

    def gather_keys():
        moved, across = spread_outer(kv)
        queries = dot(normed, w_query).astype(bf16)
        return moved, across, spread_inner(moved), queries, ring_step(cot_ring[0], 1), fetch_some(0)

    moved, across, moved_across, queries, cot_next, fetched = region(gather_keys)
    kv_blocks = spread_all(kv, moved, across, moved_across)
    cot_ring.append(cot_next)

    def attention():
        attended, lse = attend(pos, span_order, queries, kv_blocks)
        middle, rows = middle_forward(x, attended, w_out, ffn_gain)
        moved = spread_outer(normed), ring_step(cot_ring[1], 1), fetch_some(1)
        return attended, lse, middle, rows, *moved

    attended, lse, middle, rows_low, normed_moved, cot_next, got = region(attention)
    fetched += got
    cot_ring.append(cot_next)

    def own_part(k, rows, kept):
        weights = (expert_gate, expert_up, expert_down)
        return experts(pos, rows, cot_ring[k], weights, k, levels, kept, True, bf16)

    def first():
        weights = (shared_gate[None], shared_up[None], shared_down[None])
        shared = experts(pos, rows_low, cot, weights, 0, 1, None, False, f32)
        moved = ring_step(rows_low, 1), ring_step(cot_ring[2], 1)
        more = spread_outer(attended), spread_inner(normed_moved[0]), fetch_some(2)
        return moved, shared, own_part(0, rows_low, None), *more

    moved, shared, (out_k, grad_k, kept), attended_moved, normed_across, got = region(first)
    fetched += got
    normed_blocks = spread_all(normed, *normed_moved, normed_across)
    shared_out, shared_grad, (shared_hidden, shared_dgu) = shared
    rows_k = moved[0]
    cot_ring.append(moved[1])
    out_own, grad_own = [out_k], [grad_k]
    shared_pairs = [(rows_low, shared_dgu), (shared_hidden, cot)]

    def second():
        result = own_part(1, rows_k, kept)
        across = spread_inner(attended_moved[0])
        return ring_step(rows_k, 1), result, halves(pos, shared_pairs), across, fetch_some(3)

    rows_next, (out_k, grad_k, kept), (shared_sent, shared_kept), across, got = region(second)
    fetched += got
    attended_blocks = spread_all(attended, *attended_moved, across)
    rows_k = rows_next
    out_own.append(out_k)
    grad_own.append(grad_k)

    def third():
        result = own_part(2, rows_k, kept)
        moved = ring_step(rows_k, 1), swap_inner(shared_sent, "ctx"), fetch_some(4)
        return result, [swap_inner(v, "ctx") for v in fetched], *moved

    (out_k, grad_k, kept), fetched_b, rows_next, shared_got, got = region(third)
    fetched += got
    rows_k = rows_next
    out_own.append(out_k)
    grad_own.append(grad_k)

    def fourth():
        across = fetched_b + [swap_inner(v, "ctx") for v in fetched[len(fetched_b) :]]
        sent = shared_x_send(pos, shared_kept, shared_got)
        got = [swap_inner(v, "exp") for v in sent[: ring // 2]]
        out_k, grad_k, new = own_part(3, rows_k, kept)
        weights = [[v[3 * n : 3 * n + 3] for n in range(per)] for v in (fetched, across)]
        return out_k, grad_k, new, others(pos, new[0], new[1], weights), got, sent[ring // 2 :]

    out_k, grad_k, kept, other, shared_first, shared_rest = region(fourth)
    out_own.append(out_k)
    grad_own.append(grad_k)
    rows_all, cot_all, rows_t, cot_t, hid_own, dgu_own = kept
    out_other, grad_other, hid_other, dgu_other = other
    split = lambda v: [v[k * tokens : (k + 1) * tokens] for k in range(levels)]
    out_other, grad_other = split(out_other), split(grad_other)

    def back_one():
        moved = ring_step(row_sum([grad_own[3], grad_other[3]]), -1)
        made = expert_halves(pos, rows_t, cot_t, dgu_other, hid_other)
        return moved, made, [swap_inner(v, "exp") for v in shared_rest]

    moved, (sent, kept_other), shared_second = region(back_one)
    shared_x = jnp.concatenate(shared_first + shared_second, axis=0)

    def back_two():
        total = row_sum([grad_own[2], grad_other[2], moved])
        got = swap_inner(sent, "ctx")
        made = expert_halves(pos, rows_t, cot_t, dgu_own, hid_own)
        shared_moved = shared_y(pos, shared_kept, shared_got, shared_x)
        return ring_step(total, -1), got, made, expert_pieces(pos, kept_other, got, [0])[0], shared_moved

    moved_two, got_other, (sent_own, kept_own), piece, shared_moved = region(back_two)

    def back_three():
        total = row_sum([grad_own[1], grad_other[1], moved_two])
        pieces = expert_pieces(pos, kept_other, got_other, [1, 2, 3])
        shared_sum = shared_total(pos, shared_kept, shared_got, shared_x, shared_moved)
        out_total = row_sum([out_own[3], out_other[3]])
        moved = ring_step(total, -1), swap_inner(sent_own, "ctx"), swap_inner(piece, "exp")
        return *moved, pieces, shared_sum, out_total

    moved, got_own, piece, pieces, shared_sum, out_total = region(back_three)
    pieces = [piece] + list(pieces)

    def attention_back():
        mgrad, mgrad_low, ffn_gain_grad, att_grad = middle_back(
            [shared_grad, grad_own[0], grad_other[0], moved], middle, cot, ffn_gain, w_out
        )
        back = attend_back(pos, span_order, queries, att_grad, lse, kv_blocks)
        out_moved = ring_step(out_total, -1)
        got = swap_inner(pieces[1], "exp"), z_send(shared_sum, 1), expert_move(expert_send(pos, kept_own, got_own, pieces, [0]))
        return mgrad, mgrad_low, spread_outer(mgrad_low), ffn_gain_grad, back, out_moved, *got

    mgrad, mgrad_low, mgrad_moved, ffn_gain_grad, (dq, same, across), out_moved, piece, shared_z, got = (
        region(attention_back)
    )
    pieces[1] = piece
    arrived = [[a[0] for a in got]]
    shared_z = [shared_z]

    def dense_one():
        got = swap_inner(across, "ctx")
        made = []
        for k in reversed(range(ring)):
            part = slice(k * tokens, (k + 1) * tokens)
            made = row_sum([same[part], got[part]] + made)
            if k:
                made = [shift_outer(made, "ctx", -1)]
        total = row_sum([out_own[2], out_other[2], out_moved])
        mgrad_across = spread_inner(mgrad_moved[0])
        moved = ring_step(total, -1), swap_inner(pieces[2], "exp"), z_send(shared_sum, 2)
        return made, spread_outer(dq), mgrad_across, *moved

    dkv, dq_moved, mgrad_across, out_moved_two, piece, got = region(dense_one)
    shared_z.append(got)
    mgrad_blocks = spread_all(mgrad_low, *mgrad_moved, mgrad_across)
    pieces[2] = piece

    def dense_two():
        total = row_sum([out_own[1], out_other[1], out_moved_two])
        moved = ring_step(total, -1)
        dq_across = spread_inner(dq_moved[0])
        total_out = rows_product(pos, attended_blocks, mgrad_blocks)
        back = input_back(dq, dkv, w_query, w_key, w_value, x, attn_gain, mgrad)
        got = expert_move(expert_send(pos, kept_own, got_own, pieces, [1]))
        more = moved, swap_inner(pieces[3], "exp"), z_send(shared_sum, 3), got
        return spread_outer(dkv), dq_across, total_out, back, *more

    dkv_moved, dq_across, total_out, (input_grad, attn_gain_grad), out_moved_three, piece, last_z, got = (
        region(dense_two)
    )
    shared_z.append(last_z)
    arrived.append([a[0] for a in got])
    dq_blocks = spread_all(dq, *dq_moved, dq_across)
    pieces[3] = piece

    def dense_three():
        devices = n_ctx * n_exp
        moved = expert_move(expert_send(pos, kept_own, got_own, pieces, [2, 3]))
        got = arrived + [[a[q] for a in moved] for q in range(2)]
        total_query = rows_product(pos, normed_blocks, dq_blocks)
        dkv_blocks = spread_all(dkv, *dkv_moved, spread_inner(dkv_moved[0]))
        total_kv = rows_product(pos, normed_blocks, dkv_blocks)
        shared_parts = [z_take(shared_sum, 0)] + shared_z
        dense = [over_z(t, over_x(t)) for t in (total_out, total_query, total_kv)]
        layer_out = row_sum([middle, shared_out, out_own[0], out_other[0], out_moved_three])
        gains = jnp.stack(
            [attn_gain_grad.reshape(devices, -1), ffn_gain_grad.reshape(devices, -1)], axis=1
        )
        gains = lax.all_to_all(gains, BOTH, split_axis=0, concat_axis=0, tiled=True)
        grads = expert_out(expert_total(pos, kept_own, got_own, pieces, got), inner)
        pairs = [(attended, mgrad), (normed, dq), (normed, dkv)]
        dense = [dense_result([p], t)[0] for p, t in zip(pairs, dense)]
        return layer_out, jnp.sum(gains, axis=0), dense_result(shared_pairs, shared_parts), dense, grads

    layer_out, gains, (sum_gate_up, sum_down), (sum_out, sum_query, sum_kv), expert_grads = region(
        dense_three
    )
    shared_rows = sum_gate_up.reshape(sum_gate_up.shape[0], -1, 2, 256)
    kv_rows = sum_kv.reshape(sum_kv.shape[0], KVH, 2, HD)
    return (
        layer_out[None],
        input_grad[None],
        gains[0],
        sum_query,
        kv_rows[:, :, 0].reshape(sum_kv.shape[0], -1),
        kv_rows[:, :, 1].reshape(sum_kv.shape[0], -1),
        sum_out,
        gains[1],
        shared_rows[:, :, 0].reshape(sum_gate_up.shape[0], -1),
        shared_rows[:, :, 1].reshape(sum_gate_up.shape[0], -1),
        sum_down,
        *expert_grads,
    )


def solution(mesh):
    return jax.shard_map(
        shards,
        mesh=mesh,
        in_specs=(
            P("exp", "ctx", None),
            P(),
            P(),
            P(),
            P(),
            P(),
            P(),
            P(),
            P(),
            P(),
            P("exp", None, None),
            P("exp", None, None),
            P("exp", None, None),
            P("exp", "ctx", None),
            P("exp", "ctx", None),
            P(),
            P("exp", "ctx", None),
        ),
        out_specs=(
            P("exp", "ctx", None),
            P("exp", "ctx", None),
            P(("ctx", "exp")),
            P(("ctx", "exp"), None),
            P(("ctx", "exp"), None),
            P(("ctx", "exp"), None),
            P(("ctx", "exp"), None),
            P(("ctx", "exp")),
            P(("ctx", "exp"), None),
            P(("ctx", "exp"), None),
            P(("ctx", "exp"), None),
            P("exp", "ctx", None),
            P("exp", "ctx", None),
            P("exp", None, "ctx"),
        ),
        check_vma=False,
    )
```

time: 678 us -> 571 us (0.84)
  waiting for transfers between devices: 266 us -> 136 us
  Pallas kernels: 144 us -> 268 us
  matrix products: 53.8 us -> 3.41 us
  local copies, waits for them, and re-layouts: 77.4 us -> 42.2 us
  between operations: 15.7 us -> 1.63 us
  starting transfers between devices: 85.1 us -> 75 us
    pallas_call x7 -> x24, Pallas kernels: 114 us -> 239 us  [the longest x5 63.6 us: experts(): pl.pallas_call(functools.partial(experts_kernel, per, gated, extra, gated...]
    ppermute x34 -> x37, waiting for transfers between devices: 109 us -> 52.4 us  [swap_inner(): return lax.ppermute(value, axis, [(i, i ^ 1) for i in range(size)])]
    dot_general x14 -> x0, matrix products: 49.2 us -> none  [dot_tn(): lax.dot_general(left_op, right_op, (((0,), (0,)), ((), ())), preferred_el...]
    ppermute x12, waiting for transfers between devices: 63 us -> 19.2 us  [ring_step(): return lax.ppermute(value, BOTH, perm)]
    ppermute x30 -> x24, waiting for transfers between devices: 94 us -> 64.7 us  [shift_outer(): return lax.ppermute(value, axis, perm)]
    unnamed x111 -> x32, local copies, waits for them, and re-layouts: 28 us -> 4.7 us
    ppermute x30 -> x24, starting transfers between devices: 51.9 us -> 32.6 us  [shift_outer(): return lax.ppermute(value, axis, perm)]
    reshape x8 -> x4, local copies, waits for them, and re-layouts: 13.9 us -> 1.37 us  [the longest x1 0.6 us: middle_back(): gain.reshape(1, width)]
  transfers between devices with their start and end apart: 78 -> 74, of which waited for: 27 -> 18; matrix products, arithmetic and copies ran while one was open for 20% -> 11% of each run, Pallas kernels for 21% -> 47%
where the time goes in v2:
time: 571 us; the launch traced here: 562 us
  Pallas kernels  268 us (47%)
  waiting for transfers between devices  136 us (24%)
  starting transfers between devices  75 us (13%)
  local copies, waits for them, and re-layouts  42.2 us (7%)
  other arithmetic  33.4 us (6%)
    ppermute x24, waiting for transfers between devices, shift_outer(): return lax.ppermute(value, axis, perm)  64.7 us
    pallas_call x5, Pallas kernels, experts(): pl.pallas_call(functools.partial(experts_kernel, per, gated, extra, gated...  63.6 us
    ppermute x37, waiting for transfers between devices, swap_inner(): return lax.ppermute(value, axis, [(i, i ^ 1) for i in range(size)])  52.4 us
    pallas_call x2, Pallas kernels, expert_halves(): pl.pallas_call(functools.partial(expert_halves_kernel, outer, tiles), gri...  44.7 us
    pallas_call x9, Pallas kernels, sums(): pl.pallas_call(functools.partial(sums_kernel, [len(terms) for _, _, terms...  44.7 us
    ppermute x24, starting transfers between devices, shift_outer(): return lax.ppermute(value, axis, perm)  32.6 us
    pallas_call x1, Pallas kernels, others(): pl.pallas_call(functools.partial(others_kernel, sets, per, len(after)), g...  31.6 us
    ppermute x37, starting transfers between devices, swap_inner(): return lax.ppermute(value, axis, [(i, i ^ 1) for i in range(size)])  23.7 us
  transfers between devices with their start and end apart: 74, of which 18 were waited for; matrix products, arithmetic and copies ran while one was open for 11% of the time, Pallas kernels for 47%

profile of v2, /device:TPU:0, one launch (start us, length us, event | category | flops | bytes accessed | tf_op | source)
XLA Modules:
  0.0 561.6 jit_solution(18073534282960063780)
XLA Ops:
  7.2 5.1 shard_map.275
  12.4 25.8 %conditional.13 = (bf16[256,1024]{1,0:T(8,128)(2,1)}, bf16[256,1024]{1,0:T(8,128)(2,1)}, bf16[256,1024]{1,0:T(8,128)(2,1)}, bf16[256,1536]{1,0:T(8,128)(2,1)}, b...) conditional(s32[]{:T(128)} %convert_element_type.264, () %tuple.132, (bf16[256,1024]{1,0:T(8,128)(2,1)}, ...), branch_computations={%region_3.4_spmd, %region_4.5_spmd} | conditional | flops 1208352768 | bytes 42729784 | solution.py:1021
  19.7 7.9 %collective-permute-done.68 = bf16[256,1024]{1,0:T(8,128)(2,1)} collective-permute-done((bf16[256,1024]{1,0:T(8,128)(2,1)}, bf16[256,1024]{1,0:T(8,128)(2,1)}, u32[]{:S(2)}, u32[]{:S(2)}) %collective-permute-start.68) | collective-permute-done | bytes 524320 | tf_op jit(solution)/shard_map/cond/branch_1_fun/ppermute | solution.py:834
  31.1 6.3 %collective-permute-done.72 = bf16[1536,256]{1,0:T(8,128)(2,1)} collective-permute-done((bf16[1536,256]{1,0:T(8,128)(2,1)S(1)}, bf16[1536,256]{1,0:T(8,128)(2,1)}, u32[]{:S(2)}, u32[]{:S(2)}) %collective-permute-start.72) | collective-permute-done | bytes 786464 | tf_op jit(solution)/shard_map/cond/branch_1_fun/ppermute | solution.py:828
  38.2 23.4 %conditional.14 = (bf16[256,1536]{1,0:T(8,128)(2,1)}, f32[4,1,768]{2,1,0:T(1,128)S(1)}, f32[256,1536]{1,0:T(8,128)}, bf16[256,1536]{1,0:T(8,128)(2,1)}, bf16[256...) conditional(s32[]{:T(128)} %convert_element_type.264, ...), branch_computations={%region_5.6_spmd, %region_6.7_spmd} | conditional | flops 1107296256 | bytes 23867682 | solution.py:1021
  43.8 9.5 %branch_1_fun.27 = (bf16[256,1536]{1,0:T(8,128)(2,1)}, f32[4,1,768]{2,1,0:T(1,128)S(1)}) custom-call(s32[4]{0:T(128)S(1)} %get-tuple-element.470.pos, s32[8]{0:T(128)S(1)} %get-tuple-element.471.spans, bf16[256,1536]{1,0:T(8,128)(2,1)} %get-tuple-element.472.q_ref, bf16[256,1024]{1,0:T(8,128)(2,1)} %get-tuple-element.473.refs_0_, ...), custom_call_target="tpu_custom_call" | custom-call | flops 805306368 | bytes 1048576 | tf_op jit(solution)/shard_map/cond/branch_1_fun/pallas_call | solution.py:128
  53.3 5.9 %branch_1_fun.28 = (f32[256,1536]{1,0:T(8,128)}, bf16[256,1536]{1,0:T(8,128)(2,1)}) custom-call(bf16[256,1536]{1,0:T(8,128)(2,1)S(1)} %copy-done.2, bf16[256,1536]{1,0:T(8,128)(2,1)} %get-tuple-element.1120.att_ref, bf16[1536,1536]{1,0:T(8,128)(2,1)} %get-tuple-element.480.w_ref, f32[1,1536]{1,0:T(1,128)} %reshape.119.gain_ref), custom_call_target="tpu_custom_call" | custom-call | flops 301989888 | bytes 2097152 | tf_op jit(solution)/shard_map/cond/branch_1_fun/pallas_call | solution.py:228
  61.6 48.6 %conditional.15 = (bf16[256,1536]{1,0:T(8,128)(2,1)}, bf16[256,1664]{1,0:T(8,128)(2,1)}, f32[256,1536]{1,0:T(8,128)}, f32[256,1536]{1,0:T(8,128)}, bf16[256,1024...) conditional(s32[]{:T(128)} %convert_element_type.264, ...), branch_computations={%region_7.8_spmd, %region_8.9_spmd} | conditional | flops 5234491392 | bytes 38011380 | solution.py:1021
  68.8 14.3 %collective-permute-done.9 = bf16[256,1536]{1,0:T(8,128)(2,1)} collective-permute-done((bf16[256,1536]{1,0:T(8,128)(2,1)S(1)}, bf16[256,1536]{1,0:T(8,128)(2,1)}, u32[]{:S(2)}, u32[]{:S(2)}) %collective-permute-start.9) | collective-permute-done | bytes 786464 | tf_op jit(solution)/shard_map/cond/branch_1_fun/ppermute | solution.py:828
  85.2 12.9 %branch_1_fun.30 = (bf16[256,1536]{1,0:T(8,128)(2,1)}, bf16[256,1536]{1,0:T(8,128)(2,1)}, bf16[1024,1536]{1,0:T(8,128)(2,1)}, bf16[1024,1664]{1,0:T(8,128)(2,1)}...) custom-call(s32[4]{0:T(128)S(1)} %get-tuple-element.490.pos, ...), custom_call_target="tpu_custom_call" | custom-call | flops 2617245696 | bytes 3145728 | tf_op jit(solution)/shard_map/cond/branch_1_fun/pallas_call | solution.py:451
  98.2 11.9 %branch_1_fun.29 = (f32[256,1536]{1,0:T(8,128)}, f32[256,1536]{1,0:T(8,128)}, bf16[256,1024]{1,0:T(8,128)(2,1)}, bf16[256,2048]{1,0:T(8,128)(2,1)}) custom-call(s32[4]{0:T(128)S(1)} %get-tuple-element.490.pos, bf16[256,1536]{1,0:T(8,128)(2,1)} %get-tuple-element.488.x_ref, bf16[256,1536]{1,0:T(8,128)(2,1)S(1)} %copy-done.3, ...), custom_call_target="tpu_custom_call" | custom-call | flops 2617245696 | bytes 3145728 | tf_op jit(solution)/shard_map/cond/branch_1_fun/pallas_call | solution.py:451
  110.3 25.6 %conditional.16 = (bf16[256,1536]{1,0:T(8,128)(2,1)}, bf16[256,1536]{1,0:T(8,128)(2,1)}, bf16[256,1536]{1,0:T(8,128)(2,1)}, bf16[1024,1536]{1,0:T(8,128)(2,1)}, ...) conditional(s32[]{:T(128)} %convert_element_type.264, ...), branch_computations={%region_9.10_spmd, %region_10.11_spmd} | conditional | flops 3825205248 | bytes 33554560 | solution.py:1021
  114.5 8.4 %branch_1_fun.32 = (bf16[16,80,2048]{2,1,0:T(8,128)(2,1)}, bf16[16,80,2048]{2,1,0:T(8,128)(2,1)}) custom-call(s32[4]{0:T(128)S(1)} %get-tuple-element.515.pos, bf16[256,1536]{1,0:T(8,128)(2,1)} %get-tuple-element.534.refs_0_, bf16[256,2048]{1,0:T(8,128)(2,1)} %get-tuple-element.535.refs_1_, bf16[256,1024]{1,0:T(8,128)(2,1)} %get-tuple-element.536.refs_2_, ...), custom_call_target="tpu_custom_call" | custom-call | flops 1207959552 | bytes 2097152 | tf_op jit(solution)/shard_map/cond/branch_1_fun/pallas_call | solution.py:597
  122.9 12.9 %branch_1_fun.31 = (bf16[256,1536]{1,0:T(8,128)(2,1)}, bf16[256,1536]{1,0:T(8,128)(2,1)}, bf16[1024,1536]{1,0:T(8,128)(2,1)}, bf16[1024,1664]{1,0:T(8,128)(2,1)}...) custom-call(s32[4]{0:T(128)S(1)} %get-tuple-element.515.pos, ...), custom_call_target="tpu_custom_call", output_to_operand_aliasing={{2}: (6, {}), {3}: (7, {}), {4}: (8, {}), {5}: (9, {}), {6}... | custom-call | flops 2617245696 | bytes 3145728 | tf_op jit(solution)/shard_map/cond/branch_1_fun/pallas_call | solution.py:451
  135.8 44.8 %conditional.17 = (bf16[256,1536]{1,0:T(8,128)(2,1)}, bf16[256,1536]{1,0:T(8,128)(2,1)}, bf16[1024,1536]{1,0:T(8,128)(2,1)}, bf16[1024,1664]{1,0:T(8,128)(2,1)},...) conditional(s32[]{:T(128)} %convert_element_type.264, ...), branch_computations={%region_11.12_spmd, %region_12.13_spmd} | conditional | flops 2617245696 | bytes 47710708 | solution.py:1021
  141.7 17.8 %collective-permute-done.21 = bf16[256,1536]{1,0:T(8,128)(2,1)} collective-permute-done((bf16[256,1536]{1,0:T(8,128)(2,1)S(1)}, bf16[256,1536]{1,0:T(8,128)(2,1)}, u32[]{:S(2)}, u32[]{:S(2)}) %collective-permute-start.21) | collective-permute-done | bytes 786464 | tf_op jit(solution)/shard_map/cond/branch_1_fun/ppermute | solution.py:828
  160.2 12.9 %branch_1_fun.33 = (bf16[256,1536]{1,0:T(8,128)(2,1)}, bf16[256,1536]{1,0:T(8,128)(2,1)}, bf16[1024,1536]{1,0:T(8,128)(2,1)}, bf16[1024,1664]{1,0:T(8,128)(2,1)}...) custom-call(s32[4]{0:T(128)S(1)} %get-tuple-element.542.pos, ...), custom_call_target="tpu_custom_call", output_to_operand_aliasing={{2}: (6, {}), {3}: (7, {}), {4}: (8, {}), {5}: (9, {}), {6}... | custom-call | flops 2617245696 | bytes 3145728 | tf_op jit(solution)/shard_map/cond/branch_1_fun/pallas_call | solution.py:451
  173.1 7.3 %collective-permute-done.19 = bf16[256,1536]{1,0:T(8,128)(2,1)} collective-permute-done((bf16[256,1536]{1,0:T(8,128)(2,1)}, bf16[256,1536]{1,0:T(8,128)(2,1)}, u32[]{:S(2)}, u32[]{:S(2)}) %collective-permute-start.19) | collective-permute-done | bytes 786464 | tf_op jit(solution)/shard_map/cond/branch_1_fun/ppermute | solution.py:846
  180.6 56.9 %conditional.18 = (bf16[256,1536]{1,0:T(8,128)(2,1)}, bf16[256,1536]{1,0:T(8,128)(2,1)}, bf16[1536,1024]{1,0:T(8,128)(2,1)}, bf16[1536,1024]{1,0:T(8,128)(2,1)},...) conditional(s32[]{:T(128)} %convert_element_type.264, ...), branch_computations={%region_13.14_spmd, %region_14.15_spmd} | conditional | flops 13086228480 | bytes 35651784 | solution.py:1021
  180.7 5.1 branch_1_fun.36
  187.3 12.9 %branch_1_fun.34 = (bf16[256,1536]{1,0:T(8,128)(2,1)}, bf16[256,1536]{1,0:T(8,128)(2,1)}, bf16[1024,1536]{1,0:T(8,128)(2,1)}, bf16[1024,1664]{1,0:T(8,128)(2,1)}...) custom-call(s32[4]{0:T(128)S(1)} %get-tuple-element.569.pos, ...), custom_call_target="tpu_custom_call", output_to_operand_aliasing={{2}: (6, {}), {3}: (7, {}), {4}: (8, {}), {5}: (9, {}), {6}... | custom-call | flops 2617245696 | bytes 3145728 | tf_op jit(solution)/shard_map/cond/branch_1_fun/pallas_call | solution.py:451
  201.2 31.6 %branch_1_fun.35 = (bf16[1024,1536]{1,0:T(8,128)(2,1)}, bf16[1024,1536]{1,0:T(8,128)(2,1)}, bf16[1024,1024]{1,0:T(8,128)(2,1)}, bf16[1024,2048]{1,0:T(8,128)(2,1)}) custom-call(s32[4]{0:T(128)S(1)} %get-tuple-element.569.pos, bf16[1024,1536]{1,0:T(8,128)(2,1)} %get-tuple-element.587.x_ref, bf16[1024,1664]{1,0:T(8,128)(2,1)} %get-tuple-element.588.c_ref, ...), custom_call_target="tpu_custom_call" | custom-call | flops 10468982784 | bytes 3145728 | tf_op jit(solution)/shard_map/cond/branch_1_fun/pallas_call | solution.py:529
  239.2 31.2 %conditional.19 = (bf16[256,1536]{1,0:T(8,128)(2,1)}, bf16[6,128,3072]{2,1,0:T(8,128)(2,1)}, bf16[6,128,3072]{2,1,0:T(8,128)(2,1)}, bf16[4,80,2048]{2,1,0:T(8,128)(2,1)}) conditional(s32[]{:T(128)} %convert_element_type.264, () %tuple.144, (bf16[256,1536]{1,0:T(8,128)(2,1)}, bf16[256,1536]{1,0:T(8,128)(2,1)S(1)}, s32[4]{0:T(128)S(1)}, ...), branch_computations={%region_15.16_spmd, %region_16.17_spmd} | conditional | flops 4833411072 | bytes 14942320 | solution.py:1021
  242.5 22.4 %branch_1_fun.37 = (bf16[6,128,3072]{2,1,0:T(8,128)(2,1)}, bf16[6,128,3072]{2,1,0:T(8,128)(2,1)}) custom-call(s32[4]{0:T(128)S(1)} %get-tuple-element.610.pos, bf16[1536,1024]{1,0:T(8,128)(2,1)} %get-tuple-element.611.rows_ref, bf16[1536,1024]{1,0:T(8,128)(2,1)} %get-tuple-element.612.cot_ref, bf16[1024,2048]{1,0:T(8,128)(2,1)} %get-tuple-element.613.dgu_ref, ...), custom_call_target="tpu_custom_call" | custom-call | flops 4831838208 | bytes 4194304 | tf_op jit(solution)/shard_map/cond/branch_1_fun/pallas_call | solution.py:682
  264.9 5.5 collective-permute-done.23
  273.4 37.3 %conditional.20 = (bf16[256,1536]{1,0:T(8,128)(2,1)}, bf16[6,128,3072]{2,1,0:T(8,128)(2,1)}, bf16[6,128,3072]{2,1,0:T(8,128)(2,1)}, bf16[6,128,3072]{2,1,0:T(8,1...) conditional(s32[]{:T(128)} %convert_element_type.264, () %tuple.143, ...), branch_computations={%region_17.18_spmd, %region_18.19_spmd} | conditional | flops 4834197504 | bytes 38797480 | solution.py:1021
  283.1 22.3 %branch_1_fun.38 = (bf16[6,128,3072]{2,1,0:T(8,128)(2,1)}, bf16[6,128,3072]{2,1,0:T(8,128)(2,1)}) custom-call(s32[4]{0:T(128)S(1)} %get-tuple-element.622.pos, bf16[1536,1024]{1,0:T(8,128)(2,1)} %get-tuple-element.623.rows_ref, bf16[1536,1024]{1,0:T(8,128)(2,1)} %get-tuple-element.624.cot_ref, bf16[1024,2048]{1,0:T(8,128)(2,1)} %get-tuple-element.625.dgu_ref, ...), custom_call_target="tpu_custom_call" | custom-call | flops 4831838208 | bytes 4194304 | tf_op jit(solution)/shard_map/cond/branch_1_fun/pallas_call | solution.py:682
  305.4 5.3 branch_1_fun.39
  310.7 28.8 %conditional.21 = (bf16[256,1536]{1,0:T(8,128)(2,1)}, bf16[6,128,3072]{2,1,0:T(8,128)(2,1)}, bf16[6,128,768]{2,1,0:T(8,128)(2,1)}, bf16[6,128,768]{2,1,0:T(8,128...) conditional(s32[]{:T(128)} %convert_element_type.264, ...), branch_computations={%region_19.20_spmd, %region_20.21_spmd} | conditional | flops 3932160 | bytes 36438200 | solution.py:1021
  316.0 6.7 %branch_1_fun.41 = (bf16[6,128,768]{2,1,0:T(8,128)(2,1)}, bf16[6,128,768]{2,1,0:T(8,128)(2,1)}, bf16[6,128,768]{2,1,0:T(8,128)(2,1)}) custom-call(s32[4]{0:T(128)S(1)} %get-tuple-element.638.pos, bf16[6,128,3072]{2,1,0:T(8,128)(2,1)} %get-tuple-element.639.refs_0_.refs_2_.refs_4_, bf16[6,128,3072]{2,1,0:T(8,128)(2,1)} %get-tuple-element.640.refs_1_.refs_3_.refs_5_, ...), custom_call_target="tpu_custom_call" | custom-call | bytes 2097152 | tf_op jit(solution)/shard_map/cond/branch_1_fun/pallas_call | solution.py:731
  322.7 4.8 branch_1_fun.42
  332.7 6.8 %collective-permute-done.29 = bf16[6,128,768]{2,1,0:T(8,128)(2,1)} collective-permute-done((bf16[6,128,768]{2,1,0:T(8,128)(2,1)}, bf16[6,128,768]{2,1,0:T(8,128)(2,1)}, u32[]{:S(2)}, u32[]{:S(2)}) %collective-permute-start.29) | collective-permute-done | bytes 1179680 | tf_op jit(solution)/shard_map/cond/branch_1_fun/ppermute | solution.py:828
  339.5 44.7 %conditional.22 = (f32[256,1536]{1,0:T(8,128)}, bf16[256,1536]{1,0:T(8,128)(2,1)}, bf16[256,1536]{1,0:T(8,128)(2,1)}, bf16[256,1536]{1,0:T(8,128)(2,1)}, f32[1,1...) conditional(s32[]{:T(128)} %convert_element_type.264, ...), branch_computations={%region_21.22_spmd, %region_22.23_spmd} | conditional | flops 2315255808 | bytes 26882700 | solution.py:1021
  342.7 8.4 %branch_1_fun.43 = (f32[256,1536]{1,0:T(8,128)}, bf16[256,1536]{1,0:T(8,128)(2,1)}, f32[1,1536]{1,0:T(1,128)S(1)}, bf16[256,1536]{1,0:T(8,128)(2,1)}) custom-call(f32[256,1536]{1,0:T(8,128)} %get-tuple-element.650.refs_0_, bf16[256,1536]{1,0:T(8,128)(2,1)} %get-tuple-element.651.refs_1_, bf16[256,1536]{1,0:T(8,128)(2,1)} %get-tuple-element.652.refs_2_, ...), custom_call_target="tpu_custom_call" | custom-call | flops 301989888 | bytes 4194304 | tf_op jit(solution)/shard_map/cond/branch_1_fun/pallas_call | solution.py:273
  359.8 14.5 %branch_1_fun.44 = (bf16[256,1536]{1,0:T(8,128)(2,1)S(1)}, bf16[512,1024]{1,0:T(8,128)(2,1)}, bf16[512,1024]{1,0:T(8,128)(2,1)}) custom-call(s32[4]{0:T(128)S(1)} %get-tuple-element.661.pos, s32[8]{0:T(128)S(1)} %get-tuple-element.662.spans, bf16[256,1536]{1,0:T(8,128)(2,1)} %get-tuple-element.663.q_ref, bf16[256,1536]{1,0:T(8,128)(2,1)} %get-tuple-element.664.grad_ref, ...), custom_call_target="tpu_custom_call" | custom-call | flops 2013265920 | bytes 2097152 | tf_op jit(solution)/shard_map/cond/branch_1_fun/pallas_call | solution.py:190
  374.3 9.7 %collective-permute-done.35 = bf16[3,128,768]{2,1,0:T(8,128)(2,1)} collective-permute-done((bf16[3,128,768]{2,1,0:T(8,128)(2,1)}, bf16[3,128,768]{2,1,0:T(8,128)(2,1)}, u32[]{:S(2)}, u32[]{:S(2)}) %collective-permute-start.35) | collective-permute-done | bytes 589856 | tf_op jit(solution)/shard_map/cond/branch_1_fun/ppermute | solution.py:834
  384.3 46.3 %conditional.23 = (bf16[256,1024]{1,0:T(8,128)(2,1)}, bf16[256,1536]{1,0:T(8,128)(2,1)}, bf16[256,1536]{1,0:T(8,128)(2,1)}, bf16[256,1536]{1,0:T(8,128)(2,1)}, b...) conditional(s32[]{:T(128)} %convert_element_type.264, () %tuple.128, ...), branch_computations={%region_23.24_spmd, %region_24.25_spmd} | conditional | flops 4980768 | bytes 36569808 | solution.py:1021
  394.1 16.5 %collective-permute-done.43 = bf16[80,2048]{1,0:T(8,128)(2,1)} collective-permute-done((bf16[80,2048]{1,0:T(8,128)(2,1)S(1)}, bf16[80,2048]{1,0:T(8,128)(2,1)}, u32[]{:S(2)}, u32[]{:S(2)}) %collective-permute-start.43) | collective-permute-done | bytes 327712 | tf_op jit(solution)/shard_map/cond/branch_1_fun/ppermute | solution.py:834
  412.7 7.7 %collective-permute-done.41 = bf16[256,1536]{1,0:T(8,128)(2,1)} collective-permute-done((bf16[256,1536]{1,0:T(8,128)(2,1)S(1)}, bf16[256,1536]{1,0:T(8,128)(2,1)}, u32[]{:S(2)}, u32[]{:S(2)}) %collective-permute-start.41) | collective-permute-done | bytes 786464 | tf_op jit(solution)/shard_map/cond/branch_1_fun/ppermute | solution.py:846
  420.4 10.2 %collective-permute-done.38 = bf16[256,1536]{1,0:T(8,128)(2,1)} collective-permute-done((bf16[256,1536]{1,0:T(8,128)(2,1)S(1)}, bf16[256,1536]{1,0:T(8,128)(2,1)}, u32[]{:S(2)}, u32[]{:S(2)}) %collective-permute-start.38) | collective-permute-done | bytes 786464 | tf_op jit(solution)/shard_map/cond/branch_1_fun/ppermute | solution.py:834
  430.6 39.0 %conditional.24 = (bf16[256,1024]{1,0:T(8,128)(2,1)}, bf16[256,1024]{1,0:T(8,128)(2,1)}, bf16[256,1536]{1,0:T(8,128)(2,1)}, bf16[8,48,1536]{2,1,0:T(8,128)(2,1)S...) conditional(s32[]{:T(128)} %convert_element_type.264, ...), branch_computations={%region_25.26_spmd, %region_26.27_spmd} | conditional | flops 1109655552 | bytes 32125660 | solution.py:1021
  445.0 8.8 %branch_1_fun.47 = (f32[256,1536]{1,0:T(8,128)}, f32[1,1536]{1,0:T(1,128)S(1)}) custom-call(bf16[256,1536]{1,0:T(8,128)(2,1)S(1)} %get-tuple-element.699.dq_ref, bf16[256,1024]{1,0:T(8,128)(2,1)} %get-tuple-element.688.dkv_ref, bf16[1536,1536]{1,0:T(8,128)(2,1)} %get-tuple-element.700.wq_ref, bf16[1536,512]{1,0:T(8,128)(2,1)S(1)} %get-tuple-element.701.wk_ref, ...), custom_call_target="tpu_custom_call" | custom-call | flops 503316480 | bytes 3670016 | tf_op jit(solution)/shard_map/cond/branch_1_fun/pallas_call | solution.py:324
  458.5 11.2 %collective-permute-done.44 = bf16[256,1024]{1,0:T(8,128)(2,1)} collective-permute-done((bf16[256,1024]{1,0:T(8,128)(2,1)}, bf16[256,1024]{1,0:T(8,128)(2,1)}, u32[]{:S(2)}, u32[]{:S(2)}) %collective-permute-start.44) | collective-permute-done | bytes 524320 | tf_op jit(solution)/shard_map/cond/branch_1_fun/ppermute | solution.py:834
  469.7 90.6 %conditional.25 = (f32[2,48]{1,0:T(2,128)}, f32[32,1536]{1,0:T(8,128)}, f32[48,1536]{1,0:T(8,128)}, f32[48,1536]{1,0:T(8,128)}, f32[2,384,512]{2,1,0:T(8,128)}, ...) conditional(s32[]{:T(128)} %convert_element_type.264, ...), branch_computations={%region_27.28_spmd, %region_28.30_spmd} | conditional | flops 1014454272 | bytes 76977520 | solution.py:1021
  477.5 5.1 branch_1_fun.49
  521.6 6.6 %branch_1_fun.51 = (bf16[3,128,768]{2,1,0:T(8,128)(2,1)}, bf16[3,128,768]{2,1,0:T(8,128)(2,1)}, bf16[3,128,768]{2,1,0:T(8,128)(2,1)}, bf16[3,128,768]{2,1,0:T(8,128)(2,1)}) custom-call(s32[4]{0:T(128)S(1)} %get-tuple-element.723.pos, bf16[6,128,3072]{2,1,0:T(8,128)(2,1)} %get-tuple-element.732.refs_0_.refs_3_.refs_4_.refs_8_.refs_12_, ...), custom_call_target="tpu_custom_call" | custom-call | bytes 2097152 | tf_op jit(solution)/shard_map/cond/branch_1_fun/pallas_call | solution.py:731
  528.2 8.8 %branch_1_fun.52 = (f32[2,384,512]{2,1,0:T(8,128)}, f32[2,384,512]{2,1,0:T(8,128)}, f32[2,512,384]{2,1,0:T(8,128)}) custom-call(bf16[384,768]{1,0:T(8,128)(2,1)} %bitcast.146, bf16[384,768]{1,0:T(8,128)(2,1)} %bitcast.147, bf16[384,768]{1,0:T(8,128)(2,1)} %bitcast.148, bf16[384,768]{1,0:T(8,128)(2,1)} %bitcast.149), custom_call_target="tpu_custom_call" | custom-call | bytes 2097152 | tf_op jit(solution)/shard_map/cond/branch_1_fun/pallas_call | solution.py:791
  546.3 7.4 %collective-permute-done.59 = bf16[48,1536]{1,0:T(8,128)(2,1)S(1)} collective-permute-done((bf16[48,1536]{1,0:T(8,128)(2,1)S(1)}, bf16[48,1536]{1,0:T(8,128)(2,1)S(1)}, u32[]{:S(2)}, u32[]{:S(2)}) %collective-permute-start.59) | collective-permute-done | bytes 147488 | tf_op jit(solution)/shard_map/cond/branch_1_fun/ppermute | solution.py:834
  (274 shorter events, 186.7 us)
Async XLA Ops:
  15.4 22.7 %collective-permute-start.71 = (bf16[256,1664]{1,0:T(8,128)(2,1)}, bf16[256,1664]{1,0:T(8,128)(2,1)}, u32[]{:S(2)}, u32[]{:S(2)}) collective-permute-start(bf16[256,1664]{1,0:T(8,128)(2,1)} %get-tuple-element.467), channel_id=1, source_target_pairs={{0,2},{1,3},{2,4},{3,5},{4,6},{5,7},{6,0},{7,1},{8,14},{9,15},{10,... | collective-permute-start | bytes 2555912 | tf_op jit(solution)/shard_map/cond/branch_1_fun/ppermute | solution.py:846
  38.2 21.0 %collective-permute-start.1 = (bf16[256,1536]{1,0:T(8,128)(2,1)}, bf16[256,1536]{1,0:T(8,128)(2,1)}, u32[]{:S(2)}, u32[]{:S(2)}) collective-permute-start(bf16[256,1536]{1,0:T(8,128)(2,1)} %get-tuple-element.484), channel_id=1, source_target_pairs={{0,8},{8,0},{16,24},{24,16},{1,9},{9,1},{17,25},{25,17},{2,10},{10... | collective-permute-start | bytes 2359304 | tf_op jit(solution)/shard_map/cond/branch_1_fun/ppermute | solution.py:828
  38.3 21.0 %collective-permute-start = (bf16[256,1536]{1,0:T(8,128)(2,1)}, bf16[256,1536]{1,0:T(8,128)(2,1)}, u32[]{:S(2)}, u32[]{:S(2)}) collective-permute-start(bf16[256,1536]{1,0:T(8,128)(2,1)} %get-tuple-element.484), channel_id=1, source_target_pairs={{0,16},{8,24},{16,0},{24,8},{1,17},{9,25},{17,1},{25,9},{2,18},{10... | collective-permute-start | bytes 2359304 | tf_op jit(solution)/shard_map/cond/branch_1_fun/ppermute | solution.py:834
  38.9 22.7 %collective-permute-start.2 = (bf16[256,1664]{1,0:T(8,128)(2,1)}, bf16[256,1664]{1,0:T(8,128)(2,1)}, u32[]{:S(2)}, u32[]{:S(2)}) collective-permute-start(bf16[256,1664]{1,0:T(8,128)(2,1)} %get-tuple-element.485), channel_id=1, source_target_pairs={{0,2},{1,3},{2,4},{3,5},{4,6},{5,7},{6,0},{7,1},{8,14},{9,15},{10,... | collective-permute-start | bytes 2555912 | tf_op jit(solution)/shard_map/cond/branch_1_fun/ppermute | solution.py:846
  64.7 45.3 %collective-permute-start.7 = (bf16[256,1536]{1,0:T(8,128)(2,1)}, bf16[256,1536]{1,0:T(8,128)(2,1)}, u32[]{:S(2)}, u32[]{:S(2)}) collective-permute-start(bf16[256,1536]{1,0:T(8,128)(2,1)} %get-tuple-element.511), channel_id=1, source_target_pairs={{0,8},{8,0},{16,24},{24,16},{1,9},{9,1},{17,25},{25,17},{2,10},{10... | collective-permute-start | bytes 2359304 | tf_op jit(solution)/shard_map/cond/branch_1_fun/ppermute | solution.py:828
  64.9 45.2 %collective-permute-start.6 = (bf16[256,1536]{1,0:T(8,128)(2,1)}, bf16[256,1536]{1,0:T(8,128)(2,1)}, u32[]{:S(2)}, u32[]{:S(2)}) collective-permute-start(bf16[256,1536]{1,0:T(8,128)(2,1)} %get-tuple-element.511), channel_id=1, source_target_pairs={{0,16},{8,24},{16,0},{24,8},{1,17},{9,25},{17,1},{25,9},{2,18},{10... | collective-permute-start | bytes 2359304 | tf_op jit(solution)/shard_map/cond/branch_1_fun/ppermute | solution.py:834
  66.4 43.7 %collective-permute-start.5 = (bf16[256,1664]{1,0:T(8,128)(2,1)}, bf16[256,1664]{1,0:T(8,128)(2,1)}, u32[]{:S(2)}, u32[]{:S(2)}) collective-permute-start(bf16[256,1664]{1,0:T(8,128)(2,1)} %get-tuple-element.489), channel_id=1, source_target_pairs={{0,2},{1,3},{2,4},{3,5},{4,6},{5,7},{6,0},{7,1},{8,14},{9,15},{10,... | collective-permute-start | bytes 2555912 | tf_op jit(solution)/shard_map/cond/branch_1_fun/ppermute | solution.py:846
  83.1 27.0 %collective-permute-start.4 = (bf16[256,1536]{1,0:T(8,128)(2,1)}, bf16[256,1536]{1,0:T(8,128)(2,1)}, u32[]{:S(2)}, u32[]{:S(2)}) collective-permute-start(bf16[256,1536]{1,0:T(8,128)(2,1)} %get-tuple-element.488.x_ref), channel_id=1, source_target_pairs={{0,2},{1,3},{2,4},{3,5},{4,6},{5,7},{6,0},{7,1},{8,14},{9,15},{10,... | collective-permute-start | bytes 2359304 | tf_op jit(solution)/shard_map/cond/branch_1_fun/ppermute | solution.py:846
  83.7 26.4 %collective-permute-start.10 = (bf16[1536,256]{1,0:T(8,128)(2,1)}, bf16[1536,256]{1,0:T(8,128)(2,1)}, u32[]{:S(2)}, u32[]{:S(2)}) collective-permute-start(bf16[1536,256]{1,0:T(8,128)(2,1)} %slice.139), channel_id=1, source_target_pairs={{0,1},{1,0},{2,3},{3,2},{4,5},{5,4},{6,7},{7,6},{8,9},{9,8},{10,11... | collective-permute-start | bytes 2359304 | tf_op jit(solution)/shard_map/cond/branch_1_fun/ppermute | solution.py:828
  110.3 25.5 %collective-permute-start.12 = (bf16[256,1536]{1,0:T(8,128)(2,1)}, bf16[256,1536]{1,0:T(8,128)(2,1)}, u32[]{:S(2)}, u32[]{:S(2)}) collective-permute-start(bf16[256,1536]{1,0:T(8,128)(2,1)} %get-tuple-element.540), channel_id=1, source_target_pairs={{0,8},{8,0},{16,24},{24,16},{1,9},{9,1},{17,25},{25,17},{2,10},{10... | collective-permute-start | bytes 2359304 | tf_op jit(solution)/shard_map/cond/branch_1_fun/ppermute | solution.py:828
  110.4 25.5 %collective-permute-start.11 = (bf16[256,1536]{1,0:T(8,128)(2,1)}, bf16[256,1536]{1,0:T(8,128)(2,1)}, u32[]{:S(2)}, u32[]{:S(2)}) collective-permute-start(bf16[256,1536]{1,0:T(8,128)(2,1)} %get-tuple-element.514.x_ref), channel_id=1, source_target_pairs={{0,2},{1,3},{2,4},{3,5},{4,6},{5,7},{6,0},{7,1},{8,14},{9,15},{10,... | collective-permute-start | bytes 2359304 | tf_op jit(solution)/shard_map/cond/branch_1_fun/ppermute | solution.py:846
  114.0 21.8 %collective-permute-start.13 = (bf16[1536,256]{1,0:T(8,128)(2,1)}, bf16[1536,256]{1,0:T(8,128)(2,1)}, u32[]{:S(2)}, u32[]{:S(2)}) collective-permute-start(bf16[1536,256]{1,0:T(8,128)(2,1)} %slice.140), channel_id=1, source_target_pairs={{0,1},{1,0},{2,3},{3,2},{4,5},{5,4},{6,7},{7,6},{8,9},{9,8},{10,11... | collective-permute-start | bytes 2359304 | tf_op jit(solution)/shard_map/cond/branch_1_fun/ppermute | solution.py:828
  135.8 44.5 %collective-permute-start.20 = (bf16[16,80,2048]{2,1,0:T(8,128)(2,1)}, bf16[16,80,2048]{2,1,0:T(8,128)(2,1)}, u32[]{:S(2)}, u32[]{:S(2)}) collective-permute-start(bf16[16,80,2048]{2,1,0:T(8,128)(2,1)} %get-tuple-element.567), channel_id=1, source_target_pairs={{0,8},{8,0},{16,24},{24,16},{1,9},{9,1},{17,25},{25,17},{2,10},{10... | collective-permute-start | bytes 15728648 | tf_op jit(solution)/shard_map/cond/branch_1_fun/ppermute | solution.py:828
  141.7 31.4 %collective-permute-start.16 = (bf16[256,1536]{1,0:T(8,128)(2,1)}, bf16[256,1536]{1,0:T(8,128)(2,1)}, u32[]{:S(2)}, u32[]{:S(2)}) collective-permute-start(bf16[256,1536]{1,0:T(8,128)(2,1)} %get-tuple-element.564), channel_id=1, source_target_pairs={{0,8},{8,0},{16,24},{24,16},{1,9},{9,1},{17,25},{25,17},{2,10},{10... | collective-permute-start | bytes 2359304 | tf_op jit(solution)/shard_map/cond/branch_1_fun/ppermute | solution.py:828
  160.0 20.4 %collective-permute-start.19 = (bf16[256,1536]{1,0:T(8,128)(2,1)}, bf16[256,1536]{1,0:T(8,128)(2,1)}, u32[]{:S(2)}, u32[]{:S(2)}) collective-permute-start(bf16[256,1536]{1,0:T(8,128)(2,1)} %get-tuple-element.543.x_ref), channel_id=1, source_target_pairs={{0,2},{1,3},{2,4},{3,5},{4,6},{5,7},{6,0},{7,1},{8,14},{9,15},{10,... | collective-permute-start | bytes 2359304 | tf_op jit(solution)/shard_map/cond/branch_1_fun/ppermute | solution.py:846
  185.8 51.6 %collective-permute-start.52 = (bf16[4,80,2048]{2,1,0:T(8,128)(2,1)}, bf16[4,80,2048]{2,1,0:T(8,128)(2,1)}, u32[]{:S(2)}, u32[]{:S(2)}) collective-permute-start(bf16[4,80,2048]{2,1,0:T(8,128)(2,1)} %get-tuple-element.606), channel_id=1, source_target_pairs={{0,1},{1,0},{2,3},{3,2},{4,5},{5,4},{6,7},{7,6},{8,9},{9,8},{10,11... | collective-permute-start | bytes 3932168 | tf_op jit(solution)/shard_map/cond/branch_1_fun/ppermute | solution.py:828
  239.2 31.2 %collective-permute-start.23 = (bf16[4,80,2048]{2,1,0:T(8,128)(2,1)}, bf16[4,80,2048]{2,1,0:T(8,128)(2,1)}, u32[]{:S(2)}, u32[]{:S(2)}) collective-permute-start(bf16[4,80,2048]{2,1,0:T(8,128)(2,1)} %get-tuple-element.617), channel_id=1, source_target_pairs={{0,1},{1,0},{2,3},{3,2},{4,5},{5,4},{6,7},{7,6},{8,9},{9,8},{10,11... | collective-permute-start | bytes 3932168 | tf_op jit(solution)/shard_map/cond/branch_1_fun/ppermute | solution.py:828
  241.1 23.8 %collective-permute-start.22 = (bf16[256,1536]{1,0:T(8,128)(2,1)S(1)}, bf16[256,1536]{1,0:T(8,128)(2,1)}, u32[]{:S(2)}, u32[]{:S(2)}) collective-permute-start(bf16[256,1536]{1,0:T(8,128)(2,1)S(1)} %add_convert_fusion), channel_id=1, source_target_pairs={{0,6},{1,7},{2,0},{3,1},{4,2},{5,3},{6,4},{7,5},{8,10},{9,11},{10,... | collective-permute-start | bytes 2359304 | tf_op jit(solution)/shard_map/cond/branch_1_fun/ppermute | solution.py:846
  273.5 31.9 %collective-permute-start.25 = (bf16[6,128,3072]{2,1,0:T(8,128)(2,1)}, bf16[6,128,3072]{2,1,0:T(8,128)(2,1)}, u32[]{:S(2)}, u32[]{:S(2)}) collective-permute-start(bf16[6,128,3072]{2,1,0:T(8,128)(2,1)} %get-tuple-element.621), channel_id=1, source_target_pairs={{0,8},{8,0},{16,24},{24,16},{1,9},{9,1},{17,25},{25,17},{2,10},{10... | collective-permute-start | bytes 14155784 | tf_op jit(solution)/shard_map/cond/branch_1_fun/ppermute | solution.py:828
  278.0 32.7 %collective-permute-start.26 = (bf16[4,80,2048]{2,1,0:T(8,128)(2,1)}, bf16[4,80,2048]{2,1,0:T(8,128)(2,1)}, u32[]{:S(2)}, u32[]{:S(2)}) collective-permute-start(bf16[4,80,2048]{2,1,0:T(8,128)(2,1)} %branch_1_fun.40), channel_id=1, source_target_pairs={{0,16},{8,24},{16,0},{24,8},{1,17},{9,25},{17,1},{25,9},{2,18},{10... | collective-permute-start | bytes 3932168 | tf_op jit(solution)/shard_map/cond/branch_1_fun/ppermute | solution.py:834
  282.0 28.7 %collective-permute-start.24 = (bf16[256,1536]{1,0:T(8,128)(2,1)}, bf16[256,1536]{1,0:T(8,128)(2,1)}, u32[]{:S(2)}, u32[]{:S(2)}) collective-permute-start(bf16[256,1536]{1,0:T(8,128)(2,1)} %add_convert_fusion.1), channel_id=1, source_target_pairs={{0,6},{1,7},{2,0},{3,1},{4,2},{5,3},{6,4},{7,5},{8,10},{9,11},{10,... | collective-permute-start | bytes 2359304 | tf_op jit(solution)/shard_map/cond/branch_1_fun/ppermute | solution.py:846
  310.7 28.8 %collective-permute-start.28 = (bf16[6,128,3072]{2,1,0:T(8,128)(2,1)}, bf16[6,128,3072]{2,1,0:T(8,128)(2,1)}, u32[]{:S(2)}, u32[]{:S(2)}) collective-permute-start(bf16[6,128,3072]{2,1,0:T(8,128)(2,1)} %get-tuple-element.636), channel_id=1, source_target_pairs={{0,8},{8,0},{16,24},{24,16},{1,9},{9,1},{17,25},{25,17},{2,10},{10... | collective-permute-start | bytes 14155784 | tf_op jit(solution)/shard_map/cond/branch_1_fun/ppermute | solution.py:828
  310.8 28.7 %collective-permute-start.29 = (bf16[6,128,768]{2,1,0:T(8,128)(2,1)}, bf16[6,128,768]{2,1,0:T(8,128)(2,1)}, u32[]{:S(2)}, u32[]{:S(2)}) collective-permute-start(bf16[6,128,768]{2,1,0:T(8,128)(2,1)} %get-tuple-element.637), channel_id=1, source_target_pairs={{0,1},{1,0},{2,3},{3,2},{4,5},{5,4},{6,7},{7,6},{8,9},{9,8},{10,11... | collective-permute-start | bytes 3538952 | tf_op jit(solution)/shard_map/cond/branch_1_fun/ppermute | solution.py:828
  339.5 44.5 %collective-permute-start.33 = (bf16[6,128,768]{2,1,0:T(8,128)(2,1)}, bf16[6,128,768]{2,1,0:T(8,128)(2,1)}, u32[]{:S(2)}, u32[]{:S(2)}) collective-permute-start(bf16[6,128,768]{2,1,0:T(8,128)(2,1)} %get-tuple-element.674), channel_id=1, source_target_pairs={{0,1},{1,0},{2,3},{3,2},{4,5},{5,4},{6,7},{7,6},{8,9},{9,8},{10,11... | collective-permute-start | bytes 3538952 | tf_op jit(solution)/shard_map/cond/branch_1_fun/ppermute | solution.py:828
  351.1 32.9 %collective-permute-start.31 = (bf16[256,1536]{1,0:T(8,128)(2,1)}, bf16[256,1536]{1,0:T(8,128)(2,1)}, u32[]{:S(2)}, u32[]{:S(2)}) collective-permute-start(bf16[256,1536]{1,0:T(8,128)(2,1)} %get-tuple-element.1313), channel_id=1, source_target_pairs={{0,8},{8,0},{16,24},{24,16},{1,9},{9,1},{17,25},{25,17},{2,10},{10... | collective-permute-start | bytes 2359304 | tf_op jit(solution)/shard_map/cond/branch_1_fun/ppermute | solution.py:828
  351.1 32.9 %collective-permute-start.30 = (bf16[256,1536]{1,0:T(8,128)(2,1)}, bf16[256,1536]{1,0:T(8,128)(2,1)}, u32[]{:S(2)}, u32[]{:S(2)}) collective-permute-start(bf16[256,1536]{1,0:T(8,128)(2,1)} %get-tuple-element.1313), channel_id=1, source_target_pairs={{0,16},{8,24},{16,0},{24,8},{1,17},{9,25},{17,1},{25,9},{2,18},{10... | collective-permute-start | bytes 2359304 | tf_op jit(solution)/shard_map/cond/branch_1_fun/ppermute | solution.py:834
  351.6 32.4 %collective-permute-start.32 = (bf16[256,1536]{1,0:T(8,128)(2,1)}, bf16[256,1536]{1,0:T(8,128)(2,1)}, u32[]{:S(2)}, u32[]{:S(2)}) collective-permute-start(bf16[256,1536]{1,0:T(8,128)(2,1)} %get-tuple-element.673), channel_id=1, source_target_pairs={{0,6},{1,7},{2,0},{3,1},{4,2},{5,3},{6,4},{7,5},{8,10},{9,11},{10,... | collective-permute-start | bytes 2359304 | tf_op jit(solution)/shard_map/cond/branch_1_fun/ppermute | solution.py:846
  358.3 25.7 %collective-permute-start.35 = (bf16[3,128,768]{2,1,0:T(8,128)(2,1)}, bf16[3,128,768]{2,1,0:T(8,128)(2,1)}, u32[]{:S(2)}, u32[]{:S(2)}) collective-permute-start(bf16[3,128,768]{2,1,0:T(8,128)(2,1)} %branch_1_fun.45), channel_id=1, source_target_pairs={{0,16},{8,24},{16,0},{24,8},{1,17},{9,25},{17,1},{25,9},{2,18},{10... | collective-permute-start | bytes 1769480 | tf_op jit(solution)/shard_map/cond/branch_1_fun/ppermute | solution.py:834
  385.6 25.0 %collective-permute-start.43 = (bf16[80,2048]{1,0:T(8,128)(2,1)S(1)}, bf16[80,2048]{1,0:T(8,128)(2,1)}, u32[]{:S(2)}, u32[]{:S(2)}) collective-permute-start(bf16[80,2048]{1,0:T(8,128)(2,1)S(1)} %dynamic-slice_bitcast_fusion.7), channel_id=1, source_target_pairs={{0,4},{1,5},{2,6},{3,7},{4,0},{5,1},{6,2},{7,3},{8,12},{9,13},{10,... | collective-permute-start | bytes 983048 | tf_op jit(solution)/shard_map/cond/branch_1_fun/ppermute | solution.py:834
  387.5 43.2 %collective-permute-start.42 = (bf16[6,128,768]{2,1,0:T(8,128)(2,1)}, bf16[6,128,768]{2,1,0:T(8,128)(2,1)}, u32[]{:S(2)}, u32[]{:S(2)}) collective-permute-start(bf16[6,128,768]{2,1,0:T(8,128)(2,1)} %get-tuple-element.686), channel_id=1, source_target_pairs={{0,1},{1,0},{2,3},{3,2},{4,5},{5,4},{6,7},{7,6},{8,9},{9,8},{10,11... | collective-permute-start | bytes 3538952 | tf_op jit(solution)/shard_map/cond/branch_1_fun/ppermute | solution.py:828
  392.9 27.4 %collective-permute-start.41 = (bf16[256,1536]{1,0:T(8,128)(2,1)S(1)}, bf16[256,1536]{1,0:T(8,128)(2,1)}, u32[]{:S(2)}, u32[]{:S(2)}) collective-permute-start(bf16[256,1536]{1,0:T(8,128)(2,1)S(1)} %add_convert_fusion.4), channel_id=1, source_target_pairs={{0,6},{1,7},{2,0},{3,1},{4,2},{5,3},{6,4},{7,5},{8,10},{9,11},{10,... | collective-permute-start | bytes 2359304 | tf_op jit(solution)/shard_map/cond/branch_1_fun/ppermute | solution.py:846
  394.1 26.3 %collective-permute-start.40 = (bf16[256,1536]{1,0:T(8,128)(2,1)}, bf16[256,1536]{1,0:T(8,128)(2,1)}, u32[]{:S(2)}, u32[]{:S(2)}) collective-permute-start(bf16[256,1536]{1,0:T(8,128)(2,1)} %get-tuple-element.682), channel_id=1, source_target_pairs={{0,8},{8,0},{16,24},{24,16},{1,9},{9,1},{17,25},{25,17},{2,10},{10... | collective-permute-start | bytes 2359304 | tf_op jit(solution)/shard_map/cond/branch_1_fun/ppermute | solution.py:828
  434.2 35.4 %collective-permute-start.48 = (bf16[6,128,768]{2,1,0:T(8,128)(2,1)}, bf16[6,128,768]{2,1,0:T(8,128)(2,1)}, u32[]{:S(2)}, u32[]{:S(2)}) collective-permute-start(bf16[6,128,768]{2,1,0:T(8,128)(2,1)} %get-tuple-element.710), channel_id=1, source_target_pairs={{0,1},{1,0},{2,3},{3,2},{4,5},{5,4},{6,7},{7,6},{8,9},{9,8},{10,11... | collective-permute-start | bytes 3538952 | tf_op jit(solution)/shard_map/cond/branch_1_fun/ppermute | solution.py:828
  438.4 31.2 %collective-permute-start.47 = (bf16[256,1536]{1,0:T(8,128)(2,1)}, bf16[256,1536]{1,0:T(8,128)(2,1)}, u32[]{:S(2)}, u32[]{:S(2)}) collective-permute-start(bf16[256,1536]{1,0:T(8,128)(2,1)} %add_convert_fusion.7), channel_id=1, source_target_pairs={{0,6},{1,7},{2,0},{3,1},{4,2},{5,3},{6,4},{7,5},{8,10},{9,11},{10,... | collective-permute-start | bytes 2359304 | tf_op jit(solution)/shard_map/cond/branch_1_fun/ppermute | solution.py:846
  438.6 31.1 %collective-permute-start.46 = (bf16[256,1536]{1,0:T(8,128)(2,1)}, bf16[256,1536]{1,0:T(8,128)(2,1)}, u32[]{:S(2)}, u32[]{:S(2)}) collective-permute-start(bf16[256,1536]{1,0:T(8,128)(2,1)} %get-tuple-element.689), channel_id=1, source_target_pairs={{0,8},{8,0},{16,24},{24,16},{1,9},{9,1},{17,25},{25,17},{2,10},{10... | collective-permute-start | bytes 2359304 | tf_op jit(solution)/shard_map/cond/branch_1_fun/ppermute | solution.py:828
  442.4 27.3 %collective-permute-start.50 = (bf16[3,128,768]{2,1,0:T(8,128)(2,1)}, bf16[3,128,768]{2,1,0:T(8,128)(2,1)}, u32[]{:S(2)}, u32[]{:S(2)}) collective-permute-start(bf16[3,128,768]{2,1,0:T(8,128)(2,1)} %branch_1_fun.48), channel_id=1, source_target_pairs={{0,16},{8,24},{16,0},{24,8},{1,17},{9,25},{17,1},{25,9},{2,18},{10... | collective-permute-start | bytes 1769480 | tf_op jit(solution)/shard_map/cond/branch_1_fun/ppermute | solution.py:834
  442.7 26.9 %collective-permute-start.44 = (bf16[256,1024]{1,0:T(8,128)(2,1)}, bf16[256,1024]{1,0:T(8,128)(2,1)}, u32[]{:S(2)}, u32[]{:S(2)}) collective-permute-start(bf16[256,1024]{1,0:T(8,128)(2,1)} %get-tuple-element.688.dkv_ref), channel_id=1, source_target_pairs={{0,16},{8,24},{16,0},{24,8},{1,17},{9,25},{17,1},{25,9},{2,18},{10... | collective-permute-start | bytes 1572872 | tf_op jit(solution)/shard_map/cond/branch_1_fun/ppermute | solution.py:834
  470.6 31.6 %all-to-all-start = ((f32[32,2,48]{2,1,0:T(2,128)}), f32[32,2,48]{2,1,0:T(2,128)}, u32[]{:S(2)}, u32[]{:S(2)}) async-start(f32[32,2,48]{2,1,0:T(2,128)} %pad_maximum_fusion), calls=%async_computation | async-start | bytes 65536 | tf_op jit(solution)/shard_map/cond/branch_1_fun/all_to_all | solution.py:1222
  474.5 30.7 %collective-permute-start.63 = (bf16[256,1024]{1,0:T(8,128)(2,1)}, bf16[256,1024]{1,0:T(8,128)(2,1)}, u32[]{:S(2)}, u32[]{:S(2)}) collective-permute-start(bf16[256,1024]{1,0:T(8,128)(2,1)} %get-tuple-element.756.refs_6_), channel_id=1, source_target_pairs={{0,8},{8,0},{16,24},{24,16},{1,9},{9,1},{17,25},{25,17},{2,10},{10... | collective-permute-start | bytes 1572872 | tf_op jit(solution)/shard_map/cond/branch_1_fun/ppermute | solution.py:828
  475.8 34.5 %collective-permute-start.53 = (bf16[4,48,1536]{2,1,0:T(8,128)(2,1)}, bf16[4,48,1536]{2,1,0:T(8,128)(2,1)}, u32[]{:S(2)}, u32[]{:S(2)}) collective-permute-start(bf16[4,48,1536]{2,1,0:T(8,128)(2,1)} %dynamic-slice_bitcast_fusion.10), channel_id=1, source_target_pairs={{0,1},{1,0},{2,3},{3,2},{4,5},{5,4},{6,7},{7,6},{8,9},{9,8},{10,11... | collective-permute-start | bytes 1769480 | tf_op jit(solution)/shard_map/cond/branch_1_fun/ppermute | solution.py:828
  484.5 31.8 %collective-permute-start.57 = (bf16[4,48,1536]{2,1,0:T(8,128)(2,1)}, bf16[4,48,1536]{2,1,0:T(8,128)(2,1)}, u32[]{:S(2)}, u32[]{:S(2)}) collective-permute-start(bf16[4,48,1536]{2,1,0:T(8,128)(2,1)} %dynamic-slice_bitcast_fusion.9), channel_id=1, source_target_pairs={{0,1},{1,0},{2,3},{3,2},{4,5},{5,4},{6,7},{7,6},{8,9},{9,8},{10,11... | collective-permute-start | bytes 1769480 | tf_op jit(solution)/shard_map/cond/branch_1_fun/ppermute | solution.py:828
  489.3 29.2 %collective-permute-start.61 = (bf16[3,128,768]{2,1,0:T(8,128)(2,1)}, bf16[3,128,768]{2,1,0:T(8,128)(2,1)}, u32[]{:S(2)}, u32[]{:S(2)}) collective-permute-start(bf16[3,128,768]{2,1,0:T(8,128)(2,1)} %get-tuple-element.740), channel_id=1, source_target_pairs={{0,16},{8,24},{16,0},{24,8},{1,17},{9,25},{17,1},{25,9},{2,18},{10... | collective-permute-start | bytes 1769480 | tf_op jit(solution)/shard_map/cond/branch_1_fun/ppermute | solution.py:834
  491.0 29.0 %collective-permute-start.62 = (bf16[3,128,768]{2,1,0:T(8,128)(2,1)}, bf16[3,128,768]{2,1,0:T(8,128)(2,1)}, u32[]{:S(2)}, u32[]{:S(2)}) collective-permute-start(bf16[3,128,768]{2,1,0:T(8,128)(2,1)} %get-tuple-element.741), channel_id=1, source_target_pairs={{0,16},{8,24},{16,0},{24,8},{1,17},{9,25},{17,1},{25,9},{2,18},{10... | collective-permute-start | bytes 1769480 | tf_op jit(solution)/shard_map/cond/branch_1_fun/ppermute | solution.py:834
  512.6 24.4 %collective-permute-start.54 = (bf16[48,1536]{1,0:T(8,128)(2,1)}, bf16[48,1536]{1,0:T(8,128)(2,1)S(1)}, u32[]{:S(2)}, u32[]{:S(2)}) collective-permute-start(bf16[48,1536]{1,0:T(8,128)(2,1)} %get-tuple-element.1082), channel_id=1, source_target_pairs={{0,2},{1,3},{2,4},{3,5},{4,6},{5,7},{6,0},{7,1},{8,10},{9,11},{10,... | collective-permute-start | bytes 442376 | tf_op jit(solution)/shard_map/cond/branch_1_fun/ppermute | solution.py:834
  514.2 25.1 %collective-permute-start.56 = (bf16[48,1536]{1,0:T(8,128)(2,1)}, bf16[48,1536]{1,0:T(8,128)(2,1)S(1)}, u32[]{:S(2)}, u32[]{:S(2)}) collective-permute-start(bf16[48,1536]{1,0:T(8,128)(2,1)} %get-tuple-element.1083), channel_id=1, source_target_pairs={{0,6},{1,7},{2,0},{3,1},{4,2},{5,3},{6,4},{7,5},{8,14},{9,15},{10,... | collective-permute-start | bytes 442376 | tf_op jit(solution)/shard_map/cond/branch_1_fun/ppermute | solution.py:834
  516.4 23.5 %collective-permute-start.55 = (bf16[48,1536]{1,0:T(8,128)(2,1)S(1)}, bf16[48,1536]{1,0:T(8,128)(2,1)S(1)}, u32[]{:S(2)}, u32[]{:S(2)}) collective-permute-start(bf16[48,1536]{1,0:T(8,128)(2,1)S(1)} %get-tuple-element.1084), channel_id=1, source_target_pairs={{0,4},{1,5},{2,6},{3,7},{4,0},{5,1},{6,2},{7,3},{8,12},{9,13},{10,... | collective-permute-start | bytes 442376 | tf_op jit(solution)/shard_map/cond/branch_1_fun/ppermute | solution.py:834
  518.5 23.1 %collective-permute-start.64 = (bf16[4,48,1024]{2,1,0:T(8,128)(2,1)S(1)}, bf16[4,48,1024]{2,1,0:T(8,128)(2,1)S(1)}, u32[]{:S(2)}, u32[]{:S(2)}) collective-permute-start(bf16[4,48,1024]{2,1,0:T(8,128)(2,1)S(1)} %dynamic-slice_bitcast_fusion.11), channel_id=1, source_target_pairs={{0,1},{1,0},{2,3},{3,2},{4,5},{5,4},{6,7},{7,6},{8,9},{9,8},{10,11... | collective-permute-start | bytes 1179656 | tf_op jit(solution)/shard_map/cond/branch_1_fun/ppermute | solution.py:828
  520.0 25.7 %collective-permute-start.58 = (bf16[48,1536]{1,0:T(8,128)(2,1)S(1)}, bf16[48,1536]{1,0:T(8,128)(2,1)S(1)}, u32[]{:S(2)}, u32[]{:S(2)}) collective-permute-start(bf16[48,1536]{1,0:T(8,128)(2,1)S(1)} %get-tuple-element.1079), channel_id=1, source_target_pairs={{0,2},{1,3},{2,4},{3,5},{4,6},{5,7},{6,0},{7,1},{8,10},{9,11},{10,... | collective-permute-start | bytes 442376 | tf_op jit(solution)/shard_map/cond/branch_1_fun/ppermute | solution.py:834
  (56 other events, 741.5 us)

commit v3 on v2

--- a/solution.py
+++ b/solution.py
@@ -465,84 +465,97 @@
     return result[0], result[1], result[2:]
 
 
-def others_kernel(sets, per, extra, pos, x_ref, c_ref, *refs):
-    weights = refs[: 3 * sets * per]
-    out_ref, grad_ref, hid_ref, dgu_ref = refs[3 * sets * per + extra :]
+def others_kernel(sets, per, bands, extra, pos, x_ref, c_ref, *refs):
+    each = bands + per
+    weights = [refs[t * each : (t + 1) * each] for t in range(sets)]
+    *result_refs, hid_ref, dgu_ref = refs[sets * each + extra :]
+    out_refs, grad_refs = result_refs[: len(result_refs) // 2], result_refs[len(result_refs) // 2 :]
     step = pl.program_id(0)
-    chunk = weights[0].shape[1]
     width = x_ref.shape[1]
-    tile = out_ref.shape[1]
+    band = width // bands
+    chunk = weights[0][bands].shape[0]
+    rows = out_refs[0].shape[0]
 
     def places(t, n):
         at = (lax.rem(pos[1] + t, 2) * per + n) * chunk
         cut = lambda first: pl.ds(pl.multiple_of(first, chunk), chunk)
         return cut(at), cut(2 * at), cut(2 * at + chunk)
 
-    def hidden_chunk(t, n, wg_ref, wu_ref, wd_ref):
+    def columns(n):
+        return slice(n * chunk, (n + 1) * chunk), slice((per + n) * chunk, (per + n + 1) * chunk)
+
+    def hidden_chunk(t, n):
         at_hidden, at_gate, at_up = places(t, n)
+        gate_cut, up_cut = columns(n)
         expert = (2 * pos[2] + 1 - pos[3]) * sets + lax.rem(pos[1] + t, 2)
-        for p in range(2):
-            half = x_ref.shape[0] // 2
-            part = slice(p * half, (p + 1) * half)
-            x = x_ref[part, :]
-            gate = dot(x, wg_ref[...])
-            up = dot(x, wu_ref[...])
-            slope = dot_nt(c_ref[part, :width], wd_ref[...])
-            sigmoid = 1.0 / (1.0 + jnp.exp(-gate))
-            act = gate * sigmoid
-            weight = gate_column(expert, c_ref[part, width:])
-            slope = slope * weight
-            hid_ref[part, at_hidden] = (act * up * weight).astype(bf16)
-            dgu_ref[part, at_gate] = (
-                slope * up * (sigmoid * (1.0 + gate * (1.0 - sigmoid)))
-            ).astype(bf16)
-            dgu_ref[part, at_up] = (slope * act).astype(bf16)
+        gate = up = 0.0
+        for k in range(bands):
+            part = x_ref[:, k * band : (k + 1) * band]
+            gate = gate + dot(part, weights[t][k][:, gate_cut])
+            up = up + dot(part, weights[t][k][:, up_cut])
+        slope = dot_nt(c_ref[:, :width], weights[t][bands + n][...])
+        sigmoid = 1.0 / (1.0 + jnp.exp(-gate))
+        act = gate * sigmoid
+        weight = gate_column(expert, c_ref[:, width:])
+        slope = slope * weight
+        hid_ref[:, at_hidden] = (act * up * weight).astype(bf16)
+        dgu_ref[:, at_gate] = (slope * up * (sigmoid * (1.0 + gate * (1.0 - sigmoid)))).astype(bf16)
+        dgu_ref[:, at_up] = (slope * act).astype(bf16)
+
+    def results(k):
+        out = grad = 0.0
+        for t in range(sets):
+            for n in range(per):
+                at_hidden, at_gate, at_up = places(t, n)
+                gate_cut, up_cut = columns(n)
+                down = weights[t][bands + n][:, k * band : (k + 1) * band]
+                out = out + dot(hid_ref[:, at_hidden], down)
+                grad = grad + dot_nt(dgu_ref[:, at_gate], weights[t][k][:, gate_cut])
+                grad = grad + dot_nt(dgu_ref[:, at_up], weights[t][k][:, up_cut])
+        for p in range(len(out_refs)):
+            out_refs[p][...] = out[p * rows : (p + 1) * rows].astype(bf16)
+            grad_refs[p][...] = grad[p * rows : (p + 1) * rows].astype(bf16)
 
     for t in range(sets):
         for n in range(per):
-            at = t * per + n
-            pl.when(step == at)(functools.partial(hidden_chunk, t, n, *weights[3 * at : 3 * at + 3]))
-
-    @pl.when(step >= sets * per)
-    def _():
-        out = grad = 0.0
-        first = pl.multiple_of((step - sets * per) * tile, tile)
-        for t in range(sets):
-            for n in range(per):
-                at = t * per + n
-                wg_ref, wu_ref, wd_ref = weights[3 * at : 3 * at + 3]
-                at_hidden, at_gate, at_up = places(t, n)
-                out = out + dot(hid_ref[:, at_hidden], wd_ref[:, pl.ds(first, tile)])
-                grad = grad + dot_nt(dgu_ref[:, at_gate], wg_ref[pl.ds(first, tile), :])
-                grad = grad + dot_nt(dgu_ref[:, at_up], wu_ref[pl.ds(first, tile), :])
-        out_ref[...] = out.astype(bf16)
-        grad_ref[...] = grad.astype(bf16)
-
-
-def others(pos, x, c, weights, after=(), tile=512):
-    taken, width = x.shape
-    sets, per = len(weights), len(weights[0])
-    inner = per * weights[0][0][0].shape[1]
-    flat = [v for one in weights for triple in one for v in triple]
+            pl.when(step == t * per + n)(functools.partial(hidden_chunk, t, n))
+    for k in range(bands):
+        pl.when(step == sets * per + k)(functools.partial(results, k))
+
+
+def others(pos, x, c, weights, part, parts, count, kept):
+    taken, width = x.shape[0] // parts, x.shape[1]
+    sets = len(weights)
+    bands, downs = weights[0]
+    per = len(downs)
+    inner = per * downs[0].shape[0]
+    flat = [v for bands_t, downs_t in weights for v in [*bands_t, *downs_t]]
+    tile = width // len(bands)
+    rows_spec = lambda v: pl.BlockSpec(
+        (taken, v.shape[1]), lambda *_: (part, 0), pipeline_mode=pl.Buffered(1)
+    )
     resident = lambda v: pl.BlockSpec(v.shape, lambda *_: (0, 0), pipeline_mode=pl.Buffered(1))
     late = lambda i: jnp.maximum(i - sets * per, 0)
-    return pl.pallas_call(
-        functools.partial(others_kernel, sets, per, len(after)),
+    operands = [pos, x, c] + flat
+    extra = 0 if kept is None else 2
+    aliases = {len(operands) + j: 2 * count + j for j in range(extra)}
+    collected = [sets * inner, 2 * sets * inner]
+    result = pl.pallas_call(
+        functools.partial(others_kernel, sets, per, len(bands), extra),
         grid_spec=pltpu.PrefetchScalarGridSpec(
             num_scalar_prefetch=1,
-            grid=(sets * per + width // tile,),
-            in_specs=[resident(v) for v in [x, c] + flat] + anywhere(len(after)),
-            out_specs=[pl.BlockSpec((taken, tile), lambda i, _: (0, late(i)))] * 2
-            + [whole((taken, sets * inner)), whole((taken, 2 * sets * inner))],
+            grid=(sets * per + len(bands),),
+            in_specs=[rows_spec(x), rows_spec(c)] + [resident(v) for v in flat] + anywhere(extra),
+            out_specs=[pl.BlockSpec((taken // count, tile), lambda i, _: (0, late(i)))] * (2 * count)
+            + [pl.BlockSpec((taken, n), lambda *_: (part, 0)) for n in collected],
         ),
-        out_shape=[jax.ShapeDtypeStruct((taken, width), bf16)] * 2
-        + [
-            jax.ShapeDtypeStruct((taken, sets * inner), bf16),
-            jax.ShapeDtypeStruct((taken, 2 * sets * inner), bf16),
-        ],
+        out_shape=[jax.ShapeDtypeStruct((taken // count, width), bf16)] * (2 * count)
+        + [jax.ShapeDtypeStruct((parts * taken, n), bf16) for n in collected],
+        input_output_aliases=aliases,
         compiler_params=params(),
         cost_estimate=cost(26 * taken * width * sets * inner, 12 * 2**20),
-    )(pos, x, c, *flat, *after)
+    )(*operands, *(kept or []))
+    return result[:count], result[count : 2 * count], result[2 * count :]
 
 
 def side_of(outer, s, pos):
@@ -582,7 +595,8 @@
                 total = dot_tn(mine.reshape(left.shape[0], -1), right).astype(bf16)
                 total = total.reshape(outer * n_exp, -1, right.shape[1])
                 parts.append(jnp.pad(total, ((0, 0), (0, 0), (0, wide - right.shape[1]))))
-            out.append(jnp.concatenate(parts, axis=1))
+            joined = jnp.concatenate(parts, axis=1)
+            out.append(jnp.pad(joined, ((0, 0), (0, -joined.shape[1] % 16), (0, 0))))
         return out
     in_specs, operands = [], []
     for left, right in pairs:
@@ -620,48 +634,55 @@
 
 def rows_product(pos, lefts, rights, tile=512):
     n_ctx, n_exp = lax.axis_size("ctx"), lax.axis_size("exp")
-    depth, height = lefts[0].shape
-    high, wide = height // n_ctx, rights[0].shape[1]
+    depth, height = lefts[0][0].shape
+    high, wide = height // n_ctx, rights[0][0].shape[1]
     if high % 128:
         place = lax.axis_index("ctx") * high
+        cut = lambda v: lax.slice_in_dim(v[0], v[1] * depth, (v[1] + 1) * depth, axis=0)
         total = sum(
-            dot_tn(lax.dynamic_slice_in_dim(a, place, high, 1), b) for a, b in zip(lefts, rights)
+            dot_tn(lax.dynamic_slice_in_dim(cut(a), place, high, 1), cut(b))
+            for a, b in zip(lefts, rights)
         )
         return total.astype(bf16).reshape(n_exp, -1, wide)
     blocks = len(lefts)
-    left_spec = pl.BlockSpec((depth, high), lambda n, pos: (0, 2 * pos[0] + pos[1]))
+    left_specs = [
+        pl.BlockSpec((depth, high), functools.partial(lambda k, n, pos: (k, 2 * pos[0] + pos[1]), k))
+        for _, k in lefts
+    ]
+    right_specs = [
+        pl.BlockSpec((depth, tile), functools.partial(lambda k, n, pos: (k, n), k)) for _, k in rights
+    ]
     total = pl.pallas_call(
         functools.partial(rows_product_kernel, blocks),
         grid_spec=pltpu.PrefetchScalarGridSpec(
             num_scalar_prefetch=1,
             grid=(wide // tile,),
-            in_specs=[left_spec] * blocks
-            + [pl.BlockSpec((depth, tile), lambda n, pos: (0, n))] * blocks,
+            in_specs=left_specs + right_specs,
             out_specs=pl.BlockSpec((high, tile), lambda n, pos: (0, n)),
         ),
         out_shape=jax.ShapeDtypeStruct((high, wide), bf16),
         compiler_params=params(),
         cost_estimate=cost(4 * blocks * depth * high * wide, 4 * 2**20),
-    )(pos, *lefts, *rights)
+    )(pos, *[v for v, _ in lefts], *[v for v, _ in rights])
     return total.reshape(n_exp, -1, wide)
 
 
-def expert_halves_kernel(outer, tiles, pos, rows_ref, cot_ref, dgu_ref, hid_ref, *refs):
-    sent_ref, kept_ref = refs[-2:]
-    s, n = pl.program_id(0), pl.program_id(1)
-
-    def write(left_ref, right_ref):
-        total = dot(left_ref[...], right_ref[...]).astype(bf16)
-
-        def put(out_ref):
-            for i in range(out_ref.shape[0]):
-                out_ref[i] = total[i * out_ref.shape[1] : (i + 1) * out_ref.shape[1]]
-
-        pl.when(s < outer)(lambda: put(sent_ref))
-        pl.when(s >= outer)(lambda: put(kept_ref))
-
-    pl.when(n < tiles)(lambda: write(rows_ref, dgu_ref))
-    pl.when(n >= tiles)(lambda: write(cot_ref, hid_ref))
+def expert_halves_kernel(blocks, tiles, pos, *refs):
+    rows_refs, cot_refs = refs[:blocks], refs[blocks : 2 * blocks]
+    dgu_ref, hid_ref, sent_ref, kept_ref = refs[2 * blocks :]
+    n = pl.program_id(0)
+    high = sent_ref.shape[1]
+
+    def write(left_refs, right_ref):
+        left = jnp.concatenate([ref[...] for ref in left_refs], axis=0)
+        total = dot(left, right_ref[...]).astype(bf16)
+        count = sent_ref.shape[0]
+        for i in range(count):
+            sent_ref[i] = total[i * high : (i + 1) * high]
+            kept_ref[i] = total[(count + i) * high : (count + i + 1) * high]
+
+    pl.when(n < tiles)(lambda: write(rows_refs, dgu_ref))
+    pl.when(n >= tiles)(lambda: write(cot_refs, hid_ref))
 
 
 def expert_steps(width):
@@ -669,67 +690,61 @@
     return high // 128 if high % 128 == 0 else 1
 
 
-def expert_halves(pos, rows_t, cot_t, dgu, hid, after=(), tile=1024):
+def expert_halves(pos, rows_t, cot_t, dgu, hid, tile=512):
     n_ctx = lax.axis_size("ctx")
-    outer = n_ctx // 2
     width, depth = rows_t.shape
     high = width // n_ctx
     wide = dgu.shape[1] + hid.shape[1]
+    steps = expert_steps(width)
     tiles, down = dgu.shape[1] // tile, hid.shape[1] // tile
-    steps = expert_steps(width)
-    left_spec = pl.BlockSpec((high, depth), lambda s, n, pos: (side_of(outer, s, pos), 0))
-    last = tiles + down - 1
+    left_specs = [
+        pl.BlockSpec((high, depth), functools.partial(lambda s, n, pos: (side_of(n_ctx // 2, s, pos), 0), s))
+        for s in range(n_ctx)
+    ]
+    block = (n_ctx // 2 * steps, high // steps, tile)
     return pl.pallas_call(
-        functools.partial(expert_halves_kernel, outer, tiles),
+        functools.partial(expert_halves_kernel, n_ctx, tiles),
         grid_spec=pltpu.PrefetchScalarGridSpec(
             num_scalar_prefetch=1,
-            grid=(2 * outer, tiles + down),
-            in_specs=[
-                left_spec,
-                left_spec,
-                pl.BlockSpec((depth, tile), lambda s, n, pos: (0, jnp.minimum(n, tiles - 1))),
-                pl.BlockSpec((depth, tile), lambda s, n, pos: (0, jnp.maximum(n - tiles, 0))),
-            ]
-            + anywhere(len(after)),
-            out_specs=[
-                pl.BlockSpec(
-                    (steps, high // steps, tile),
-                    lambda s, n, pos: (jnp.minimum(s, outer - 1), 0, jnp.where(s < outer, n, last)),
-                ),
-                pl.BlockSpec(
-                    (steps, high // steps, tile),
-                    lambda s, n, pos: (jnp.maximum(s - outer, 0), 0, jnp.where(s < outer, 0, n)),
-                ),
+            grid=(tiles + down,),
+            in_specs=left_specs * 2
+            + [
+                pl.BlockSpec((depth, tile), lambda n, pos: (0, jnp.minimum(n, tiles - 1))),
+                pl.BlockSpec((depth, tile), lambda n, pos: (0, jnp.maximum(n - tiles, 0))),
             ],
+            out_specs=[pl.BlockSpec(block, lambda n, pos: (0, 0, n))] * 2,
         ),
-        out_shape=[jax.ShapeDtypeStruct((outer * steps, high // steps, wide), bf16)] * 2,
+        out_shape=[jax.ShapeDtypeStruct(block[:2] + (wide,), bf16)] * 2,
         compiler_params=params(),
         cost_estimate=cost(4 * depth * width * wide, 16 * 2**20),
-    )(pos, rows_t, cot_t, dgu, hid, *after)
-
-
-def sums_kernel(shape, extra, pos, *refs):
+    )(pos, *[rows_t] * n_ctx, *[cot_t] * n_ctx, dgu, hid)
+
+
+def sums_kernel(shape, only, extra, pos, *refs):
     ins, outs = refs[: sum(shape)], refs[sum(shape) + extra :]
     at = 0
     for count, out in zip(shape, outs):
         total = ins[at][...].astype(f32)
-        for ref in ins[at + 1 : at + count]:
-            total = total + ref[...].astype(f32)
+        for k in range(at + 1, at + count):
+            term = ins[k][...].astype(f32)
+            if only[k] is not None:
+                term = jnp.where(pl.program_id(0) == only[k], term, 0.0)
+            total = total + term
         out[...] = total.astype(out.dtype)
         at += count
 
 
 def sums(pos, steps, outputs, after=()):
-    operands, in_specs, out_specs, out_shape = [], [], [], []
+    operands, in_specs, out_specs, out_shape, only = [], [], [], [], []
     for kind, block, terms in outputs:
-        block = (1,) + tuple(block)
-        for array, index in terms:
+        for array, index, *step in terms:
             operands.append(array)
+            only.append(step[0] if step else None)
             in_specs.append(pl.BlockSpec(block, functools.partial(place_of, index)))
         out_specs.append(pl.BlockSpec(block, lambda i, pos: (i, 0, 0)))
-        out_shape.append(jax.ShapeDtypeStruct((steps,) + block[1:], kind))
+        out_shape.append(jax.ShapeDtypeStruct((steps * block[0],) + tuple(block[1:]), kind))
     return pl.pallas_call(
-        functools.partial(sums_kernel, [len(terms) for _, _, terms in outputs], len(after)),
+        functools.partial(sums_kernel, [len(terms) for _, _, terms in outputs], only, len(after)),
         grid_spec=pltpu.PrefetchScalarGridSpec(
             num_scalar_prefetch=1,
             grid=(steps,),
@@ -810,6 +825,56 @@
     )(*quarters)
 
 
+def last_sum(refs):
+    total = refs[0][...].astype(f32)
+    for ref in refs[1:]:
+        total = total + ref[...].astype(f32)
+    return total
+
+
+def dense_out_kernel(count, *refs):
+    total = last_sum(refs[:count])
+    out_ref, query_ref, key_ref, value_ref = refs[count:]
+    wide = out_ref.shape[1]
+    out_ref[...] = total[:, :wide]
+    query_ref[...] = total[:, wide : 2 * wide]
+    for g in range(KVH):
+        first = 2 * wide + 2 * g * HD
+        key_ref[:, g * HD : (g + 1) * HD] = total[:, first : first + HD]
+        value_ref[:, g * HD : (g + 1) * HD] = total[:, first + HD : first + 2 * HD]
+
+
+def dense_out(terms, wide):
+    rows = terms[0].shape[0]
+    shapes = [wide, wide, KVH * HD, KVH * HD]
+    return pl.pallas_call(
+        functools.partial(dense_out_kernel, len(terms)),
+        out_shape=[jax.ShapeDtypeStruct((rows, n), f32) for n in shapes],
+        compiler_params=params(),
+        cost_estimate=cost(0, 2**20),
+    )(*terms)
+
+
+def shared_out_kernel(count, chunk, *refs):
+    total = last_sum(refs[:count])
+    gate_ref, up_ref, down_ref = refs[count:]
+    rows = gate_ref.shape[0]
+    for n in range(gate_ref.shape[1] // chunk):
+        cut = slice(n * chunk, (n + 1) * chunk)
+        gate_ref[:, cut] = total[:rows, 2 * n * chunk : (2 * n + 1) * chunk]
+        up_ref[:, cut] = total[:rows, (2 * n + 1) * chunk : (2 * n + 2) * chunk]
+    down_ref[...] = total[rows : rows + down_ref.shape[0], : down_ref.shape[1]]
+
+
+def shared_grads(terms, gate, down, chunk=256):
+    return pl.pallas_call(
+        functools.partial(shared_out_kernel, len(terms), chunk),
+        out_shape=[jax.ShapeDtypeStruct(v, f32) for v in (gate, gate, down)],
+        compiler_params=params(),
+        cost_estimate=cost(0, 2**20),
+    )(*terms)
+
+
 def hold(values, after):
     count = len(values)
     return pl.pallas_call(
@@ -862,6 +927,25 @@
     return [swap_inner(v, "ctx") for v in moved]
 
 
+def outer_blocks(value):
+    moved, out = value, []
+    for _ in range(1, lax.axis_size("ctx") // 2):
+        moved = shift_outer(moved, "ctx", 1)
+        out.append(moved)
+    return out
+
+
+def inner_blocks(value, moved):
+    return swap_inner(jnp.concatenate([value] + moved, axis=0), "ctx")
+
+
+def all_blocks(value, moved, across):
+    out = []
+    for k, v in enumerate([value] + moved):
+        out += [(v, 0), (across, k)]
+    return out
+
+
 def spread_all(value, moved, across, moved_across):
     blocks = [value, across]
     for a, b in zip(moved, moved_across):
@@ -869,39 +953,42 @@
     return blocks
 
 
-def shared_x_send(pos, kept, got):
-    outer, levels = lax.axis_size("ctx") // 2, lax.axis_size("exp") // 2
-    outputs = []
-    for y in range(outer):
-        index = functools.partial(
-            lambda y, i, pos: (y * levels + i) * 2 + 1 - pos[3], y
-        )
-        outputs.append((bf16, kept.shape[1:], [(v, index) for v in (kept, got)]))
-    return sums(pos, levels, outputs)
-
-
-def shared_terms(kept, got, arrived, d):
-    outer, levels = lax.axis_size("ctx") // 2, lax.axis_size("exp") // 2
-    place = lambda pos: lax.rem(pos[0] + d, outer) * levels
-    terms = [(v, lambda i, pos: (place(pos) + i) * 2 + pos[3]) for v in (kept, got)]
-    return terms + [(arrived, lambda i, pos: place(pos) + i)]
-
-
-def shared_y(pos, kept, got, arrived):
-    outer, levels = lax.axis_size("ctx") // 2, lax.axis_size("exp") // 2
-    out = []
-    for d in range(1, outer):
-        terms = shared_terms(kept, got, arrived, d)
-        (sent,) = sums(pos, levels, [(bf16, kept.shape[1:], terms)])
-        out.append(shift_outer(sent, "ctx", d))
-    return out
-
-
-def shared_total(pos, kept, got, arrived, moved):
-    levels = lax.axis_size("exp") // 2
-    terms = shared_terms(kept, got, arrived, 0) + [(v, straight) for v in moved]
-    (total,) = sums(pos, levels, [(bf16, kept.shape[1:], terms)])
-    return total
+class Shared:
+    def __init__(self, pos, kept, got):
+        self.pos = pos
+        self.outer, self.levels = lax.axis_size("ctx") // 2, lax.axis_size("exp") // 2
+        self.rows, self.wide = kept.shape[1:]
+        self.pair = lambda v: v.reshape(-1, 2 * self.rows, self.wide)
+        self.terms = [self.pair(v) for v in (kept, got)]
+        self.together = 2 if self.levels % 2 == 0 else 1
+        self.steps = self.levels // self.together
+
+    def _sum(self, d, rows, inner, moved=()):
+        at = lambda i, pos: lax.rem(pos[0] + d, self.outer) * self.steps + i
+        terms = [(v, lambda i, pos: (at(i, pos), inner(pos), 0)) for v in self.terms]
+        for parts in moved:
+            for k, v in enumerate(parts):
+                terms.append((self.pair(v), lambda i, pos: (0, inner(pos), 0), k))
+        return terms, (self.together, rows, self.wide)
+
+    def first(self):
+        out = []
+        for d in range(1, self.outer):
+            terms, block = self._sum(d, 2 * self.rows, lambda pos: 0)
+            outputs = []
+            for k in range(self.steps):
+                part = [(v, functools.partial(lambda f, k, i, pos: f(k, pos), f, k)) for v, f in terms]
+                outputs.append((bf16, block, part))
+            out.append(sums(self.pos, 1, outputs))
+        return out
+
+    def second(self, moved):
+        terms, block = self._sum(0, self.rows, lambda pos: 1 - pos[3], moved)
+        return swap_inner(sums(self.pos, self.steps, [(bf16, block, terms)])[0], "exp")
+
+    def total(self, moved, crossed):
+        terms, block = self._sum(0, self.rows, lambda pos: pos[3], moved)
+        return sums(self.pos, self.steps, [(bf16, block, terms + [(crossed, straight)])])[0]
 
 
 def z_take(total, d):
@@ -918,27 +1005,21 @@
     return swap_inner(lax.dynamic_index_in_dim(pairs, 1 - lax.axis_index("exp") % 2, 1, False), "exp")
 
 
-def over_z(total, arrived):
+def mine_x(total):
     pairs = total.reshape((-1, 2) + total.shape[1:])
-    mine = lax.dynamic_index_in_dim(pairs, lax.axis_index("exp") % 2, 1, False)
+    return lax.dynamic_index_in_dim(pairs, lax.axis_index("exp") % 2, 1, False)
+
+
+def over_z(mine, arrived):
     mine = mine.astype(f32) + arrived.astype(f32)
     levels, level = mine.shape[0], lax.axis_index("exp") // 2
     take = lambda d: lax.dynamic_index_in_dim(mine, (level + d) % levels, 0, False)
     return [take(0)] + [shift_outer(take(d).astype(bf16), "exp", d) for d in range(1, levels)]
 
 
-def dense_result(pairs, terms):
-    devices = lax.axis_size("ctx") * lax.axis_size("exp")
-    out, first = [], 0
-    for left, right in pairs:
-        rows = left.shape[1] // devices
-        out.append(sum(t[first : first + rows, : right.shape[1]].astype(f32) for t in terms))
-        first += rows
-    return out
-
-
 def expert_quarter(kept, got, q, row):
-    block = (kept.shape[1], kept.shape[2] // 4)
+    steps = kept.shape[0] // (lax.axis_size("ctx") // 2)
+    block = (steps, kept.shape[1], kept.shape[2] // 4)
     return block, [(v, lambda i, pos: (row(i, pos), 0, q)) for v in (kept, got)]
 
 
@@ -947,39 +1028,38 @@
     for q in quarters:
         block, terms = expert_quarter(kept, got, q, straight)
         outputs.append((bf16, block, terms))
-    return sums(pos, kept.shape[0], outputs)
-
-
-def expert_rows(kept, d):
+    return sums(pos, lax.axis_size("ctx") // 2, outputs)
+
+
+def expert_row(d):
     outer = lax.axis_size("ctx") // 2
-    steps = kept.shape[0] // outer
-    return steps, lambda i, pos: lax.rem(pos[0] + d, outer) * steps + i
-
-
-def expert_send(pos, kept, got, pieces, quarters):
+    return lambda i, pos: lax.rem(pos[0] + d, outer)
+
+
+def expert_send(pos, kept, got, pieces, half):
     sent = []
     for d in range(1, lax.axis_size("ctx") // 2):
-        steps, row = expert_rows(kept, d)
-        outputs = []
-        for q in quarters:
-            block, terms = expert_quarter(kept, got, q, row)
-            outputs.append((bf16, block, terms + [(pieces[q], row)]))
-        sent.append(sums(pos, steps, outputs))
+        row = expert_row(d)
+        block, terms = expert_quarter(kept, got, 0, row)
+        terms = [(v, lambda i, pos: (row(i, pos), 0, 2 * half + i)) for v, _ in terms]
+        terms += [(pieces[2 * half + k], lambda i, pos: row(0, pos), k) for k in range(2)]
+        sent += sums(pos, 2, [(bf16, block, terms)])
     return sent
 
 
 def expert_move(sent):
-    return [[shift_outer(v, "ctx", d + 1) for v in part] for d, part in enumerate(sent)]
+    return [shift_outer(v, "ctx", d + 1) for d, v in enumerate(sent)]
 
 
 def expert_total(pos, kept, got, pieces, arrived):
-    steps, row = expert_rows(kept, 0)
+    row = expert_row(0)
     outputs = []
     for q in range(4):
         block, terms = expert_quarter(kept, got, q, row)
-        terms = terms + [(pieces[q], row)] + [(v, straight) for v in arrived[q]]
+        at = functools.partial(lambda k, i, pos: k, q % 2)
+        terms = terms + [(pieces[q], row)] + [(v, at) for v in arrived[q // 2]]
         outputs.append((bf16, block, terms))
-    return [v.reshape(-1, v.shape[2]) for v in sums(pos, steps, outputs)]
+    return [v.reshape(-1, v.shape[2]) for v in sums(pos, 1, outputs)]
 
 
 def shards(
@@ -1032,40 +1112,49 @@
         )
     ]
 
-    normed, kv = keyvalue(x, attn_gain, w_key, w_value)
-    chunk = 256
-    per = inner // chunk
-
-    def fetch(part):
-        which, n = part % 3, part // 3
-        array = (expert_gate, expert_up, expert_down)[which]
-        mine = lax.dynamic_index_in_dim(array, pos[1], 0, keepdims=False)
-        dim = 0 if which == 2 else 1
-        return swap_inner(lax.slice_in_dim(mine, n * chunk, (n + 1) * chunk, axis=dim), "exp")
-
-    fetches = [range(0, 1), range(1, 2), range(2, 4), range(4, 5), range(5, 3 * per)]
-
-    def fetch_some(k):
-        return [fetch(p) for p in fetches[k]]
+    chunk, bands = 256, 3
+    mine = lambda v: lax.dynamic_index_in_dim(v, pos[1], 0, keepdims=False)
+    over_core = lambda v: swap_inner(v, "ctx")
+
+    def fetch(k):
+        return swap_inner(asked[k], "exp")
+
+    def arranged(parts):
+        return parts[inner // chunk :], parts[: inner // chunk]
+
+    def ask():
+        down = mine(expert_down)
+        out = [down[n * chunk : (n + 1) * chunk] for n in range(inner // chunk)]
+        gate, up = mine(expert_gate), mine(expert_up)
+        band = width // bands
+        for k in range(bands):
+            cut = slice(k * band, (k + 1) * band)
+            out.append(jnp.concatenate([gate[cut], up[cut]], axis=1))
+        return out
 
     def gather_keys():
+        normed, kv = keyvalue(x, attn_gain, w_key, w_value)
         moved, across = spread_outer(kv)
         queries = dot(normed, w_query).astype(bf16)
-        return moved, across, spread_inner(moved), queries, ring_step(cot_ring[0], 1), fetch_some(0)
-
-    moved, across, moved_across, queries, cot_next, fetched = region(gather_keys)
-    kv_blocks = spread_all(kv, moved, across, moved_across)
+        asked = ask()
+        keys = kv, moved, across, spread_inner(moved)
+        return normed, keys, queries, ring_step(cot_ring[0], 1), asked, swap_inner(asked[0], "exp")
+
+    normed, keys, queries, cot_next, asked, got = region(gather_keys)
+    kv_blocks = spread_all(*keys)
     cot_ring.append(cot_next)
+    fetched, crossed = [got], []
 
     def attention():
         attended, lse = attend(pos, span_order, queries, kv_blocks)
         middle, rows = middle_forward(x, attended, w_out, ffn_gain)
-        moved = spread_outer(normed), ring_step(cot_ring[1], 1), fetch_some(1)
+        moved = outer_blocks(normed), ring_step(cot_ring[1], 1), fetch(1), over_core(fetched[0])
         return attended, lse, middle, rows, *moved
 
-    attended, lse, middle, rows_low, normed_moved, cot_next, got = region(attention)
-    fetched += got
+    attended, lse, middle, rows_low, normed_moved, cot_next, got, crossing = region(attention)
     cot_ring.append(cot_next)
+    fetched.append(got)
+    crossed.append(crossing)
 
     def own_part(k, rows, kept):
         weights = (expert_gate, expert_up, expert_down)
@@ -1074,101 +1163,105 @@
     def first():
         weights = (shared_gate[None], shared_up[None], shared_down[None])
         shared = experts(pos, rows_low, cot, weights, 0, 1, None, False, f32)
-        moved = ring_step(rows_low, 1), ring_step(cot_ring[2], 1)
-        more = spread_outer(attended), spread_inner(normed_moved[0]), fetch_some(2)
-        return moved, shared, own_part(0, rows_low, None), *more
-
-    moved, shared, (out_k, grad_k, kept), attended_moved, normed_across, got = region(first)
-    fetched += got
-    normed_blocks = spread_all(normed, *normed_moved, normed_across)
+        more = inner_blocks(normed, normed_moved), fetch(2), over_core(fetched[1]), outer_blocks(attended)
+        return ring_step(rows_low, 1), shared, own_part(0, rows_low, None), *more
+
+    rows_k, shared, (out_k, grad_k, kept), across, got, crossing, attended_moved = region(first)
+    fetched.append(got)
+    crossed.append(crossing)
+    normed_blocks = all_blocks(normed, normed_moved, across)
     shared_out, shared_grad, (shared_hidden, shared_dgu) = shared
-    rows_k = moved[0]
-    cot_ring.append(moved[1])
     out_own, grad_own = [out_k], [grad_k]
     shared_pairs = [(rows_low, shared_dgu), (shared_hidden, cot)]
 
     def second():
         result = own_part(1, rows_k, kept)
-        across = spread_inner(attended_moved[0])
-        return ring_step(rows_k, 1), result, halves(pos, shared_pairs), across, fetch_some(3)
-
-    rows_next, (out_k, grad_k, kept), (shared_sent, shared_kept), across, got = region(second)
-    fetched += got
-    attended_blocks = spread_all(attended, *attended_moved, across)
+        more = fetch(3), over_core(fetched[2]), inner_blocks(attended, attended_moved)
+        return ring_step(rows_k, 1), result, halves(pos, shared_pairs), *more
+
+    rows_next, (out_k, grad_k, kept), (shared_sent, shared_kept), got, crossing, across = region(second)
+    attended_blocks = all_blocks(attended, attended_moved, across)
+    fetched.append(got)
+    crossed.append(crossing)
     rows_k = rows_next
     out_own.append(out_k)
     grad_own.append(grad_k)
 
     def third():
         result = own_part(2, rows_k, kept)
-        moved = ring_step(rows_k, 1), swap_inner(shared_sent, "ctx"), fetch_some(4)
-        return result, [swap_inner(v, "ctx") for v in fetched], *moved
-
-    (out_k, grad_k, kept), fetched_b, rows_next, shared_got, got = region(third)
-    fetched += got
+        more = over_core(shared_sent), fetch(4), over_core(fetched[3])
+        return ring_step(rows_k, 1), result, *more
+
+    rows_next, (out_k, grad_k, kept), shared_got, got, crossing = region(third)
+    fetched.append(got)
+    crossed.append(crossing)
     rows_k = rows_next
     out_own.append(out_k)
     grad_own.append(grad_k)
 
+    def over_y(parts, k):
+        return [shift_outer(v[k], "ctx", d + 1) for d, v in enumerate(parts)]
+
     def fourth():
-        across = fetched_b + [swap_inner(v, "ctx") for v in fetched[len(fetched_b) :]]
-        sent = shared_x_send(pos, shared_kept, shared_got)
-        got = [swap_inner(v, "exp") for v in sent[: ring // 2]]
-        out_k, grad_k, new = own_part(3, rows_k, kept)
-        weights = [[v[3 * n : 3 * n + 3] for n in range(per)] for v in (fetched, across)]
-        return out_k, grad_k, new, others(pos, new[0], new[1], weights), got, sent[ring // 2 :]
-
-    out_k, grad_k, kept, other, shared_first, shared_rest = region(fourth)
+        moved = ring_step(cot_ring[2], 1)
+        weights = [arranged(fetched), arranged(crossed + [over_core(fetched[4])])]
+        half = levels // 2
+        sent = Shared(pos, shared_kept, shared_got).first()
+        arrived = [over_y(sent, k) for k in range(len(sent[0]) // 2)]
+        out_a, grad_a, new = others(pos, kept[0], kept[1], weights, 0, 2, half, None)
+        out_k, grad_k, more = experts(
+            pos, rows_k, moved, (expert_gate, expert_up, expert_down), 3, levels, kept, True, bf16
+        )
+        out_b, grad_b, new = others(pos, more[0], more[1], weights, 1, 2, half, new)
+        rest = [v[len(v) // 2 :] for v in sent]
+        return out_k, grad_k, more, [*out_a, *out_b], [*grad_a, *grad_b], new, arrived, rest
+
+    out_k, grad_k, kept, out_other, grad_other, kept_other, shared_first, shared_rest = region(fourth)
     out_own.append(out_k)
     grad_own.append(grad_k)
     rows_all, cot_all, rows_t, cot_t, hid_own, dgu_own = kept
-    out_other, grad_other, hid_other, dgu_other = other
-    split = lambda v: [v[k * tokens : (k + 1) * tokens] for k in range(levels)]
-    out_other, grad_other = split(out_other), split(grad_other)
+    hid_other, dgu_other = kept_other
 
     def back_one():
         moved = ring_step(row_sum([grad_own[3], grad_other[3]]), -1)
-        made = expert_halves(pos, rows_t, cot_t, dgu_other, hid_other)
-        return moved, made, [swap_inner(v, "exp") for v in shared_rest]
-
-    moved, (sent, kept_other), shared_second = region(back_one)
-    shared_x = jnp.concatenate(shared_first + shared_second, axis=0)
+        arrived = [over_y(shared_rest, k) for k in range(len(shared_rest[0]))]
+        return moved, expert_halves(pos, rows_t, cot_t, dgu_other, hid_other), arrived
+
+    moved, (sent, kept_other), got = region(back_one)
+    shared_moved = [list(v) for v in zip(*(list(shared_first) + list(got)))]
 
     def back_two():
         total = row_sum([grad_own[2], grad_other[2], moved])
         got = swap_inner(sent, "ctx")
+        crossed = Shared(pos, shared_kept, shared_got).second(shared_moved)
         made = expert_halves(pos, rows_t, cot_t, dgu_own, hid_own)
-        shared_moved = shared_y(pos, shared_kept, shared_got, shared_x)
-        return ring_step(total, -1), got, made, expert_pieces(pos, kept_other, got, [0])[0], shared_moved
-
-    moved_two, got_other, (sent_own, kept_own), piece, shared_moved = region(back_two)
+        return ring_step(total, -1), got, made, expert_pieces(pos, kept_other, got, [0])[0], crossed
+
+    moved_two, got_other, (sent_own, kept_own), piece, shared_crossed = region(back_two)
 
     def back_three():
         total = row_sum([grad_own[1], grad_other[1], moved_two])
-        pieces = expert_pieces(pos, kept_other, got_other, [1, 2, 3])
-        shared_sum = shared_total(pos, shared_kept, shared_got, shared_x, shared_moved)
+        made = expert_pieces(pos, kept_other, got_other, [1, 2, 3])
+        shared_sum = Shared(pos, shared_kept, shared_got).total(shared_moved, shared_crossed)
         out_total = row_sum([out_own[3], out_other[3]])
         moved = ring_step(total, -1), swap_inner(sent_own, "ctx"), swap_inner(piece, "exp")
-        return *moved, pieces, shared_sum, out_total
-
-    moved, got_own, piece, pieces, shared_sum, out_total = region(back_three)
-    pieces = [piece] + list(pieces)
+        return *moved, made, shared_sum, out_total
+
+    moved, got_own, piece, made, shared_sum, out_total = region(back_three)
+    pieces = [piece, *made]
 
     def attention_back():
         mgrad, mgrad_low, ffn_gain_grad, att_grad = middle_back(
             [shared_grad, grad_own[0], grad_other[0], moved], middle, cot, ffn_gain, w_out
         )
         back = attend_back(pos, span_order, queries, att_grad, lse, kv_blocks)
-        out_moved = ring_step(out_total, -1)
-        got = swap_inner(pieces[1], "exp"), z_send(shared_sum, 1), expert_move(expert_send(pos, kept_own, got_own, pieces, [0]))
-        return mgrad, mgrad_low, spread_outer(mgrad_low), ffn_gain_grad, back, out_moved, *got
-
-    mgrad, mgrad_low, mgrad_moved, ffn_gain_grad, (dq, same, across), out_moved, piece, shared_z, got = (
-        region(attention_back)
+        got = ring_step(out_total, -1), swap_inner(pieces[1], "exp")
+        return mgrad, mgrad_low, outer_blocks(mgrad_low), ffn_gain_grad, back, *got
+
+    mgrad, mgrad_low, mgrad_moved, ffn_gain_grad, (dq, same, across), out_moved, piece = region(
+        attention_back
     )
     pieces[1] = piece
-    arrived = [[a[0] for a in got]]
-    shared_z = [shared_z]
 
     def dense_one():
         got = swap_inner(across, "ctx")
@@ -1179,68 +1272,67 @@
             if k:
                 made = [shift_outer(made, "ctx", -1)]
         total = row_sum([out_own[2], out_other[2], out_moved])
-        mgrad_across = spread_inner(mgrad_moved[0])
-        moved = ring_step(total, -1), swap_inner(pieces[2], "exp"), z_send(shared_sum, 2)
-        return made, spread_outer(dq), mgrad_across, *moved
-
-    dkv, dq_moved, mgrad_across, out_moved_two, piece, got = region(dense_one)
-    shared_z.append(got)
-    mgrad_blocks = spread_all(mgrad_low, *mgrad_moved, mgrad_across)
+        mgrad_blocks = all_blocks(mgrad_low, mgrad_moved, inner_blocks(mgrad_low, mgrad_moved))
+        total_out = rows_product(pos, attended_blocks, mgrad_blocks)
+        sent = expert_send(pos, kept_own, got_own, pieces, 0)
+        moved = ring_step(total, -1), swap_inner(pieces[2], "exp")
+        return made, outer_blocks(dq), total_out, sent, *moved
+
+    dkv, dq_moved, total_out, sent, out_moved_two, piece = region(dense_one)
     pieces[2] = piece
 
     def dense_two():
         total = row_sum([out_own[1], out_other[1], out_moved_two])
-        moved = ring_step(total, -1)
-        dq_across = spread_inner(dq_moved[0])
-        total_out = rows_product(pos, attended_blocks, mgrad_blocks)
+        dkv_moved = outer_blocks(dkv)
+        dkv_blocks = all_blocks(dkv, dkv_moved, inner_blocks(dkv, dkv_moved))
+        dq_blocks = all_blocks(dq, dq_moved, inner_blocks(dq, dq_moved))
+        total_query = rows_product(pos, normed_blocks, dq_blocks)
+        total_kv = rows_product(pos, normed_blocks, dkv_blocks)
         back = input_back(dq, dkv, w_query, w_key, w_value, x, attn_gain, mgrad)
-        got = expert_move(expert_send(pos, kept_own, got_own, pieces, [1]))
-        more = moved, swap_inner(pieces[3], "exp"), z_send(shared_sum, 3), got
-        return spread_outer(dkv), dq_across, total_out, back, *more
-
-    dkv_moved, dq_across, total_out, (input_grad, attn_gain_grad), out_moved_three, piece, last_z, got = (
-        region(dense_two)
-    )
-    shared_z.append(last_z)
-    arrived.append([a[0] for a in got])
-    dq_blocks = spread_all(dq, *dq_moved, dq_across)
+        moved = ring_step(total, -1), swap_inner(pieces[3], "exp"), expert_move(sent)
+        return total_query, total_kv, back, *moved
+
+    total_query, total_kv, (input_grad, attn_gain_grad), out_moved_three, piece, got = region(dense_two)
     pieces[3] = piece
+    arrived = [got]
 
     def dense_three():
         devices = n_ctx * n_exp
-        moved = expert_move(expert_send(pos, kept_own, got_own, pieces, [2, 3]))
-        got = arrived + [[a[q] for a in moved] for q in range(2)]
-        total_query = rows_product(pos, normed_blocks, dq_blocks)
-        dkv_blocks = spread_all(dkv, *dkv_moved, spread_inner(dkv_moved[0]))
-        total_kv = rows_product(pos, normed_blocks, dkv_blocks)
-        shared_parts = [z_take(shared_sum, 0)] + shared_z
-        dense = [over_z(t, over_x(t)) for t in (total_out, total_query, total_kv)]
+        total = jnp.concatenate([total_out, total_query, total_kv], axis=2)
+        got = expert_move(expert_send(pos, kept_own, got_own, pieces, 1))
         layer_out = row_sum([middle, shared_out, out_own[0], out_other[0], out_moved_three])
+        shared_z = [z_send(shared_sum, d) for d in range(1, levels)]
         gains = jnp.stack(
             [attn_gain_grad.reshape(devices, -1), ffn_gain_grad.reshape(devices, -1)], axis=1
         )
         gains = lax.all_to_all(gains, BOTH, split_axis=0, concat_axis=0, tiled=True)
-        grads = expert_out(expert_total(pos, kept_own, got_own, pieces, got), inner)
-        pairs = [(attended, mgrad), (normed, dq), (normed, dkv)]
-        dense = [dense_result([p], t)[0] for p, t in zip(pairs, dense)]
-        return layer_out, jnp.sum(gains, axis=0), dense_result(shared_pairs, shared_parts), dense, grads
-
-    layer_out, gains, (sum_gate_up, sum_down), (sum_out, sum_query, sum_kv), expert_grads = region(
-        dense_three
-    )
-    shared_rows = sum_gate_up.reshape(sum_gate_up.shape[0], -1, 2, 256)
-    kv_rows = sum_kv.reshape(sum_kv.shape[0], KVH, 2, HD)
+        return mine_x(total), over_x(total), got, layer_out, shared_z, gains
+
+    total, total_x, got, layer_out, shared_z, gains = region(dense_three)
+    arrived.append(got)
+
+    def dense_four():
+        grads = expert_out(expert_total(pos, kept_own, got_own, pieces, arrived), inner)
+        shape = lambda v: (v.shape[0] // (n_ctx * n_exp), v.shape[1])
+        shared = shared_grads(
+            [z_take(shared_sum, 0)] + shared_z, shape(shared_gate), shape(shared_down)
+        )
+        dense = dense_out(over_z(total, total_x), x.shape[1])
+        return jnp.sum(gains, axis=0), shared, dense, grads
+
+    gains, (sum_gate, sum_up, sum_down), dense, expert_grads = region(dense_four)
+    sum_out, sum_query, sum_key, sum_value = dense
     return (
         layer_out[None],
         input_grad[None],
         gains[0],
         sum_query,
-        kv_rows[:, :, 0].reshape(sum_kv.shape[0], -1),
-        kv_rows[:, :, 1].reshape(sum_kv.shape[0], -1),
+        sum_key,
+        sum_value,
         sum_out,
         gains[1],
-        shared_rows[:, :, 0].reshape(sum_gate_up.shape[0], -1),
-        shared_rows[:, :, 1].reshape(sum_gate_up.shape[0], -1),
+        sum_gate,
+        sum_up,
         sum_down,
         *expert_grads,
     )

time: 571 us -> 511 us (0.89)
  starting transfers between devices: 75 us -> 51 us
  local copies, waits for them, and re-layouts: 42.2 us -> 19.3 us
  waiting for transfers between devices: 136 us -> 121 us
  other arithmetic: 33.4 us -> 44.7 us
  Pallas kernels: 268 us -> 259 us
    ppermute x37 -> x27, waiting for transfers between devices: 52.4 us -> 24.8 us  [swap_inner(): return lax.ppermute(value, axis, [(i, i ^ 1) for i in range(size)])]
    concatenate x0 -> x9, other arithmetic: none -> 16.9 us  [the longest x5 11.4 us: inner_blocks(): return swap_inner(jnp.concatenate([value] + moved, axis=0), 'ctx')]
    all_to_all x1, waiting for transfers between devices: 0.01 us -> 16.9 us  [dense_three(): gains = lax.all_to_all(gains, BOTH, split_axis=0, concat_axis=0, tiled=True)]
    ppermute x24 -> x17, waiting for transfers between devices: 64.7 us -> 53.6 us  [shift_outer(): return lax.ppermute(value, axis, perm)]
    ppermute x24 -> x17, starting transfers between devices: 32.6 us -> 22.4 us  [shift_outer(): return lax.ppermute(value, axis, perm)]
    pallas_call x9 -> x8, Pallas kernels: 44.7 us -> 35.3 us  [sums(): pl.pallas_call(functools.partial(sums_kernel, [len(terms) for _, _, terms...]
    slice x8 -> x2, local copies, waits for them, and re-layouts: 11.8 us -> 3.27 us  [the longest x1 2.03 us: ask(): out.append(jnp.concatenate([gate[cut], up[cut]], axis=1))]
    ppermute x37 -> x27, starting transfers between devices: 23.7 us -> 15.6 us  [swap_inner(): return lax.ppermute(value, axis, [(i, i ^ 1) for i in range(size)])]
  transfers between devices with their start and end apart: 74 -> 57, of which waited for: 18 -> 24; matrix products, arithmetic and copies ran while one was open for 11% -> 10% of each run, Pallas kernels for 47% -> 50%
where the time goes in v3:
time: 511 us; the launch traced here: 503 us
  Pallas kernels  259 us (51%)
  waiting for transfers between devices  121 us (24%)
  starting transfers between devices  51 us (10%)
  other arithmetic  44.7 us (9%)
  local copies, waits for them, and re-layouts  19.3 us (4%)
    pallas_call x5, Pallas kernels, experts(): pl.pallas_call(functools.partial(experts_kernel, per, gated, extra, gated...  64 us
    ppermute x17, waiting for transfers between devices, shift_outer(): return lax.ppermute(value, axis, perm)  53.6 us
    pallas_call x2, Pallas kernels, others(): pl.pallas_call(functools.partial(others_kernel, sets, per, len(bands), ex...  39.3 us
    pallas_call x8, Pallas kernels, sums(): pl.pallas_call(functools.partial(sums_kernel, [len(terms) for _, _, terms...  35.3 us
    pallas_call x2, Pallas kernels, expert_halves(): pl.pallas_call(functools.partial(expert_halves_kernel, n_ctx, tiles), gri...  31.3 us
    ppermute x12, waiting for transfers between devices, ring_step(): return lax.ppermute(value, BOTH, perm)  25.4 us
    ppermute x27, waiting for transfers between devices, swap_inner(): return lax.ppermute(value, axis, [(i, i ^ 1) for i in range(size)])  24.8 us
    ppermute x17, starting transfers between devices, shift_outer(): return lax.ppermute(value, axis, perm)  22.4 us
  transfers between devices with their start and end apart: 57, of which 24 were waited for; matrix products, arithmetic and copies ran while one was open for 10% of the time, Pallas kernels for 50%

profile of v3, /device:TPU:0, one launch (start us, length us, event | category | flops | bytes accessed | tf_op | source)
XLA Modules:
  0.0 502.6 jit_solution(13513812667407966899)
XLA Ops:
  5.9 32.3 %conditional.14 = (bf16[256,1536]{1,0:T(8,128)(2,1)}, bf16[256,1024]{1,0:T(8,128)(2,1)}, bf16[256,1024]{1,0:T(8,128)(2,1)}, bf16[256,1024]{1,0:T(8,128)(2,1)}, b...) conditional(s32[]{:T(128)} %convert_element_type.154, ...), branch_computations={%region_3.4_spmd, %region_4.5_spmd} | conditional | flops 1415970816 | bytes 48771484 | solution.py:1101
  6.6 5.3 %branch_1_fun.30 = (bf16[256,1536]{1,0:T(8,128)(2,1)}, bf16[256,1024]{1,0:T(8,128)(2,1)}) custom-call(bf16[256,1536]{1,0:T(8,128)(2,1)} %get-tuple-element.444.x_ref, f32[1,1536]{1,0:T(1,128)} %reshape.110.gain_ref, bf16[1536,512]{1,0:T(8,128)(2,1)} %get-tuple-element.446.wk_ref, bf16[1536,512]{1,0:T(8,128)(2,1)} %get-tuple-element.447.wv_ref), custom_call_target="tpu_custom_call" | custom-call | flops 201326592 | bytes 1310720 | tf_op jit(solution)/shard_map/cond/branch_1_fun/pallas_call | solution.py:66
  28.9 4.8 convolution_convert_fusion
  38.3 21.6 %conditional.15 = (bf16[256,1536]{1,0:T(8,128)(2,1)}, f32[4,1,768]{2,1,0:T(1,128)S(1)}, f32[256,1536]{1,0:T(8,128)}, bf16[256,1536]{1,0:T(8,128)(2,1)}, bf16[256...) conditional(s32[]{:T(128)} %convert_element_type.154, ...), branch_computations={%region_5.6_spmd, %region_6.7_spmd} | conditional | flops 1107296256 | bytes 19149052 | solution.py:1101
  42.2 9.5 %branch_1_fun.31 = (bf16[256,1536]{1,0:T(8,128)(2,1)}, f32[4,1,768]{2,1,0:T(1,128)S(1)}) custom-call(s32[4]{0:T(128)S(1)} %get-tuple-element.456.pos, s32[8]{0:T(128)S(1)} %get-tuple-element.457.spans, bf16[256,1536]{1,0:T(8,128)(2,1)} %get-tuple-element.458.q_ref, bf16[256,1024]{1,0:T(8,128)(2,1)} %get-tuple-element.459.refs_0_, ...), custom_call_target="tpu_custom_call" | custom-call | flops 805306368 | bytes 1048576 | tf_op jit(solution)/shard_map/cond/branch_1_fun/pallas_call | solution.py:128
  51.7 5.9 %branch_1_fun.32 = (f32[256,1536]{1,0:T(8,128)}, bf16[256,1536]{1,0:T(8,128)(2,1)}) custom-call(bf16[256,1536]{1,0:T(8,128)(2,1)S(1)} %copy-done.2, bf16[256,1536]{1,0:T(8,128)(2,1)} %get-tuple-element.1124.att_ref, bf16[1536,1536]{1,0:T(8,128)(2,1)} %get-tuple-element.466.w_ref, f32[1,1536]{1,0:T(1,128)} %reshape.111.gain_ref), custom_call_target="tpu_custom_call" | custom-call | flops 301989888 | bytes 2097152 | tf_op jit(solution)/shard_map/cond/branch_1_fun/pallas_call | solution.py:228
  59.9 31.7 %conditional.16 = (bf16[256,1536]{1,0:T(8,128)(2,1)}, f32[256,1536]{1,0:T(8,128)}, f32[256,1536]{1,0:T(8,128)}, bf16[256,1024]{1,0:T(8,128)(2,1)}, bf16[256,2048...) conditional(s32[]{:T(128)} %convert_element_type.154, ...), branch_computations={%region_7.8_spmd, %region_8.9_spmd} | conditional | flops 5237637120 | bytes 32506220 | solution.py:1101
  66.3 11.9 %branch_1_fun.33 = (f32[256,1536]{1,0:T(8,128)}, f32[256,1536]{1,0:T(8,128)}, bf16[256,1024]{1,0:T(8,128)(2,1)}, bf16[256,2048]{1,0:T(8,128)(2,1)}) custom-call(s32[4]{0:T(128)S(1)} %get-tuple-element.475.pos, bf16[256,1536]{1,0:T(8,128)(2,1)} %get-tuple-element.474.x_ref, bf16[256,1536]{1,0:T(8,128)(2,1)S(1)} %copy-done.4, bf16[1,1536,1024]{2,1,0:T(8,128)(2,1)} %bitcast.89, ...), custom_call_target="tpu_custom_call" | custom-call | flops 2617245696 | bytes 3145728 | tf_op jit(solution)/shard_map/cond/branch_1_fun/pallas_call | solution.py:451
  78.2 13.1 %branch_1_fun.34 = (bf16[256,1536]{1,0:T(8,128)(2,1)}, bf16[256,1536]{1,0:T(8,128)(2,1)}, bf16[1024,1536]{1,0:T(8,128)(2,1)}, bf16[1024,1664]{1,0:T(8,128)(2,1)}...) custom-call(s32[4]{0:T(128)S(1)} %get-tuple-element.475.pos, ...), custom_call_target="tpu_custom_call" | custom-call | flops 2617245696 | bytes 3145728 | tf_op jit(solution)/shard_map/cond/branch_1_fun/pallas_call | solution.py:451
  91.6 29.3 %conditional.17 = (bf16[256,1536]{1,0:T(8,128)(2,1)}, bf16[256,1536]{1,0:T(8,128)(2,1)}, bf16[256,1536]{1,0:T(8,128)(2,1)}, bf16[1024,1536]{1,0:T(8,128)(2,1)}, ...) conditional(s32[]{:T(128)} %convert_element_type.154, ...), branch_computations={%region_9.10_spmd, %region_10.11_spmd} | conditional | flops 3828350976 | bytes 35651720 | solution.py:1101
  96.2 8.7 %branch_1_fun.36 = (bf16[16,80,2048]{2,1,0:T(8,128)(2,1)}, bf16[16,80,2048]{2,1,0:T(8,128)(2,1)}) custom-call(s32[4]{0:T(128)S(1)} %get-tuple-element.502.pos, bf16[256,1536]{1,0:T(8,128)(2,1)} %get-tuple-element.521.refs_0_, bf16[256,2048]{1,0:T(8,128)(2,1)} %get-tuple-element.522.refs_1_, bf16[256,1024]{1,0:T(8,128)(2,1)} %get-tuple-element.523.refs_2_, ...), custom_call_target="tpu_custom_call" | custom-call | flops 1207959552 | bytes 2097152 | tf_op jit(solution)/shard_map/cond/branch_1_fun/pallas_call | solution.py:611
  104.8 13.0 %branch_1_fun.35 = (bf16[256,1536]{1,0:T(8,128)(2,1)}, bf16[256,1536]{1,0:T(8,128)(2,1)}, bf16[1024,1536]{1,0:T(8,128)(2,1)}, bf16[1024,1664]{1,0:T(8,128)(2,1)}...) custom-call(s32[4]{0:T(128)S(1)} %get-tuple-element.502.pos, ...), custom_call_target="tpu_custom_call", output_to_operand_aliasing={{2}: (6, {}), {3}: (7, {}), {4}: (8, {}), {5}: (9, {}), {6}... | custom-call | flops 2617245696 | bytes 3145728 | tf_op jit(solution)/shard_map/cond/branch_1_fun/pallas_call | solution.py:451
  121.0 26.0 %conditional.18 = (bf16[256,1536]{1,0:T(8,128)(2,1)}, bf16[256,1536]{1,0:T(8,128)(2,1)}, bf16[256,1536]{1,0:T(8,128)(2,1)}, bf16[1024,1536]{1,0:T(8,128)(2,1)}, ...) conditional(s32[]{:T(128)} %convert_element_type.154, ...), branch_computations={%region_11.12_spmd, %region_12.13_spmd} | conditional | flops 2617245696 | bytes 35651840 | solution.py:1101
  122.1 13.0 %branch_1_fun.37 = (bf16[256,1536]{1,0:T(8,128)(2,1)}, bf16[256,1536]{1,0:T(8,128)(2,1)}, bf16[1024,1536]{1,0:T(8,128)(2,1)}, bf16[1024,1664]{1,0:T(8,128)(2,1)}...) custom-call(s32[4]{0:T(128)S(1)} %get-tuple-element.532.pos, ...), custom_call_target="tpu_custom_call", output_to_operand_aliasing={{2}: (6, {}), {3}: (7, {}), {4}: (8, {}), {5}: (9, {}), {6}... | custom-call | flops 2617245696 | bytes 3145728 | tf_op jit(solution)/shard_map/cond/branch_1_fun/pallas_call | solution.py:451
  135.1 7.6 %collective-permute-done.4 = bf16[256,1536]{1,0:T(8,128)(2,1)} collective-permute-done((bf16[256,1536]{1,0:T(8,128)(2,1)}, bf16[256,1536]{1,0:T(8,128)(2,1)}, u32[]{:S(2)}, u32[]{:S(2)}) %collective-permute-start.4) | collective-permute-done | bytes 786464 | tf_op jit(solution)/shard_map/cond/branch_1_fun/ppermute | solution.py:911
  146.9 60.0 %conditional.19 = (bf16[256,1536]{1,0:T(8,128)(2,1)}, bf16[256,1536]{1,0:T(8,128)(2,1)}, bf16[1536,1024]{1,0:T(8,128)(2,1)}, bf16[1536,1024]{1,0:T(8,128)(2,1)S(...) conditional(s32[]{:T(128)} %convert_element_type.154, ...), branch_computations={%region_13.14_spmd, %region_14.15_spmd} | conditional | flops 13086228480 | bytes 29360308 | solution.py:1101
  147.9 4.8 branch_1_fun.41
  154.2 20.0 %branch_1_fun.39 = (bf16[256,1536]{1,0:T(8,128)(2,1)}, bf16[256,1536]{1,0:T(8,128)(2,1)}, bf16[256,1536]{1,0:T(8,128)(2,1)}, bf16[256,1536]{1,0:T(8,128)(2,1)}, ...) custom-call(s32[4]{0:T(128)S(1)} %get-tuple-element.554.pos, bf16[1024,1536]{1,0:T(8,128)(2,1)} %get-tuple-element.560.refs_3_.x_ref, ...), custom_call_target="tpu_custom_call" | custom-call | flops 5234491392 | bytes 3145728 | tf_op jit(solution)/shard_map/cond/branch_1_fun/pallas_call | solution.py:543
  174.2 13.0 %branch_1_fun.38 = (bf16[256,1536]{1,0:T(8,128)(2,1)}, bf16[256,1536]{1,0:T(8,128)(2,1)}, bf16[1024,1536]{1,0:T(8,128)(2,1)}, bf16[1024,1664]{1,0:T(8,128)(2,1)}...) custom-call(s32[4]{0:T(128)S(1)} %get-tuple-element.554.pos, ...), custom_call_target="tpu_custom_call", output_to_operand_aliasing={{2}: (6, {}), {3}: (7, {}), {4}: (8, {}), {5}: (9, {}), {6}... | custom-call | flops 2617245696 | bytes 3145728 | tf_op jit(solution)/shard_map/cond/branch_1_fun/pallas_call | solution.py:451
  187.2 19.4 %branch_1_fun.40 = (bf16[256,1536]{1,0:T(8,128)(2,1)}, bf16[256,1536]{1,0:T(8,128)(2,1)}, bf16[256,1536]{1,0:T(8,128)(2,1)}, bf16[256,1536]{1,0:T(8,128)(2,1)}, ...) custom-call(s32[4]{0:T(128)S(1)} %get-tuple-element.554.pos, ...), custom_call_target="tpu_custom_call", output_to_operand_aliasing={{4}: (13, {}), {5}: (14, {})} | custom-call | flops 5234491392 | bytes 3145728 | tf_op jit(solution)/shard_map/cond/branch_1_fun/pallas_call | solution.py:543
  207.0 31.7 %conditional.20 = (bf16[256,1536]{1,0:T(8,128)(2,1)}, bf16[6,128,3072]{2,1,0:T(8,128)(2,1)}, bf16[6,128,3072]{2,1,0:T(8,128)(2,1)}, bf16[2,160,2048]{2,1,0:T(8,128)(2,1)}) conditional(s32[]{:T(128)} %convert_element_type.154, () %tuple.143, (bf16[256,1536]{1,0:T(8,128)(2,1)}, bf16[256,1536]{1,0:T(8,128)(2,1)}, s32[4]{0:T(128)S(1)}, ...), branch_computations={%region_15.16_spmd, %region_16.17_spmd} | conditional | flops 4833411072 | bytes 14942320 | solution.py:1101
  212.9 15.7 %branch_1_fun.42 = (bf16[6,128,3072]{2,1,0:T(8,128)(2,1)}, bf16[6,128,3072]{2,1,0:T(8,128)(2,1)}) custom-call(s32[4]{0:T(128)S(1)} %get-tuple-element.601.pos, bf16[1536,1024]{1,0:T(8,128)(2,1)} %get-tuple-element.602.refs_0_.refs_1_.refs_2_.refs_3_, bf16[1536,1024]{1,0:T(8,128)(2,1)} %get-tuple-element.602.refs_0_.refs_1_.refs_2_.refs_3_, ...), custom_call_target="tpu_custom_call" | custom-call | flops 4831838208 | bytes 4194304 | tf_op jit(solution)/shard_map/cond/branch_1_fun/pallas_call | solution.py:705
  231.4 7.2 %collective-permute-done.24 = bf16[2,160,2048]{2,1,0:T(8,128)(2,1)} collective-permute-done((bf16[2,160,2048]{2,1,0:T(8,128)(2,1)}, bf16[2,160,2048]{2,1,0:T(8,128)(2,1)}, u32[]{:S(2)}, u32[]{:S(2)}) %collective-permute-start.24) | collective-permute-done | bytes 1310752 | tf_op jit(solution)/shard_map/cond/branch_1_fun/ppermute | solution.py:899
  238.7 35.5 %conditional.21 = (bf16[256,1536]{1,0:T(8,128)(2,1)}, bf16[6,128,3072]{2,1,0:T(8,128)(2,1)}, bf16[6,128,3072]{2,1,0:T(8,128)(2,1)}, bf16[6,128,3072]{2,1,0:T(8,1...) conditional(s32[]{:T(128)} %convert_element_type.154, () %tuple.142, ...), branch_computations={%region_17.18_spmd, %region_18.19_spmd} | conditional | flops 4834197504 | bytes 38797480 | solution.py:1101
  247.1 15.6 %branch_1_fun.43 = (bf16[6,128,3072]{2,1,0:T(8,128)(2,1)}, bf16[6,128,3072]{2,1,0:T(8,128)(2,1)}) custom-call(s32[4]{0:T(128)S(1)} %get-tuple-element.613.pos, bf16[1536,1024]{1,0:T(8,128)(2,1)} %get-tuple-element.614.refs_0_.refs_1_.refs_2_.refs_3_, bf16[1536,1024]{1,0:T(8,128)(2,1)} %get-tuple-element.614.refs_0_.refs_1_.refs_2_.refs_3_, ...), custom_call_target="tpu_custom_call" | custom-call | flops 4831838208 | bytes 4194304 | tf_op jit(solution)/shard_map/cond/branch_1_fun/pallas_call | solution.py:705
  266.7 7.4 %collective-permute-done.27 = bf16[4,80,2048]{2,1,0:T(8,128)(2,1)} collective-permute-done((bf16[4,80,2048]{2,1,0:T(8,128)(2,1)}, bf16[4,80,2048]{2,1,0:T(8,128)(2,1)}, u32[]{:S(2)}, u32[]{:S(2)}) %collective-permute-start.27) | collective-permute-done | bytes 1310752 | tf_op jit(solution)/shard_map/cond/branch_1_fun/ppermute | solution.py:893
  274.2 28.7 %conditional.22 = (bf16[256,1536]{1,0:T(8,128)(2,1)}, bf16[6,128,3072]{2,1,0:T(8,128)(2,1)}, bf16[6,128,768]{2,1,0:T(8,128)(2,1)}, bf16[6,128,768]{2,1,0:T(8,128...) conditional(s32[]{:T(128)} %convert_element_type.154, ...), branch_computations={%region_19.20_spmd, %region_20.21_spmd} | conditional | flops 3932160 | bytes 36438200 | solution.py:1101
  278.0 5.1 %branch_1_fun.46 = (bf16[6,128,768]{2,1,0:T(8,128)(2,1)}, bf16[6,128,768]{2,1,0:T(8,128)(2,1)}, bf16[6,128,768]{2,1,0:T(8,128)(2,1)}) custom-call(s32[4]{0:T(128)S(1)} %get-tuple-element.630.pos, bf16[6,128,3072]{2,1,0:T(8,128)(2,1)} %get-tuple-element.631.refs_0_.refs_2_.refs_4_, bf16[6,128,3072]{2,1,0:T(8,128)(2,1)} %get-tuple-element.632.refs_1_.refs_3_.refs_5_, ...), custom_call_target="tpu_custom_call" | custom-call | bytes 2097152 | tf_op jit(solution)/shard_map/cond/branch_1_fun/pallas_call | solution.py:746
  290.0 7.3 %collective-permute-done.28 = bf16[256,1536]{1,0:T(8,128)(2,1)} collective-permute-done((bf16[256,1536]{1,0:T(8,128)(2,1)S(1)}, bf16[256,1536]{1,0:T(8,128)(2,1)}, u32[]{:S(2)}, u32[]{:S(2)}) %collective-permute-start.28) | collective-permute-done | bytes 786464 | tf_op jit(solution)/shard_map/cond/branch_1_fun/ppermute | solution.py:911
  297.3 5.5 %collective-permute-done.30 = bf16[6,128,768]{2,1,0:T(8,128)(2,1)} collective-permute-done((bf16[6,128,768]{2,1,0:T(8,128)(2,1)}, bf16[6,128,768]{2,1,0:T(8,128)(2,1)}, u32[]{:S(2)}, u32[]{:S(2)}) %collective-permute-start.30) | collective-permute-done | bytes 1179680 | tf_op jit(solution)/shard_map/cond/branch_1_fun/ppermute | solution.py:893
  302.9 30.9 %conditional.23 = (f32[256,1536]{1,0:T(8,128)}, bf16[256,1536]{1,0:T(8,128)(2,1)}, bf16[256,1536]{1,0:T(8,128)(2,1)}, f32[1,1536]{1,0:T(1,128)S(1)}, bf16[256,15...) conditional(s32[]{:T(128)} %convert_element_type.154, ...), branch_computations={%region_21.22_spmd, %region_22.23_spmd} | conditional | flops 2315255808 | bytes 17313984 | solution.py:1101
  304.3 7.9 %branch_1_fun.48 = (f32[256,1536]{1,0:T(8,128)}, bf16[256,1536]{1,0:T(8,128)(2,1)}, f32[1,1536]{1,0:T(1,128)S(1)}, bf16[256,1536]{1,0:T(8,128)(2,1)}) custom-call(f32[256,1536]{1,0:T(8,128)} %get-tuple-element.643.refs_0_, bf16[256,1536]{1,0:T(8,128)(2,1)} %get-tuple-element.644.refs_1_, bf16[256,1536]{1,0:T(8,128)(2,1)} %get-tuple-element.645.refs_2_, ...), custom_call_target="tpu_custom_call" | custom-call | flops 301989888 | bytes 4194304 | tf_op jit(solution)/shard_map/cond/branch_1_fun/pallas_call | solution.py:273
  314.4 14.5 %branch_1_fun.49 = (bf16[256,1536]{1,0:T(8,128)(2,1)S(1)}, bf16[512,1024]{1,0:T(8,128)(2,1)}, bf16[512,1024]{1,0:T(8,128)(2,1)}) custom-call(s32[4]{0:T(128)S(1)} %get-tuple-element.654.pos, s32[8]{0:T(128)S(1)} %get-tuple-element.655.spans, bf16[256,1536]{1,0:T(8,128)(2,1)} %get-tuple-element.656.q_ref, bf16[256,1536]{1,0:T(8,128)(2,1)} %get-tuple-element.657.grad_ref, ...), custom_call_target="tpu_custom_call" | custom-call | flops 2013265920 | bytes 2097152 | tf_op jit(solution)/shard_map/cond/branch_1_fun/pallas_call | solution.py:190
  333.8 36.8 %conditional.24 = (bf16[256,1024]{1,0:T(8,128)(2,1)S(1)}, bf16[256,1536]{1,0:T(8,128)(2,1)}, bf16[8,48,1536]{2,1,0:T(8,128)(2,1)}, bf16[6,128,768]{2,1,0:T(8,128...) conditional(s32[]{:T(128)} %convert_element_type.154, () %tuple.127, ...), branch_computations={%region_23.24_spmd, %region_24.25_spmd} | conditional | flops 612106240 | bytes 40894780 | solution.py:1101
  348.9 6.0 %collective-permute-done.32 = bf16[256,1024]{1,0:T(8,128)(2,1)S(1)} collective-permute-done((bf16[256,1024]{1,0:T(8,128)(2,1)S(1)}, bf16[256,1024]{1,0:T(8,128)(2,1)S(1)}, u32[]{:S(2)}, u32[]{:S(2)}) %collective-permute-start.32) | collective-permute-done | bytes 524320 | tf_op jit(solution)/shard_map/cond/branch_1_fun/ppermute | solution.py:899
  356.4 5.5 %branch_1_fun.50 = bf16[384,1536]{1,0:T(8,128)(2,1)} custom-call(s32[4]{0:T(128)S(1)} %get-tuple-element.671.pos, bf16[256,1536]{1,0:T(8,128)(2,1)} %get-tuple-element.672.refs_0_, bf16[512,1536]{1,0:T(8,128)(2,1)} %get-tuple-element.673.refs_1_.refs_3_, bf16[256,1536]{1,0:T(8,128)(2,1)} %get-tuple-element.674.refs_2_, ...), custom_call_target="tpu_custom_call" | custom-call | flops 603979776 | bytes 1048576 | tf_op jit(solution)/shard_map/cond/branch_1_fun/pallas_call | solution.py:655
  364.7 5.9 %collective-permute-done.33 = bf16[256,1536]{1,0:T(8,128)(2,1)} collective-permute-done((bf16[256,1536]{1,0:T(8,128)(2,1)S(1)}, bf16[256,1536]{1,0:T(8,128)(2,1)}, u32[]{:S(2)}, u32[]{:S(2)}) %collective-permute-start.33) | collective-permute-done | bytes 786464 | tf_op jit(solution)/shard_map/cond/branch_1_fun/ppermute | solution.py:899
  370.6 38.3 %conditional.25 = (bf16[8,48,1536]{2,1,0:T(8,128)(2,1)}, bf16[8,48,1024]{2,1,0:T(8,128)(2,1)}, f32[1,1536]{1,0:T(1,128)S(1)}, bf16[256,1536]{1,0:T(8,128)(2,1)},...) conditional(s32[]{:T(128)} %convert_element_type.154, () %tuple.149, ...), branch_computations={%region_25.26_spmd, %region_26.27_spmd} | conditional | flops 1517551616 | bytes 41431364 | solution.py:1101
  375.5 9.9 %collective-permute-done.38.refs_6_ = bf16[256,1024]{1,0:T(8,128)(2,1)S(1)} collective-permute-done((bf16[256,1024]{1,0:T(8,128)(2,1)S(1)}, bf16[256,1024]{1,0:T(8,128)(2,1)S(1)}, u32[]{:S(2)}, u32[]{:S(2)}) %collective-permute-start.38) | collective-permute-done | bytes 524320 | tf_op jit(solution)/shard_map/cond/branch_1_fun/ppermute | solution.py:899
  390.2 9.3 %branch_1_fun.54 = (f32[256,1536]{1,0:T(8,128)}, f32[1,1536]{1,0:T(1,128)S(1)}) custom-call(bf16[256,1536]{1,0:T(8,128)(2,1)S(1)} %get-tuple-element.689.refs_4_.dq_ref, bf16[256,1024]{1,0:T(8,128)(2,1)S(1)} %get-tuple-element.691.refs_4_.dkv_ref, bf16[1536,1536]{1,0:T(8,128)(2,1)} %get-tuple-element.692.wq_ref, ...), custom_call_target="tpu_custom_call" | custom-call | flops 503316480 | bytes 3670016 | tf_op jit(solution)/shard_map/cond/branch_1_fun/pallas_call | solution.py:324
  403.4 5.2 %branch_1_fun.52 = bf16[384,1536]{1,0:T(8,128)(2,1)} custom-call(s32[4]{0:T(128)S(1)} %get-tuple-element.685.pos, bf16[256,1536]{1,0:T(8,128)(2,1)} %get-tuple-element.686.refs_0_, bf16[512,1536]{1,0:T(8,128)(2,1)} %get-tuple-element.687.refs_1_.refs_3_, bf16[256,1536]{1,0:T(8,128)(2,1)} %get-tuple-element.688.refs_2_, ...), custom_call_target="tpu_custom_call" | custom-call | flops 603979776 | bytes 1048576 | tf_op jit(solution)/shard_map/cond/branch_1_fun/pallas_call | solution.py:655
  408.9 49.2 %conditional.26 = (bf16[4,48,4096]{2,1,0:T(8,128)(2,1)S(1)}, bf16[4,48,4096]{2,1,0:T(8,128)(2,1)}, bf16[6,128,768]{2,1,0:T(8,128)(2,1)}, bf16[80,2048]{1,0:T(8,1...) conditional(s32[]{:T(128)} %convert_element_type.154, ...), branch_computations={%region_27.28_spmd, %region_28.29_spmd} | conditional | flops 12586057 | bytes 38032412 | solution.py:1101
  433.9 16.9 %all-to-all-done = f32[32,2,48]{2,1,0:T(2,128)} async-done(((f32[32,2,48]{2,1,0:T(2,128)}), f32[32,2,48]{2,1,0:T(2,128)}, u32[]{:S(2)}, u32[]{:S(2)}) %all-to-all-start) | async-done | bytes 12320 | tf_op jit(solution)/shard_map/cond/branch_1_fun/all_to_all | solution.py:1308
  450.8 7.2 %collective-permute-done.46 = bf16[80,2048]{1,0:T(8,128)(2,1)} collective-permute-done((bf16[80,2048]{1,0:T(8,128)(2,1)}, bf16[80,2048]{1,0:T(8,128)(2,1)}, u32[]{:S(2)}, u32[]{:S(2)}) %collective-permute-start.46) | collective-permute-done | bytes 327712 | tf_op jit(solution)/shard_map/cond/branch_1_fun/ppermute | solution.py:899
  458.1 43.8 %conditional.27 = (f32[2,48]{1,0:T(2,128)}, f32[48,1024]{1,0:T(8,128)}, f32[48,1024]{1,0:T(8,128)}, f32[32,1536]{1,0:T(8,128)}, f32[48,1536]{1,0:T(8,128)}, /*in...) conditional(s32[]{:T(128)} %convert_element_type.154, ...), branch_computations={%region_29.30_spmd, %region_30.32_spmd} | conditional | flops 2362348 | bytes 26625254 | solution.py:1101
  473.6 6.3 %branch_1_fun.58 = (bf16[3,128,768]{2,1,0:T(8,128)(2,1)}, bf16[3,128,768]{2,1,0:T(8,128)(2,1)}, bf16[3,128,768]{2,1,0:T(8,128)(2,1)}, bf16[3,128,768]{2,1,0:T(8,128)(2,1)}) custom-call(s32[4]{0:T(128)S(1)} %get-tuple-element.735.pos, bf16[6,128,3072]{2,1,0:T(8,128)(2,1)} %get-tuple-element.736.refs_0_.refs_4_.refs_8_.refs_12_, ...), custom_call_target="tpu_custom_call" | custom-call | bytes 2097152 | tf_op jit(solution)/shard_map/cond/branch_1_fun/pallas_call | solution.py:746
  479.9 8.8 %branch_1_fun.59 = (f32[2,384,512]{2,1,0:T(8,128)}, f32[2,384,512]{2,1,0:T(8,128)}, f32[2,512,384]{2,1,0:T(8,128)}) custom-call(bf16[384,768]{1,0:T(8,128)(2,1)} %bitcast.92, bf16[384,768]{1,0:T(8,128)(2,1)} %bitcast.93, bf16[384,768]{1,0:T(8,128)(2,1)} %bitcast.94, bf16[384,768]{1,0:T(8,128)(2,1)} %bitcast.95), custom_call_target="tpu_custom_call" | custom-call | bytes 2097152 | tf_op jit(solution)/shard_map/cond/branch_1_fun/pallas_call | solution.py:806
  489.6 9.9 %collective-permute-done.49.refs_2_ = bf16[48,4096]{1,0:T(8,128)(2,1)} collective-permute-done((bf16[48,4096]{1,0:T(8,128)(2,1)}, bf16[48,4096]{1,0:T(8,128)(2,1)}, u32[]{:S(2)}, u32[]{:S(2)}) %collective-permute-start.49) | collective-permute-done | bytes 393248 | tf_op jit(solution)/shard_map/cond/branch_1_fun/ppermute | solution.py:899
  (192 shorter events, 172.5 us)
Async XLA Ops:
  11.8 21.9 %collective-permute-start.52 = (bf16[256,1024]{1,0:T(8,128)(2,1)}, bf16[256,1024]{1,0:T(8,128)(2,1)}, u32[]{:S(2)}, u32[]{:S(2)}) collective-permute-start(bf16[256,1024]{1,0:T(8,128)(2,1)} %get-tuple-element.1105), channel_id=1, source_target_pairs={{0,8},{8,0},{16,24},{24,16},{1,9},{9,1},{17,25},{25,17},{2,10},{10... | collective-permute-start | bytes 1572872 | tf_op jit(solution)/shard_map/cond/branch_1_fun/ppermute | solution.py:893
  14.8 23.4 %collective-permute-start.54 = (bf16[256,1664]{1,0:T(8,128)(2,1)}, bf16[256,1664]{1,0:T(8,128)(2,1)}, u32[]{:S(2)}, u32[]{:S(2)}) collective-permute-start(bf16[256,1664]{1,0:T(8,128)(2,1)} %get-tuple-element.451), channel_id=1, source_target_pairs={{0,2},{1,3},{2,4},{3,5},{4,6},{5,7},{6,0},{7,1},{8,14},{9,15},{10,... | collective-permute-start | bytes 2555912 | tf_op jit(solution)/shard_map/cond/branch_1_fun/ppermute | solution.py:911
  17.7 19.8 %collective-permute-start.55 = (bf16[256,1536]{1,0:T(8,128)(2,1)}, bf16[256,1536]{1,0:T(8,128)(2,1)}, u32[]{:S(2)}, u32[]{:S(2)}) collective-permute-start(bf16[256,1536]{1,0:T(8,128)(2,1)} %get-tuple-element.1071), channel_id=1, source_target_pairs={{0,1},{1,0},{2,3},{3,2},{4,5},{5,4},{6,7},{7,6},{8,9},{9,8},{10,11... | collective-permute-start | bytes 2359304 | tf_op jit(solution)/shard_map/cond/branch_1_fun/ppermute | solution.py:893
  38.3 21.6 %collective-permute-start.1 = (bf16[256,1664]{1,0:T(8,128)(2,1)}, bf16[256,1664]{1,0:T(8,128)(2,1)}, u32[]{:S(2)}, u32[]{:S(2)}) collective-permute-start(bf16[256,1664]{1,0:T(8,128)(2,1)} %get-tuple-element.471), channel_id=1, source_target_pairs={{0,2},{1,3},{2,4},{3,5},{4,6},{5,7},{6,0},{7,1},{8,14},{9,15},{10,... | collective-permute-start | bytes 2555912 | tf_op jit(solution)/shard_map/cond/branch_1_fun/ppermute | solution.py:911
  38.4 20.1 %collective-permute-start = (bf16[256,1536]{1,0:T(8,128)(2,1)}, bf16[256,1536]{1,0:T(8,128)(2,1)}, u32[]{:S(2)}, u32[]{:S(2)}) collective-permute-start(bf16[256,1536]{1,0:T(8,128)(2,1)} %get-tuple-element.470), channel_id=1, source_target_pairs={{0,16},{8,24},{16,0},{24,8},{1,17},{9,25},{17,1},{25,9},{2,18},{10... | collective-permute-start | bytes 2359304 | tf_op jit(solution)/shard_map/cond/branch_1_fun/ppermute | solution.py:899
  38.9 20.3 %collective-permute-start.2 = (bf16[256,1536]{1,0:T(8,128)(2,1)}, bf16[256,1536]{1,0:T(8,128)(2,1)}, u32[]{:S(2)}, u32[]{:S(2)}) collective-permute-start(bf16[256,1536]{1,0:T(8,128)(2,1)} %get-tuple-element.472), channel_id=1, source_target_pairs={{0,1},{1,0},{2,3},{3,2},{4,5},{5,4},{6,7},{7,6},{8,9},{9,8},{10,11... | collective-permute-start | bytes 2359304 | tf_op jit(solution)/shard_map/cond/branch_1_fun/ppermute | solution.py:893
  62.6 28.8 %collective-permute-start.15 = (bf16[512,1536]{1,0:T(8,128)(2,1)}, bf16[512,1536]{1,0:T(8,128)(2,1)}, u32[]{:S(2)}, u32[]{:S(2)}) collective-permute-start(bf16[512,1536]{1,0:T(8,128)(2,1)} %pad_maximum_fusion.3), channel_id=1, source_target_pairs={{0,8},{8,0},{16,24},{24,16},{1,9},{9,1},{17,25},{25,17},{2,10},{10... | collective-permute-start | bytes 4718600 | tf_op jit(solution)/shard_map/cond/branch_1_fun/ppermute | solution.py:893
  62.6 28.8 %collective-permute-start.16 = (bf16[512,1024]{1,0:T(8,128)(2,1)}, bf16[512,1024]{1,0:T(8,128)(2,1)}, u32[]{:S(2)}, u32[]{:S(2)}) collective-permute-start(bf16[512,1024]{1,0:T(8,128)(2,1)} %get-tuple-element.498), channel_id=1, source_target_pairs={{0,1},{1,0},{2,3},{3,2},{4,5},{5,4},{6,7},{7,6},{8,9},{9,8},{10,11... | collective-permute-start | bytes 3145736 | tf_op jit(solution)/shard_map/cond/branch_1_fun/ppermute | solution.py:893
  64.0 27.3 %collective-permute-start.17 = (bf16[256,1536]{1,0:T(8,128)(2,1)}, bf16[256,1536]{1,0:T(8,128)(2,1)}, u32[]{:S(2)}, u32[]{:S(2)}) collective-permute-start(bf16[256,1536]{1,0:T(8,128)(2,1)} %get-tuple-element.499), channel_id=1, source_target_pairs={{0,8},{8,0},{16,24},{24,16},{1,9},{9,1},{17,25},{25,17},{2,10},{10... | collective-permute-start | bytes 2359304 | tf_op jit(solution)/shard_map/cond/branch_1_fun/ppermute | solution.py:893
  64.3 27.0 %collective-permute-start.18 = (bf16[256,1536]{1,0:T(8,128)(2,1)}, bf16[256,1536]{1,0:T(8,128)(2,1)}, u32[]{:S(2)}, u32[]{:S(2)}) collective-permute-start(bf16[256,1536]{1,0:T(8,128)(2,1)} %get-tuple-element.500), channel_id=1, source_target_pairs={{0,16},{8,24},{16,0},{24,8},{1,17},{9,25},{17,1},{25,9},{2,18},{10... | collective-permute-start | bytes 2359304 | tf_op jit(solution)/shard_map/cond/branch_1_fun/ppermute | solution.py:899
  65.2 26.1 %collective-permute-start.14 = (bf16[256,1536]{1,0:T(8,128)(2,1)}, bf16[256,1536]{1,0:T(8,128)(2,1)}, u32[]{:S(2)}, u32[]{:S(2)}) collective-permute-start(bf16[256,1536]{1,0:T(8,128)(2,1)} %get-tuple-element.474.x_ref), channel_id=1, source_target_pairs={{0,2},{1,3},{2,4},{3,5},{4,6},{5,7},{6,0},{7,1},{8,14},{9,15},{10,... | collective-permute-start | bytes 2359304 | tf_op jit(solution)/shard_map/cond/branch_1_fun/ppermute | solution.py:911
  94.2 26.7 %collective-permute-start.22 = (bf16[512,1536]{1,0:T(8,128)(2,1)}, bf16[512,1536]{1,0:T(8,128)(2,1)}, u32[]{:S(2)}, u32[]{:S(2)}) collective-permute-start(bf16[512,1536]{1,0:T(8,128)(2,1)} %pad_maximum_fusion.4), channel_id=1, source_target_pairs={{0,8},{8,0},{16,24},{24,16},{1,9},{9,1},{17,25},{25,17},{2,10},{10... | collective-permute-start | bytes 4718600 | tf_op jit(solution)/shard_map/cond/branch_1_fun/ppermute | solution.py:893
  95.6 25.4 %collective-permute-start.20 = (bf16[512,1024]{1,0:T(8,128)(2,1)}, bf16[512,1024]{1,0:T(8,128)(2,1)}, u32[]{:S(2)}, u32[]{:S(2)}) collective-permute-start(bf16[512,1024]{1,0:T(8,128)(2,1)} %get-tuple-element.527), channel_id=1, source_target_pairs={{0,1},{1,0},{2,3},{3,2},{4,5},{5,4},{6,7},{7,6},{8,9},{9,8},{10,11... | collective-permute-start | bytes 3145736 | tf_op jit(solution)/shard_map/cond/branch_1_fun/ppermute | solution.py:893
  96.1 24.8 %collective-permute-start.21 = (bf16[512,1024]{1,0:T(8,128)(2,1)}, bf16[512,1024]{1,0:T(8,128)(2,1)}, u32[]{:S(2)}, u32[]{:S(2)}) collective-permute-start(bf16[512,1024]{1,0:T(8,128)(2,1)} %get-tuple-element.528), channel_id=1, source_target_pairs={{0,8},{8,0},{16,24},{24,16},{1,9},{9,1},{17,25},{25,17},{2,10},{10... | collective-permute-start | bytes 3145736 | tf_op jit(solution)/shard_map/cond/branch_1_fun/ppermute | solution.py:893
  96.1 21.8 %collective-permute-start.19 = (bf16[256,1536]{1,0:T(8,128)(2,1)}, bf16[256,1536]{1,0:T(8,128)(2,1)}, u32[]{:S(2)}, u32[]{:S(2)}) collective-permute-start(bf16[256,1536]{1,0:T(8,128)(2,1)} %get-tuple-element.501.x_ref), channel_id=1, source_target_pairs={{0,2},{1,3},{2,4},{3,5},{4,6},{5,7},{6,0},{7,1},{8,14},{9,15},{10,... | collective-permute-start | bytes 2359304 | tf_op jit(solution)/shard_map/cond/branch_1_fun/ppermute | solution.py:911
  121.0 26.0 %collective-permute-start.5 = (bf16[16,80,2048]{2,1,0:T(8,128)(2,1)}, bf16[16,80,2048]{2,1,0:T(8,128)(2,1)}, u32[]{:S(2)}, u32[]{:S(2)}) collective-permute-start(bf16[16,80,2048]{2,1,0:T(8,128)(2,1)} %get-tuple-element.551), channel_id=1, source_target_pairs={{0,8},{8,0},{16,24},{24,16},{1,9},{9,1},{17,25},{25,17},{2,10},{10... | collective-permute-start | bytes 15728648 | tf_op jit(solution)/shard_map/cond/branch_1_fun/ppermute | solution.py:893
  121.0 25.9 %collective-permute-start.6 = (bf16[512,1024]{1,0:T(8,128)(2,1)}, bf16[512,1024]{1,0:T(8,128)(2,1)}, u32[]{:S(2)}, u32[]{:S(2)}) collective-permute-start(bf16[512,1024]{1,0:T(8,128)(2,1)} %get-tuple-element.552), channel_id=1, source_target_pairs={{0,1},{1,0},{2,3},{3,2},{4,5},{5,4},{6,7},{7,6},{8,9},{9,8},{10,11... | collective-permute-start | bytes 3145736 | tf_op jit(solution)/shard_map/cond/branch_1_fun/ppermute | solution.py:893
  121.6 25.3 %collective-permute-start.7 = (bf16[512,1024]{1,0:T(8,128)(2,1)}, bf16[512,1024]{1,0:T(8,128)(2,1)}, u32[]{:S(2)}, u32[]{:S(2)}) collective-permute-start(bf16[512,1024]{1,0:T(8,128)(2,1)} %get-tuple-element.553), channel_id=1, source_target_pairs={{0,8},{8,0},{16,24},{24,16},{1,9},{9,1},{17,25},{25,17},{2,10},{10... | collective-permute-start | bytes 3145736 | tf_op jit(solution)/shard_map/cond/branch_1_fun/ppermute | solution.py:893
  121.8 20.9 %collective-permute-start.4 = (bf16[256,1536]{1,0:T(8,128)(2,1)}, bf16[256,1536]{1,0:T(8,128)(2,1)}, u32[]{:S(2)}, u32[]{:S(2)}) collective-permute-start(bf16[256,1536]{1,0:T(8,128)(2,1)} %get-tuple-element.531.x_ref), channel_id=1, source_target_pairs={{0,2},{1,3},{2,4},{3,5},{4,6},{5,7},{6,0},{7,1},{8,14},{9,15},{10,... | collective-permute-start | bytes 2359304 | tf_op jit(solution)/shard_map/cond/branch_1_fun/ppermute | solution.py:911
  147.5 26.7 %collective-permute-start.8 = (bf16[256,1664]{1,0:T(8,128)(2,1)}, bf16[256,1664]{1,0:T(8,128)(2,1)}, u32[]{:S(2)}, u32[]{:S(2)}) collective-permute-start(bf16[256,1664]{1,0:T(8,128)(2,1)} %get-tuple-element.556), channel_id=1, source_target_pairs={{0,2},{1,3},{2,4},{3,5},{4,6},{5,7},{6,0},{7,1},{8,14},{9,15},{10,... | collective-permute-start | bytes 2555912 | tf_op jit(solution)/shard_map/cond/branch_1_fun/ppermute | solution.py:911
  152.7 53.9 %collective-permute-start.10 = (bf16[2,160,2048]{2,1,0:T(8,128)(2,1)}, bf16[2,160,2048]{2,1,0:T(8,128)(2,1)}, u32[]{:S(2)}, u32[]{:S(2)}) collective-permute-start(bf16[2,160,2048]{2,1,0:T(8,128)(2,1)} %get-tuple-element.597), channel_id=1, source_target_pairs={{0,16},{8,24},{16,0},{24,8},{1,17},{9,25},{17,1},{25,9},{2,18},{10... | collective-permute-start | bytes 3932168 | tf_op jit(solution)/shard_map/cond/branch_1_fun/ppermute | solution.py:899
  207.0 31.7 %collective-permute-start.24 = (bf16[2,160,2048]{2,1,0:T(8,128)(2,1)}, bf16[2,160,2048]{2,1,0:T(8,128)(2,1)}, u32[]{:S(2)}, u32[]{:S(2)}) collective-permute-start(bf16[2,160,2048]{2,1,0:T(8,128)(2,1)} %get-tuple-element.608), channel_id=1, source_target_pairs={{0,16},{8,24},{16,0},{24,8},{1,17},{9,25},{17,1},{25,9},{2,18},{10... | collective-permute-start | bytes 3932168 | tf_op jit(solution)/shard_map/cond/branch_1_fun/ppermute | solution.py:899
  211.0 20.4 %collective-permute-start.23 = (bf16[256,1536]{1,0:T(8,128)(2,1)}, bf16[256,1536]{1,0:T(8,128)(2,1)}, u32[]{:S(2)}, u32[]{:S(2)}) collective-permute-start(bf16[256,1536]{1,0:T(8,128)(2,1)} %add_convert_fusion), channel_id=1, source_target_pairs={{0,6},{1,7},{2,0},{3,1},{4,2},{5,3},{6,4},{7,5},{8,10},{9,11},{10,... | collective-permute-start | bytes 2359304 | tf_op jit(solution)/shard_map/cond/branch_1_fun/ppermute | solution.py:911
  238.7 24.0 %collective-permute-start.26 = (bf16[6,128,3072]{2,1,0:T(8,128)(2,1)}, bf16[6,128,3072]{2,1,0:T(8,128)(2,1)}, u32[]{:S(2)}, u32[]{:S(2)}) collective-permute-start(bf16[6,128,3072]{2,1,0:T(8,128)(2,1)} %get-tuple-element.612), channel_id=1, source_target_pairs={{0,8},{8,0},{16,24},{24,16},{1,9},{9,1},{17,25},{25,17},{2,10},{10... | collective-permute-start | bytes 14155784 | tf_op jit(solution)/shard_map/cond/branch_1_fun/ppermute | solution.py:893
  242.7 31.5 %collective-permute-start.27 = (bf16[4,80,2048]{2,1,0:T(8,128)(2,1)}, bf16[4,80,2048]{2,1,0:T(8,128)(2,1)}, u32[]{:S(2)}, u32[]{:S(2)}) collective-permute-start(bf16[4,80,2048]{2,1,0:T(8,128)(2,1)} %branch_1_fun.45), channel_id=1, source_target_pairs={{0,1},{1,0},{2,3},{3,2},{4,5},{5,4},{6,7},{7,6},{8,9},{9,8},{10,11... | collective-permute-start | bytes 3932168 | tf_op jit(solution)/shard_map/cond/branch_1_fun/ppermute | solution.py:893
  246.0 20.7 %collective-permute-start.25 = (bf16[256,1536]{1,0:T(8,128)(2,1)}, bf16[256,1536]{1,0:T(8,128)(2,1)}, u32[]{:S(2)}, u32[]{:S(2)}) collective-permute-start(bf16[256,1536]{1,0:T(8,128)(2,1)} %add_convert_fusion.1), channel_id=1, source_target_pairs={{0,6},{1,7},{2,0},{3,1},{4,2},{5,3},{6,4},{7,5},{8,10},{9,11},{10,... | collective-permute-start | bytes 2359304 | tf_op jit(solution)/shard_map/cond/branch_1_fun/ppermute | solution.py:911
  274.2 28.7 %collective-permute-start.29 = (bf16[6,128,3072]{2,1,0:T(8,128)(2,1)}, bf16[6,128,3072]{2,1,0:T(8,128)(2,1)}, u32[]{:S(2)}, u32[]{:S(2)}) collective-permute-start(bf16[6,128,3072]{2,1,0:T(8,128)(2,1)} %get-tuple-element.628), channel_id=1, source_target_pairs={{0,8},{8,0},{16,24},{24,16},{1,9},{9,1},{17,25},{25,17},{2,10},{10... | collective-permute-start | bytes 14155784 | tf_op jit(solution)/shard_map/cond/branch_1_fun/ppermute | solution.py:893
  274.2 28.7 %collective-permute-start.30 = (bf16[6,128,768]{2,1,0:T(8,128)(2,1)}, bf16[6,128,768]{2,1,0:T(8,128)(2,1)}, u32[]{:S(2)}, u32[]{:S(2)}) collective-permute-start(bf16[6,128,768]{2,1,0:T(8,128)(2,1)} %get-tuple-element.629), channel_id=1, source_target_pairs={{0,1},{1,0},{2,3},{3,2},{4,5},{5,4},{6,7},{7,6},{8,9},{9,8},{10,11... | collective-permute-start | bytes 3538952 | tf_op jit(solution)/shard_map/cond/branch_1_fun/ppermute | solution.py:893
  276.8 20.6 %collective-permute-start.28 = (bf16[256,1536]{1,0:T(8,128)(2,1)S(1)}, bf16[256,1536]{1,0:T(8,128)(2,1)}, u32[]{:S(2)}, u32[]{:S(2)}) collective-permute-start(bf16[256,1536]{1,0:T(8,128)(2,1)S(1)} %add_convert_fusion.3), channel_id=1, source_target_pairs={{0,6},{1,7},{2,0},{3,1},{4,2},{5,3},{6,4},{7,5},{8,10},{9,11},{10,... | collective-permute-start | bytes 2359304 | tf_op jit(solution)/shard_map/cond/branch_1_fun/ppermute | solution.py:911
  303.1 30.7 %collective-permute-start.13 = (bf16[6,128,768]{2,1,0:T(8,128)(2,1)}, bf16[6,128,768]{2,1,0:T(8,128)(2,1)}, u32[]{:S(2)}, u32[]{:S(2)}) collective-permute-start(bf16[6,128,768]{2,1,0:T(8,128)(2,1)} %get-tuple-element.667), channel_id=1, source_target_pairs={{0,1},{1,0},{2,3},{3,2},{4,5},{5,4},{6,7},{7,6},{8,9},{9,8},{10,11... | collective-permute-start | bytes 3538952 | tf_op jit(solution)/shard_map/cond/branch_1_fun/ppermute | solution.py:893
  313.0 20.7 %collective-permute-start.12 = (bf16[256,1536]{1,0:T(8,128)(2,1)}, bf16[256,1536]{1,0:T(8,128)(2,1)}, u32[]{:S(2)}, u32[]{:S(2)}) collective-permute-start(bf16[256,1536]{1,0:T(8,128)(2,1)} %get-tuple-element.666), channel_id=1, source_target_pairs={{0,6},{1,7},{2,0},{3,1},{4,2},{5,3},{6,4},{7,5},{8,10},{9,11},{10,... | collective-permute-start | bytes 2359304 | tf_op jit(solution)/shard_map/cond/branch_1_fun/ppermute | solution.py:911
  336.4 20.0 %collective-permute-start.34 = (bf16[512,1536]{1,0:T(8,128)(2,1)}, bf16[512,1536]{1,0:T(8,128)(2,1)}, u32[]{:S(2)}, u32[]{:S(2)}) collective-permute-start(bf16[512,1536]{1,0:T(8,128)(2,1)} %pad_maximum_fusion.5), channel_id=1, source_target_pairs={{0,8},{8,0},{16,24},{24,16},{1,9},{9,1},{17,25},{25,17},{2,10},{10... | collective-permute-start | bytes 4718600 | tf_op jit(solution)/shard_map/cond/branch_1_fun/ppermute | solution.py:893
  336.9 33.7 %collective-permute-start.36 = (bf16[6,128,768]{2,1,0:T(8,128)(2,1)}, bf16[6,128,768]{2,1,0:T(8,128)(2,1)}, u32[]{:S(2)}, u32[]{:S(2)}) collective-permute-start(bf16[6,128,768]{2,1,0:T(8,128)(2,1)} %get-tuple-element.684), channel_id=1, source_target_pairs={{0,1},{1,0},{2,3},{3,2},{4,5},{5,4},{6,7},{7,6},{8,9},{9,8},{10,11... | collective-permute-start | bytes 3538952 | tf_op jit(solution)/shard_map/cond/branch_1_fun/ppermute | solution.py:893
  343.9 20.7 %collective-permute-start.35 = (bf16[256,1536]{1,0:T(8,128)(2,1)}, bf16[256,1536]{1,0:T(8,128)(2,1)}, u32[]{:S(2)}, u32[]{:S(2)}) collective-permute-start(bf16[256,1536]{1,0:T(8,128)(2,1)} %add_convert_fusion.4), channel_id=1, source_target_pairs={{0,6},{1,7},{2,0},{3,1},{4,2},{5,3},{6,4},{7,5},{8,10},{9,11},{10,... | collective-permute-start | bytes 2359304 | tf_op jit(solution)/shard_map/cond/branch_1_fun/ppermute | solution.py:911
  344.3 26.3 %collective-permute-start.33 = (bf16[256,1536]{1,0:T(8,128)(2,1)S(1)}, bf16[256,1536]{1,0:T(8,128)(2,1)}, u32[]{:S(2)}, u32[]{:S(2)}) collective-permute-start(bf16[256,1536]{1,0:T(8,128)(2,1)S(1)} %get-tuple-element.670), channel_id=1, source_target_pairs={{0,16},{8,24},{16,0},{24,8},{1,17},{9,25},{17,1},{25,9},{2,18},{10... | collective-permute-start | bytes 2359304 | tf_op jit(solution)/shard_map/cond/branch_1_fun/ppermute | solution.py:899
  374.0 29.4 %collective-permute-start.37 = (bf16[512,1536]{1,0:T(8,128)(2,1)}, bf16[512,1536]{1,0:T(8,128)(2,1)}, u32[]{:S(2)}, u32[]{:S(2)}) collective-permute-start(bf16[512,1536]{1,0:T(8,128)(2,1)} %pad_maximum_fusion.6), channel_id=1, source_target_pairs={{0,8},{8,0},{16,24},{24,16},{1,9},{9,1},{17,25},{25,17},{2,10},{10... | collective-permute-start | bytes 4718600 | tf_op jit(solution)/shard_map/cond/branch_1_fun/ppermute | solution.py:893
  374.0 34.6 %collective-permute-start.41 = (bf16[6,128,768]{2,1,0:T(8,128)(2,1)}, bf16[6,128,768]{2,1,0:T(8,128)(2,1)}, u32[]{:S(2)}, u32[]{:S(2)}) collective-permute-start(bf16[6,128,768]{2,1,0:T(8,128)(2,1)} %get-tuple-element.702), channel_id=1, source_target_pairs={{0,1},{1,0},{2,3},{3,2},{4,5},{5,4},{6,7},{7,6},{8,9},{9,8},{10,11... | collective-permute-start | bytes 3538952 | tf_op jit(solution)/shard_map/cond/branch_1_fun/ppermute | solution.py:893
  374.6 34.0 %collective-permute-start.42 = (bf16[6,128,768]{2,1,0:T(8,128)(2,1)}, bf16[6,128,768]{2,1,0:T(8,128)(2,1)}, u32[]{:S(2)}, u32[]{:S(2)}) collective-permute-start(bf16[6,128,768]{2,1,0:T(8,128)(2,1)} %get-tuple-element.703), channel_id=1, source_target_pairs={{0,16},{8,24},{16,0},{24,8},{1,17},{9,25},{17,1},{25,9},{2,18},{10... | collective-permute-start | bytes 3538952 | tf_op jit(solution)/shard_map/cond/branch_1_fun/ppermute | solution.py:899
  389.4 19.3 %collective-permute-start.40 = (bf16[256,1536]{1,0:T(8,128)(2,1)}, bf16[256,1536]{1,0:T(8,128)(2,1)}, u32[]{:S(2)}, u32[]{:S(2)}) collective-permute-start(bf16[256,1536]{1,0:T(8,128)(2,1)} %add_convert_fusion.7), channel_id=1, source_target_pairs={{0,6},{1,7},{2,0},{3,1},{4,2},{5,3},{6,4},{7,5},{8,10},{9,11},{10,... | collective-permute-start | bytes 2359304 | tf_op jit(solution)/shard_map/cond/branch_1_fun/ppermute | solution.py:911
  412.4 45.7 %collective-permute-start.43 = (bf16[4,48,4096]{2,1,0:T(8,128)(2,1)}, bf16[4,48,4096]{2,1,0:T(8,128)(2,1)}, u32[]{:S(2)}, u32[]{:S(2)}) collective-permute-start(bf16[4,48,4096]{2,1,0:T(8,128)(2,1)} %get-tuple-element.1087), channel_id=1, source_target_pairs={{0,1},{1,0},{2,3},{3,2},{4,5},{5,4},{6,7},{7,6},{8,9},{9,8},{10,11... | collective-permute-start | bytes 4718600 | tf_op jit(solution)/shard_map/cond/branch_1_fun/ppermute | solution.py:893
  418.2 39.9 %collective-permute-start.44 = (bf16[6,128,768]{2,1,0:T(8,128)(2,1)}, bf16[6,128,768]{2,1,0:T(8,128)(2,1)}, u32[]{:S(2)}, u32[]{:S(2)}) collective-permute-start(bf16[6,128,768]{2,1,0:T(8,128)(2,1)} %branch_1_fun.55), channel_id=1, source_target_pairs={{0,16},{8,24},{16,0},{24,8},{1,17},{9,25},{17,1},{25,9},{2,18},{10... | collective-permute-start | bytes 3538952 | tf_op jit(solution)/shard_map/cond/branch_1_fun/ppermute | solution.py:899
  420.2 30.6 %all-to-all-start = ((f32[32,2,48]{2,1,0:T(2,128)}), f32[32,2,48]{2,1,0:T(2,128)}, u32[]{:S(2)}, u32[]{:S(2)}) async-start(f32[32,2,48]{2,1,0:T(2,128)} %pad_maximum_fusion.9), calls=%async_computation | async-start | bytes 65536 | tf_op jit(solution)/shard_map/cond/branch_1_fun/all_to_all | solution.py:1308
  425.8 25.0 %collective-permute-start.47 = (bf16[80,2048]{1,0:T(8,128)(2,1)}, bf16[80,2048]{1,0:T(8,128)(2,1)}, u32[]{:S(2)}, u32[]{:S(2)}) collective-permute-start(bf16[80,2048]{1,0:T(8,128)(2,1)} %get-tuple-element.1089), channel_id=1, source_target_pairs={{0,6},{1,7},{2,0},{3,1},{4,2},{5,3},{6,4},{7,5},{8,14},{9,15},{10,... | collective-permute-start | bytes 983048 | tf_op jit(solution)/shard_map/cond/branch_1_fun/ppermute | solution.py:899
  429.3 28.7 %collective-permute-start.46 = (bf16[80,2048]{1,0:T(8,128)(2,1)}, bf16[80,2048]{1,0:T(8,128)(2,1)}, u32[]{:S(2)}, u32[]{:S(2)}) collective-permute-start(bf16[80,2048]{1,0:T(8,128)(2,1)} %get-tuple-element.1090), channel_id=1, source_target_pairs={{0,4},{1,5},{2,6},{3,7},{4,0},{5,1},{6,2},{7,3},{8,12},{9,13},{10,... | collective-permute-start | bytes 983048 | tf_op jit(solution)/shard_map/cond/branch_1_fun/ppermute | solution.py:899
  429.3 28.7 %collective-permute-start.45 = (bf16[80,2048]{1,0:T(8,128)(2,1)S(1)}, bf16[80,2048]{1,0:T(8,128)(2,1)}, u32[]{:S(2)}, u32[]{:S(2)}) collective-permute-start(bf16[80,2048]{1,0:T(8,128)(2,1)S(1)} %get-tuple-element.1091), channel_id=1, source_target_pairs={{0,2},{1,3},{2,4},{3,5},{4,6},{5,7},{6,0},{7,1},{8,10},{9,11},{10,... | collective-permute-start | bytes 983048 | tf_op jit(solution)/shard_map/cond/branch_1_fun/ppermute | solution.py:899
  462.6 27.0 %collective-permute-start.50 = (bf16[48,4096]{1,0:T(8,128)(2,1)}, bf16[48,4096]{1,0:T(8,128)(2,1)}, u32[]{:S(2)}, u32[]{:S(2)}) collective-permute-start(bf16[48,4096]{1,0:T(8,128)(2,1)} %get-tuple-element.1082), channel_id=1, source_target_pairs={{0,6},{1,7},{2,0},{3,1},{4,2},{5,3},{6,4},{7,5},{8,14},{9,15},{10,... | collective-permute-start | bytes 1179656 | tf_op jit(solution)/shard_map/cond/branch_1_fun/ppermute | solution.py:899
  462.6 36.9 %collective-permute-start.49 = (bf16[48,4096]{1,0:T(8,128)(2,1)}, bf16[48,4096]{1,0:T(8,128)(2,1)}, u32[]{:S(2)}, u32[]{:S(2)}) collective-permute-start(bf16[48,4096]{1,0:T(8,128)(2,1)} %get-tuple-element.1083), channel_id=1, source_target_pairs={{0,4},{1,5},{2,6},{3,7},{4,0},{5,1},{6,2},{7,3},{8,12},{9,13},{10,... | collective-permute-start | bytes 1179656 | tf_op jit(solution)/shard_map/cond/branch_1_fun/ppermute | solution.py:899
  465.2 34.2 %collective-permute-start.48 = (bf16[48,4096]{1,0:T(8,128)(2,1)S(1)}, bf16[48,4096]{1,0:T(8,128)(2,1)}, u32[]{:S(2)}, u32[]{:S(2)}) collective-permute-start(bf16[48,4096]{1,0:T(8,128)(2,1)S(1)} %get-tuple-element.1084), channel_id=1, source_target_pairs={{0,2},{1,3},{2,4},{3,5},{4,6},{5,7},{6,0},{7,1},{8,10},{9,11},{10,... | collective-permute-start | bytes 1179656 | tf_op jit(solution)/shard_map/cond/branch_1_fun/ppermute | solution.py:899
  (24 other events, 346.8 us)

commit v4 on v3

--- a/solution.py
+++ b/solution.py
@@ -566,10 +566,14 @@
     sent_ref, kept_ref = refs[-2:]
 
     def write(out_ref):
-        out_ref[...] = jnp.zeros_like(out_ref)
         first = 0
         for i, rows in enumerate(shape):
             total = dot_tn(refs[2 * i][...], refs[2 * i + 1][...]).astype(bf16)
+            blank = out_ref.shape[2] - total.shape[1]
+            if blank:
+                out_ref[:, first : first + rows, total.shape[1] :] = jnp.zeros(
+                    (out_ref.shape[0], rows, blank), bf16
+                )
             for e in range(out_ref.shape[0]):
                 part = total[e * rows : (e + 1) * rows]
                 out_ref[e, first : first + rows, : total.shape[1]] = part
@@ -953,6 +957,13 @@
     return blocks
 
 
+def paired_blocks(value, across, moved, moved_across):
+    out = [(value, 0), (across, 0)]
+    for a, b in zip(moved, moved_across):
+        out += [(a, 0), (b, 0)]
+    return out
+
+
 class Shared:
     def __init__(self, pos, kept, got):
         self.pos = pos
@@ -984,11 +995,16 @@
 
     def second(self, moved):
         terms, block = self._sum(0, self.rows, lambda pos: 1 - pos[3], moved)
-        return swap_inner(sums(self.pos, self.steps, [(bf16, block, terms)])[0], "exp")
+        outputs = []
+        for k in range(self.steps):
+            part = [(v, functools.partial(lambda f, k, i, pos: f(k, pos), f, k)) for v, f, *o in terms if not o or o[0] == k]
+            outputs.append((bf16, block, part))
+        return sums(self.pos, 1, outputs)
 
     def total(self, moved, crossed):
         terms, block = self._sum(0, self.rows, lambda pos: pos[3], moved)
-        return sums(self.pos, self.steps, [(bf16, block, terms + [(crossed, straight)])])[0]
+        terms = terms + [(v, lambda i, pos: 0, k) for k, v in enumerate(crossed)]
+        return sums(self.pos, self.steps, [(bf16, block, terms)])[0]
 
 
 def z_take(total, d):
@@ -1149,9 +1165,10 @@
         attended, lse = attend(pos, span_order, queries, kv_blocks)
         middle, rows = middle_forward(x, attended, w_out, ffn_gain)
         moved = outer_blocks(normed), ring_step(cot_ring[1], 1), fetch(1), over_core(fetched[0])
-        return attended, lse, middle, rows, *moved
-
-    attended, lse, middle, rows_low, normed_moved, cot_next, got, crossing = region(attention)
+        return attended, lse, middle, rows, over_core(normed), *moved
+
+    attended, lse, middle, rows_low, across, normed_moved, cot_next, got, crossing = region(attention)
+    normed_across = across
     cot_ring.append(cot_next)
     fetched.append(got)
     crossed.append(crossing)
@@ -1163,41 +1180,39 @@
     def first():
         weights = (shared_gate[None], shared_up[None], shared_down[None])
         shared = experts(pos, rows_low, cot, weights, 0, 1, None, False, f32)
-        more = inner_blocks(normed, normed_moved), fetch(2), over_core(fetched[1]), outer_blocks(attended)
-        return ring_step(rows_low, 1), shared, own_part(0, rows_low, None), *more
-
-    rows_k, shared, (out_k, grad_k, kept), across, got, crossing, attended_moved = region(first)
+        more = spread_inner(normed_moved), fetch(2), over_core(fetched[1]), outer_blocks(attended)
+        return ring_step(rows_low, 1), shared, *more
+
+    rows_one, shared, across, got, crossing, attended_moved = region(first)
     fetched.append(got)
     crossed.append(crossing)
-    normed_blocks = all_blocks(normed, normed_moved, across)
+    normed_blocks = paired_blocks(normed, normed_across, normed_moved, across)
     shared_out, shared_grad, (shared_hidden, shared_dgu) = shared
-    out_own, grad_own = [out_k], [grad_k]
     shared_pairs = [(rows_low, shared_dgu), (shared_hidden, cot)]
 
     def second():
-        result = own_part(1, rows_k, kept)
-        more = fetch(3), over_core(fetched[2]), inner_blocks(attended, attended_moved)
-        return ring_step(rows_k, 1), result, halves(pos, shared_pairs), *more
-
-    rows_next, (out_k, grad_k, kept), (shared_sent, shared_kept), got, crossing, across = region(second)
-    attended_blocks = all_blocks(attended, attended_moved, across)
+        result = own_part(0, rows_low, None)
+        more = fetch(3), over_core(fetched[2]), [over_core(attended), *spread_inner(attended_moved)]
+        return ring_step(rows_one, 1), result, halves(pos, shared_pairs), *more
+
+    rows_two, (out_k, grad_k, kept), (shared_sent, shared_kept), got, crossing, across = region(second)
+    attended_blocks = paired_blocks(attended, across[0], attended_moved, across[1:])
     fetched.append(got)
     crossed.append(crossing)
-    rows_k = rows_next
-    out_own.append(out_k)
-    grad_own.append(grad_k)
+    out_own, grad_own = [out_k], [grad_k]
 
     def third():
-        result = own_part(2, rows_k, kept)
         more = over_core(shared_sent), fetch(4), over_core(fetched[3])
-        return ring_step(rows_k, 1), result, *more
-
-    rows_next, (out_k, grad_k, kept), shared_got, got, crossing = region(third)
+        one = own_part(1, rows_one, kept)
+        two = own_part(2, rows_two, one[2])
+        return ring_step(rows_two, 1), one[:2], two, *more
+
+    rows_k, one, two, shared_got, got, crossing = region(third)
     fetched.append(got)
     crossed.append(crossing)
-    rows_k = rows_next
-    out_own.append(out_k)
-    grad_own.append(grad_k)
+    kept = two[2]
+    out_own += [one[0], two[0]]
+    grad_own += [one[1], two[1]]
 
     def over_y(parts, k):
         return [shift_outer(v[k], "ctx", d + 1) for d, v in enumerate(parts)]
@@ -1207,16 +1222,16 @@
         weights = [arranged(fetched), arranged(crossed + [over_core(fetched[4])])]
         half = levels // 2
         sent = Shared(pos, shared_kept, shared_got).first()
-        arrived = [over_y(sent, k) for k in range(len(sent[0]) // 2)]
+        arrived = [over_y(sent, k) for k in range(len(sent[0]))]
         out_a, grad_a, new = others(pos, kept[0], kept[1], weights, 0, 2, half, None)
         out_k, grad_k, more = experts(
             pos, rows_k, moved, (expert_gate, expert_up, expert_down), 3, levels, kept, True, bf16
         )
         out_b, grad_b, new = others(pos, more[0], more[1], weights, 1, 2, half, new)
-        rest = [v[len(v) // 2 :] for v in sent]
-        return out_k, grad_k, more, [*out_a, *out_b], [*grad_a, *grad_b], new, arrived, rest
-
-    out_k, grad_k, kept, out_other, grad_other, kept_other, shared_first, shared_rest = region(fourth)
+        return out_k, grad_k, more, [*out_a, *out_b], [*grad_a, *grad_b], new, arrived
+
+    out_k, grad_k, kept, out_other, grad_other, kept_other, got = region(fourth)
+    shared_moved = [list(v) for v in zip(*got)]
     out_own.append(out_k)
     grad_own.append(grad_k)
     rows_all, cot_all, rows_t, cot_t, hid_own, dgu_own = kept
@@ -1224,47 +1239,55 @@
 
     def back_one():
         moved = ring_step(row_sum([grad_own[3], grad_other[3]]), -1)
-        arrived = [over_y(shared_rest, k) for k in range(len(shared_rest[0]))]
-        return moved, expert_halves(pos, rows_t, cot_t, dgu_other, hid_other), arrived
-
-    moved, (sent, kept_other), got = region(back_one)
-    shared_moved = [list(v) for v in zip(*(list(shared_first) + list(got)))]
+        parts = Shared(pos, shared_kept, shared_got).second(shared_moved)
+        crossed = [swap_inner(v, "exp") for v in parts[: len(parts) // 2]]
+        made = expert_halves(pos, rows_t, cot_t, dgu_other, hid_other)
+        return moved, made, crossed, parts[len(parts) // 2 :]
+
+    moved, (sent, kept_other), shared_crossed, shared_rest = region(back_one)
 
     def back_two():
         total = row_sum([grad_own[2], grad_other[2], moved])
         got = swap_inner(sent, "ctx")
-        crossed = Shared(pos, shared_kept, shared_got).second(shared_moved)
+        crossed = [swap_inner(v, "exp") for v in shared_rest]
         made = expert_halves(pos, rows_t, cot_t, dgu_own, hid_own)
         return ring_step(total, -1), got, made, expert_pieces(pos, kept_other, got, [0])[0], crossed
 
-    moved_two, got_other, (sent_own, kept_own), piece, shared_crossed = region(back_two)
+    moved_two, got_other, (sent_own, kept_own), piece, got = region(back_two)
+    shared_crossed = shared_crossed + got
 
     def back_three():
         total = row_sum([grad_own[1], grad_other[1], moved_two])
         made = expert_pieces(pos, kept_other, got_other, [1, 2, 3])
         shared_sum = Shared(pos, shared_kept, shared_got).total(shared_moved, shared_crossed)
         out_total = row_sum([out_own[3], out_other[3]])
-        moved = ring_step(total, -1), swap_inner(sent_own, "ctx"), swap_inner(piece, "exp")
-        return *moved, made, shared_sum, out_total
-
-    moved, got_own, piece, made, shared_sum, out_total = region(back_three)
+        middle_grads = middle_back(
+            [shared_grad, grad_own[0], grad_other[0], ring_step(total, -1)],
+            middle,
+            cot,
+            ffn_gain,
+            w_out,
+        )
+        moved = middle_grads, swap_inner(sent_own, "ctx"), swap_inner(piece, "exp")
+        shared_z = [z_take(shared_sum, d) for d in range(levels)]
+        return *moved, made, shared_z, out_total
+
+    middle_grads, got_own, piece, made, shared_z, out_total = region(back_three)
+    mgrad, mgrad_low, ffn_gain_grad, att_grad = middle_grads
     pieces = [piece, *made]
 
     def attention_back():
-        mgrad, mgrad_low, ffn_gain_grad, att_grad = middle_back(
-            [shared_grad, grad_own[0], grad_other[0], moved], middle, cot, ffn_gain, w_out
-        )
-        back = attend_back(pos, span_order, queries, att_grad, lse, kv_blocks)
-        got = ring_step(out_total, -1), swap_inner(pieces[1], "exp")
-        return mgrad, mgrad_low, outer_blocks(mgrad_low), ffn_gain_grad, back, *got
-
-    mgrad, mgrad_low, mgrad_moved, ffn_gain_grad, (dq, same, across), out_moved, piece = region(
-        attention_back
-    )
+        dq, same, across = attend_back(pos, span_order, queries, att_grad, lse, kv_blocks)
+        got = ring_step(out_total, -1), swap_inner(pieces[1], "exp"), shift_outer(shared_z[1], "exp", 1)
+        mgrad_parts = mgrad_low, over_core(mgrad_low), outer_blocks(mgrad_low)
+        return mgrad_parts, dq, same, across, *got
+
+    mgrad_parts, dq, same, across, out_moved, piece, got = region(attention_back)
     pieces[1] = piece
+    shared_parts = [shared_z[0], got]
 
     def dense_one():
-        got = swap_inner(across, "ctx")
+        got = over_core(across)
         made = []
         for k in reversed(range(ring)):
             part = slice(k * tokens, (k + 1) * tokens)
@@ -1272,24 +1295,23 @@
             if k:
                 made = [shift_outer(made, "ctx", -1)]
         total = row_sum([out_own[2], out_other[2], out_moved])
-        mgrad_blocks = all_blocks(mgrad_low, mgrad_moved, inner_blocks(mgrad_low, mgrad_moved))
+        mgrad_blocks = paired_blocks(*mgrad_parts, spread_inner(mgrad_parts[2]))
         total_out = rows_product(pos, attended_blocks, mgrad_blocks)
         sent = expert_send(pos, kept_own, got_own, pieces, 0)
-        moved = ring_step(total, -1), swap_inner(pieces[2], "exp")
-        return made, outer_blocks(dq), total_out, sent, *moved
-
-    dkv, dq_moved, total_out, sent, out_moved_two, piece = region(dense_one)
+        total = row_sum([out_own[1], out_other[1], ring_step(total, -1)])
+        return made, outer_blocks(dq), total_out, sent, total, swap_inner(pieces[2], "exp")
+
+    dkv, dq_moved, total_out, sent, out_total_two, piece = region(dense_one)
     pieces[2] = piece
 
     def dense_two():
-        total = row_sum([out_own[1], out_other[1], out_moved_two])
         dkv_moved = outer_blocks(dkv)
         dkv_blocks = all_blocks(dkv, dkv_moved, inner_blocks(dkv, dkv_moved))
         dq_blocks = all_blocks(dq, dq_moved, inner_blocks(dq, dq_moved))
         total_query = rows_product(pos, normed_blocks, dq_blocks)
         total_kv = rows_product(pos, normed_blocks, dkv_blocks)
         back = input_back(dq, dkv, w_query, w_key, w_value, x, attn_gain, mgrad)
-        moved = ring_step(total, -1), swap_inner(pieces[3], "exp"), expert_move(sent)
+        moved = ring_step(out_total_two, -1), swap_inner(pieces[3], "exp"), expert_move(sent)
         return total_query, total_kv, back, *moved
 
     total_query, total_kv, (input_grad, attn_gain_grad), out_moved_three, piece, got = region(dense_two)
@@ -1301,21 +1323,22 @@
         total = jnp.concatenate([total_out, total_query, total_kv], axis=2)
         got = expert_move(expert_send(pos, kept_own, got_own, pieces, 1))
         layer_out = row_sum([middle, shared_out, out_own[0], out_other[0], out_moved_three])
-        shared_z = [z_send(shared_sum, d) for d in range(1, levels)]
+        more = [shift_outer(shared_z[d], "exp", d) for d in range(2, levels)]
         gains = jnp.stack(
             [attn_gain_grad.reshape(devices, -1), ffn_gain_grad.reshape(devices, -1)], axis=1
         )
         gains = lax.all_to_all(gains, BOTH, split_axis=0, concat_axis=0, tiled=True)
-        return mine_x(total), over_x(total), got, layer_out, shared_z, gains
-
-    total, total_x, got, layer_out, shared_z, gains = region(dense_three)
+        return mine_x(total), over_x(total), got, layer_out, more, gains
+
+    total, total_x, got, layer_out, more, gains = region(dense_three)
+    shared_parts += more
     arrived.append(got)
 
     def dense_four():
         grads = expert_out(expert_total(pos, kept_own, got_own, pieces, arrived), inner)
         shape = lambda v: (v.shape[0] // (n_ctx * n_exp), v.shape[1])
         shared = shared_grads(
-            [z_take(shared_sum, 0)] + shared_z, shape(shared_gate), shape(shared_down)
+            shared_parts, shape(shared_gate), shape(shared_down)
         )
         dense = dense_out(over_z(total, total_x), x.shape[1])
         return jnp.sum(gains, axis=0), shared, dense, grads

time: 511 us -> 485 us (0.949)
  waiting for transfers between devices: 121 us -> 103 us
  other arithmetic: 44.7 us -> 36.9 us
    ppermute x27 -> x31, waiting for transfers between devices: 24.8 us -> 6.95 us  [swap_inner(): return lax.ppermute(value, axis, [(i, i ^ 1) for i in range(size)])]
    ppermute x12, waiting for transfers between devices: 25.4 us -> 15.3 us  [ring_step(): return lax.ppermute(value, BOTH, perm)]
    ppermute x17, waiting for transfers between devices: 53.6 us -> 62.2 us  [shift_outer(): return lax.ppermute(value, axis, perm)]
    concatenate x5 -> x2, other arithmetic: 11.4 us -> 3.5 us  [inner_blocks(): return swap_inner(jnp.concatenate([value] + moved, axis=0), 'ctx')]
    ppermute x27 -> x31, starting transfers between devices: 15.6 us -> 20.4 us  [swap_inner(): return lax.ppermute(value, axis, [(i, i ^ 1) for i in range(size)])]
  transfers between devices with their start and end apart: 57 -> 61, of which waited for: 24 -> 19; matrix products, arithmetic and copies ran while one was open for 10% -> 9% of each run, Pallas kernels for 50% -> 52%
where the time goes in v4:
time: 485 us; the launch traced here: 477 us
  Pallas kernels  255 us (53%)
  waiting for transfers between devices  103 us (21%)
  starting transfers between devices  54.1 us (11%)
  other arithmetic  36.9 us (8%)
  local copies, waits for them, and re-layouts  20 us (4%)
  matrix products  4.87 us (1%)
    pallas_call x5, Pallas kernels, experts(): pl.pallas_call(functools.partial(experts_kernel, per, gated, extra, gated...  63.6 us
    ppermute x17, waiting for transfers between devices, shift_outer(): return lax.ppermute(value, axis, perm)  62.2 us
    pallas_call x2, Pallas kernels, others(): pl.pallas_call(functools.partial(others_kernel, sets, per, len(bands), ex...  38.9 us
    pallas_call x8, Pallas kernels, sums(): pl.pallas_call(functools.partial(sums_kernel, [len(terms) for _, _, terms...  35.8 us
    pallas_call x2, Pallas kernels, expert_halves(): pl.pallas_call(functools.partial(expert_halves_kernel, n_ctx, tiles), gri...  31.2 us
    ppermute x31, starting transfers between devices, swap_inner(): return lax.ppermute(value, axis, [(i, i ^ 1) for i in range(size)])  20.4 us
    ppermute x17, starting transfers between devices, shift_outer(): return lax.ppermute(value, axis, perm)  19.1 us
    convert_element_type x8, other arithmetic, row_sum(): return total.astype(kind)  18.4 us
  transfers between devices with their start and end apart: 61, of which 19 were waited for; matrix products, arithmetic and copies ran while one was open for 9% of the time, Pallas kernels for 52%

profile of v4, /device:TPU:0, one launch (start us, length us, event | category | flops | bytes accessed | tf_op | source)
XLA Modules:
  0.0 476.7 jit_solution(3675238123618025507)
XLA Ops:
  5.9 32.3 %conditional.14 = (bf16[256,1536]{1,0:T(8,128)(2,1)}, bf16[256,1024]{1,0:T(8,128)(2,1)}, bf16[256,1024]{1,0:T(8,128)(2,1)}, bf16[256,1024]{1,0:T(8,128)(2,1)}, b...) conditional(s32[]{:T(128)} %convert_element_type.154, ...), branch_computations={%region_3.4_spmd, %region_4.5_spmd} | conditional | flops 1415970816 | bytes 48771484 | solution.py:1117
  6.6 5.3 %branch_1_fun.30 = (bf16[256,1536]{1,0:T(8,128)(2,1)}, bf16[256,1024]{1,0:T(8,128)(2,1)}) custom-call(bf16[256,1536]{1,0:T(8,128)(2,1)} %get-tuple-element.440.x_ref, f32[1,1536]{1,0:T(1,128)} %reshape.110.gain_ref, bf16[1536,512]{1,0:T(8,128)(2,1)} %get-tuple-element.442.wk_ref, bf16[1536,512]{1,0:T(8,128)(2,1)} %get-tuple-element.443.wv_ref), custom_call_target="tpu_custom_call" | custom-call | flops 201326592 | bytes 1310720 | tf_op jit(solution)/shard_map/cond/branch_1_fun/pallas_call | solution.py:66
  23.4 4.3 collective-permute-done.55
  28.8 4.9 %convolution_convert_fusion = bf16[256,1536]{1,0:T(8,128)(2,1)} fusion(bf16[256,1536]{1,0:T(8,128)(2,1)} %get-tuple-element.1105, bf16[1536,1536]{1,0:T(8,128)(2,1)} %get-tuple-element.446), kind=kOutput, calls=%fused_computation | convolution fusion | flops 1208352768 | bytes 6291456 | tf_op jit(solution)/shard_map/cond/branch_1_fun/dot_general | solution.py:26
  38.3 22.9 %conditional.15 = (bf16[256,1536]{1,0:T(8,128)(2,1)}, f32[4,1,768]{2,1,0:T(1,128)S(1)}, f32[256,1536]{1,0:T(8,128)}, bf16[256,1536]{1,0:T(8,128)(2,1)S(1)}, bf16...) conditional(s32[]{:T(128)} %convert_element_type.154, ...), branch_computations={%region_5.6_spmd, %region_6.7_spmd} | conditional | flops 1107296256 | bytes 22294828 | solution.py:1117
  42.5 9.5 %branch_1_fun.31 = (bf16[256,1536]{1,0:T(8,128)(2,1)}, f32[4,1,768]{2,1,0:T(1,128)S(1)}) custom-call(s32[4]{0:T(128)S(1)} %get-tuple-element.452.pos, s32[8]{0:T(128)S(1)} %get-tuple-element.453.spans, bf16[256,1536]{1,0:T(8,128)(2,1)} %get-tuple-element.454.q_ref, bf16[256,1024]{1,0:T(8,128)(2,1)} %get-tuple-element.455.refs_0_, ...), custom_call_target="tpu_custom_call" | custom-call | flops 805306368 | bytes 1048576 | tf_op jit(solution)/shard_map/cond/branch_1_fun/pallas_call | solution.py:128
  52.0 5.6 %branch_1_fun.32 = (f32[256,1536]{1,0:T(8,128)}, bf16[256,1536]{1,0:T(8,128)(2,1)S(1)}) custom-call(bf16[256,1536]{1,0:T(8,128)(2,1)S(1)} %copy-done.3, bf16[256,1536]{1,0:T(8,128)(2,1)} %get-tuple-element.1126.att_ref, bf16[1536,1536]{1,0:T(8,128)(2,1)} %get-tuple-element.462.w_ref, f32[1,1536]{1,0:T(1,128)} %reshape.111.gain_ref), custom_call_target="tpu_custom_call" | custom-call | flops 301989888 | bytes 2097152 | tf_op jit(solution)/shard_map/cond/branch_1_fun/pallas_call | solution.py:228
  61.2 24.6 %conditional.16 = (bf16[256,1536]{1,0:T(8,128)(2,1)}, f32[256,1536]{1,0:T(8,128)}, f32[256,1536]{1,0:T(8,128)}, bf16[256,1024]{1,0:T(8,128)(2,1)S(1)}, bf16[256,...) conditional(s32[]{:T(128)} %convert_element_type.154, ...), branch_computations={%region_7.8_spmd, %region_8.9_spmd} | conditional | flops 2617245696 | bytes 19923216 | solution.py:1117
  63.7 11.3 %branch_1_fun.33 = (f32[256,1536]{1,0:T(8,128)}, f32[256,1536]{1,0:T(8,128)}, bf16[256,1024]{1,0:T(8,128)(2,1)S(1)}, bf16[256,2048]{1,0:T(8,128)(2,1)S(1)}) custom-call(s32[4]{0:T(128)S(1)} %get-tuple-element.471.pos, bf16[256,1536]{1,0:T(8,128)(2,1)S(1)} %get-tuple-element.470.x_ref, bf16[256,1536]{1,0:T(8,128)(2,1)S(1)} %get-tuple-element.472.c_ref, ...), custom_call_target="tpu_custom_call" | custom-call | flops 2617245696 | bytes 3145728 | tf_op jit(solution)/shard_map/cond/branch_1_fun/pallas_call | solution.py:451
  75.0 7.1 %collective-permute-done.9 = bf16[256,1536]{1,0:T(8,128)(2,1)} collective-permute-done((bf16[256,1536]{1,0:T(8,128)(2,1)}, bf16[256,1536]{1,0:T(8,128)(2,1)}, u32[]{:S(2)}, u32[]{:S(2)}) %collective-permute-start.9) | collective-permute-done | bytes 786464 | tf_op jit(solution)/shard_map/cond/branch_1_fun/ppermute | solution.py:903
  85.8 24.6 %conditional.17 = (bf16[256,1536]{1,0:T(8,128)(2,1)}, bf16[256,1536]{1,0:T(8,128)(2,1)}, bf16[256,1536]{1,0:T(8,128)(2,1)}, bf16[1024,1536]{1,0:T(8,128)(2,1)}, ...) conditional(s32[]{:T(128)} %convert_element_type.154, ...), branch_computations={%region_9.10_spmd, %region_10.11_spmd} | conditional | flops 3825205248 | bytes 35651728 | solution.py:1117
  90.2 7.1 %branch_1_fun.35 = (bf16[16,80,2048]{2,1,0:T(8,128)(2,1)}, bf16[16,80,2048]{2,1,0:T(8,128)(2,1)}) custom-call(s32[4]{0:T(128)S(1)} %get-tuple-element.485.pos, bf16[256,1536]{1,0:T(8,128)(2,1)S(1)} %get-tuple-element.486.x_ref.refs_0_, bf16[256,2048]{1,0:T(8,128)(2,1)S(1)} %get-tuple-element.499.refs_1_, bf16[256,1024]{1,0:T(8,128)(2,1)S(1)} %get-tuple-element.500.refs_2_, ...), custom_call_target="tpu_custom_call" | custom-call | flops 1207959552 | bytes 2097152 | tf_op jit(solution)/shard_map/cond/branch_1_fun/pallas_call | solution.py:615
  97.2 13.1 %branch_1_fun.34 = (bf16[256,1536]{1,0:T(8,128)(2,1)}, bf16[256,1536]{1,0:T(8,128)(2,1)}, bf16[1024,1536]{1,0:T(8,128)(2,1)}, bf16[1024,1664]{1,0:T(8,128)(2,1)}...) custom-call(s32[4]{0:T(128)S(1)} %get-tuple-element.485.pos, ...), custom_call_target="tpu_custom_call" | custom-call | flops 2617245696 | bytes 3145728 | tf_op jit(solution)/shard_map/cond/branch_1_fun/pallas_call | solution.py:451
  110.4 28.5 %conditional.18 = (bf16[256,1536]{1,0:T(8,128)(2,1)}, bf16[256,1536]{1,0:T(8,128)(2,1)}, bf16[256,1536]{1,0:T(8,128)(2,1)}, bf16[256,1536]{1,0:T(8,128)(2,1)}, b...) conditional(s32[]{:T(128)} %convert_element_type.154, ...), branch_computations={%region_11.12_spmd, %region_12.13_spmd} | conditional | flops 5234491392 | bytes 38797584 | solution.py:1117
  112.5 13.1 %branch_1_fun.36 = (bf16[256,1536]{1,0:T(8,128)(2,1)}, bf16[256,1536]{1,0:T(8,128)(2,1)}, bf16[1024,1536]{1,0:T(8,128)(2,1)}, bf16[1024,1664]{1,0:T(8,128)(2,1)}...) custom-call(s32[4]{0:T(128)S(1)} %get-tuple-element.509.pos, ...), custom_call_target="tpu_custom_call", output_to_operand_aliasing={{2}: (6, {}), {3}: (7, {}), {4}: (8, {}), {5}: (9, {}), {6}... | custom-call | flops 2617245696 | bytes 3145728 | tf_op jit(solution)/shard_map/cond/branch_1_fun/pallas_call | solution.py:451
  125.6 13.1 %branch_1_fun.37 = (bf16[256,1536]{1,0:T(8,128)(2,1)}, bf16[256,1536]{1,0:T(8,128)(2,1)}, bf16[1024,1536]{1,0:T(8,128)(2,1)}, bf16[1024,1664]{1,0:T(8,128)(2,1)}...) custom-call(s32[4]{0:T(128)S(1)} %get-tuple-element.509.pos, ...), custom_call_target="tpu_custom_call", output_to_operand_aliasing={{2}: (6, {}), {3}: (7, {}), {4}: (8, {}), {5}: (9, {}), {6}... | custom-call | flops 2617245696 | bytes 3145728 | tf_op jit(solution)/shard_map/cond/branch_1_fun/pallas_call | solution.py:451
  138.9 66.6 %conditional.19 = (bf16[256,1536]{1,0:T(8,128)(2,1)}, bf16[256,1536]{1,0:T(8,128)(2,1)}, bf16[1536,1024]{1,0:T(8,128)(2,1)}, bf16[1536,1024]{1,0:T(8,128)(2,1)S(...) conditional(s32[]{:T(128)} %convert_element_type.154, ...), branch_computations={%region_13.14_spmd, %region_14.15_spmd} | conditional | flops 13086228480 | bytes 29622576 | solution.py:1117
  141.2 4.8 %branch_1_fun.41 = (bf16[2,160,2048]{2,1,0:T(8,128)(2,1)}, bf16[2,160,2048]{2,1,0:T(8,128)(2,1)}) custom-call(s32[4]{0:T(128)S(1)} %get-tuple-element.541.pos, bf16[8,160,2048]{2,1,0:T(8,128)(2,1)} %bitcast.11.refs_0_.refs_2_, bf16[8,160,2048]{2,1,0:T(8,128)(2,1)} %bitcast.12.refs_1_.refs_3_, bf16[8,160,2048]{2,1,0:T(8,128)(2,1)} %bitcast.11.refs_0_.refs_2_, ...), custom_call_target="tpu_custom_call" | custom-call | bytes 2097152 | tf_op jit(solution)/shard_map/cond/branch_1_fun/pallas_call | solution.py:750
  148.1 19.6 %branch_1_fun.39 = (bf16[256,1536]{1,0:T(8,128)(2,1)}, bf16[256,1536]{1,0:T(8,128)(2,1)}, bf16[256,1536]{1,0:T(8,128)(2,1)}, bf16[256,1536]{1,0:T(8,128)(2,1)}, ...) custom-call(s32[4]{0:T(128)S(1)} %get-tuple-element.541.pos, bf16[1024,1536]{1,0:T(8,128)(2,1)} %get-tuple-element.547.refs_3_.x_ref, ...), custom_call_target="tpu_custom_call" | custom-call | flops 5234491392 | bytes 3145728 | tf_op jit(solution)/shard_map/cond/branch_1_fun/pallas_call | solution.py:543
  167.7 13.0 %branch_1_fun.38 = (bf16[256,1536]{1,0:T(8,128)(2,1)}, bf16[256,1536]{1,0:T(8,128)(2,1)}, bf16[1024,1536]{1,0:T(8,128)(2,1)}, bf16[1024,1664]{1,0:T(8,128)(2,1)}...) custom-call(s32[4]{0:T(128)S(1)} %get-tuple-element.541.pos, ...), custom_call_target="tpu_custom_call", output_to_operand_aliasing={{2}: (6, {}), {3}: (7, {}), {4}: (8, {}), {5}: (9, {}), {6}... | custom-call | flops 2617245696 | bytes 3145728 | tf_op jit(solution)/shard_map/cond/branch_1_fun/pallas_call | solution.py:451
  180.7 19.3 %branch_1_fun.40 = (bf16[256,1536]{1,0:T(8,128)(2,1)}, bf16[256,1536]{1,0:T(8,128)(2,1)}, bf16[256,1536]{1,0:T(8,128)(2,1)}, bf16[256,1536]{1,0:T(8,128)(2,1)}, ...) custom-call(s32[4]{0:T(128)S(1)} %get-tuple-element.541.pos, ...), custom_call_target="tpu_custom_call", output_to_operand_aliasing={{4}: (13, {}), {5}: (14, {})} | custom-call | flops 5234491392 | bytes 3145728 | tf_op jit(solution)/shard_map/cond/branch_1_fun/pallas_call | solution.py:543
  200.0 5.3 %collective-permute-done.22 = bf16[2,160,2048]{2,1,0:T(8,128)(2,1)} collective-permute-done((bf16[2,160,2048]{2,1,0:T(8,128)(2,1)}, bf16[2,160,2048]{2,1,0:T(8,128)(2,1)}, u32[]{:S(2)}, u32[]{:S(2)}) %collective-permute-start.22) | collective-permute-done | bytes 1310752 | tf_op jit(solution)/shard_map/cond/branch_1_fun/ppermute | solution.py:903
  205.5 25.3 %conditional.20 = (bf16[256,1536]{1,0:T(8,128)(2,1)}, bf16[6,128,3072]{2,1,0:T(8,128)(2,1)}, bf16[6,128,3072]{2,1,0:T(8,128)(2,1)}, bf16[2,80,2048]{2,1,0:T(8,128)(2,1)}, bf16[2,80,2048]{2,1,0:T(8,128)(2,1)}) conditional(s32[]{:T(128)} %convert_element_type.154, () %tuple.143, (bf16[256,1536]{1,0:T(8,128)(2,1)}, bf16[256,1536]{1,0:T(8,128)(2,1)}, ...), branch_computations={%region_15.16_spmd, %region_16.17_spmd} | conditional | flops 4833411072 | bytes 14418040 | solution.py:1117
  215.2 15.7 %branch_1_fun.42 = (bf16[6,128,3072]{2,1,0:T(8,128)(2,1)}, bf16[6,128,3072]{2,1,0:T(8,128)(2,1)}) custom-call(s32[4]{0:T(128)S(1)} %get-tuple-element.588.pos, bf16[1536,1024]{1,0:T(8,128)(2,1)} %get-tuple-element.589.refs_0_.refs_1_.refs_2_.refs_3_, bf16[1536,1024]{1,0:T(8,128)(2,1)} %get-tuple-element.589.refs_0_.refs_1_.refs_2_.refs_3_, ...), custom_call_target="tpu_custom_call" | custom-call | flops 4831838208 | bytes 4194304 | tf_op jit(solution)/shard_map/cond/branch_1_fun/pallas_call | solution.py:709
  230.8 24.3 %conditional.21 = (bf16[256,1536]{1,0:T(8,128)(2,1)}, bf16[6,128,3072]{2,1,0:T(8,128)(2,1)}, bf16[6,128,3072]{2,1,0:T(8,128)(2,1)}, bf16[6,128,3072]{2,1,0:T(8,1...) conditional(s32[]{:T(128)} %convert_element_type.154, () %tuple.142, ...), branch_computations={%region_17.18_spmd, %region_18.19_spmd} | conditional | flops 4834197504 | bytes 34078888 | solution.py:1117
  236.4 15.6 %branch_1_fun.44 = (bf16[6,128,3072]{2,1,0:T(8,128)(2,1)}, bf16[6,128,3072]{2,1,0:T(8,128)(2,1)}) custom-call(s32[4]{0:T(128)S(1)} %get-tuple-element.605.pos, bf16[1536,1024]{1,0:T(8,128)(2,1)} %get-tuple-element.606.refs_0_.refs_1_.refs_2_.refs_3_, bf16[1536,1024]{1,0:T(8,128)(2,1)} %get-tuple-element.606.refs_0_.refs_1_.refs_2_.refs_3_, ...), custom_call_target="tpu_custom_call" | custom-call | flops 4831838208 | bytes 4194304 | tf_op jit(solution)/shard_map/cond/branch_1_fun/pallas_call | solution.py:709
  255.1 33.9 %conditional.22 = (f32[256,1536]{1,0:T(8,128)}, bf16[256,1536]{1,0:T(8,128)(2,1)S(1)}, f32[1,1536]{1,0:T(1,128)S(1)}, bf16[256,1536]{1,0:T(8,128)(2,1)}, bf16[6,...) conditional(s32[]{:T(128)} %convert_element_type.154, ...), branch_computations={%region_19.20_spmd, %region_20.21_spmd} | conditional | flops 305922048 | bytes 55850036 | solution.py:1117
  262.1 5.1 %branch_1_fun.47 = (bf16[6,128,768]{2,1,0:T(8,128)(2,1)}, bf16[6,128,768]{2,1,0:T(8,128)(2,1)}, bf16[6,128,768]{2,1,0:T(8,128)(2,1)}) custom-call(s32[4]{0:T(128)S(1)} %get-tuple-element.630.pos, bf16[6,128,3072]{2,1,0:T(8,128)(2,1)} %get-tuple-element.631.refs_0_.refs_2_.refs_4_, bf16[6,128,3072]{2,1,0:T(8,128)(2,1)} %get-tuple-element.632.refs_1_.refs_3_.refs_5_, ...), custom_call_target="tpu_custom_call" | custom-call | bytes 2097152 | tf_op jit(solution)/shard_map/cond/branch_1_fun/pallas_call | solution.py:750
  267.2 4.9 %branch_1_fun.48 = bf16[4,80,2048]{2,1,0:T(8,128)(2,1)} custom-call(s32[4]{0:T(128)S(1)} %get-tuple-element.630.pos, bf16[8,160,2048]{2,1,0:T(8,128)(2,1)} %bitcast.15.refs_0_, bf16[8,160,2048]{2,1,0:T(8,128)(2,1)} %bitcast.16.refs_1_, bf16[2,160,2048]{2,1,0:T(8,128)(2,1)} %get-tuple-element.638.refs_2_, bf16[2,160,2048]{2,1,0:T(8,128)(2,1)} %get-tuple-element.639.refs_3_, ...), custom_call_target="tpu_custom_call" | custom-call | bytes 2097152 | tf_op jit(solution)/shard_map/cond/branch_1_fun/pallas_call | solution.py:750
  281.3 7.5 %branch_1_fun.46 = (f32[256,1536]{1,0:T(8,128)}, bf16[256,1536]{1,0:T(8,128)(2,1)S(1)}, f32[1,1536]{1,0:T(1,128)S(1)}, bf16[256,1536]{1,0:T(8,128)(2,1)}) custom-call(f32[256,1536]{1,0:T(8,128)} %get-tuple-element.614.refs_0_, bf16[256,1536]{1,0:T(8,128)(2,1)} %get-tuple-element.615.refs_1_, bf16[256,1536]{1,0:T(8,128)(2,1)} %get-tuple-element.616.refs_2_, ...), custom_call_target="tpu_custom_call" | custom-call | flops 301989888 | bytes 4194304 | tf_op jit(solution)/shard_map/cond/branch_1_fun/pallas_call | solution.py:273
  289.8 28.4 %conditional.23 = (bf16[256,1536]{1,0:T(8,128)(2,1)S(1)}, bf16[256,1536]{1,0:T(8,128)(2,1)}, bf16[256,1536]{1,0:T(8,128)(2,1)}, bf16[256,1536]{1,0:T(8,128)(2,1)...) conditional(s32[]{:T(128)} %convert_element_type.154, ...), branch_computations={%region_21.22_spmd, %region_22.23_spmd} | conditional | flops 2013265920 | bytes 19136784 | solution.py:1117
  293.0 14.5 %branch_1_fun.49 = (bf16[256,1536]{1,0:T(8,128)(2,1)S(1)}, bf16[512,1024]{1,0:T(8,128)(2,1)}, bf16[512,1024]{1,0:T(8,128)(2,1)}) custom-call(s32[4]{0:T(128)S(1)} %get-tuple-element.645.pos, s32[8]{0:T(128)S(1)} %get-tuple-element.646.spans, bf16[256,1536]{1,0:T(8,128)(2,1)} %get-tuple-element.647.q_ref, bf16[256,1536]{1,0:T(8,128)(2,1)} %get-tuple-element.648.grad_ref, ...), custom_call_target="tpu_custom_call" | custom-call | flops 2013265920 | bytes 2097152 | tf_op jit(solution)/shard_map/cond/branch_1_fun/pallas_call | solution.py:190
  307.5 9.0 %collective-permute-done.27 = bf16[80,2048]{1,0:T(8,128)(2,1)} collective-permute-done((bf16[80,2048]{1,0:T(8,128)(2,1)}, bf16[80,2048]{1,0:T(8,128)(2,1)}, u32[]{:S(2)}, u32[]{:S(2)}) %collective-permute-start.27) | collective-permute-done | bytes 327712 | tf_op jit(solution)/shard_map/cond/branch_1_fun/ppermute | solution.py:903
  318.2 36.6 %conditional.24 = (bf16[256,1024]{1,0:T(8,128)(2,1)S(1)}, bf16[256,1536]{1,0:T(8,128)(2,1)}, bf16[8,48,1536]{2,1,0:T(8,128)(2,1)S(1)}, bf16[6,128,768]{2,1,0:T(8...) conditional(s32[]{:T(128)} %convert_element_type.154, () %tuple.127, ...), branch_computations={%region_23.24_spmd, %region_24.25_spmd} | conditional | flops 611319808 | bytes 48234896 | solution.py:1117
  328.2 4.6 branch_1_fun.50
  335.8 6.5 %collective-permute-done.40 = bf16[256,1536]{1,0:T(8,128)(2,1)S(1)} collective-permute-done((bf16[256,1536]{1,0:T(8,128)(2,1)}, bf16[256,1536]{1,0:T(8,128)(2,1)S(1)}, u32[]{:S(2)}, u32[]{:S(2)}) %collective-permute-start.40) | collective-permute-done | bytes 786464 | tf_op jit(solution)/shard_map/cond/branch_1_fun/ppermute | solution.py:915
  344.8 8.7 %collective-permute-done.37 = bf16[256,1024]{1,0:T(8,128)(2,1)S(1)} collective-permute-done((bf16[256,1024]{1,0:T(8,128)(2,1)S(1)}, bf16[256,1024]{1,0:T(8,128)(2,1)S(1)}, u32[]{:S(2)}, u32[]{:S(2)}) %collective-permute-start.37) | collective-permute-done | bytes 524320 | tf_op jit(solution)/shard_map/cond/branch_1_fun/ppermute | solution.py:903
  355.8 38.1 %conditional.25 = (bf16[8,48,1536]{2,1,0:T(8,128)(2,1)}, bf16[8,48,1024]{2,1,0:T(8,128)(2,1)}, f32[1,1536]{1,0:T(1,128)S(1)}, bf16[256,1536]{1,0:T(8,128)(2,1)},...) conditional(s32[]{:T(128)} %convert_element_type.154, () %tuple.149, ...), branch_computations={%region_25.26_spmd, %region_26.27_spmd} | conditional | flops 1515192320 | bytes 38285636 | solution.py:1117
  360.9 9.8 %collective-permute-done.43.refs_6_ = bf16[256,1024]{1,0:T(8,128)(2,1)S(1)} collective-permute-done((bf16[256,1024]{1,0:T(8,128)(2,1)S(1)}, bf16[256,1024]{1,0:T(8,128)(2,1)S(1)}, u32[]{:S(2)}, u32[]{:S(2)}) %collective-permute-start.43) | collective-permute-done | bytes 524320 | tf_op jit(solution)/shard_map/cond/branch_1_fun/ppermute | solution.py:903
  372.4 9.3 %branch_1_fun.54 = (f32[256,1536]{1,0:T(8,128)}, f32[1,1536]{1,0:T(1,128)S(1)}) custom-call(bf16[256,1536]{1,0:T(8,128)(2,1)S(1)} %get-tuple-element.686.refs_4_.dq_ref, bf16[256,1024]{1,0:T(8,128)(2,1)S(1)} %get-tuple-element.688.refs_4_.dkv_ref, bf16[1536,1536]{1,0:T(8,128)(2,1)} %get-tuple-element.689.wq_ref, ...), custom_call_target="tpu_custom_call" | custom-call | flops 503316480 | bytes 3670016 | tf_op jit(solution)/shard_map/cond/branch_1_fun/pallas_call | solution.py:324
  381.7 4.0 branch_1_fun.53
  385.7 5.2 %branch_1_fun.52 = bf16[384,1536]{1,0:T(8,128)(2,1)} custom-call(s32[4]{0:T(128)S(1)} %get-tuple-element.681.pos, bf16[256,1536]{1,0:T(8,128)(2,1)} %get-tuple-element.682.refs_0_, bf16[256,1536]{1,0:T(8,128)(2,1)} %get-tuple-element.683.refs_1_, bf16[256,1536]{1,0:T(8,128)(2,1)} %get-tuple-element.684.refs_2_, ...), custom_call_target="tpu_custom_call" | custom-call | flops 603979776 | bytes 1048576 | tf_op jit(solution)/shard_map/cond/branch_1_fun/pallas_call | solution.py:659
  394.0 38.8 %conditional.26 = (bf16[4,48,4096]{2,1,0:T(8,128)(2,1)S(1)}, bf16[4,48,4096]{2,1,0:T(8,128)(2,1)}, bf16[6,128,768]{2,1,0:T(8,128)(2,1)}, bf16[80,2048]{1,0:T(8,1...) conditional(s32[]{:T(128)} %convert_element_type.154, ...), branch_computations={%region_27.28_spmd, %region_28.29_spmd} | conditional | flops 12586004 | bytes 34755032 | solution.py:1117
  414.1 18.4 %all-to-all-done = f32[32,2,48]{2,1,0:T(2,128)} async-done(((f32[32,2,48]{2,1,0:T(2,128)}), f32[32,2,48]{2,1,0:T(2,128)}, u32[]{:S(2)}, u32[]{:S(2)}) %all-to-all-start) | async-done | bytes 12320 | tf_op jit(solution)/shard_map/cond/branch_1_fun/all_to_all | solution.py:1330
  432.7 43.2 %conditional.27 = (f32[2,48]{1,0:T(2,128)}, f32[48,1024]{1,0:T(8,128)}, f32[48,1024]{1,0:T(8,128)}, f32[32,1536]{1,0:T(8,128)}, f32[48,1536]{1,0:T(8,128)}, /*in...) conditional(s32[]{:T(128)} %convert_element_type.154, ...), branch_computations={%region_29.30_spmd, %region_30.32_spmd} | conditional | flops 2362348 | bytes 25970686 | solution.py:1117
  443.8 6.2 %branch_1_fun.58 = (bf16[3,128,768]{2,1,0:T(8,128)(2,1)}, bf16[3,128,768]{2,1,0:T(8,128)(2,1)}, bf16[3,128,768]{2,1,0:T(8,128)(2,1)}, bf16[3,128,768]{2,1,0:T(8,128)(2,1)}) custom-call(s32[4]{0:T(128)S(1)} %get-tuple-element.731.pos, bf16[6,128,3072]{2,1,0:T(8,128)(2,1)} %get-tuple-element.732.refs_0_.refs_4_.refs_8_.refs_12_, ...), custom_call_target="tpu_custom_call" | custom-call | bytes 2097152 | tf_op jit(solution)/shard_map/cond/branch_1_fun/pallas_call | solution.py:750
  450.1 8.8 %branch_1_fun.59 = (f32[2,384,512]{2,1,0:T(8,128)}, f32[2,384,512]{2,1,0:T(8,128)}, f32[2,512,384]{2,1,0:T(8,128)}) custom-call(bf16[384,768]{1,0:T(8,128)(2,1)} %bitcast.93, bf16[384,768]{1,0:T(8,128)(2,1)} %bitcast.94, bf16[384,768]{1,0:T(8,128)(2,1)} %bitcast.95, bf16[384,768]{1,0:T(8,128)(2,1)} %bitcast.96), custom_call_target="tpu_custom_call" | custom-call | bytes 2097152 | tf_op jit(solution)/shard_map/cond/branch_1_fun/pallas_call | solution.py:810
  459.7 13.8 %collective-permute-done.53.refs_2_ = bf16[48,4096]{1,0:T(8,128)(2,1)} collective-permute-done((bf16[48,4096]{1,0:T(8,128)(2,1)}, bf16[48,4096]{1,0:T(8,128)(2,1)}, u32[]{:S(2)}, u32[]{:S(2)}) %collective-permute-start.53) | collective-permute-done | bytes 393248 | tf_op jit(solution)/shard_map/cond/branch_1_fun/ppermute | solution.py:903
  (219 shorter events, 150.1 us)
Async XLA Ops:
  11.9 21.9 %collective-permute-start.56 = (bf16[256,1024]{1,0:T(8,128)(2,1)}, bf16[256,1024]{1,0:T(8,128)(2,1)}, u32[]{:S(2)}, u32[]{:S(2)}) collective-permute-start(bf16[256,1024]{1,0:T(8,128)(2,1)} %get-tuple-element.1106), channel_id=1, source_target_pairs={{0,8},{8,0},{16,24},{24,16},{1,9},{9,1},{17,25},{25,17},{2,10},{10... | collective-permute-start | bytes 1572872 | tf_op jit(solution)/shard_map/cond/branch_1_fun/ppermute | solution.py:897
  14.8 23.4 %collective-permute-start.58 = (bf16[256,1664]{1,0:T(8,128)(2,1)}, bf16[256,1664]{1,0:T(8,128)(2,1)}, u32[]{:S(2)}, u32[]{:S(2)}) collective-permute-start(bf16[256,1664]{1,0:T(8,128)(2,1)} %get-tuple-element.447), channel_id=1, source_target_pairs={{0,2},{1,3},{2,4},{3,5},{4,6},{5,7},{6,0},{7,1},{8,14},{9,15},{10,... | collective-permute-start | bytes 2555912 | tf_op jit(solution)/shard_map/cond/branch_1_fun/ppermute | solution.py:915
  17.7 19.8 %collective-permute-start.59 = (bf16[256,1536]{1,0:T(8,128)(2,1)}, bf16[256,1536]{1,0:T(8,128)(2,1)}, u32[]{:S(2)}, u32[]{:S(2)}) collective-permute-start(bf16[256,1536]{1,0:T(8,128)(2,1)} %get-tuple-element.1071), channel_id=1, source_target_pairs={{0,1},{1,0},{2,3},{3,2},{4,5},{5,4},{6,7},{7,6},{8,9},{9,8},{10,11... | collective-permute-start | bytes 2359304 | tf_op jit(solution)/shard_map/cond/branch_1_fun/ppermute | solution.py:897
  38.3 22.9 %collective-permute-start.2 = (bf16[256,1664]{1,0:T(8,128)(2,1)}, bf16[256,1664]{1,0:T(8,128)(2,1)}, u32[]{:S(2)}, u32[]{:S(2)}) collective-permute-start(bf16[256,1664]{1,0:T(8,128)(2,1)} %get-tuple-element.467), channel_id=1, source_target_pairs={{0,2},{1,3},{2,4},{3,5},{4,6},{5,7},{6,0},{7,1},{8,14},{9,15},{10,... | collective-permute-start | bytes 2555912 | tf_op jit(solution)/shard_map/cond/branch_1_fun/ppermute | solution.py:915
  38.4 20.1 %collective-permute-start.3 = (bf16[256,1536]{1,0:T(8,128)(2,1)}, bf16[256,1536]{1,0:T(8,128)(2,1)}, u32[]{:S(2)}, u32[]{:S(2)}) collective-permute-start(bf16[256,1536]{1,0:T(8,128)(2,1)} %get-tuple-element.468), channel_id=1, source_target_pairs={{0,1},{1,0},{2,3},{3,2},{4,5},{5,4},{6,7},{7,6},{8,9},{9,8},{10,11... | collective-permute-start | bytes 2359304 | tf_op jit(solution)/shard_map/cond/branch_1_fun/ppermute | solution.py:897
  41.4 19.8 %collective-permute-start.1 = (bf16[256,1536]{1,0:T(8,128)(2,1)}, bf16[256,1536]{1,0:T(8,128)(2,1)}, u32[]{:S(2)}, u32[]{:S(2)}) collective-permute-start(bf16[256,1536]{1,0:T(8,128)(2,1)} %get-tuple-element.466), channel_id=1, source_target_pairs={{0,16},{8,24},{16,0},{24,8},{1,17},{9,25},{17,1},{25,9},{2,18},{10... | collective-permute-start | bytes 2359304 | tf_op jit(solution)/shard_map/cond/branch_1_fun/ppermute | solution.py:903
  61.2 24.6 %collective-permute-start.7 = (bf16[512,1024]{1,0:T(8,128)(2,1)}, bf16[512,1024]{1,0:T(8,128)(2,1)}, u32[]{:S(2)}, u32[]{:S(2)}) collective-permute-start(bf16[512,1024]{1,0:T(8,128)(2,1)} %get-tuple-element.481), channel_id=1, source_target_pairs={{0,1},{1,0},{2,3},{3,2},{4,5},{5,4},{6,7},{7,6},{8,9},{9,8},{10,11... | collective-permute-start | bytes 3145736 | tf_op jit(solution)/shard_map/cond/branch_1_fun/ppermute | solution.py:897
  62.3 19.8 %collective-permute-start.9 = (bf16[256,1536]{1,0:T(8,128)(2,1)}, bf16[256,1536]{1,0:T(8,128)(2,1)}, u32[]{:S(2)}, u32[]{:S(2)}) collective-permute-start(bf16[256,1536]{1,0:T(8,128)(2,1)} %get-tuple-element.483), channel_id=1, source_target_pairs={{0,16},{8,24},{16,0},{24,8},{1,17},{9,25},{17,1},{25,9},{2,18},{10... | collective-permute-start | bytes 2359304 | tf_op jit(solution)/shard_map/cond/branch_1_fun/ppermute | solution.py:903
  62.8 20.6 %collective-permute-start.5 = (bf16[256,1536]{1,0:T(8,128)(2,1)S(1)}, bf16[256,1536]{1,0:T(8,128)(2,1)}, u32[]{:S(2)}, u32[]{:S(2)}) collective-permute-start(bf16[256,1536]{1,0:T(8,128)(2,1)S(1)} %get-tuple-element.470.x_ref), channel_id=1, source_target_pairs={{0,2},{1,3},{2,4},{3,5},{4,6},{5,7},{6,0},{7,1},{8,14},{9,15},{10,... | collective-permute-start | bytes 2359304 | tf_op jit(solution)/shard_map/cond/branch_1_fun/ppermute | solution.py:915
  86.0 24.4 %collective-permute-start.11 = (bf16[512,1024]{1,0:T(8,128)(2,1)}, bf16[512,1024]{1,0:T(8,128)(2,1)}, u32[]{:S(2)}, u32[]{:S(2)}) collective-permute-start(bf16[512,1024]{1,0:T(8,128)(2,1)} %get-tuple-element.504), channel_id=1, source_target_pairs={{0,1},{1,0},{2,3},{3,2},{4,5},{5,4},{6,7},{7,6},{8,9},{9,8},{10,11... | collective-permute-start | bytes 3145736 | tf_op jit(solution)/shard_map/cond/branch_1_fun/ppermute | solution.py:897
  86.6 23.8 %collective-permute-start.12 = (bf16[512,1024]{1,0:T(8,128)(2,1)}, bf16[512,1024]{1,0:T(8,128)(2,1)}, u32[]{:S(2)}, u32[]{:S(2)}) collective-permute-start(bf16[512,1024]{1,0:T(8,128)(2,1)} %get-tuple-element.505), channel_id=1, source_target_pairs={{0,8},{8,0},{16,24},{24,16},{1,9},{9,1},{17,25},{25,17},{2,10},{10... | collective-permute-start | bytes 3145736 | tf_op jit(solution)/shard_map/cond/branch_1_fun/ppermute | solution.py:897
  86.6 23.8 %collective-permute-start.10 = (bf16[256,1536]{1,0:T(8,128)(2,1)}, bf16[256,1536]{1,0:T(8,128)(2,1)}, u32[]{:S(2)}, u32[]{:S(2)}) collective-permute-start(bf16[256,1536]{1,0:T(8,128)(2,1)} %get-tuple-element.484), channel_id=1, source_target_pairs={{0,2},{1,3},{2,4},{3,5},{4,6},{5,7},{6,0},{7,1},{8,14},{9,15},{10,... | collective-permute-start | bytes 2359304 | tf_op jit(solution)/shard_map/cond/branch_1_fun/ppermute | solution.py:915
  88.0 22.3 %collective-permute-start.13 = (bf16[256,1536]{1,0:T(8,128)(2,1)}, bf16[256,1536]{1,0:T(8,128)(2,1)}, u32[]{:S(2)}, u32[]{:S(2)}) collective-permute-start(bf16[256,1536]{1,0:T(8,128)(2,1)} %get-tuple-element.506), channel_id=1, source_target_pairs={{0,8},{8,0},{16,24},{24,16},{1,9},{9,1},{17,25},{25,17},{2,10},{10... | collective-permute-start | bytes 2359304 | tf_op jit(solution)/shard_map/cond/branch_1_fun/ppermute | solution.py:897
  90.2 20.2 %collective-permute-start.14 = (bf16[256,1536]{1,0:T(8,128)(2,1)}, bf16[256,1536]{1,0:T(8,128)(2,1)}, u32[]{:S(2)}, u32[]{:S(2)}) collective-permute-start(bf16[256,1536]{1,0:T(8,128)(2,1)} %get-tuple-element.507), channel_id=1, source_target_pairs={{0,8},{8,0},{16,24},{24,16},{1,9},{9,1},{17,25},{25,17},{2,10},{10... | collective-permute-start | bytes 2359304 | tf_op jit(solution)/shard_map/cond/branch_1_fun/ppermute | solution.py:897
  110.4 28.3 %collective-permute-start.16 = (bf16[16,80,2048]{2,1,0:T(8,128)(2,1)}, bf16[16,80,2048]{2,1,0:T(8,128)(2,1)}, u32[]{:S(2)}, u32[]{:S(2)}) collective-permute-start(bf16[16,80,2048]{2,1,0:T(8,128)(2,1)} %get-tuple-element.538), channel_id=1, source_target_pairs={{0,8},{8,0},{16,24},{24,16},{1,9},{9,1},{17,25},{25,17},{2,10},{10... | collective-permute-start | bytes 15728648 | tf_op jit(solution)/shard_map/cond/branch_1_fun/ppermute | solution.py:897
  111.0 27.7 %collective-permute-start.17 = (bf16[512,1024]{1,0:T(8,128)(2,1)}, bf16[512,1024]{1,0:T(8,128)(2,1)}, u32[]{:S(2)}, u32[]{:S(2)}) collective-permute-start(bf16[512,1024]{1,0:T(8,128)(2,1)} %get-tuple-element.539), channel_id=1, source_target_pairs={{0,1},{1,0},{2,3},{3,2},{4,5},{5,4},{6,7},{7,6},{8,9},{9,8},{10,11... | collective-permute-start | bytes 3145736 | tf_op jit(solution)/shard_map/cond/branch_1_fun/ppermute | solution.py:897
  112.5 26.2 %collective-permute-start.18 = (bf16[512,1024]{1,0:T(8,128)(2,1)}, bf16[512,1024]{1,0:T(8,128)(2,1)}, u32[]{:S(2)}, u32[]{:S(2)}) collective-permute-start(bf16[512,1024]{1,0:T(8,128)(2,1)} %get-tuple-element.540), channel_id=1, source_target_pairs={{0,8},{8,0},{16,24},{24,16},{1,9},{9,1},{17,25},{25,17},{2,10},{10... | collective-permute-start | bytes 3145736 | tf_op jit(solution)/shard_map/cond/branch_1_fun/ppermute | solution.py:897
  112.5 26.2 %collective-permute-start.15 = (bf16[256,1536]{1,0:T(8,128)(2,1)}, bf16[256,1536]{1,0:T(8,128)(2,1)}, u32[]{:S(2)}, u32[]{:S(2)}) collective-permute-start(bf16[256,1536]{1,0:T(8,128)(2,1)} %get-tuple-element.508.x_ref), channel_id=1, source_target_pairs={{0,2},{1,3},{2,4},{3,5},{4,6},{5,7},{6,0},{7,1},{8,14},{9,15},{10,... | collective-permute-start | bytes 2359304 | tf_op jit(solution)/shard_map/cond/branch_1_fun/ppermute | solution.py:915
  141.0 26.7 %collective-permute-start.19 = (bf16[256,1664]{1,0:T(8,128)(2,1)}, bf16[256,1664]{1,0:T(8,128)(2,1)}, u32[]{:S(2)}, u32[]{:S(2)}) collective-permute-start(bf16[256,1664]{1,0:T(8,128)(2,1)} %get-tuple-element.543), channel_id=1, source_target_pairs={{0,2},{1,3},{2,4},{3,5},{4,6},{5,7},{6,0},{7,1},{8,14},{9,15},{10,... | collective-permute-start | bytes 2555912 | tf_op jit(solution)/shard_map/cond/branch_1_fun/ppermute | solution.py:915
  146.1 54.0 %collective-permute-start.21 = (bf16[2,160,2048]{2,1,0:T(8,128)(2,1)}, bf16[2,160,2048]{2,1,0:T(8,128)(2,1)}, u32[]{:S(2)}, u32[]{:S(2)}) collective-permute-start(bf16[2,160,2048]{2,1,0:T(8,128)(2,1)} %get-tuple-element.584), channel_id=1, source_target_pairs={{0,16},{8,24},{16,0},{24,8},{1,17},{9,25},{17,1},{25,9},{2,18},{10... | collective-permute-start | bytes 3932168 | tf_op jit(solution)/shard_map/cond/branch_1_fun/ppermute | solution.py:903
  146.6 58.7 %collective-permute-start.22 = (bf16[2,160,2048]{2,1,0:T(8,128)(2,1)}, bf16[2,160,2048]{2,1,0:T(8,128)(2,1)}, u32[]{:S(2)}, u32[]{:S(2)}) collective-permute-start(bf16[2,160,2048]{2,1,0:T(8,128)(2,1)} %get-tuple-element.585), channel_id=1, source_target_pairs={{0,16},{8,24},{16,0},{24,8},{1,17},{9,25},{17,1},{25,9},{2,18},{10... | collective-permute-start | bytes 3932168 | tf_op jit(solution)/shard_map/cond/branch_1_fun/ppermute | solution.py:903
  208.0 22.9 %collective-permute-start.28 = (bf16[256,1536]{1,0:T(8,128)(2,1)}, bf16[256,1536]{1,0:T(8,128)(2,1)}, u32[]{:S(2)}, u32[]{:S(2)}) collective-permute-start(bf16[256,1536]{1,0:T(8,128)(2,1)} %add_convert_fusion), channel_id=1, source_target_pairs={{0,6},{1,7},{2,0},{3,1},{4,2},{5,3},{6,4},{7,5},{8,10},{9,11},{10,... | collective-permute-start | bytes 2359304 | tf_op jit(solution)/shard_map/cond/branch_1_fun/ppermute | solution.py:915
  230.9 21.1 %collective-permute-start.31 = (bf16[6,128,3072]{2,1,0:T(8,128)(2,1)}, bf16[6,128,3072]{2,1,0:T(8,128)(2,1)}, u32[]{:S(2)}, u32[]{:S(2)}) collective-permute-start(bf16[6,128,3072]{2,1,0:T(8,128)(2,1)} %get-tuple-element.604), channel_id=1, source_target_pairs={{0,8},{8,0},{16,24},{24,16},{1,9},{9,1},{17,25},{25,17},{2,10},{10... | collective-permute-start | bytes 14155784 | tf_op jit(solution)/shard_map/cond/branch_1_fun/ppermute | solution.py:897
  233.7 21.4 %collective-permute-start.30 = (bf16[256,1536]{1,0:T(8,128)(2,1)}, bf16[256,1536]{1,0:T(8,128)(2,1)}, u32[]{:S(2)}, u32[]{:S(2)}) collective-permute-start(bf16[256,1536]{1,0:T(8,128)(2,1)} %add_convert_fusion.1), channel_id=1, source_target_pairs={{0,6},{1,7},{2,0},{3,1},{4,2},{5,3},{6,4},{7,5},{8,10},{9,11},{10,... | collective-permute-start | bytes 2359304 | tf_op jit(solution)/shard_map/cond/branch_1_fun/ppermute | solution.py:915
  235.7 19.4 %collective-permute-start.32 = (bf16[2,80,2048]{2,1,0:T(8,128)(2,1)}, bf16[2,80,2048]{2,1,0:T(8,128)(2,1)}, u32[]{:S(2)}, u32[]{:S(2)}) collective-permute-start(bf16[2,80,2048]{2,1,0:T(8,128)(2,1)} %get-tuple-element.613), channel_id=1, source_target_pairs={{0,1},{1,0},{2,3},{3,2},{4,5},{5,4},{6,7},{7,6},{8,9},{9,8},{10,11... | collective-permute-start | bytes 1966088 | tf_op jit(solution)/shard_map/cond/branch_1_fun/ppermute | solution.py:897
  255.1 33.7 %collective-permute-start.34 = (bf16[6,128,3072]{2,1,0:T(8,128)(2,1)}, bf16[6,128,3072]{2,1,0:T(8,128)(2,1)}, u32[]{:S(2)}, u32[]{:S(2)}) collective-permute-start(bf16[6,128,3072]{2,1,0:T(8,128)(2,1)} %get-tuple-element.628), channel_id=1, source_target_pairs={{0,8},{8,0},{16,24},{24,16},{1,9},{9,1},{17,25},{25,17},{2,10},{10... | collective-permute-start | bytes 14155784 | tf_op jit(solution)/shard_map/cond/branch_1_fun/ppermute | solution.py:897
  255.2 33.7 %collective-permute-start.35 = (bf16[6,128,768]{2,1,0:T(8,128)(2,1)}, bf16[6,128,768]{2,1,0:T(8,128)(2,1)}, u32[]{:S(2)}, u32[]{:S(2)}) collective-permute-start(bf16[6,128,768]{2,1,0:T(8,128)(2,1)} %get-tuple-element.629), channel_id=1, source_target_pairs={{0,1},{1,0},{2,3},{3,2},{4,5},{5,4},{6,7},{7,6},{8,9},{9,8},{10,11... | collective-permute-start | bytes 3538952 | tf_op jit(solution)/shard_map/cond/branch_1_fun/ppermute | solution.py:897
  259.4 21.0 %collective-permute-start.33 = (bf16[256,1536]{1,0:T(8,128)(2,1)}, bf16[256,1536]{1,0:T(8,128)(2,1)S(1)}, u32[]{:S(2)}, u32[]{:S(2)}) collective-permute-start(bf16[256,1536]{1,0:T(8,128)(2,1)} %add_convert_fusion.3), channel_id=1, source_target_pairs={{0,6},{1,7},{2,0},{3,1},{4,2},{5,3},{6,4},{7,5},{8,10},{9,11},{10,... | collective-permute-start | bytes 2359304 | tf_op jit(solution)/shard_map/cond/branch_1_fun/ppermute | solution.py:915
  289.8 28.4 %collective-permute-start.26 = (bf16[6,128,768]{2,1,0:T(8,128)(2,1)}, bf16[6,128,768]{2,1,0:T(8,128)(2,1)}, u32[]{:S(2)}, u32[]{:S(2)}) collective-permute-start(bf16[6,128,768]{2,1,0:T(8,128)(2,1)} %get-tuple-element.658), channel_id=1, source_target_pairs={{0,1},{1,0},{2,3},{3,2},{4,5},{5,4},{6,7},{7,6},{8,9},{9,8},{10,11... | collective-permute-start | bytes 3538952 | tf_op jit(solution)/shard_map/cond/branch_1_fun/ppermute | solution.py:897
  290.4 27.8 %collective-permute-start.25 = (bf16[256,1536]{1,0:T(8,128)(2,1)}, bf16[256,1536]{1,0:T(8,128)(2,1)}, u32[]{:S(2)}, u32[]{:S(2)}) collective-permute-start(bf16[256,1536]{1,0:T(8,128)(2,1)} %get-tuple-element.657), channel_id=1, source_target_pairs={{0,6},{1,7},{2,0},{3,1},{4,2},{5,3},{6,4},{7,5},{8,10},{9,11},{10,... | collective-permute-start | bytes 2359304 | tf_op jit(solution)/shard_map/cond/branch_1_fun/ppermute | solution.py:915
  291.7 26.5 %collective-permute-start.24 = (bf16[256,1536]{1,0:T(8,128)(2,1)S(1)}, bf16[256,1536]{1,0:T(8,128)(2,1)}, u32[]{:S(2)}, u32[]{:S(2)}) collective-permute-start(bf16[256,1536]{1,0:T(8,128)(2,1)S(1)} %get-tuple-element.1306), channel_id=1, source_target_pairs={{0,16},{8,24},{16,0},{24,8},{1,17},{9,25},{17,1},{25,9},{2,18},{10... | collective-permute-start | bytes 2359304 | tf_op jit(solution)/shard_map/cond/branch_1_fun/ppermute | solution.py:903
  292.2 26.0 %collective-permute-start.23 = (bf16[256,1536]{1,0:T(8,128)(2,1)S(1)}, bf16[256,1536]{1,0:T(8,128)(2,1)}, u32[]{:S(2)}, u32[]{:S(2)}) collective-permute-start(bf16[256,1536]{1,0:T(8,128)(2,1)S(1)} %get-tuple-element.1306), channel_id=1, source_target_pairs={{0,8},{8,0},{16,24},{24,16},{1,9},{9,1},{17,25},{25,17},{2,10},{10... | collective-permute-start | bytes 2359304 | tf_op jit(solution)/shard_map/cond/branch_1_fun/ppermute | solution.py:897
  292.2 24.4 %collective-permute-start.27 = (bf16[80,2048]{1,0:T(8,128)(2,1)}, bf16[80,2048]{1,0:T(8,128)(2,1)}, u32[]{:S(2)}, u32[]{:S(2)}) collective-permute-start(bf16[80,2048]{1,0:T(8,128)(2,1)} %get-tuple-element.659), channel_id=1, source_target_pairs={{0,2},{1,3},{2,4},{3,5},{4,6},{5,7},{6,0},{7,1},{8,10},{9,11},{10,... | collective-permute-start | bytes 983048 | tf_op jit(solution)/shard_map/cond/branch_1_fun/ppermute | solution.py:903
  321.6 20.6 %collective-permute-start.40 = (bf16[256,1536]{1,0:T(8,128)(2,1)}, bf16[256,1536]{1,0:T(8,128)(2,1)S(1)}, u32[]{:S(2)}, u32[]{:S(2)}) collective-permute-start(bf16[256,1536]{1,0:T(8,128)(2,1)} %add_convert_fusion.5), channel_id=1, source_target_pairs={{0,6},{1,7},{2,0},{3,1},{4,2},{5,3},{6,4},{7,5},{8,10},{9,11},{10,... | collective-permute-start | bytes 2359304 | tf_op jit(solution)/shard_map/cond/branch_1_fun/ppermute | solution.py:915
  321.6 33.2 %collective-permute-start.41 = (bf16[6,128,768]{2,1,0:T(8,128)(2,1)}, bf16[6,128,768]{2,1,0:T(8,128)(2,1)}, u32[]{:S(2)}, u32[]{:S(2)}) collective-permute-start(bf16[6,128,768]{2,1,0:T(8,128)(2,1)} %get-tuple-element.680), channel_id=1, source_target_pairs={{0,1},{1,0},{2,3},{3,2},{4,5},{5,4},{6,7},{7,6},{8,9},{9,8},{10,11... | collective-permute-start | bytes 3538952 | tf_op jit(solution)/shard_map/cond/branch_1_fun/ppermute | solution.py:897
  323.0 31.8 %collective-permute-start.38 = (bf16[256,1536]{1,0:T(8,128)(2,1)S(1)}, bf16[256,1536]{1,0:T(8,128)(2,1)}, u32[]{:S(2)}, u32[]{:S(2)}) collective-permute-start(bf16[256,1536]{1,0:T(8,128)(2,1)S(1)} %get-tuple-element.662), channel_id=1, source_target_pairs={{0,16},{8,24},{16,0},{24,8},{1,17},{9,25},{17,1},{25,9},{2,18},{10... | collective-permute-start | bytes 2359304 | tf_op jit(solution)/shard_map/cond/branch_1_fun/ppermute | solution.py:903
  358.7 27.0 %collective-permute-start.42 = (bf16[512,1536]{1,0:T(8,128)(2,1)}, bf16[512,1536]{1,0:T(8,128)(2,1)}, u32[]{:S(2)}, u32[]{:S(2)}) collective-permute-start(bf16[512,1536]{1,0:T(8,128)(2,1)} %pad_maximum_fusion.3), channel_id=1, source_target_pairs={{0,8},{8,0},{16,24},{24,16},{1,9},{9,1},{17,25},{25,17},{2,10},{10... | collective-permute-start | bytes 4718600 | tf_op jit(solution)/shard_map/cond/branch_1_fun/ppermute | solution.py:897
  358.7 33.8 %collective-permute-start.46 = (bf16[6,128,768]{2,1,0:T(8,128)(2,1)}, bf16[6,128,768]{2,1,0:T(8,128)(2,1)}, u32[]{:S(2)}, u32[]{:S(2)}) collective-permute-start(bf16[6,128,768]{2,1,0:T(8,128)(2,1)} %get-tuple-element.697), channel_id=1, source_target_pairs={{0,1},{1,0},{2,3},{3,2},{4,5},{5,4},{6,7},{7,6},{8,9},{9,8},{10,11... | collective-permute-start | bytes 3538952 | tf_op jit(solution)/shard_map/cond/branch_1_fun/ppermute | solution.py:897
  359.4 34.6 %collective-permute-start.47 = (bf16[6,128,768]{2,1,0:T(8,128)(2,1)}, bf16[6,128,768]{2,1,0:T(8,128)(2,1)}, u32[]{:S(2)}, u32[]{:S(2)}) collective-permute-start(bf16[6,128,768]{2,1,0:T(8,128)(2,1)} %get-tuple-element.698), channel_id=1, source_target_pairs={{0,16},{8,24},{16,0},{24,8},{1,17},{9,25},{17,1},{25,9},{2,18},{10... | collective-permute-start | bytes 3538952 | tf_op jit(solution)/shard_map/cond/branch_1_fun/ppermute | solution.py:903
  371.8 20.7 %collective-permute-start.45 = (bf16[256,1536]{1,0:T(8,128)(2,1)}, bf16[256,1536]{1,0:T(8,128)(2,1)}, u32[]{:S(2)}, u32[]{:S(2)}) collective-permute-start(bf16[256,1536]{1,0:T(8,128)(2,1)} %get-tuple-element.696), channel_id=1, source_target_pairs={{0,6},{1,7},{2,0},{3,1},{4,2},{5,3},{6,4},{7,5},{8,10},{9,11},{10,... | collective-permute-start | bytes 2359304 | tf_op jit(solution)/shard_map/cond/branch_1_fun/ppermute | solution.py:915
  397.5 35.0 %collective-permute-start.48 = (bf16[4,48,4096]{2,1,0:T(8,128)(2,1)}, bf16[4,48,4096]{2,1,0:T(8,128)(2,1)}, u32[]{:S(2)}, u32[]{:S(2)}) collective-permute-start(bf16[4,48,4096]{2,1,0:T(8,128)(2,1)} %get-tuple-element.1091), channel_id=1, source_target_pairs={{0,1},{1,0},{2,3},{3,2},{4,5},{5,4},{6,7},{7,6},{8,9},{9,8},{10,11... | collective-permute-start | bytes 4718600 | tf_op jit(solution)/shard_map/cond/branch_1_fun/ppermute | solution.py:897
  401.9 30.6 %collective-permute-start.49 = (bf16[6,128,768]{2,1,0:T(8,128)(2,1)}, bf16[6,128,768]{2,1,0:T(8,128)(2,1)}, u32[]{:S(2)}, u32[]{:S(2)}) collective-permute-start(bf16[6,128,768]{2,1,0:T(8,128)(2,1)} %branch_1_fun.55), channel_id=1, source_target_pairs={{0,16},{8,24},{16,0},{24,8},{1,17},{9,25},{17,1},{25,9},{2,18},{10... | collective-permute-start | bytes 3538952 | tf_op jit(solution)/shard_map/cond/branch_1_fun/ppermute | solution.py:903
  403.3 29.2 %all-to-all-start = ((f32[32,2,48]{2,1,0:T(2,128)}), f32[32,2,48]{2,1,0:T(2,128)}, u32[]{:S(2)}, u32[]{:S(2)}) async-start(f32[32,2,48]{2,1,0:T(2,128)} %pad_maximum_fusion.6), calls=%async_computation | async-start | bytes 65536 | tf_op jit(solution)/shard_map/cond/branch_1_fun/all_to_all | solution.py:1330
  406.6 26.0 %collective-permute-start.50 = (bf16[80,2048]{1,0:T(8,128)(2,1)}, bf16[80,2048]{1,0:T(8,128)(2,1)}, u32[]{:S(2)}, u32[]{:S(2)}) collective-permute-start(bf16[80,2048]{1,0:T(8,128)(2,1)} %get-tuple-element.708), channel_id=1, source_target_pairs={{0,4},{1,5},{2,6},{3,7},{4,0},{5,1},{6,2},{7,3},{8,12},{9,13},{10,... | collective-permute-start | bytes 983048 | tf_op jit(solution)/shard_map/cond/branch_1_fun/ppermute | solution.py:903
  409.2 23.3 %collective-permute-start.51 = (bf16[80,2048]{1,0:T(8,128)(2,1)}, bf16[80,2048]{1,0:T(8,128)(2,1)}, u32[]{:S(2)}, u32[]{:S(2)}) collective-permute-start(bf16[80,2048]{1,0:T(8,128)(2,1)} %get-tuple-element.709), channel_id=1, source_target_pairs={{0,6},{1,7},{2,0},{3,1},{4,2},{5,3},{6,4},{7,5},{8,14},{9,15},{10,... | collective-permute-start | bytes 983048 | tf_op jit(solution)/shard_map/cond/branch_1_fun/ppermute | solution.py:903
  437.4 22.4 %collective-permute-start.54 = (bf16[48,4096]{1,0:T(8,128)(2,1)}, bf16[48,4096]{1,0:T(8,128)(2,1)}, u32[]{:S(2)}, u32[]{:S(2)}) collective-permute-start(bf16[48,4096]{1,0:T(8,128)(2,1)} %get-tuple-element.1086), channel_id=1, source_target_pairs={{0,6},{1,7},{2,0},{3,1},{4,2},{5,3},{6,4},{7,5},{8,14},{9,15},{10,... | collective-permute-start | bytes 1179656 | tf_op jit(solution)/shard_map/cond/branch_1_fun/ppermute | solution.py:903
  440.4 33.2 %collective-permute-start.53 = (bf16[48,4096]{1,0:T(8,128)(2,1)}, bf16[48,4096]{1,0:T(8,128)(2,1)}, u32[]{:S(2)}, u32[]{:S(2)}) collective-permute-start(bf16[48,4096]{1,0:T(8,128)(2,1)} %get-tuple-element.1087), channel_id=1, source_target_pairs={{0,4},{1,5},{2,6},{3,7},{4,0},{5,1},{6,2},{7,3},{8,12},{9,13},{10,... | collective-permute-start | bytes 1179656 | tf_op jit(solution)/shard_map/cond/branch_1_fun/ppermute | solution.py:903
  440.4 33.2 %collective-permute-start.52 = (bf16[48,4096]{1,0:T(8,128)(2,1)}, bf16[48,4096]{1,0:T(8,128)(2,1)}, u32[]{:S(2)}, u32[]{:S(2)}) collective-permute-start(bf16[48,4096]{1,0:T(8,128)(2,1)} %get-tuple-element.1088), channel_id=1, source_target_pairs={{0,2},{1,3},{2,4},{3,5},{4,6},{5,7},{6,0},{7,1},{8,10},{9,11},{10,... | collective-permute-start | bytes 1179656 | tf_op jit(solution)/shard_map/cond/branch_1_fun/ppermute | solution.py:903
  (39 other events, 521.1 us)

commit v5 on v4

--- a/solution.py
+++ b/solution.py
@@ -351,25 +351,28 @@
     return jnp.sum(jnp.where(chosen, gates.astype(f32), 0.0), axis=1, keepdims=True)
 
 
-def experts_kernel(per, gated, extra, keeps, pos, x_ref, c_ref, *refs):
-    weights = refs[:3]
-    out_ref, grad_ref, *kept_refs, acc_o, acc_g = refs[3 + extra :]
+def experts_kernel(count, per, gated, extra, pos, *refs):
+    x_refs, c_refs, weights = refs[:count], refs[count : 2 * count], refs[2 * count : 2 * count + 3]
+    *outs, acc_o, acc_g = refs[2 * count + 3 + extra :]
+    out_refs, grad_refs, kept_refs = outs[:count], outs[count : 2 * count], outs[2 * count :]
+    wg_ref, wu_ref, wd_ref = weights
+    hid_ref, dgu_ref = kept_refs[-2:]
     step = pl.program_id(0)
     last = pl.num_programs(0) - 1
-    width = x_ref.shape[1]
-    if keeps:
+    rows, width = x_refs[0].shape
+    chunk = wg_ref.shape[1]
+    parts = [slice(b * rows, (b + 1) * rows) for b in range(count)]
+    if gated:
 
         @pl.when(step == 0)
         def _():
-            kept_refs[0][...] = x_ref[...]
-            kept_refs[1][...] = c_ref[...]
-            kept_refs[2][...] = jnp.transpose(x_ref[...])
-            kept_refs[3][...] = jnp.transpose(c_ref[:, :width])
-
-    hid_ref, dgu_ref = kept_refs[-2:]
-
-    def work(wg_ref, wu_ref, wd_ref):
-        chunk = wg_ref.shape[1]
+            for part, x_ref, c_ref in zip(parts, x_refs, c_refs):
+                kept_refs[0][part, :] = x_ref[...]
+                kept_refs[1][part, :] = c_ref[...]
+                kept_refs[2][:, part] = jnp.transpose(x_ref[...])
+                kept_refs[3][:, part] = jnp.transpose(c_ref[:, :width])
+
+    for part, x_ref, c_ref in zip(parts, x_refs, c_refs):
         x = x_ref[...]
         gate = dot(x, wg_ref[...])
         up = dot(x, wu_ref[...])
@@ -386,32 +389,33 @@
         hidden = hidden.astype(bf16)
         dg = (slope * up * (sigmoid * (1.0 + gate * (1.0 - sigmoid)))).astype(bf16)
         du = (slope * act).astype(bf16)
-        hid_ref[...] = hidden
-        dgu_ref[:, :chunk] = dg
-        dgu_ref[:, chunk:] = du
+        hid_ref[part, :] = hidden
+        dgu_ref[part, :chunk] = dg
+        dgu_ref[part, chunk:] = du
         out_term = dot(hidden, wd_ref[...])
         grad_term = dot_nt(dg, wg_ref[...]) + dot_nt(du, wu_ref[...])
 
         @pl.when(step == 0)
         def _():
-            acc_o[...] = out_term
-            acc_g[...] = grad_term
+            acc_o[part, :] = out_term
+            acc_g[part, :] = grad_term
 
         @pl.when(step > 0)
         def _():
-            acc_o[...] += out_term
-            acc_g[...] += grad_term
-
-    work(*weights)
+            acc_o[part, :] += out_term
+            acc_g[part, :] += grad_term
 
     @pl.when(step == last)
     def _():
-        out_ref[...] = acc_o[...].astype(out_ref.dtype)
-        grad_ref[...] = acc_g[...].astype(grad_ref.dtype)
-
-
-def experts(pos, x, c, weights, part, parts, kept, gated, kind, after=(), chunk=256):
-    rows, width = x.shape
+        for part, out_ref, grad_ref in zip(parts, out_refs, grad_refs):
+            out_ref[...] = acc_o[part, :].astype(out_ref.dtype)
+            grad_ref[...] = acc_g[part, :].astype(grad_ref.dtype)
+
+
+def experts(pos, xs, cs, weights, part, parts, kept, gated, kind, chunk=256):
+    count = len(xs)
+    rows, width = xs[0].shape
+    taken = count * rows
     inner = weights[2].shape[1]
     per = inner // chunk
     steps = weights[0].shape[0] * per
@@ -420,49 +424,49 @@
         pl.BlockSpec((None, width, chunk), lambda i, _: (i // per, 0, i % per)),
         pl.BlockSpec((None, chunk, width), lambda i, _: (i // per, i % per, 0)),
     ]
+    all_rows = parts * taken
     collected = [
-        jax.ShapeDtypeStruct((parts * rows, steps * chunk), bf16),
-        jax.ShapeDtypeStruct((parts * rows, 2 * steps * chunk), bf16),
+        jax.ShapeDtypeStruct((all_rows, steps * chunk), bf16),
+        jax.ShapeDtypeStruct((all_rows, 2 * steps * chunk), bf16),
     ]
     collected_specs = [
-        pl.BlockSpec((rows, chunk), lambda i, _: (part, i)),
-        pl.BlockSpec((rows, 2 * chunk), lambda i, _: (part, i)),
+        pl.BlockSpec((taken, chunk), lambda i, _: (part, i)),
+        pl.BlockSpec((taken, 2 * chunk), lambda i, _: (part, i)),
     ]
     if gated:
         collected = [
-            jax.ShapeDtypeStruct((parts * rows, width), bf16),
-            jax.ShapeDtypeStruct((parts * rows, c.shape[1]), bf16),
-            jax.ShapeDtypeStruct((width, parts * rows), bf16),
-            jax.ShapeDtypeStruct((width, parts * rows), bf16),
+            jax.ShapeDtypeStruct((all_rows, width), bf16),
+            jax.ShapeDtypeStruct((all_rows, cs[0].shape[1]), bf16),
+            jax.ShapeDtypeStruct((width, all_rows), bf16),
+            jax.ShapeDtypeStruct((width, all_rows), bf16),
         ] + collected
         collected_specs = [
-            pl.BlockSpec((rows, width), lambda i, _: (part, 0)),
-            pl.BlockSpec((rows, c.shape[1]), lambda i, _: (part, 0)),
-            pl.BlockSpec((width, rows), lambda i, _: (0, part)),
-            pl.BlockSpec((width, rows), lambda i, _: (0, part)),
+            pl.BlockSpec((taken, width), lambda i, _: (part, 0)),
+            pl.BlockSpec((taken, cs[0].shape[1]), lambda i, _: (part, 0)),
+            pl.BlockSpec((width, taken), lambda i, _: (0, part)),
+            pl.BlockSpec((width, taken), lambda i, _: (0, part)),
         ] + collected_specs
-    operands = [pos, x, c, *weights]
+    operands = [pos, *xs, *cs, *weights]
     aliases = {}
     if kept is not None:
-        aliases = {len(operands) + j: 2 + j for j in range(len(collected))}
+        aliases = {len(operands) + j: 2 * count + j for j in range(len(collected))}
         operands += list(kept)
-    extra = len(after) + (0 if kept is None else len(collected))
-    operands += list(after)
+    extra = 0 if kept is None else len(collected)
     result = pl.pallas_call(
-        functools.partial(experts_kernel, per, gated, extra, gated),
+        functools.partial(experts_kernel, count, per, gated, extra),
         grid_spec=pltpu.PrefetchScalarGridSpec(
             num_scalar_prefetch=1,
             grid=(steps,),
-            in_specs=[whole((rows, width)), whole(c.shape)] + specs + anywhere(extra),
-            out_specs=[whole((rows, width))] * 2 + collected_specs,
-            scratch_shapes=[pltpu.VMEM((rows, width), f32)] * 2,
+            in_specs=[whole((rows, width))] * count + [whole(cs[0].shape)] * count + specs + anywhere(extra),
+            out_specs=[whole((rows, width))] * (2 * count) + collected_specs,
+            scratch_shapes=[pltpu.VMEM((taken, width), f32)] * 2,
         ),
-        out_shape=[jax.ShapeDtypeStruct((rows, width), kind)] * 2 + collected,
+        out_shape=[jax.ShapeDtypeStruct((rows, width), kind)] * (2 * count) + collected,
         input_output_aliases=aliases,
         compiler_params=params(),
-        cost_estimate=cost(26 * rows * width * steps * chunk, 12 * 2**20),
+        cost_estimate=cost(26 * taken * width * steps * chunk, 12 * 2**20),
     )(*operands)
-    return result[0], result[1], result[2:]
+    return result[:count], result[count : 2 * count], result[2 * count :]
 
 
 def others_kernel(sets, per, bands, extra, pos, x_ref, c_ref, *refs):
@@ -1026,11 +1030,14 @@
     return lax.dynamic_index_in_dim(pairs, lax.axis_index("exp") % 2, 1, False)
 
 
-def over_z(mine, arrived):
-    mine = mine.astype(f32) + arrived.astype(f32)
-    levels, level = mine.shape[0], lax.axis_index("exp") // 2
-    take = lambda d: lax.dynamic_index_in_dim(mine, (level + d) % levels, 0, False)
-    return [take(0)] + [shift_outer(take(d).astype(bf16), "exp", d) for d in range(1, levels)]
+def over_z(pos, mine, arrived):
+    levels, rows, wide = mine.shape
+    outputs = []
+    for d in range(levels):
+        at = functools.partial(lambda d, i, pos: lax.rem(pos[2] + d, levels), d)
+        outputs.append((bf16 if d else f32, (1, rows, wide), [(mine, at), (arrived, at)]))
+    own, *sent = [v[0] for v in sums(pos, 1, outputs)]
+    return [own] + [shift_outer(v, "exp", d + 1) for d, v in enumerate(sent)]
 
 
 def expert_quarter(kept, got, q, row):
@@ -1173,13 +1180,14 @@
     fetched.append(got)
     crossed.append(crossing)
 
-    def own_part(k, rows, kept):
-        weights = (expert_gate, expert_up, expert_down)
-        return experts(pos, rows, cot_ring[k], weights, k, levels, kept, True, bf16)
+    own_weights = (expert_gate, expert_up, expert_down)
+
+    def own_part(ks, rows, part, parts, kept):
+        return experts(pos, rows, [cot_ring[k] for k in ks], own_weights, part, parts, kept, True, bf16)
 
     def first():
         weights = (shared_gate[None], shared_up[None], shared_down[None])
-        shared = experts(pos, rows_low, cot, weights, 0, 1, None, False, f32)
+        shared = experts(pos, [rows_low], [cot], weights, 0, 1, None, False, f32)
         more = spread_inner(normed_moved), fetch(2), over_core(fetched[1]), outer_blocks(attended)
         return ring_step(rows_low, 1), shared, *more
 
@@ -1187,11 +1195,11 @@
     fetched.append(got)
     crossed.append(crossing)
     normed_blocks = paired_blocks(normed, normed_across, normed_moved, across)
-    shared_out, shared_grad, (shared_hidden, shared_dgu) = shared
+    (shared_out,), (shared_grad,), (shared_hidden, shared_dgu) = shared
     shared_pairs = [(rows_low, shared_dgu), (shared_hidden, cot)]
 
     def second():
-        result = own_part(0, rows_low, None)
+        result = own_part([0], [rows_low], 2, 4, None)
         more = fetch(3), over_core(fetched[2]), [over_core(attended), *spread_inner(attended_moved)]
         return ring_step(rows_one, 1), result, halves(pos, shared_pairs), *more
 
@@ -1199,20 +1207,19 @@
     attended_blocks = paired_blocks(attended, across[0], attended_moved, across[1:])
     fetched.append(got)
     crossed.append(crossing)
-    out_own, grad_own = [out_k], [grad_k]
+    out_own, grad_own = list(out_k), list(grad_k)
 
     def third():
         more = over_core(shared_sent), fetch(4), over_core(fetched[3])
-        one = own_part(1, rows_one, kept)
-        two = own_part(2, rows_two, one[2])
-        return ring_step(rows_two, 1), one[:2], two, *more
-
-    rows_k, one, two, shared_got, got, crossing = region(third)
+        pair = own_part([1, 2], [rows_one, rows_two], 0, 2, kept)
+        sent = Shared(pos, shared_kept, more[0]).first()
+        return ring_step(rows_two, 1), pair, sent, *more
+
+    rows_k, (out_k, grad_k, kept), shared_sent, shared_got, got, crossing = region(third)
     fetched.append(got)
     crossed.append(crossing)
-    kept = two[2]
-    out_own += [one[0], two[0]]
-    grad_own += [one[1], two[1]]
+    out_own += out_k
+    grad_own += grad_k
 
     def over_y(parts, k):
         return [shift_outer(v[k], "ctx", d + 1) for d, v in enumerate(parts)]
@@ -1221,19 +1228,16 @@
         moved = ring_step(cot_ring[2], 1)
         weights = [arranged(fetched), arranged(crossed + [over_core(fetched[4])])]
         half = levels // 2
-        sent = Shared(pos, shared_kept, shared_got).first()
-        arrived = [over_y(sent, k) for k in range(len(sent[0]))]
+        arrived = [over_y(shared_sent, k) for k in range(len(shared_sent[0]))]
         out_a, grad_a, new = others(pos, kept[0], kept[1], weights, 0, 2, half, None)
-        out_k, grad_k, more = experts(
-            pos, rows_k, moved, (expert_gate, expert_up, expert_down), 3, levels, kept, True, bf16
-        )
-        out_b, grad_b, new = others(pos, more[0], more[1], weights, 1, 2, half, new)
-        return out_k, grad_k, more, [*out_a, *out_b], [*grad_a, *grad_b], new, arrived
-
-    out_k, grad_k, kept, out_other, grad_other, kept_other, got = region(fourth)
+        last = experts(pos, [rows_k], [moved], own_weights, 3, 4, kept, True, bf16)
+        out_b, grad_b, new = others(pos, last[2][0], last[2][1], weights, 1, 2, half, new)
+        return last, [out_b[0], *out_a, out_b[1]], [grad_b[0], *grad_a, grad_b[1]], new, arrived
+
+    (out_k, grad_k, kept), out_other, grad_other, kept_other, got = region(fourth)
     shared_moved = [list(v) for v in zip(*got)]
-    out_own.append(out_k)
-    grad_own.append(grad_k)
+    out_own += out_k
+    grad_own += grad_k
     rows_all, cot_all, rows_t, cot_t, hid_own, dgu_own = kept
     hid_other, dgu_other = kept_other
 
@@ -1340,7 +1344,7 @@
         shared = shared_grads(
             shared_parts, shape(shared_gate), shape(shared_down)
         )
-        dense = dense_out(over_z(total, total_x), x.shape[1])
+        dense = dense_out(over_z(pos, total, total_x), x.shape[1])
         return jnp.sum(gains, axis=0), shared, dense, grads
 
     gains, (sum_gate, sum_up, sum_down), dense, expert_grads = region(dense_four)

time: 485 us -> 480 us (0.990)
  the two profiles are of different devices: /device:TPU:0 before, /device:TPU:9 now
where the time goes in v5:
time: 480 us; the launch traced here: 471 us
  Pallas kernels  255 us (53%)
  waiting for transfers between devices  79.9 us (17%)
  starting transfers between devices  74.8 us (16%)
  other arithmetic  34 us (7%)
  local copies, waits for them, and re-layouts  19.8 us (4%)
  matrix products  4.87 us (1%)
    pallas_call x4, Pallas kernels, experts(): pl.pallas_call(functools.partial(experts_kernel, count, per, gated, extra...  60 us
    ppermute x17, waiting for transfers between devices, shift_outer(): return lax.ppermute(value, axis, perm)  44.7 us
    ppermute x31, starting transfers between devices, swap_inner(): return lax.ppermute(value, axis, [(i, i ^ 1) for i in range(size)])  43.1 us
    pallas_call x9, Pallas kernels, sums(): pl.pallas_call(functools.partial(sums_kernel, [len(terms) for _, _, terms...  39.1 us
    pallas_call x2, Pallas kernels, others(): pl.pallas_call(functools.partial(others_kernel, sets, per, len(bands), ex...  38.3 us
    pallas_call x2, Pallas kernels, expert_halves(): pl.pallas_call(functools.partial(expert_halves_kernel, n_ctx, tiles), gri...  31.3 us
    all_to_all x1, waiting for transfers between devices, dense_three(): gains = lax.all_to_all(gains, BOTH, split_axis=0, concat_axis=0, tiled=True)  18.2 us
    convert_element_type x8, other arithmetic, row_sum(): return total.astype(kind)  17.7 us
  transfers between devices with their start and end apart: 61, of which 17 were waited for; matrix products, arithmetic and copies ran while one was open for 9% of the time, Pallas kernels for 52%

profile of v5, /device:TPU:9, one launch (start us, length us, event | category | flops | bytes accessed | tf_op | source)
XLA Modules:
  0.0 471.4 jit_solution(13601143008622493622)
XLA Ops:
  6.0 27.4 %conditional.14 = (bf16[256,1536]{1,0:T(8,128)(2,1)}, bf16[256,1024]{1,0:T(8,128)(2,1)}, bf16[256,1024]{1,0:T(8,128)(2,1)}, bf16[256,1024]{1,0:T(8,128)(2,1)}, b...) conditional(s32[]{:T(128)} %convert_element_type.130, ...), branch_computations={%region_3.4_spmd, %region_4.5_spmd} | conditional | flops 1415970816 | bytes 48771484 | solution.py:1124
  6.6 5.1 %branch_1_fun.30 = (bf16[256,1536]{1,0:T(8,128)(2,1)}, bf16[256,1024]{1,0:T(8,128)(2,1)}) custom-call(bf16[256,1536]{1,0:T(8,128)(2,1)} %get-tuple-element.442.x_ref, f32[1,1536]{1,0:T(1,128)} %reshape.107.gain_ref, bf16[1536,512]{1,0:T(8,128)(2,1)} %get-tuple-element.444.wk_ref, bf16[1536,512]{1,0:T(8,128)(2,1)} %get-tuple-element.445.wv_ref), custom_call_target="tpu_custom_call" | custom-call | flops 201326592 | bytes 1310720 | tf_op jit(solution)/shard_map/cond/branch_1_fun/pallas_call | solution.py:66
  20.7 5.5 %collective-permute-done.55 = bf16[256,1024]{1,0:T(8,128)(2,1)} collective-permute-done((bf16[256,1024]{1,0:T(8,128)(2,1)}, bf16[256,1024]{1,0:T(8,128)(2,1)}, u32[]{:S(2)}, u32[]{:S(2)}) %collective-permute-start.55) | collective-permute-done | bytes 524320 | tf_op jit(solution)/shard_map/cond/branch_1_fun/ppermute | solution.py:907
  28.2 4.9 %convolution_convert_fusion = bf16[256,1536]{1,0:T(8,128)(2,1)} fusion(bf16[256,1536]{1,0:T(8,128)(2,1)} %get-tuple-element.1107, bf16[1536,1536]{1,0:T(8,128)(2,1)} %get-tuple-element.448), kind=kOutput, calls=%fused_computation | convolution fusion | flops 1208352768 | bytes 6291456 | tf_op jit(solution)/shard_map/cond/branch_1_fun/dot_general | solution.py:26
  33.4 25.3 %conditional.15 = (bf16[256,1536]{1,0:T(8,128)(2,1)}, f32[4,1,768]{2,1,0:T(1,128)S(1)}, f32[256,1536]{1,0:T(8,128)}, bf16[256,1536]{1,0:T(8,128)(2,1)S(1)}, bf16...) conditional(s32[]{:T(128)} %convert_element_type.130, ...), branch_computations={%region_5.6_spmd, %region_6.7_spmd} | conditional | flops 1107296256 | bytes 22294828 | solution.py:1124
  40.4 9.5 %branch_1_fun.31 = (bf16[256,1536]{1,0:T(8,128)(2,1)}, f32[4,1,768]{2,1,0:T(1,128)S(1)}) custom-call(s32[4]{0:T(128)S(1)} %get-tuple-element.454.pos, s32[8]{0:T(128)S(1)} %get-tuple-element.455.spans, bf16[256,1536]{1,0:T(8,128)(2,1)} %get-tuple-element.456.q_ref, bf16[256,1024]{1,0:T(8,128)(2,1)} %get-tuple-element.457.refs_0_, ...), custom_call_target="tpu_custom_call" | custom-call | flops 805306368 | bytes 1048576 | tf_op jit(solution)/shard_map/cond/branch_1_fun/pallas_call | solution.py:128
  49.9 5.6 %branch_1_fun.32 = (f32[256,1536]{1,0:T(8,128)}, bf16[256,1536]{1,0:T(8,128)(2,1)S(1)}) custom-call(bf16[256,1536]{1,0:T(8,128)(2,1)S(1)} %copy-done.3, bf16[256,1536]{1,0:T(8,128)(2,1)} %get-tuple-element.1128.att_ref, bf16[1536,1536]{1,0:T(8,128)(2,1)} %get-tuple-element.464.w_ref, f32[1,1536]{1,0:T(1,128)} %reshape.108.gain_ref), custom_call_target="tpu_custom_call" | custom-call | flops 301989888 | bytes 2097152 | tf_op jit(solution)/shard_map/cond/branch_1_fun/pallas_call | solution.py:228
  58.7 24.3 %conditional.16 = (bf16[256,1536]{1,0:T(8,128)(2,1)}, f32[256,1536]{1,0:T(8,128)}, f32[256,1536]{1,0:T(8,128)}, bf16[256,1024]{1,0:T(8,128)(2,1)S(1)}, bf16[256,...) conditional(s32[]{:T(128)} %convert_element_type.130, ...), branch_computations={%region_7.8_spmd, %region_8.9_spmd} | conditional | flops 2617245696 | bytes 19923216 | solution.py:1124
  61.3 11.4 %branch_1_fun.33 = (f32[256,1536]{1,0:T(8,128)}, f32[256,1536]{1,0:T(8,128)}, bf16[256,1024]{1,0:T(8,128)(2,1)S(1)}, bf16[256,2048]{1,0:T(8,128)(2,1)}) custom-call(s32[4]{0:T(128)S(1)} %get-tuple-element.473.pos, bf16[256,1536]{1,0:T(8,128)(2,1)S(1)} %get-tuple-element.472.refs_0_, bf16[256,1536]{1,0:T(8,128)(2,1)S(1)} %get-tuple-element.474.refs_1_, ...), custom_call_target="tpu_custom_call" | custom-call | flops 2617245696 | bytes 3145728 | tf_op jit(solution)/shard_map/cond/branch_1_fun/pallas_call | solution.py:455
  72.6 6.4 %collective-permute-done.9 = bf16[256,1536]{1,0:T(8,128)(2,1)} collective-permute-done((bf16[256,1536]{1,0:T(8,128)(2,1)}, bf16[256,1536]{1,0:T(8,128)(2,1)}, u32[]{:S(2)}, u32[]{:S(2)}) %collective-permute-start.9) | collective-permute-done | bytes 786464 | tf_op jit(solution)/shard_map/cond/branch_1_fun/ppermute | solution.py:907
  83.0 25.1 %conditional.17 = (bf16[256,1536]{1,0:T(8,128)(2,1)}, bf16[256,1536]{1,0:T(8,128)(2,1)}, bf16[256,1536]{1,0:T(8,128)(2,1)}, bf16[1024,1536]{1,0:T(8,128)(2,1)}, ...) conditional(s32[]{:T(128)} %convert_element_type.130, ...), branch_computations={%region_9.10_spmd, %region_10.11_spmd} | conditional | flops 3825205248 | bytes 35651728 | solution.py:1124
  87.1 8.3 %branch_1_fun.35 = (bf16[16,80,2048]{2,1,0:T(8,128)(2,1)}, bf16[16,80,2048]{2,1,0:T(8,128)(2,1)}) custom-call(s32[4]{0:T(128)S(1)} %get-tuple-element.487.pos, bf16[256,1536]{1,0:T(8,128)(2,1)S(1)} %get-tuple-element.488.refs_0_, bf16[256,2048]{1,0:T(8,128)(2,1)} %get-tuple-element.501.refs_1_, bf16[256,1024]{1,0:T(8,128)(2,1)S(1)} %get-tuple-element.502.refs_2_, ...), custom_call_target="tpu_custom_call" | custom-call | flops 1207959552 | bytes 2097152 | tf_op jit(solution)/shard_map/cond/branch_1_fun/pallas_call | solution.py:619
  95.4 12.7 %branch_1_fun.34 = (bf16[256,1536]{1,0:T(8,128)(2,1)}, bf16[256,1536]{1,0:T(8,128)(2,1)}, bf16[1024,1536]{1,0:T(8,128)(2,1)}, bf16[1024,1664]{1,0:T(8,128)(2,1)}...) custom-call(s32[4]{0:T(128)S(1)} %get-tuple-element.487.pos, ...), custom_call_target="tpu_custom_call" | custom-call | flops 2617245696 | bytes 3145728 | tf_op jit(solution)/shard_map/cond/branch_1_fun/pallas_call | solution.py:455
  108.1 32.4 %conditional.18 = (bf16[256,1536]{1,0:T(8,128)(2,1)}, bf16[256,1536]{1,0:T(8,128)(2,1)}, bf16[256,1536]{1,0:T(8,128)(2,1)}, bf16[256,1536]{1,0:T(8,128)(2,1)}, b...) conditional(s32[]{:T(128)} %convert_element_type.130, ...), branch_computations={%region_11.12_spmd, %region_12.13_spmd} | conditional | flops 5234491392 | bytes 37749024 | solution.py:1124
  112.6 22.7 %branch_1_fun.36 = (bf16[256,1536]{1,0:T(8,128)(2,1)}, bf16[256,1536]{1,0:T(8,128)(2,1)}, bf16[256,1536]{1,0:T(8,128)(2,1)}, bf16[256,1536]{1,0:T(8,128)(2,1)}, ...) custom-call(s32[4]{0:T(128)S(1)} %get-tuple-element.511.pos, ...), custom_call_target="tpu_custom_call", output_to_operand_aliasing={{4}: (8, {}), {5}: (9, {}), {6}: (10, {}), {7}: (11, {}), {... | custom-call | flops 5234491392 | bytes 3145728 | tf_op jit(solution)/shard_map/cond/branch_1_fun/pallas_call | solution.py:455
  135.3 4.9 %branch_1_fun.37 = (bf16[2,160,2048]{2,1,0:T(8,128)(2,1)}, bf16[2,160,2048]{2,1,0:T(8,128)(2,1)}) custom-call(s32[4]{0:T(128)S(1)} %get-tuple-element.511.pos, bf16[8,160,2048]{2,1,0:T(8,128)(2,1)} %bitcast.11.refs_0_.refs_2_, bf16[8,160,2048]{2,1,0:T(8,128)(2,1)} %bitcast.12.refs_1_.refs_3_, bf16[8,160,2048]{2,1,0:T(8,128)(2,1)} %bitcast.11.refs_0_.refs_2_, ...), custom_call_target="tpu_custom_call" | custom-call | bytes 2097152 | tf_op jit(solution)/shard_map/cond/branch_1_fun/pallas_call | solution.py:754
  140.6 59.9 %conditional.19 = (bf16[256,1536]{1,0:T(8,128)(2,1)}, bf16[256,1536]{1,0:T(8,128)(2,1)}, bf16[1536,1024]{1,0:T(8,128)(2,1)}, bf16[1536,1024]{1,0:T(8,128)(2,1)S(...) conditional(s32[]{:T(128)} %convert_element_type.130, ...), branch_computations={%region_13.14_spmd, %region_14.15_spmd} | conditional | flops 13086228480 | bytes 30933324 | solution.py:1124
  143.7 19.1 %branch_1_fun.39 = (bf16[256,1536]{1,0:T(8,128)(2,1)}, bf16[256,1536]{1,0:T(8,128)(2,1)}, bf16[256,1536]{1,0:T(8,128)(2,1)}, bf16[256,1536]{1,0:T(8,128)(2,1)}, ...) custom-call(s32[4]{0:T(128)S(1)} %get-tuple-element.540.pos, bf16[1024,1536]{1,0:T(8,128)(2,1)} %get-tuple-element.546.refs_5_.x_ref, ...), custom_call_target="tpu_custom_call" | custom-call | flops 5234491392 | bytes 3145728 | tf_op jit(solution)/shard_map/cond/branch_1_fun/pallas_call | solution.py:547
  163.7 13.1 %branch_1_fun.38 = (bf16[256,1536]{1,0:T(8,128)(2,1)}, bf16[256,1536]{1,0:T(8,128)(2,1)}, bf16[1024,1536]{1,0:T(8,128)(2,1)}, bf16[1024,1664]{1,0:T(8,128)(2,1)}...) custom-call(s32[4]{0:T(128)S(1)} %get-tuple-element.540.pos, ...), custom_call_target="tpu_custom_call", output_to_operand_aliasing={{2}: (6, {}), {3}: (7, {}), {4}: (8, {}), {5}: (9, {}), {6}... | custom-call | flops 2617245696 | bytes 3145728 | tf_op jit(solution)/shard_map/cond/branch_1_fun/pallas_call | solution.py:455
  176.8 19.2 %branch_1_fun.40 = (bf16[256,1536]{1,0:T(8,128)(2,1)}, bf16[256,1536]{1,0:T(8,128)(2,1)}, bf16[256,1536]{1,0:T(8,128)(2,1)}, bf16[256,1536]{1,0:T(8,128)(2,1)S(1...) custom-call(s32[4]{0:T(128)S(1)} %get-tuple-element.540.pos, ...), custom_call_target="tpu_custom_call", output_to_operand_aliasing={{4}: (13, {}), {5}: (14, {})} | custom-call | flops 5234491392 | bytes 3145728 | tf_op jit(solution)/shard_map/cond/branch_1_fun/pallas_call | solution.py:547
  200.5 23.1 %conditional.20 = (bf16[256,1536]{1,0:T(8,128)(2,1)}, bf16[6,128,3072]{2,1,0:T(8,128)(2,1)}, bf16[6,128,3072]{2,1,0:T(8,128)(2,1)}, bf16[2,80,2048]{2,1,0:T(8,128)(2,1)}, bf16[2,80,2048]{2,1,0:T(8,128)(2,1)}) conditional(s32[]{:T(128)} %convert_element_type.130, () %tuple.143, (bf16[256,1536]{1,0:T(8,128)(2,1)}, bf16[256,1536]{1,0:T(8,128)(2,1)S(1)}, ...), branch_computations={%region_15.16_spmd, %region_16.17_spmd} | conditional | flops 4833411072 | bytes 14418040 | solution.py:1124
  207.8 15.7 %branch_1_fun.41 = (bf16[6,128,3072]{2,1,0:T(8,128)(2,1)}, bf16[6,128,3072]{2,1,0:T(8,128)(2,1)}) custom-call(s32[4]{0:T(128)S(1)} %get-tuple-element.585.pos, bf16[1536,1024]{1,0:T(8,128)(2,1)} %get-tuple-element.586.refs_0_.refs_1_.refs_2_.refs_3_, bf16[1536,1024]{1,0:T(8,128)(2,1)} %get-tuple-element.586.refs_0_.refs_1_.refs_2_.refs_3_, ...), custom_call_target="tpu_custom_call" | custom-call | flops 4831838208 | bytes 4194304 | tf_op jit(solution)/shard_map/cond/branch_1_fun/pallas_call | solution.py:713
  223.5 23.8 %conditional.21 = (bf16[256,1536]{1,0:T(8,128)(2,1)}, bf16[6,128,3072]{2,1,0:T(8,128)(2,1)}, bf16[6,128,3072]{2,1,0:T(8,128)(2,1)}, bf16[6,128,3072]{2,1,0:T(8,1...) conditional(s32[]{:T(128)} %convert_element_type.130, () %tuple.142, ...), branch_computations={%region_17.18_spmd, %region_18.19_spmd} | conditional | flops 4834197504 | bytes 34078888 | solution.py:1124
  228.5 15.6 %branch_1_fun.43 = (bf16[6,128,3072]{2,1,0:T(8,128)(2,1)}, bf16[6,128,3072]{2,1,0:T(8,128)(2,1)}) custom-call(s32[4]{0:T(128)S(1)} %get-tuple-element.602.pos, bf16[1536,1024]{1,0:T(8,128)(2,1)} %get-tuple-element.603.refs_0_.refs_1_.refs_2_.refs_3_, bf16[1536,1024]{1,0:T(8,128)(2,1)} %get-tuple-element.603.refs_0_.refs_1_.refs_2_.refs_3_, ...), custom_call_target="tpu_custom_call" | custom-call | flops 4831838208 | bytes 4194304 | tf_op jit(solution)/shard_map/cond/branch_1_fun/pallas_call | solution.py:713
  247.3 31.3 %conditional.22 = (f32[256,1536]{1,0:T(8,128)}, bf16[256,1536]{1,0:T(8,128)(2,1)}, f32[1,1536]{1,0:T(1,128)S(1)}, bf16[256,1536]{1,0:T(8,128)(2,1)}, bf16[6,128,...) conditional(s32[]{:T(128)} %convert_element_type.130, ...), branch_computations={%region_19.20_spmd, %region_20.21_spmd} | conditional | flops 305922048 | bytes 55850036 | solution.py:1124
  253.6 5.2 %branch_1_fun.46 = (bf16[6,128,768]{2,1,0:T(8,128)(2,1)}, bf16[6,128,768]{2,1,0:T(8,128)(2,1)}, bf16[6,128,768]{2,1,0:T(8,128)(2,1)}) custom-call(s32[4]{0:T(128)S(1)} %get-tuple-element.627.pos, bf16[6,128,3072]{2,1,0:T(8,128)(2,1)} %get-tuple-element.628.refs_0_.refs_2_.refs_4_, bf16[6,128,3072]{2,1,0:T(8,128)(2,1)} %get-tuple-element.629.refs_1_.refs_3_.refs_5_, ...), custom_call_target="tpu_custom_call" | custom-call | bytes 2097152 | tf_op jit(solution)/shard_map/cond/branch_1_fun/pallas_call | solution.py:754
  258.7 4.9 %branch_1_fun.47 = bf16[4,80,2048]{2,1,0:T(8,128)(2,1)} custom-call(s32[4]{0:T(128)S(1)} %get-tuple-element.627.pos, bf16[8,160,2048]{2,1,0:T(8,128)(2,1)} %bitcast.15.refs_0_, bf16[8,160,2048]{2,1,0:T(8,128)(2,1)} %bitcast.16.refs_1_, bf16[2,160,2048]{2,1,0:T(8,128)(2,1)} %get-tuple-element.635.refs_2_, bf16[2,160,2048]{2,1,0:T(8,128)(2,1)} %get-tuple-element.636.refs_3_, ...), custom_call_target="tpu_custom_call" | custom-call | bytes 2097152 | tf_op jit(solution)/shard_map/cond/branch_1_fun/pallas_call | solution.py:754
  270.8 7.6 %branch_1_fun.45 = (f32[256,1536]{1,0:T(8,128)}, bf16[256,1536]{1,0:T(8,128)(2,1)}, f32[1,1536]{1,0:T(1,128)S(1)}, bf16[256,1536]{1,0:T(8,128)(2,1)}) custom-call(f32[256,1536]{1,0:T(8,128)} %get-tuple-element.611.refs_0_, bf16[256,1536]{1,0:T(8,128)(2,1)} %get-tuple-element.612.refs_1_, bf16[256,1536]{1,0:T(8,128)(2,1)S(1)} %copy-done.11, ...), custom_call_target="tpu_custom_call" | custom-call | flops 301989888 | bytes 4194304 | tf_op jit(solution)/shard_map/cond/branch_1_fun/pallas_call | solution.py:273
  279.3 27.9 %conditional.23 = (bf16[256,1536]{1,0:T(8,128)(2,1)S(1)}, bf16[256,1536]{1,0:T(8,128)(2,1)}, bf16[256,1536]{1,0:T(8,128)(2,1)}, bf16[256,1536]{1,0:T(8,128)(2,1)...) conditional(s32[]{:T(128)} %convert_element_type.130, ...), branch_computations={%region_21.22_spmd, %region_22.23_spmd} | conditional | flops 2013265920 | bytes 19136784 | solution.py:1124
  280.6 5.8 %collective-permute-start.23 = (bf16[256,1536]{1,0:T(8,128)(2,1)}, bf16[256,1536]{1,0:T(8,128)(2,1)}, u32[]{:S(2)}, u32[]{:S(2)}) collective-permute-start(bf16[256,1536]{1,0:T(8,128)(2,1)} %get-tuple-element.1312), channel_id=1, source_target_pairs={{0,8},{8,0},{16,24},{24,16},{1,9},{9,1},{17,25},{25,17},{2,10},{10... | collective-permute-start | bytes 2359304 | tf_op jit(solution)/shard_map/cond/branch_1_fun/ppermute | solution.py:901
  287.6 14.5 %branch_1_fun.48 = (bf16[256,1536]{1,0:T(8,128)(2,1)S(1)}, bf16[512,1024]{1,0:T(8,128)(2,1)}, bf16[512,1024]{1,0:T(8,128)(2,1)}) custom-call(s32[4]{0:T(128)S(1)} %get-tuple-element.642.pos, s32[8]{0:T(128)S(1)} %get-tuple-element.643.spans, bf16[256,1536]{1,0:T(8,128)(2,1)} %get-tuple-element.644.q_ref, bf16[256,1536]{1,0:T(8,128)(2,1)} %get-tuple-element.645.grad_ref, ...), custom_call_target="tpu_custom_call" | custom-call | flops 2013265920 | bytes 2097152 | tf_op jit(solution)/shard_map/cond/branch_1_fun/pallas_call | solution.py:190
  302.1 5.1 %collective-permute-done.27 = bf16[80,2048]{1,0:T(8,128)(2,1)} collective-permute-done((bf16[80,2048]{1,0:T(8,128)(2,1)}, bf16[80,2048]{1,0:T(8,128)(2,1)}, u32[]{:S(2)}, u32[]{:S(2)}) %collective-permute-start.27) | collective-permute-done | bytes 327712 | tf_op jit(solution)/shard_map/cond/branch_1_fun/ppermute | solution.py:907
  307.2 35.8 %conditional.24 = (bf16[256,1024]{1,0:T(8,128)(2,1)S(1)}, bf16[256,1536]{1,0:T(8,128)(2,1)}, bf16[8,48,1536]{2,1,0:T(8,128)(2,1)S(1)}, bf16[6,128,768]{2,1,0:T(8...) conditional(s32[]{:T(128)} %convert_element_type.130, () %tuple.127, ...), branch_computations={%region_23.24_spmd, %region_24.25_spmd} | conditional | flops 611319808 | bytes 50332076 | solution.py:1124
  319.5 4.4 branch_1_fun.49
  326.7 7.6 %collective-permute-done.40 = bf16[256,1536]{1,0:T(8,128)(2,1)} collective-permute-done((bf16[256,1536]{1,0:T(8,128)(2,1)}, bf16[256,1536]{1,0:T(8,128)(2,1)}, u32[]{:S(2)}, u32[]{:S(2)}) %collective-permute-start.40) | collective-permute-done | bytes 786464 | tf_op jit(solution)/shard_map/cond/branch_1_fun/ppermute | solution.py:919
  336.9 4.8 %collective-permute-done.37 = bf16[256,1024]{1,0:T(8,128)(2,1)S(1)} collective-permute-done((bf16[256,1024]{1,0:T(8,128)(2,1)S(1)}, bf16[256,1024]{1,0:T(8,128)(2,1)S(1)}, u32[]{:S(2)}, u32[]{:S(2)}) %collective-permute-start.37) | collective-permute-done | bytes 524320 | tf_op jit(solution)/shard_map/cond/branch_1_fun/ppermute | solution.py:907
  344.1 40.9 %conditional.25 = (bf16[8,48,1536]{2,1,0:T(8,128)(2,1)}, bf16[8,48,1024]{2,1,0:T(8,128)(2,1)}, f32[1,1536]{1,0:T(1,128)S(1)}, bf16[256,1536]{1,0:T(8,128)(2,1)},...) conditional(s32[]{:T(128)} %convert_element_type.130, () %tuple.149, ...), branch_computations={%region_25.26_spmd, %region_26.27_spmd} | conditional | flops 1515192320 | bytes 41431392 | solution.py:1124
  355.4 7.9 %collective-permute-start.44 = (bf16[512,1024]{1,0:T(8,128)(2,1)}, bf16[512,1024]{1,0:T(8,128)(2,1)}, u32[]{:S(2)}, u32[]{:S(2)}) collective-permute-start(bf16[512,1024]{1,0:T(8,128)(2,1)} %pad_maximum_fusion.4), channel_id=1, source_target_pairs={{0,8},{8,0},{16,24},{24,16},{1,9},{9,1},{17,25},{25,17},{2,10},{10... | collective-permute-start | bytes 3145736 | tf_op jit(solution)/shard_map/cond/branch_1_fun/ppermute | solution.py:901
  365.5 9.0 %branch_1_fun.53 = (f32[256,1536]{1,0:T(8,128)}, f32[1,1536]{1,0:T(1,128)S(1)}) custom-call(bf16[256,1536]{1,0:T(8,128)(2,1)S(1)} %get-tuple-element.683.refs_4_.dq_ref, bf16[256,1024]{1,0:T(8,128)(2,1)S(1)} %get-tuple-element.685.refs_4_.dkv_ref, bf16[1536,1536]{1,0:T(8,128)(2,1)} %get-tuple-element.686.wq_ref, ...), custom_call_target="tpu_custom_call" | custom-call | flops 503316480 | bytes 3670016 | tf_op jit(solution)/shard_map/cond/branch_1_fun/pallas_call | solution.py:324
  378.5 5.2 %branch_1_fun.51 = bf16[384,1536]{1,0:T(8,128)(2,1)} custom-call(s32[4]{0:T(128)S(1)} %get-tuple-element.678.pos, bf16[256,1536]{1,0:T(8,128)(2,1)} %get-tuple-element.679.refs_0_, bf16[256,1536]{1,0:T(8,128)(2,1)} %get-tuple-element.680.refs_1_, bf16[256,1536]{1,0:T(8,128)(2,1)} %get-tuple-element.681.refs_2_, ...), custom_call_target="tpu_custom_call" | custom-call | flops 603979776 | bytes 1048576 | tf_op jit(solution)/shard_map/cond/branch_1_fun/pallas_call | solution.py:663
  385.0 40.9 %conditional.26 = (bf16[4,48,4096]{2,1,0:T(8,128)(2,1)S(1)}, bf16[4,48,4096]{2,1,0:T(8,128)(2,1)}, bf16[6,128,768]{2,1,0:T(8,128)(2,1)}, bf16[80,2048]{1,0:T(8,1...) conditional(s32[]{:T(128)} %convert_element_type.130, ...), branch_computations={%region_27.28_spmd, %region_28.29_spmd} | conditional | flops 12586004 | bytes 34755032 | solution.py:1124
  394.7 6.7 %all-to-all-start = ((f32[32,2,48]{2,1,0:T(2,128)}), f32[32,2,48]{2,1,0:T(2,128)}, u32[]{:S(2)}, u32[]{:S(2)}) async-start(f32[32,2,48]{2,1,0:T(2,128)} %pad_maximum_fusion.6), calls=%async_computation | async-start | bytes 65536 | tf_op jit(solution)/shard_map/cond/branch_1_fun/all_to_all | solution.py:1334
  407.4 18.2 %all-to-all-done = f32[32,2,48]{2,1,0:T(2,128)} async-done(((f32[32,2,48]{2,1,0:T(2,128)}), f32[32,2,48]{2,1,0:T(2,128)}, u32[]{:S(2)}, u32[]{:S(2)}) %all-to-all-start) | async-done | bytes 12320 | tf_op jit(solution)/shard_map/cond/branch_1_fun/all_to_all | solution.py:1334
  425.9 44.7 %conditional.27 = (f32[2,48]{1,0:T(2,128)}, f32[48,1024]{1,0:T(8,128)}, f32[48,1024]{1,0:T(8,128)}, f32[32,1536]{1,0:T(8,128)}, f32[48,1536]{1,0:T(8,128)}, /*in...) conditional(s32[]{:T(128)} %convert_element_type.130, ...), branch_computations={%region_29.30_spmd, %region_30.32_spmd} | conditional | flops 2976 | bytes 16270620 | solution.py:1124
  436.6 6.2 %branch_1_fun.58 = (bf16[3,128,768]{2,1,0:T(8,128)(2,1)}, bf16[3,128,768]{2,1,0:T(8,128)(2,1)}, bf16[3,128,768]{2,1,0:T(8,128)(2,1)}, bf16[3,128,768]{2,1,0:T(8,128)(2,1)}) custom-call(s32[4]{0:T(128)S(1)} %get-tuple-element.722.pos, bf16[6,128,3072]{2,1,0:T(8,128)(2,1)} %get-tuple-element.733.refs_0_.refs_4_.refs_8_.refs_12_, ...), custom_call_target="tpu_custom_call" | custom-call | bytes 2097152 | tf_op jit(solution)/shard_map/cond/branch_1_fun/pallas_call | solution.py:754
  442.8 8.8 %branch_1_fun.59 = (f32[2,384,512]{2,1,0:T(8,128)}, f32[2,384,512]{2,1,0:T(8,128)}, f32[2,512,384]{2,1,0:T(8,128)}) custom-call(bf16[384,768]{1,0:T(8,128)(2,1)} %bitcast.90, bf16[384,768]{1,0:T(8,128)(2,1)} %bitcast.91, bf16[384,768]{1,0:T(8,128)(2,1)} %bitcast.92, bf16[384,768]{1,0:T(8,128)(2,1)} %bitcast.93), custom_call_target="tpu_custom_call" | custom-call | bytes 2097152 | tf_op jit(solution)/shard_map/cond/branch_1_fun/pallas_call | solution.py:814
  451.6 11.5 %collective-permute-done.53.refs_2_ = bf16[48,4096]{1,0:T(8,128)(2,1)S(1)} collective-permute-done((bf16[48,4096]{1,0:T(8,128)(2,1)}, bf16[48,4096]{1,0:T(8,128)(2,1)S(1)}, u32[]{:S(2)}, u32[]{:S(2)}) %collective-permute-start.53) | collective-permute-done | bytes 393248 | tf_op jit(solution)/shard_map/cond/branch_1_fun/ppermute | solution.py:907
  463.1 4.4 collective-permute-done.54.refs_3_
  (228 shorter events, 151.0 us)
Async XLA Ops:
  11.7 21.3 %collective-permute-start.56 = (bf16[256,1024]{1,0:T(8,128)(2,1)}, bf16[256,1024]{1,0:T(8,128)(2,1)}, u32[]{:S(2)}, u32[]{:S(2)}) collective-permute-start(bf16[256,1024]{1,0:T(8,128)(2,1)} %get-tuple-element.1108), channel_id=1, source_target_pairs={{0,8},{8,0},{16,24},{24,16},{1,9},{9,1},{17,25},{25,17},{2,10},{10... | collective-permute-start | bytes 1572872 | tf_op jit(solution)/shard_map/cond/branch_1_fun/ppermute | solution.py:901
  13.6 19.8 %collective-permute-start.58 = (bf16[256,1664]{1,0:T(8,128)(2,1)}, bf16[256,1664]{1,0:T(8,128)(2,1)}, u32[]{:S(2)}, u32[]{:S(2)}) collective-permute-start(bf16[256,1664]{1,0:T(8,128)(2,1)} %get-tuple-element.449), channel_id=1, source_target_pairs={{0,2},{1,3},{2,4},{3,5},{4,6},{5,7},{6,0},{7,1},{8,14},{9,15},{10,... | collective-permute-start | bytes 2555912 | tf_op jit(solution)/shard_map/cond/branch_1_fun/ppermute | solution.py:919
  33.5 25.3 %collective-permute-start.2 = (bf16[256,1664]{1,0:T(8,128)(2,1)}, bf16[256,1664]{1,0:T(8,128)(2,1)}, u32[]{:S(2)}, u32[]{:S(2)}) collective-permute-start(bf16[256,1664]{1,0:T(8,128)(2,1)} %get-tuple-element.469), channel_id=1, source_target_pairs={{0,2},{1,3},{2,4},{3,5},{4,6},{5,7},{6,0},{7,1},{8,14},{9,15},{10,... | collective-permute-start | bytes 2555912 | tf_op jit(solution)/shard_map/cond/branch_1_fun/ppermute | solution.py:919
  37.2 18.9 %collective-permute-start.3 = (bf16[256,1536]{1,0:T(8,128)(2,1)}, bf16[256,1536]{1,0:T(8,128)(2,1)}, u32[]{:S(2)}, u32[]{:S(2)}) collective-permute-start(bf16[256,1536]{1,0:T(8,128)(2,1)} %get-tuple-element.470), channel_id=1, source_target_pairs={{0,1},{1,0},{2,3},{3,2},{4,5},{5,4},{6,7},{7,6},{8,9},{9,8},{10,11... | collective-permute-start | bytes 2359304 | tf_op jit(solution)/shard_map/cond/branch_1_fun/ppermute | solution.py:901
  39.2 19.5 %collective-permute-start.1 = (bf16[256,1536]{1,0:T(8,128)(2,1)}, bf16[256,1536]{1,0:T(8,128)(2,1)}, u32[]{:S(2)}, u32[]{:S(2)}) collective-permute-start(bf16[256,1536]{1,0:T(8,128)(2,1)} %get-tuple-element.468), channel_id=1, source_target_pairs={{0,16},{8,24},{16,0},{24,8},{1,17},{9,25},{17,1},{25,9},{2,18},{10... | collective-permute-start | bytes 2359304 | tf_op jit(solution)/shard_map/cond/branch_1_fun/ppermute | solution.py:907
  39.5 19.3 %collective-permute-start = (bf16[256,1536]{1,0:T(8,128)(2,1)}, bf16[256,1536]{1,0:T(8,128)(2,1)}, u32[]{:S(2)}, u32[]{:S(2)}) collective-permute-start(bf16[256,1536]{1,0:T(8,128)(2,1)} %get-tuple-element.468), channel_id=1, source_target_pairs={{0,8},{8,0},{16,24},{24,16},{1,9},{9,1},{17,25},{25,17},{2,10},{10... | collective-permute-start | bytes 2359304 | tf_op jit(solution)/shard_map/cond/branch_1_fun/ppermute | solution.py:901
  58.8 24.3 %collective-permute-start.7 = (bf16[512,1024]{1,0:T(8,128)(2,1)}, bf16[512,1024]{1,0:T(8,128)(2,1)}, u32[]{:S(2)}, u32[]{:S(2)}) collective-permute-start(bf16[512,1024]{1,0:T(8,128)(2,1)} %get-tuple-element.483), channel_id=1, source_target_pairs={{0,1},{1,0},{2,3},{3,2},{4,5},{5,4},{6,7},{7,6},{8,9},{9,8},{10,11... | collective-permute-start | bytes 3145736 | tf_op jit(solution)/shard_map/cond/branch_1_fun/ppermute | solution.py:901
  60.2 18.9 %collective-permute-start.9 = (bf16[256,1536]{1,0:T(8,128)(2,1)}, bf16[256,1536]{1,0:T(8,128)(2,1)}, u32[]{:S(2)}, u32[]{:S(2)}) collective-permute-start(bf16[256,1536]{1,0:T(8,128)(2,1)} %get-tuple-element.485), channel_id=1, source_target_pairs={{0,16},{8,24},{16,0},{24,8},{1,17},{9,25},{17,1},{25,9},{2,18},{10... | collective-permute-start | bytes 2359304 | tf_op jit(solution)/shard_map/cond/branch_1_fun/ppermute | solution.py:907
  60.4 18.7 %collective-permute-start.5 = (bf16[256,1536]{1,0:T(8,128)(2,1)S(1)}, bf16[256,1536]{1,0:T(8,128)(2,1)}, u32[]{:S(2)}, u32[]{:S(2)}) collective-permute-start(bf16[256,1536]{1,0:T(8,128)(2,1)S(1)} %get-tuple-element.472.refs_0_), channel_id=1, source_target_pairs={{0,2},{1,3},{2,4},{3,5},{4,6},{5,7},{6,0},{7,1},{8,14},{9,15},{10,... | collective-permute-start | bytes 2359304 | tf_op jit(solution)/shard_map/cond/branch_1_fun/ppermute | solution.py:919
  83.2 24.9 %collective-permute-start.11 = (bf16[512,1024]{1,0:T(8,128)(2,1)}, bf16[512,1024]{1,0:T(8,128)(2,1)}, u32[]{:S(2)}, u32[]{:S(2)}) collective-permute-start(bf16[512,1024]{1,0:T(8,128)(2,1)} %get-tuple-element.506), channel_id=1, source_target_pairs={{0,1},{1,0},{2,3},{3,2},{4,5},{5,4},{6,7},{7,6},{8,9},{9,8},{10,11... | collective-permute-start | bytes 3145736 | tf_op jit(solution)/shard_map/cond/branch_1_fun/ppermute | solution.py:901
  83.6 24.6 %collective-permute-start.12 = (bf16[512,1024]{1,0:T(8,128)(2,1)}, bf16[512,1024]{1,0:T(8,128)(2,1)}, u32[]{:S(2)}, u32[]{:S(2)}) collective-permute-start(bf16[512,1024]{1,0:T(8,128)(2,1)} %get-tuple-element.507), channel_id=1, source_target_pairs={{0,8},{8,0},{16,24},{24,16},{1,9},{9,1},{17,25},{25,17},{2,10},{10... | collective-permute-start | bytes 3145736 | tf_op jit(solution)/shard_map/cond/branch_1_fun/ppermute | solution.py:901
  85.5 22.6 %collective-permute-start.10 = (bf16[256,1536]{1,0:T(8,128)(2,1)}, bf16[256,1536]{1,0:T(8,128)(2,1)}, u32[]{:S(2)}, u32[]{:S(2)}) collective-permute-start(bf16[256,1536]{1,0:T(8,128)(2,1)} %get-tuple-element.486), channel_id=1, source_target_pairs={{0,2},{1,3},{2,4},{3,5},{4,6},{5,7},{6,0},{7,1},{8,14},{9,15},{10,... | collective-permute-start | bytes 2359304 | tf_op jit(solution)/shard_map/cond/branch_1_fun/ppermute | solution.py:919
  85.8 22.3 %collective-permute-start.13 = (bf16[256,1536]{1,0:T(8,128)(2,1)}, bf16[256,1536]{1,0:T(8,128)(2,1)}, u32[]{:S(2)}, u32[]{:S(2)}) collective-permute-start(bf16[256,1536]{1,0:T(8,128)(2,1)} %get-tuple-element.508), channel_id=1, source_target_pairs={{0,8},{8,0},{16,24},{24,16},{1,9},{9,1},{17,25},{25,17},{2,10},{10... | collective-permute-start | bytes 2359304 | tf_op jit(solution)/shard_map/cond/branch_1_fun/ppermute | solution.py:901
  87.1 21.0 %collective-permute-start.14 = (bf16[256,1536]{1,0:T(8,128)(2,1)}, bf16[256,1536]{1,0:T(8,128)(2,1)}, u32[]{:S(2)}, u32[]{:S(2)}) collective-permute-start(bf16[256,1536]{1,0:T(8,128)(2,1)} %get-tuple-element.509), channel_id=1, source_target_pairs={{0,8},{8,0},{16,24},{24,16},{1,9},{9,1},{17,25},{25,17},{2,10},{10... | collective-permute-start | bytes 2359304 | tf_op jit(solution)/shard_map/cond/branch_1_fun/ppermute | solution.py:901
  108.2 27.1 %collective-permute-start.16 = (bf16[16,80,2048]{2,1,0:T(8,128)(2,1)}, bf16[16,80,2048]{2,1,0:T(8,128)(2,1)}, u32[]{:S(2)}, u32[]{:S(2)}) collective-permute-start(bf16[16,80,2048]{2,1,0:T(8,128)(2,1)} %get-tuple-element.535), channel_id=1, source_target_pairs={{0,8},{8,0},{16,24},{24,16},{1,9},{9,1},{17,25},{25,17},{2,10},{10... | collective-permute-start | bytes 15728648 | tf_op jit(solution)/shard_map/cond/branch_1_fun/ppermute | solution.py:901
  109.2 31.0 %collective-permute-start.17 = (bf16[512,1024]{1,0:T(8,128)(2,1)}, bf16[512,1024]{1,0:T(8,128)(2,1)}, u32[]{:S(2)}, u32[]{:S(2)}) collective-permute-start(bf16[512,1024]{1,0:T(8,128)(2,1)} %get-tuple-element.538), channel_id=1, source_target_pairs={{0,1},{1,0},{2,3},{3,2},{4,5},{5,4},{6,7},{7,6},{8,9},{9,8},{10,11... | collective-permute-start | bytes 3145736 | tf_op jit(solution)/shard_map/cond/branch_1_fun/ppermute | solution.py:901
  110.0 30.2 %collective-permute-start.18 = (bf16[512,1024]{1,0:T(8,128)(2,1)}, bf16[512,1024]{1,0:T(8,128)(2,1)}, u32[]{:S(2)}, u32[]{:S(2)}) collective-permute-start(bf16[512,1024]{1,0:T(8,128)(2,1)} %get-tuple-element.539), channel_id=1, source_target_pairs={{0,8},{8,0},{16,24},{24,16},{1,9},{9,1},{17,25},{25,17},{2,10},{10... | collective-permute-start | bytes 3145736 | tf_op jit(solution)/shard_map/cond/branch_1_fun/ppermute | solution.py:901
  110.3 29.9 %collective-permute-start.15 = (bf16[256,1536]{1,0:T(8,128)(2,1)}, bf16[256,1536]{1,0:T(8,128)(2,1)}, u32[]{:S(2)}, u32[]{:S(2)}) collective-permute-start(bf16[256,1536]{1,0:T(8,128)(2,1)} %get-tuple-element.510.refs_1_), channel_id=1, source_target_pairs={{0,2},{1,3},{2,4},{3,5},{4,6},{5,7},{6,0},{7,1},{8,14},{9,15},{10,... | collective-permute-start | bytes 2359304 | tf_op jit(solution)/shard_map/cond/branch_1_fun/ppermute | solution.py:919
  140.7 22.1 %collective-permute-start.19 = (bf16[256,1664]{1,0:T(8,128)(2,1)}, bf16[256,1664]{1,0:T(8,128)(2,1)S(1)}, u32[]{:S(2)}, u32[]{:S(2)}) collective-permute-start(bf16[256,1664]{1,0:T(8,128)(2,1)} %get-tuple-element.542), channel_id=1, source_target_pairs={{0,2},{1,3},{2,4},{3,5},{4,6},{5,7},{6,0},{7,1},{8,14},{9,15},{10,... | collective-permute-start | bytes 2555912 | tf_op jit(solution)/shard_map/cond/branch_1_fun/ppermute | solution.py:919
  141.4 54.7 %collective-permute-start.21 = (bf16[2,160,2048]{2,1,0:T(8,128)(2,1)}, bf16[2,160,2048]{2,1,0:T(8,128)(2,1)}, u32[]{:S(2)}, u32[]{:S(2)}) collective-permute-start(bf16[2,160,2048]{2,1,0:T(8,128)(2,1)} %get-tuple-element.581), channel_id=1, source_target_pairs={{0,16},{8,24},{16,0},{24,8},{1,17},{9,25},{17,1},{25,9},{2,18},{10... | collective-permute-start | bytes 3932168 | tf_op jit(solution)/shard_map/cond/branch_1_fun/ppermute | solution.py:907
  141.6 58.7 %collective-permute-start.22 = (bf16[2,160,2048]{2,1,0:T(8,128)(2,1)}, bf16[2,160,2048]{2,1,0:T(8,128)(2,1)}, u32[]{:S(2)}, u32[]{:S(2)}) collective-permute-start(bf16[2,160,2048]{2,1,0:T(8,128)(2,1)} %get-tuple-element.582), channel_id=1, source_target_pairs={{0,16},{8,24},{16,0},{24,8},{1,17},{9,25},{17,1},{25,9},{2,18},{10... | collective-permute-start | bytes 3932168 | tf_op jit(solution)/shard_map/cond/branch_1_fun/ppermute | solution.py:907
  202.7 20.8 %collective-permute-start.28 = (bf16[256,1536]{1,0:T(8,128)(2,1)}, bf16[256,1536]{1,0:T(8,128)(2,1)}, u32[]{:S(2)}, u32[]{:S(2)}) collective-permute-start(bf16[256,1536]{1,0:T(8,128)(2,1)} %add_convert_fusion), channel_id=1, source_target_pairs={{0,6},{1,7},{2,0},{3,1},{4,2},{5,3},{6,4},{7,5},{8,10},{9,11},{10,... | collective-permute-start | bytes 2359304 | tf_op jit(solution)/shard_map/cond/branch_1_fun/ppermute | solution.py:919
  223.6 20.6 %collective-permute-start.31 = (bf16[6,128,3072]{2,1,0:T(8,128)(2,1)}, bf16[6,128,3072]{2,1,0:T(8,128)(2,1)}, u32[]{:S(2)}, u32[]{:S(2)}) collective-permute-start(bf16[6,128,3072]{2,1,0:T(8,128)(2,1)} %get-tuple-element.601), channel_id=1, source_target_pairs={{0,8},{8,0},{16,24},{24,16},{1,9},{9,1},{17,25},{25,17},{2,10},{10... | collective-permute-start | bytes 14155784 | tf_op jit(solution)/shard_map/cond/branch_1_fun/ppermute | solution.py:901
  227.0 20.3 %collective-permute-start.30 = (bf16[256,1536]{1,0:T(8,128)(2,1)S(1)}, bf16[256,1536]{1,0:T(8,128)(2,1)}, u32[]{:S(2)}, u32[]{:S(2)}) collective-permute-start(bf16[256,1536]{1,0:T(8,128)(2,1)S(1)} %add_convert_fusion.1), channel_id=1, source_target_pairs={{0,6},{1,7},{2,0},{3,1},{4,2},{5,3},{6,4},{7,5},{8,10},{9,11},{10,... | collective-permute-start | bytes 2359304 | tf_op jit(solution)/shard_map/cond/branch_1_fun/ppermute | solution.py:919
  228.3 19.0 %collective-permute-start.32 = (bf16[2,80,2048]{2,1,0:T(8,128)(2,1)}, bf16[2,80,2048]{2,1,0:T(8,128)(2,1)}, u32[]{:S(2)}, u32[]{:S(2)}) collective-permute-start(bf16[2,80,2048]{2,1,0:T(8,128)(2,1)} %get-tuple-element.610), channel_id=1, source_target_pairs={{0,1},{1,0},{2,3},{3,2},{4,5},{5,4},{6,7},{7,6},{8,9},{9,8},{10,11... | collective-permute-start | bytes 1966088 | tf_op jit(solution)/shard_map/cond/branch_1_fun/ppermute | solution.py:901
  247.4 31.1 %collective-permute-start.34 = (bf16[6,128,3072]{2,1,0:T(8,128)(2,1)}, bf16[6,128,3072]{2,1,0:T(8,128)(2,1)}, u32[]{:S(2)}, u32[]{:S(2)}) collective-permute-start(bf16[6,128,3072]{2,1,0:T(8,128)(2,1)} %get-tuple-element.625), channel_id=1, source_target_pairs={{0,8},{8,0},{16,24},{24,16},{1,9},{9,1},{17,25},{25,17},{2,10},{10... | collective-permute-start | bytes 14155784 | tf_op jit(solution)/shard_map/cond/branch_1_fun/ppermute | solution.py:901
  249.4 29.0 %collective-permute-start.35 = (bf16[6,128,768]{2,1,0:T(8,128)(2,1)}, bf16[6,128,768]{2,1,0:T(8,128)(2,1)}, u32[]{:S(2)}, u32[]{:S(2)}) collective-permute-start(bf16[6,128,768]{2,1,0:T(8,128)(2,1)} %get-tuple-element.626), channel_id=1, source_target_pairs={{0,1},{1,0},{2,3},{3,2},{4,5},{5,4},{6,7},{7,6},{8,9},{9,8},{10,11... | collective-permute-start | bytes 3538952 | tf_op jit(solution)/shard_map/cond/branch_1_fun/ppermute | solution.py:901
  279.3 27.9 %collective-permute-start.26 = (bf16[6,128,768]{2,1,0:T(8,128)(2,1)}, bf16[6,128,768]{2,1,0:T(8,128)(2,1)}, u32[]{:S(2)}, u32[]{:S(2)}) collective-permute-start(bf16[6,128,768]{2,1,0:T(8,128)(2,1)} %get-tuple-element.655), channel_id=1, source_target_pairs={{0,1},{1,0},{2,3},{3,2},{4,5},{5,4},{6,7},{7,6},{8,9},{9,8},{10,11... | collective-permute-start | bytes 3538952 | tf_op jit(solution)/shard_map/cond/branch_1_fun/ppermute | solution.py:901
  280.4 26.8 %collective-permute-start.25 = (bf16[256,1536]{1,0:T(8,128)(2,1)}, bf16[256,1536]{1,0:T(8,128)(2,1)}, u32[]{:S(2)}, u32[]{:S(2)}) collective-permute-start(bf16[256,1536]{1,0:T(8,128)(2,1)} %get-tuple-element.654), channel_id=1, source_target_pairs={{0,6},{1,7},{2,0},{3,1},{4,2},{5,3},{6,4},{7,5},{8,10},{9,11},{10,... | collective-permute-start | bytes 2359304 | tf_op jit(solution)/shard_map/cond/branch_1_fun/ppermute | solution.py:919
  280.4 26.8 %collective-permute-start.24 = (bf16[256,1536]{1,0:T(8,128)(2,1)}, bf16[256,1536]{1,0:T(8,128)(2,1)}, u32[]{:S(2)}, u32[]{:S(2)}) collective-permute-start(bf16[256,1536]{1,0:T(8,128)(2,1)} %get-tuple-element.1312), channel_id=1, source_target_pairs={{0,16},{8,24},{16,0},{24,8},{1,17},{9,25},{17,1},{25,9},{2,18},{10... | collective-permute-start | bytes 2359304 | tf_op jit(solution)/shard_map/cond/branch_1_fun/ppermute | solution.py:907
  280.6 26.6 %collective-permute-start.23 = (bf16[256,1536]{1,0:T(8,128)(2,1)}, bf16[256,1536]{1,0:T(8,128)(2,1)}, u32[]{:S(2)}, u32[]{:S(2)}) collective-permute-start(bf16[256,1536]{1,0:T(8,128)(2,1)} %get-tuple-element.1312), channel_id=1, source_target_pairs={{0,8},{8,0},{16,24},{24,16},{1,9},{9,1},{17,25},{25,17},{2,10},{10... | collective-permute-start | bytes 2359304 | tf_op jit(solution)/shard_map/cond/branch_1_fun/ppermute | solution.py:901
  286.4 20.7 %collective-permute-start.27 = (bf16[80,2048]{1,0:T(8,128)(2,1)}, bf16[80,2048]{1,0:T(8,128)(2,1)}, u32[]{:S(2)}, u32[]{:S(2)}) collective-permute-start(bf16[80,2048]{1,0:T(8,128)(2,1)} %get-tuple-element.656), channel_id=1, source_target_pairs={{0,2},{1,3},{2,4},{3,5},{4,6},{5,7},{6,0},{7,1},{8,10},{9,11},{10,... | collective-permute-start | bytes 983048 | tf_op jit(solution)/shard_map/cond/branch_1_fun/ppermute | solution.py:907
  314.2 20.1 %collective-permute-start.40 = (bf16[256,1536]{1,0:T(8,128)(2,1)}, bf16[256,1536]{1,0:T(8,128)(2,1)}, u32[]{:S(2)}, u32[]{:S(2)}) collective-permute-start(bf16[256,1536]{1,0:T(8,128)(2,1)} %add_convert_fusion.5), channel_id=1, source_target_pairs={{0,6},{1,7},{2,0},{3,1},{4,2},{5,3},{6,4},{7,5},{8,10},{9,11},{10,... | collective-permute-start | bytes 2359304 | tf_op jit(solution)/shard_map/cond/branch_1_fun/ppermute | solution.py:919
  314.2 28.9 %collective-permute-start.41 = (bf16[6,128,768]{2,1,0:T(8,128)(2,1)}, bf16[6,128,768]{2,1,0:T(8,128)(2,1)}, u32[]{:S(2)}, u32[]{:S(2)}) collective-permute-start(bf16[6,128,768]{2,1,0:T(8,128)(2,1)} %get-tuple-element.677), channel_id=1, source_target_pairs={{0,1},{1,0},{2,3},{3,2},{4,5},{5,4},{6,7},{7,6},{8,9},{9,8},{10,11... | collective-permute-start | bytes 3538952 | tf_op jit(solution)/shard_map/cond/branch_1_fun/ppermute | solution.py:901
  314.5 28.5 %collective-permute-start.38 = (bf16[256,1536]{1,0:T(8,128)(2,1)S(1)}, bf16[256,1536]{1,0:T(8,128)(2,1)}, u32[]{:S(2)}, u32[]{:S(2)}) collective-permute-start(bf16[256,1536]{1,0:T(8,128)(2,1)S(1)} %get-tuple-element.659), channel_id=1, source_target_pairs={{0,16},{8,24},{16,0},{24,8},{1,17},{9,25},{17,1},{25,9},{2,18},{10... | collective-permute-start | bytes 2359304 | tf_op jit(solution)/shard_map/cond/branch_1_fun/ppermute | solution.py:907
  346.8 31.7 %collective-permute-start.42 = (bf16[512,1536]{1,0:T(8,128)(2,1)}, bf16[512,1536]{1,0:T(8,128)(2,1)}, u32[]{:S(2)}, u32[]{:S(2)}) collective-permute-start(bf16[512,1536]{1,0:T(8,128)(2,1)} %pad_maximum_fusion.3), channel_id=1, source_target_pairs={{0,8},{8,0},{16,24},{24,16},{1,9},{9,1},{17,25},{25,17},{2,10},{10... | collective-permute-start | bytes 4718600 | tf_op jit(solution)/shard_map/cond/branch_1_fun/ppermute | solution.py:901
  351.0 34.0 %collective-permute-start.46 = (bf16[6,128,768]{2,1,0:T(8,128)(2,1)}, bf16[6,128,768]{2,1,0:T(8,128)(2,1)}, u32[]{:S(2)}, u32[]{:S(2)}) collective-permute-start(bf16[6,128,768]{2,1,0:T(8,128)(2,1)} %get-tuple-element.694), channel_id=1, source_target_pairs={{0,1},{1,0},{2,3},{3,2},{4,5},{5,4},{6,7},{7,6},{8,9},{9,8},{10,11... | collective-permute-start | bytes 3538952 | tf_op jit(solution)/shard_map/cond/branch_1_fun/ppermute | solution.py:901
  352.1 32.9 %collective-permute-start.47 = (bf16[6,128,768]{2,1,0:T(8,128)(2,1)}, bf16[6,128,768]{2,1,0:T(8,128)(2,1)}, u32[]{:S(2)}, u32[]{:S(2)}) collective-permute-start(bf16[6,128,768]{2,1,0:T(8,128)(2,1)} %get-tuple-element.695), channel_id=1, source_target_pairs={{0,16},{8,24},{16,0},{24,8},{1,17},{9,25},{17,1},{25,9},{2,18},{10... | collective-permute-start | bytes 3538952 | tf_op jit(solution)/shard_map/cond/branch_1_fun/ppermute | solution.py:907
  355.4 19.2 %collective-permute-start.44 = (bf16[512,1024]{1,0:T(8,128)(2,1)}, bf16[512,1024]{1,0:T(8,128)(2,1)}, u32[]{:S(2)}, u32[]{:S(2)}) collective-permute-start(bf16[512,1024]{1,0:T(8,128)(2,1)} %pad_maximum_fusion.4), channel_id=1, source_target_pairs={{0,8},{8,0},{16,24},{24,16},{1,9},{9,1},{17,25},{25,17},{2,10},{10... | collective-permute-start | bytes 3145736 | tf_op jit(solution)/shard_map/cond/branch_1_fun/ppermute | solution.py:901
  363.2 21.7 %collective-permute-start.45 = (bf16[256,1536]{1,0:T(8,128)(2,1)}, bf16[256,1536]{1,0:T(8,128)(2,1)}, u32[]{:S(2)}, u32[]{:S(2)}) collective-permute-start(bf16[256,1536]{1,0:T(8,128)(2,1)} %get-tuple-element.693), channel_id=1, source_target_pairs={{0,6},{1,7},{2,0},{3,1},{4,2},{5,3},{6,4},{7,5},{8,10},{9,11},{10,... | collective-permute-start | bytes 2359304 | tf_op jit(solution)/shard_map/cond/branch_1_fun/ppermute | solution.py:919
  388.6 37.1 %collective-permute-start.48 = (bf16[4,48,4096]{2,1,0:T(8,128)(2,1)}, bf16[4,48,4096]{2,1,0:T(8,128)(2,1)}, u32[]{:S(2)}, u32[]{:S(2)}) collective-permute-start(bf16[4,48,4096]{2,1,0:T(8,128)(2,1)} %get-tuple-element.1093), channel_id=1, source_target_pairs={{0,1},{1,0},{2,3},{3,2},{4,5},{5,4},{6,7},{7,6},{8,9},{9,8},{10,11... | collective-permute-start | bytes 4718600 | tf_op jit(solution)/shard_map/cond/branch_1_fun/ppermute | solution.py:901
  393.5 32.2 %collective-permute-start.49 = (bf16[6,128,768]{2,1,0:T(8,128)(2,1)}, bf16[6,128,768]{2,1,0:T(8,128)(2,1)}, u32[]{:S(2)}, u32[]{:S(2)}) collective-permute-start(bf16[6,128,768]{2,1,0:T(8,128)(2,1)} %branch_1_fun.54), channel_id=1, source_target_pairs={{0,16},{8,24},{16,0},{24,8},{1,17},{9,25},{17,1},{25,9},{2,18},{10... | collective-permute-start | bytes 3538952 | tf_op jit(solution)/shard_map/cond/branch_1_fun/ppermute | solution.py:907
  394.7 31.0 %all-to-all-start = ((f32[32,2,48]{2,1,0:T(2,128)}), f32[32,2,48]{2,1,0:T(2,128)}, u32[]{:S(2)}, u32[]{:S(2)}) async-start(f32[32,2,48]{2,1,0:T(2,128)} %pad_maximum_fusion.6), calls=%async_computation | async-start | bytes 65536 | tf_op jit(solution)/shard_map/cond/branch_1_fun/all_to_all | solution.py:1334
  401.4 24.3 %collective-permute-start.50 = (bf16[80,2048]{1,0:T(8,128)(2,1)}, bf16[80,2048]{1,0:T(8,128)(2,1)}, u32[]{:S(2)}, u32[]{:S(2)}) collective-permute-start(bf16[80,2048]{1,0:T(8,128)(2,1)} %get-tuple-element.705), channel_id=1, source_target_pairs={{0,4},{1,5},{2,6},{3,7},{4,0},{5,1},{6,2},{7,3},{8,12},{9,13},{10,... | collective-permute-start | bytes 983048 | tf_op jit(solution)/shard_map/cond/branch_1_fun/ppermute | solution.py:907
  403.7 22.0 %collective-permute-start.51 = (bf16[80,2048]{1,0:T(8,128)(2,1)}, bf16[80,2048]{1,0:T(8,128)(2,1)}, u32[]{:S(2)}, u32[]{:S(2)}) collective-permute-start(bf16[80,2048]{1,0:T(8,128)(2,1)} %get-tuple-element.706), channel_id=1, source_target_pairs={{0,6},{1,7},{2,0},{3,1},{4,2},{5,3},{6,4},{7,5},{8,14},{9,15},{10,... | collective-permute-start | bytes 983048 | tf_op jit(solution)/shard_map/cond/branch_1_fun/ppermute | solution.py:907
  429.3 22.3 %collective-permute-start.52 = (bf16[48,4096]{1,0:T(8,128)(2,1)}, bf16[48,4096]{1,0:T(8,128)(2,1)S(1)}, u32[]{:S(2)}, u32[]{:S(2)}) collective-permute-start(bf16[48,4096]{1,0:T(8,128)(2,1)} %bitcast.97), channel_id=1, source_target_pairs={{0,2},{1,3},{2,4},{3,5},{4,6},{5,7},{6,0},{7,1},{8,10},{9,11},{10,... | collective-permute-start | bytes 1179656 | tf_op jit(solution)/shard_map/cond/branch_1_fun/ppermute | solution.py:907
  429.3 33.8 %collective-permute-start.53 = (bf16[48,4096]{1,0:T(8,128)(2,1)}, bf16[48,4096]{1,0:T(8,128)(2,1)S(1)}, u32[]{:S(2)}, u32[]{:S(2)}) collective-permute-start(bf16[48,4096]{1,0:T(8,128)(2,1)} %bitcast.96), channel_id=1, source_target_pairs={{0,4},{1,5},{2,6},{3,7},{4,0},{5,1},{6,2},{7,3},{8,12},{9,13},{10,... | collective-permute-start | bytes 1179656 | tf_op jit(solution)/shard_map/cond/branch_1_fun/ppermute | solution.py:907
  432.3 35.1 %collective-permute-start.54 = (bf16[48,4096]{1,0:T(8,128)(2,1)}, bf16[48,4096]{1,0:T(8,128)(2,1)S(1)}, u32[]{:S(2)}, u32[]{:S(2)}) collective-permute-start(bf16[48,4096]{1,0:T(8,128)(2,1)} %bitcast.95), channel_id=1, source_target_pairs={{0,6},{1,7},{2,0},{3,1},{4,2},{5,3},{6,4},{7,5},{8,14},{9,15},{10,... | collective-permute-start | bytes 1179656 | tf_op jit(solution)/shard_map/cond/branch_1_fun/ppermute | solution.py:907
  (45 other events, 535.4 us)

commit v6 on v5

--- a/solution.py
+++ b/solution.py
@@ -369,8 +369,6 @@
             for part, x_ref, c_ref in zip(parts, x_refs, c_refs):
                 kept_refs[0][part, :] = x_ref[...]
                 kept_refs[1][part, :] = c_ref[...]
-                kept_refs[2][:, part] = jnp.transpose(x_ref[...])
-                kept_refs[3][:, part] = jnp.transpose(c_ref[:, :width])
 
     for part, x_ref, c_ref in zip(parts, x_refs, c_refs):
         x = x_ref[...]
@@ -437,14 +435,10 @@
         collected = [
             jax.ShapeDtypeStruct((all_rows, width), bf16),
             jax.ShapeDtypeStruct((all_rows, cs[0].shape[1]), bf16),
-            jax.ShapeDtypeStruct((width, all_rows), bf16),
-            jax.ShapeDtypeStruct((width, all_rows), bf16),
         ] + collected
         collected_specs = [
             pl.BlockSpec((taken, width), lambda i, _: (part, 0)),
             pl.BlockSpec((taken, cs[0].shape[1]), lambda i, _: (part, 0)),
-            pl.BlockSpec((width, taken), lambda i, _: (0, part)),
-            pl.BlockSpec((width, taken), lambda i, _: (0, part)),
         ] + collected_specs
     operands = [pos, *xs, *cs, *weights]
     aliases = {}
@@ -682,8 +676,8 @@
     high = sent_ref.shape[1]
 
     def write(left_refs, right_ref):
-        left = jnp.concatenate([ref[...] for ref in left_refs], axis=0)
-        total = dot(left, right_ref[...]).astype(bf16)
+        left = jnp.concatenate([ref[...] for ref in left_refs], axis=1)
+        total = dot_tn(left, right_ref[...]).astype(bf16)
         count = sent_ref.shape[0]
         for i in range(count):
             sent_ref[i] = total[i * high : (i + 1) * high]
@@ -698,15 +692,25 @@
     return high // 128 if high % 128 == 0 else 1
 
 
-def expert_halves(pos, rows_t, cot_t, dgu, hid, tile=512):
+def expert_halves(pos, rows_all, cot_all, dgu, hid, tile=512):
     n_ctx = lax.axis_size("ctx")
-    width, depth = rows_t.shape
+    depth, width = rows_all.shape
     high = width // n_ctx
     wide = dgu.shape[1] + hid.shape[1]
     steps = expert_steps(width)
+    if high % 128:
+        out = []
+        for side in (1, 0):
+            place = lambda y: (2 * y + (pos[1] + side) % 2) * high
+            pick = lambda v: jnp.concatenate(
+                [lax.dynamic_slice_in_dim(v, place(y), high, 1) for y in range(n_ctx // 2)], axis=1
+            )
+            parts = [dot_tn(pick(v), w).astype(bf16) for v, w in ((rows_all, dgu), (cot_all, hid))]
+            out.append(jnp.concatenate(parts, axis=1).reshape(n_ctx // 2 * steps, -1, wide))
+        return out
     tiles, down = dgu.shape[1] // tile, hid.shape[1] // tile
     left_specs = [
-        pl.BlockSpec((high, depth), functools.partial(lambda s, n, pos: (side_of(n_ctx // 2, s, pos), 0), s))
+        pl.BlockSpec((depth, high), functools.partial(lambda s, n, pos: (0, side_of(n_ctx // 2, s, pos)), s))
         for s in range(n_ctx)
     ]
     block = (n_ctx // 2 * steps, high // steps, tile)
@@ -725,7 +729,7 @@
         out_shape=[jax.ShapeDtypeStruct(block[:2] + (wide,), bf16)] * 2,
         compiler_params=params(),
         cost_estimate=cost(4 * depth * width * wide, 16 * 2**20),
-    )(pos, *[rows_t] * n_ctx, *[cot_t] * n_ctx, dgu, hid)
+    )(pos, *[rows_all] * n_ctx, *[cot_all] * n_ctx, dgu, hid)
 
 
 def sums_kernel(shape, only, extra, pos, *refs):
@@ -975,8 +979,8 @@
         self.rows, self.wide = kept.shape[1:]
         self.pair = lambda v: v.reshape(-1, 2 * self.rows, self.wide)
         self.terms = [self.pair(v) for v in (kept, got)]
-        self.together = 2 if self.levels % 2 == 0 else 1
-        self.steps = self.levels // self.together
+        self.together = 1
+        self.steps = self.levels
 
     def _sum(self, d, rows, inner, moved=()):
         at = lambda i, pos: lax.rem(pos[0] + d, self.outer) * self.steps + i
@@ -997,17 +1001,20 @@
             out.append(sums(self.pos, 1, outputs))
         return out
 
-    def second(self, moved):
+    def second(self, moved, first, last):
+        moved = [v[first:last] for v in moved]
         terms, block = self._sum(0, self.rows, lambda pos: 1 - pos[3], moved)
-        outputs = []
-        for k in range(self.steps):
-            part = [(v, functools.partial(lambda f, k, i, pos: f(k, pos), f, k)) for v, f, *o in terms if not o or o[0] == k]
-            outputs.append((bf16, block, part))
-        return sums(self.pos, 1, outputs)
+        later = lambda f: lambda i, pos: f(first + i, pos)
+        terms = [(v, f, *o) if o else (v, later(f)) for v, f, *o in terms]
+        return sums(self.pos, last - first, [(bf16, block, terms)])
 
     def total(self, moved, crossed):
         terms, block = self._sum(0, self.rows, lambda pos: pos[3], moved)
-        terms = terms + [(v, lambda i, pos: 0, k) for k, v in enumerate(crossed)]
+        at = 0
+        for v in crossed:
+            for k in range(v.shape[0]):
+                terms.append((v, functools.partial(lambda k, i, pos: k, k), at))
+                at += 1
         return sums(self.pos, self.steps, [(bf16, block, terms)])[0]
 
 
@@ -1228,7 +1235,7 @@
         moved = ring_step(cot_ring[2], 1)
         weights = [arranged(fetched), arranged(crossed + [over_core(fetched[4])])]
         half = levels // 2
-        arrived = [over_y(shared_sent, k) for k in range(len(shared_sent[0]))]
+        arrived = [over_y(shared_sent, k) for k in range(levels - 1)]
         out_a, grad_a, new = others(pos, kept[0], kept[1], weights, 0, 2, half, None)
         last = experts(pos, [rows_k], [moved], own_weights, 3, 4, kept, True, bf16)
         out_b, grad_b, new = others(pos, last[2][0], last[2][1], weights, 1, 2, half, new)
@@ -1238,27 +1245,29 @@
     shared_moved = [list(v) for v in zip(*got)]
     out_own += out_k
     grad_own += grad_k
-    rows_all, cot_all, rows_t, cot_t, hid_own, dgu_own = kept
+    rows_all, cot_all, hid_own, dgu_own = kept
     hid_other, dgu_other = kept_other
 
     def back_one():
         moved = ring_step(row_sum([grad_own[3], grad_other[3]]), -1)
-        parts = Shared(pos, shared_kept, shared_got).second(shared_moved)
-        crossed = [swap_inner(v, "exp") for v in parts[: len(parts) // 2]]
-        made = expert_halves(pos, rows_t, cot_t, dgu_other, hid_other)
-        return moved, made, crossed, parts[len(parts) // 2 :]
-
-    moved, (sent, kept_other), shared_crossed, shared_rest = region(back_one)
+        (part,) = Shared(pos, shared_kept, shared_got).second(shared_moved, 0, levels // 2)
+        made = expert_halves(pos, rows_all, cot_all, dgu_other, hid_other)
+        return moved, made, swap_inner(part, "exp"), over_y(shared_sent, levels - 1)
+
+    moved, (sent, kept_other), crossed, got = region(back_one)
+    shared_moved = [v + [w] for v, w in zip(shared_moved, got)]
+    shared_crossed = [crossed]
 
     def back_two():
         total = row_sum([grad_own[2], grad_other[2], moved])
         got = swap_inner(sent, "ctx")
-        crossed = [swap_inner(v, "exp") for v in shared_rest]
-        made = expert_halves(pos, rows_t, cot_t, dgu_own, hid_own)
-        return ring_step(total, -1), got, made, expert_pieces(pos, kept_other, got, [0])[0], crossed
-
-    moved_two, got_other, (sent_own, kept_own), piece, got = region(back_two)
-    shared_crossed = shared_crossed + got
+        (part,) = Shared(pos, shared_kept, shared_got).second(shared_moved, levels // 2, levels)
+        made = expert_halves(pos, rows_all, cot_all, dgu_own, hid_own)
+        piece = expert_pieces(pos, kept_other, got, [0])[0]
+        return ring_step(total, -1), got, made, piece, swap_inner(part, "exp")
+
+    moved_two, got_other, (sent_own, kept_own), piece, crossed = region(back_two)
+    shared_crossed.append(crossed)
 
     def back_three():
         total = row_sum([grad_own[1], grad_other[1], moved_two])

time: 480 us -> 485 us (1.010)
  the two profiles are of different devices: /device:TPU:9 before, /device:TPU:0 now
where the time goes in v6:
time: 485 us; the launch traced here: 478 us
  Pallas kernels  254 us (52%)
  waiting for transfers between devices  88.1 us (18%)
  starting transfers between devices  59 us (12%)
  other arithmetic  35 us (7%)
  local copies, waits for them, and re-layouts  18.8 us (4%)
  loops' own time  17.3 us (4%)
  matrix products  4.87 us (1%)
    pallas_call x4, Pallas kernels, experts(): pl.pallas_call(functools.partial(experts_kernel, count, per, gated, extra...  56.1 us
    ppermute x19, waiting for transfers between devices, shift_outer(): return lax.ppermute(value, axis, perm)  51.3 us
    pallas_call x10, Pallas kernels, sums(): pl.pallas_call(functools.partial(sums_kernel, [len(terms) for _, _, terms...  42.5 us
    pallas_call x2, Pallas kernels, others(): pl.pallas_call(functools.partial(others_kernel, sets, per, len(bands), ex...  37.2 us
    pallas_call x2, Pallas kernels, expert_halves(): pl.pallas_call(functools.partial(expert_halves_kernel, n_ctx, tiles), gri...  32.2 us
    ppermute x19, starting transfers between devices, shift_outer(): return lax.ppermute(value, axis, perm)  20.6 us
    ppermute x31, starting transfers between devices, swap_inner(): return lax.ppermute(value, axis, [(i, i ^ 1) for i in range(size)])  20.2 us
    convert_element_type x8, other arithmetic, row_sum(): return total.astype(kind)  18.8 us
  transfers between devices with their start and end apart: 63, of which 19 were waited for; matrix products, arithmetic and copies ran while one was open for 9% of the time, Pallas kernels for 51%

profile of v6, /device:TPU:0, one launch (start us, length us, event | category | flops | bytes accessed | tf_op | source)
XLA Modules:
  0.0 478.1 jit_solution(6154466472835035655)
XLA Ops:
  6.0 32.1 %conditional.14 = (bf16[256,1536]{1,0:T(8,128)(2,1)}, bf16[256,1024]{1,0:T(8,128)(2,1)}, bf16[256,1024]{1,0:T(8,128)(2,1)}, bf16[256,1024]{1,0:T(8,128)(2,1)}, b...) conditional(s32[]{:T(128)} %convert_element_type.130, ...), branch_computations={%region_3.4_spmd, %region_4.5_spmd} | conditional | flops 1415970816 | bytes 48771484 | solution.py:1131
  6.6 5.1 %branch_1_fun.31 = (bf16[256,1536]{1,0:T(8,128)(2,1)}, bf16[256,1024]{1,0:T(8,128)(2,1)}) custom-call(bf16[256,1536]{1,0:T(8,128)(2,1)} %get-tuple-element.448.x_ref, f32[1,1536]{1,0:T(1,128)} %reshape.111.gain_ref, bf16[1536,512]{1,0:T(8,128)(2,1)} %get-tuple-element.450.wk_ref, bf16[1536,512]{1,0:T(8,128)(2,1)} %get-tuple-element.451.wv_ref), custom_call_target="tpu_custom_call" | custom-call | flops 201326592 | bytes 1310720 | tf_op jit(solution)/shard_map/cond/branch_1_fun/pallas_call | solution.py:66
  23.3 4.3 collective-permute-done.57
  28.7 4.9 %convolution_convert_fusion = bf16[256,1536]{1,0:T(8,128)(2,1)} fusion(bf16[256,1536]{1,0:T(8,128)(2,1)} %get-tuple-element.1108, bf16[1536,1536]{1,0:T(8,128)(2,1)} %get-tuple-element.454), kind=kOutput, calls=%fused_computation | convolution fusion | flops 1208352768 | bytes 6291456 | tf_op jit(solution)/shard_map/cond/branch_1_fun/dot_general | solution.py:26
  38.2 22.9 %conditional.15 = (bf16[256,1536]{1,0:T(8,128)(2,1)}, f32[4,1,768]{2,1,0:T(1,128)S(1)}, f32[256,1536]{1,0:T(8,128)}, bf16[256,1536]{1,0:T(8,128)(2,1)S(1)}, bf16...) conditional(s32[]{:T(128)} %convert_element_type.130, ...), branch_computations={%region_5.6_spmd, %region_6.7_spmd} | conditional | flops 1107296256 | bytes 22294828 | solution.py:1131
  42.4 9.5 %branch_1_fun.32 = (bf16[256,1536]{1,0:T(8,128)(2,1)}, f32[4,1,768]{2,1,0:T(1,128)S(1)}) custom-call(s32[4]{0:T(128)S(1)} %get-tuple-element.460.pos, s32[8]{0:T(128)S(1)} %get-tuple-element.461.spans, bf16[256,1536]{1,0:T(8,128)(2,1)} %get-tuple-element.462.q_ref, bf16[256,1024]{1,0:T(8,128)(2,1)} %get-tuple-element.463.refs_0_, ...), custom_call_target="tpu_custom_call" | custom-call | flops 805306368 | bytes 1048576 | tf_op jit(solution)/shard_map/cond/branch_1_fun/pallas_call | solution.py:128
  51.9 5.6 %branch_1_fun.33 = (f32[256,1536]{1,0:T(8,128)}, bf16[256,1536]{1,0:T(8,128)(2,1)S(1)}) custom-call(bf16[256,1536]{1,0:T(8,128)(2,1)S(1)} %copy-done.3, bf16[256,1536]{1,0:T(8,128)(2,1)} %get-tuple-element.1129.att_ref, bf16[1536,1536]{1,0:T(8,128)(2,1)} %get-tuple-element.470.w_ref, f32[1,1536]{1,0:T(1,128)} %reshape.112.gain_ref), custom_call_target="tpu_custom_call" | custom-call | flops 301989888 | bytes 2097152 | tf_op jit(solution)/shard_map/cond/branch_1_fun/pallas_call | solution.py:228
  61.1 24.6 %conditional.16 = (bf16[256,1536]{1,0:T(8,128)(2,1)}, f32[256,1536]{1,0:T(8,128)}, f32[256,1536]{1,0:T(8,128)}, bf16[256,1024]{1,0:T(8,128)(2,1)S(1)}, bf16[256,...) conditional(s32[]{:T(128)} %convert_element_type.130, ...), branch_computations={%region_7.8_spmd, %region_8.9_spmd} | conditional | flops 2617245696 | bytes 19923216 | solution.py:1131
  63.6 11.3 %branch_1_fun.34 = (f32[256,1536]{1,0:T(8,128)}, f32[256,1536]{1,0:T(8,128)}, bf16[256,1024]{1,0:T(8,128)(2,1)S(1)}, bf16[256,2048]{1,0:T(8,128)(2,1)S(1)}) custom-call(s32[4]{0:T(128)S(1)} %get-tuple-element.479.pos, bf16[256,1536]{1,0:T(8,128)(2,1)S(1)} %get-tuple-element.478.refs_0_, bf16[256,1536]{1,0:T(8,128)(2,1)S(1)} %get-tuple-element.480.refs_1_, ...), custom_call_target="tpu_custom_call" | custom-call | flops 2617245696 | bytes 3145728 | tf_op jit(solution)/shard_map/cond/branch_1_fun/pallas_call | solution.py:449
  74.9 7.1 %collective-permute-done.9 = bf16[256,1536]{1,0:T(8,128)(2,1)} collective-permute-done((bf16[256,1536]{1,0:T(8,128)(2,1)}, bf16[256,1536]{1,0:T(8,128)(2,1)}, u32[]{:S(2)}, u32[]{:S(2)}) %collective-permute-start.9) | collective-permute-done | bytes 786464 | tf_op jit(solution)/shard_map/cond/branch_1_fun/ppermute | solution.py:911
  85.7 23.9 %conditional.17 = (bf16[256,1536]{1,0:T(8,128)(2,1)}, bf16[256,1536]{1,0:T(8,128)(2,1)}, bf16[256,1536]{1,0:T(8,128)(2,1)}, bf16[1024,1536]{1,0:T(8,128)(2,1)}, ...) conditional(s32[]{:T(128)} %convert_element_type.130, ...), branch_computations={%region_9.10_spmd, %region_10.11_spmd} | conditional | flops 3825205248 | bytes 29360258 | solution.py:1131
  90.1 7.1 %branch_1_fun.36 = (bf16[16,80,2048]{2,1,0:T(8,128)(2,1)}, bf16[16,80,2048]{2,1,0:T(8,128)(2,1)}) custom-call(s32[4]{0:T(128)S(1)} %get-tuple-element.493.pos, bf16[256,1536]{1,0:T(8,128)(2,1)S(1)} %get-tuple-element.494.refs_0_, bf16[256,2048]{1,0:T(8,128)(2,1)S(1)} %get-tuple-element.505.refs_1_, bf16[256,1024]{1,0:T(8,128)(2,1)S(1)} %get-tuple-element.506.refs_2_, ...), custom_call_target="tpu_custom_call" | custom-call | flops 1207959552 | bytes 2097152 | tf_op jit(solution)/shard_map/cond/branch_1_fun/pallas_call | solution.py:613
  97.2 12.0 %branch_1_fun.35 = (bf16[256,1536]{1,0:T(8,128)(2,1)}, bf16[256,1536]{1,0:T(8,128)(2,1)}, bf16[1024,1536]{1,0:T(8,128)(2,1)}, bf16[1024,1664]{1,0:T(8,128)(2,1)S...) custom-call(s32[4]{0:T(128)S(1)} %get-tuple-element.493.pos, bf16[256,1536]{1,0:T(8,128)(2,1)} %copy-done.6, ...), custom_call_target="tpu_custom_call" | custom-call | flops 2617245696 | bytes 3145728 | tf_op jit(solution)/shard_map/cond/branch_1_fun/pallas_call | solution.py:449
  109.6 43.7 %conditional.18 = (bf16[256,1536]{1,0:T(8,128)(2,1)}, bf16[256,1536]{1,0:T(8,128)(2,1)}, bf16[256,1536]{1,0:T(8,128)(2,1)}, bf16[256,1536]{1,0:T(8,128)(2,1)}, b...) conditional(s32[]{:T(128)} %convert_element_type.130, ...), branch_computations={%region_11.12_spmd, %region_12.13_spmd} | conditional | flops 5234491392 | bytes 37749024 | solution.py:1131
  112.4 20.8 %branch_1_fun.37 = (bf16[256,1536]{1,0:T(8,128)(2,1)}, bf16[256,1536]{1,0:T(8,128)(2,1)}, bf16[256,1536]{1,0:T(8,128)(2,1)}, bf16[256,1536]{1,0:T(8,128)(2,1)}, ...) custom-call(s32[4]{0:T(128)S(1)} %get-tuple-element.515.pos, ...), custom_call_target="tpu_custom_call", output_to_operand_aliasing={{4}: (8, {}), {5}: (9, {}), {6}: (10, {}), {7}: (11, {})} | custom-call | flops 5234491392 | bytes 3145728 | tf_op jit(solution)/shard_map/cond/branch_1_fun/pallas_call | solution.py:449
  133.2 4.7 branch_1_fun.38
  153.4 54.7 %conditional.19 = (bf16[256,1536]{1,0:T(8,128)(2,1)}, bf16[256,1536]{1,0:T(8,128)(2,1)}, bf16[1024,1536]{1,0:T(8,128)(2,1)}, bf16[1024,1664]{1,0:T(8,128)(2,1)S(...) conditional(s32[]{:T(128)} %convert_element_type.130, ...), branch_computations={%region_13.14_spmd, %region_14.15_spmd} | conditional | flops 13086228480 | bytes 28967102 | solution.py:1131
  158.1 18.6 %branch_1_fun.40 = (bf16[256,1536]{1,0:T(8,128)(2,1)}, bf16[256,1536]{1,0:T(8,128)(2,1)}, bf16[256,1536]{1,0:T(8,128)(2,1)}, bf16[256,1536]{1,0:T(8,128)(2,1)}, ...) custom-call(s32[4]{0:T(128)S(1)} %get-tuple-element.542.pos, bf16[1024,1536]{1,0:T(8,128)(2,1)} %get-tuple-element.548.refs_5_.x_ref, ...), custom_call_target="tpu_custom_call" | custom-call | flops 5234491392 | bytes 3145728 | tf_op jit(solution)/shard_map/cond/branch_1_fun/pallas_call | solution.py:541
  177.1 12.0 %branch_1_fun.39 = (bf16[256,1536]{1,0:T(8,128)(2,1)}, bf16[256,1536]{1,0:T(8,128)(2,1)}, bf16[1024,1536]{1,0:T(8,128)(2,1)}, bf16[1024,1664]{1,0:T(8,128)(2,1)S...) custom-call(s32[4]{0:T(128)S(1)} %get-tuple-element.542.pos, ...), custom_call_target="tpu_custom_call", output_to_operand_aliasing={{2}: (6, {}), {3}: (7, {}), {4}: (8, {}), {5}: (9, {})} | custom-call | flops 2617245696 | bytes 3145728 | tf_op jit(solution)/shard_map/cond/branch_1_fun/pallas_call | solution.py:449
  189.1 18.6 %branch_1_fun.41 = (bf16[256,1536]{1,0:T(8,128)(2,1)}, bf16[256,1536]{1,0:T(8,128)(2,1)}, bf16[256,1536]{1,0:T(8,128)(2,1)}, bf16[256,1536]{1,0:T(8,128)(2,1)}, ...) custom-call(s32[4]{0:T(128)S(1)} %get-tuple-element.542.pos, ...), custom_call_target="tpu_custom_call", output_to_operand_aliasing={{4}: (13, {}), {5}: (14, {})} | custom-call | flops 5234491392 | bytes 3145728 | tf_op jit(solution)/shard_map/cond/branch_1_fun/pallas_call | solution.py:541
  208.1 28.1 %conditional.20 = (bf16[256,1536]{1,0:T(8,128)(2,1)}, bf16[6,128,3072]{2,1,0:T(8,128)(2,1)}, bf16[6,128,3072]{2,1,0:T(8,128)(2,1)}, bf16[2,80,2048]{2,1,0:T(8,128)(2,1)}, bf16[1,160,2048]{2,1,0:T(8,128)(2,1)}) conditional(s32[]{:T(128)} %convert_element_type.130, () %tuple.143, (bf16[256,1536]{1,0:T(8,128)(2,1)}, bf16[256,1536]{1,0:T(8,128)(2,1)}, ...), branch_computations={%region_15.16_spmd, %region_16.17_spmd} | conditional | flops 4833411072 | bytes 17039520 | solution.py:1131
  220.0 16.1 %branch_1_fun.42 = (bf16[6,128,3072]{2,1,0:T(8,128)(2,1)}, bf16[6,128,3072]{2,1,0:T(8,128)(2,1)}) custom-call(s32[4]{0:T(128)S(1)} %get-tuple-element.584.pos, bf16[1024,1536]{1,0:T(8,128)(2,1)} %get-tuple-element.585.refs_0_.refs_1_.refs_2_.refs_3_, bf16[1024,1536]{1,0:T(8,128)(2,1)} %get-tuple-element.585.refs_0_.refs_1_.refs_2_.refs_3_, ...), custom_call_target="tpu_custom_call" | custom-call | flops 4831838208 | bytes 4194304 | tf_op jit(solution)/shard_map/cond/branch_1_fun/pallas_call | solution.py:717
  236.2 25.7 %conditional.21 = (bf16[256,1536]{1,0:T(8,128)(2,1)}, bf16[6,128,3072]{2,1,0:T(8,128)(2,1)}, bf16[6,128,3072]{2,1,0:T(8,128)(2,1)}, bf16[6,128,3072]{2,1,0:T(8,1...) conditional(s32[]{:T(128)} %convert_element_type.130, () %tuple.142, ...), branch_computations={%region_17.18_spmd, %region_18.19_spmd} | conditional | flops 4834197504 | bytes 36176040 | solution.py:1131
  242.7 16.0 %branch_1_fun.44 = (bf16[6,128,3072]{2,1,0:T(8,128)(2,1)}, bf16[6,128,3072]{2,1,0:T(8,128)(2,1)}) custom-call(s32[4]{0:T(128)S(1)} %get-tuple-element.600.pos, bf16[1024,1536]{1,0:T(8,128)(2,1)} %get-tuple-element.601.refs_0_.refs_1_.refs_2_.refs_3_, bf16[1024,1536]{1,0:T(8,128)(2,1)} %get-tuple-element.601.refs_0_.refs_1_.refs_2_.refs_3_, ...), custom_call_target="tpu_custom_call" | custom-call | flops 4831838208 | bytes 4194304 | tf_op jit(solution)/shard_map/cond/branch_1_fun/pallas_call | solution.py:717
  261.8 34.1 %conditional.22 = (f32[256,1536]{1,0:T(8,128)}, bf16[256,1536]{1,0:T(8,128)(2,1)}, f32[1,1536]{1,0:T(1,128)S(1)}, bf16[256,1536]{1,0:T(8,128)(2,1)}, bf16[6,128,...) conditional(s32[]{:T(128)} %convert_element_type.130, ...), branch_computations={%region_19.20_spmd, %region_20.21_spmd} | conditional | flops 305922048 | bytes 55850036 | solution.py:1131
  270.7 5.2 %branch_1_fun.48 = (bf16[6,128,768]{2,1,0:T(8,128)(2,1)}, bf16[6,128,768]{2,1,0:T(8,128)(2,1)}, bf16[6,128,768]{2,1,0:T(8,128)(2,1)}) custom-call(s32[4]{0:T(128)S(1)} %get-tuple-element.628.pos, bf16[6,128,3072]{2,1,0:T(8,128)(2,1)} %get-tuple-element.629.refs_0_.refs_2_.refs_4_, bf16[6,128,3072]{2,1,0:T(8,128)(2,1)} %get-tuple-element.630.refs_1_.refs_3_.refs_5_, ...), custom_call_target="tpu_custom_call" | custom-call | bytes 2097152 | tf_op jit(solution)/shard_map/cond/branch_1_fun/pallas_call | solution.py:758
  275.9 6.3 %branch_1_fun.49 = bf16[4,80,2048]{2,1,0:T(8,128)(2,1)} custom-call(s32[4]{0:T(128)S(1)} %get-tuple-element.628.pos, bf16[8,160,2048]{2,1,0:T(8,128)(2,1)} %bitcast.17.refs_0_, bf16[8,160,2048]{2,1,0:T(8,128)(2,1)} %bitcast.18.refs_1_, bf16[1,160,2048]{2,1,0:T(8,128)(2,1)} %get-tuple-element.636.refs_2_, bf16[1,160,2048]{2,1,0:T(8,128)(2,1)} %get-tuple-element.637.refs_3_, ...), custom_call_target="tpu_custom_call" | custom-call | bytes 2097152 | tf_op jit(solution)/shard_map/cond/branch_1_fun/pallas_call | solution.py:758
  287.9 7.8 %branch_1_fun.47 = (f32[256,1536]{1,0:T(8,128)}, bf16[256,1536]{1,0:T(8,128)(2,1)}, f32[1,1536]{1,0:T(1,128)S(1)}, bf16[256,1536]{1,0:T(8,128)(2,1)}) custom-call(f32[256,1536]{1,0:T(8,128)} %get-tuple-element.612.refs_0_, bf16[256,1536]{1,0:T(8,128)(2,1)} %get-tuple-element.613.refs_1_, bf16[256,1536]{1,0:T(8,128)(2,1)} %get-tuple-element.614.refs_2_, ...), custom_call_target="tpu_custom_call" | custom-call | flops 301989888 | bytes 4194304 | tf_op jit(solution)/shard_map/cond/branch_1_fun/pallas_call | solution.py:273
  296.7 29.1 %conditional.23 = (bf16[256,1536]{1,0:T(8,128)(2,1)S(1)}, bf16[256,1536]{1,0:T(8,128)(2,1)}, bf16[256,1536]{1,0:T(8,128)(2,1)}, bf16[256,1536]{1,0:T(8,128)(2,1)...) conditional(s32[]{:T(128)} %convert_element_type.130, ...), branch_computations={%region_21.22_spmd, %region_22.23_spmd} | conditional | flops 2013265920 | bytes 19136940 | solution.py:1131
  302.0 14.7 %branch_1_fun.50 = (bf16[256,1536]{1,0:T(8,128)(2,1)S(1)}, bf16[512,1024]{1,0:T(8,128)(2,1)S(1)}, bf16[512,1024]{1,0:T(8,128)(2,1)}) custom-call(s32[4]{0:T(128)S(1)} %get-tuple-element.645.pos, s32[8]{0:T(128)} %copy-done.24, bf16[256,1536]{1,0:T(8,128)(2,1)} %get-tuple-element.647.q_ref, bf16[256,1536]{1,0:T(8,128)(2,1)} %get-tuple-element.648.grad_ref, ...), custom_call_target="tpu_custom_call" | custom-call | flops 2013265920 | bytes 2097152 | tf_op jit(solution)/shard_map/cond/branch_1_fun/pallas_call | solution.py:190
  316.6 9.1 %collective-permute-done.28 = bf16[80,2048]{1,0:T(8,128)(2,1)} collective-permute-done((bf16[80,2048]{1,0:T(8,128)(2,1)}, bf16[80,2048]{1,0:T(8,128)(2,1)}, u32[]{:S(2)}, u32[]{:S(2)}) %collective-permute-start.28) | collective-permute-done | bytes 327712 | tf_op jit(solution)/shard_map/cond/branch_1_fun/ppermute | solution.py:911
  325.8 36.7 %conditional.24 = (bf16[256,1024]{1,0:T(8,128)(2,1)S(1)}, bf16[256,1536]{1,0:T(8,128)(2,1)}, bf16[8,48,1536]{2,1,0:T(8,128)(2,1)S(1)}, bf16[6,128,768]{2,1,0:T(8...) conditional(s32[]{:T(128)} %convert_element_type.130, () %tuple.127, ...), branch_computations={%region_23.24_spmd, %region_24.25_spmd} | conditional | flops 611319808 | bytes 39846232 | solution.py:1131
  331.2 3.8 branch_1_fun.52
  336.0 4.6 branch_1_fun.51
  343.4 6.6 %collective-permute-done.42 = bf16[256,1536]{1,0:T(8,128)(2,1)} collective-permute-done((bf16[256,1536]{1,0:T(8,128)(2,1)}, bf16[256,1536]{1,0:T(8,128)(2,1)}, u32[]{:S(2)}, u32[]{:S(2)}) %collective-permute-start.42) | collective-permute-done | bytes 786464 | tf_op jit(solution)/shard_map/cond/branch_1_fun/ppermute | solution.py:923
  352.8 8.4 %collective-permute-done.39 = bf16[256,1024]{1,0:T(8,128)(2,1)S(1)} collective-permute-done((bf16[256,1024]{1,0:T(8,128)(2,1)S(1)}, bf16[256,1024]{1,0:T(8,128)(2,1)S(1)}, u32[]{:S(2)}, u32[]{:S(2)}) %collective-permute-start.39) | collective-permute-done | bytes 524320 | tf_op jit(solution)/shard_map/cond/branch_1_fun/ppermute | solution.py:911
  363.6 38.1 %conditional.25 = (bf16[8,48,1536]{2,1,0:T(8,128)(2,1)}, bf16[8,48,1024]{2,1,0:T(8,128)(2,1)}, f32[1,1536]{1,0:T(1,128)S(1)}, bf16[256,1536]{1,0:T(8,128)(2,1)},...) conditional(s32[]{:T(128)} %convert_element_type.130, () %tuple.149, ...), branch_computations={%region_25.26_spmd, %region_26.27_spmd} | conditional | flops 1515192320 | bytes 38285636 | solution.py:1131
  368.5 9.9 %collective-permute-done.45.refs_6_ = bf16[256,1024]{1,0:T(8,128)(2,1)S(1)} collective-permute-done((bf16[256,1024]{1,0:T(8,128)(2,1)S(1)}, bf16[256,1024]{1,0:T(8,128)(2,1)S(1)}, u32[]{:S(2)}, u32[]{:S(2)}) %collective-permute-start.45) | collective-permute-done | bytes 524320 | tf_op jit(solution)/shard_map/cond/branch_1_fun/ppermute | solution.py:911
  380.2 9.3 %branch_1_fun.55 = (f32[256,1536]{1,0:T(8,128)}, f32[1,1536]{1,0:T(1,128)S(1)}) custom-call(bf16[256,1536]{1,0:T(8,128)(2,1)S(1)} %get-tuple-element.686.refs_4_.dq_ref, bf16[256,1024]{1,0:T(8,128)(2,1)S(1)} %get-tuple-element.688.refs_4_.dkv_ref, bf16[1536,1536]{1,0:T(8,128)(2,1)} %get-tuple-element.689.wq_ref, ...), custom_call_target="tpu_custom_call" | custom-call | flops 503316480 | bytes 3670016 | tf_op jit(solution)/shard_map/cond/branch_1_fun/pallas_call | solution.py:324
  389.5 4.0 branch_1_fun.54
  393.4 5.2 %branch_1_fun.53 = bf16[384,1536]{1,0:T(8,128)(2,1)} custom-call(s32[4]{0:T(128)S(1)} %get-tuple-element.681.pos, bf16[256,1536]{1,0:T(8,128)(2,1)} %get-tuple-element.682.refs_0_, bf16[256,1536]{1,0:T(8,128)(2,1)} %get-tuple-element.683.refs_1_, bf16[256,1536]{1,0:T(8,128)(2,1)} %get-tuple-element.684.refs_2_, ...), custom_call_target="tpu_custom_call" | custom-call | flops 603979776 | bytes 1048576 | tf_op jit(solution)/shard_map/cond/branch_1_fun/pallas_call | solution.py:657
  401.7 38.8 %conditional.26 = (bf16[4,48,4096]{2,1,0:T(8,128)(2,1)S(1)}, bf16[4,48,4096]{2,1,0:T(8,128)(2,1)}, bf16[6,128,768]{2,1,0:T(8,128)(2,1)}, bf16[80,2048]{1,0:T(8,1...) conditional(s32[]{:T(128)} %convert_element_type.130, ...), branch_computations={%region_27.28_spmd, %region_28.29_spmd} | conditional | flops 12586004 | bytes 34755032 | solution.py:1131
  405.8 3.8 branch_1_fun.56
  421.8 18.5 %all-to-all-done = f32[32,2,48]{2,1,0:T(2,128)} async-done(((f32[32,2,48]{2,1,0:T(2,128)}), f32[32,2,48]{2,1,0:T(2,128)}, u32[]{:S(2)}, u32[]{:S(2)}) %all-to-all-start) | async-done | bytes 12320 | tf_op jit(solution)/shard_map/cond/branch_1_fun/all_to_all | solution.py:1343
  440.6 36.7 %conditional.27 = (f32[2,48]{1,0:T(2,128)}, f32[48,1024]{1,0:T(8,128)}, f32[48,1024]{1,0:T(8,128)}, f32[32,1536]{1,0:T(8,128)}, f32[48,1536]{1,0:T(8,128)}, /*in...) conditional(s32[]{:T(128)} %convert_element_type.130, ...), branch_computations={%region_29.30_spmd, %region_30.32_spmd} | conditional | flops 2976 | bytes 16270620 | solution.py:1131
  450.7 6.2 %branch_1_fun.60 = (bf16[3,128,768]{2,1,0:T(8,128)(2,1)}, bf16[3,128,768]{2,1,0:T(8,128)(2,1)}, bf16[3,128,768]{2,1,0:T(8,128)(2,1)}, bf16[3,128,768]{2,1,0:T(8,128)(2,1)}) custom-call(s32[4]{0:T(128)S(1)} %get-tuple-element.725.pos, bf16[6,128,3072]{2,1,0:T(8,128)(2,1)} %get-tuple-element.736.refs_0_.refs_4_.refs_8_.refs_12_, ...), custom_call_target="tpu_custom_call" | custom-call | bytes 2097152 | tf_op jit(solution)/shard_map/cond/branch_1_fun/pallas_call | solution.py:758
  456.9 8.8 %branch_1_fun.61 = (f32[2,384,512]{2,1,0:T(8,128)}, f32[2,384,512]{2,1,0:T(8,128)}, f32[2,512,384]{2,1,0:T(8,128)}) custom-call(bf16[384,768]{1,0:T(8,128)(2,1)} %bitcast.92, bf16[384,768]{1,0:T(8,128)(2,1)} %bitcast.93, bf16[384,768]{1,0:T(8,128)(2,1)} %bitcast.94, bf16[384,768]{1,0:T(8,128)(2,1)} %bitcast.95), custom_call_target="tpu_custom_call" | custom-call | bytes 2097152 | tf_op jit(solution)/shard_map/cond/branch_1_fun/pallas_call | solution.py:818
  465.7 8.3 %collective-permute-done.55.refs_2_ = bf16[48,4096]{1,0:T(8,128)(2,1)S(1)} collective-permute-done((bf16[48,4096]{1,0:T(8,128)(2,1)}, bf16[48,4096]{1,0:T(8,128)(2,1)S(1)}, u32[]{:S(2)}, u32[]{:S(2)}) %collective-permute-start.55) | collective-permute-done | bytes 393248 | tf_op jit(solution)/shard_map/cond/branch_1_fun/ppermute | solution.py:911
  (227 shorter events, 145.6 us)
Async XLA Ops:
  11.7 21.9 %collective-permute-start.58 = (bf16[256,1024]{1,0:T(8,128)(2,1)}, bf16[256,1024]{1,0:T(8,128)(2,1)}, u32[]{:S(2)}, u32[]{:S(2)}) collective-permute-start(bf16[256,1024]{1,0:T(8,128)(2,1)} %get-tuple-element.1109), channel_id=1, source_target_pairs={{0,8},{8,0},{16,24},{24,16},{1,9},{9,1},{17,25},{25,17},{2,10},{10... | collective-permute-start | bytes 1572872 | tf_op jit(solution)/shard_map/cond/branch_1_fun/ppermute | solution.py:905
  14.7 23.4 %collective-permute-start.60 = (bf16[256,1664]{1,0:T(8,128)(2,1)}, bf16[256,1664]{1,0:T(8,128)(2,1)}, u32[]{:S(2)}, u32[]{:S(2)}) collective-permute-start(bf16[256,1664]{1,0:T(8,128)(2,1)} %get-tuple-element.455), channel_id=1, source_target_pairs={{0,2},{1,3},{2,4},{3,5},{4,6},{5,7},{6,0},{7,1},{8,14},{9,15},{10,... | collective-permute-start | bytes 2555912 | tf_op jit(solution)/shard_map/cond/branch_1_fun/ppermute | solution.py:923
  17.6 19.8 %collective-permute-start.61 = (bf16[256,1536]{1,0:T(8,128)(2,1)}, bf16[256,1536]{1,0:T(8,128)(2,1)}, u32[]{:S(2)}, u32[]{:S(2)}) collective-permute-start(bf16[256,1536]{1,0:T(8,128)(2,1)} %get-tuple-element.1079), channel_id=1, source_target_pairs={{0,1},{1,0},{2,3},{3,2},{4,5},{5,4},{6,7},{7,6},{8,9},{9,8},{10,11... | collective-permute-start | bytes 2359304 | tf_op jit(solution)/shard_map/cond/branch_1_fun/ppermute | solution.py:905
  38.2 22.9 %collective-permute-start.2 = (bf16[256,1664]{1,0:T(8,128)(2,1)}, bf16[256,1664]{1,0:T(8,128)(2,1)}, u32[]{:S(2)}, u32[]{:S(2)}) collective-permute-start(bf16[256,1664]{1,0:T(8,128)(2,1)} %get-tuple-element.475), channel_id=1, source_target_pairs={{0,2},{1,3},{2,4},{3,5},{4,6},{5,7},{6,0},{7,1},{8,14},{9,15},{10,... | collective-permute-start | bytes 2555912 | tf_op jit(solution)/shard_map/cond/branch_1_fun/ppermute | solution.py:923
  38.3 20.1 %collective-permute-start.3 = (bf16[256,1536]{1,0:T(8,128)(2,1)}, bf16[256,1536]{1,0:T(8,128)(2,1)}, u32[]{:S(2)}, u32[]{:S(2)}) collective-permute-start(bf16[256,1536]{1,0:T(8,128)(2,1)} %get-tuple-element.476), channel_id=1, source_target_pairs={{0,1},{1,0},{2,3},{3,2},{4,5},{5,4},{6,7},{7,6},{8,9},{9,8},{10,11... | collective-permute-start | bytes 2359304 | tf_op jit(solution)/shard_map/cond/branch_1_fun/ppermute | solution.py:905
  41.3 19.8 %collective-permute-start.1 = (bf16[256,1536]{1,0:T(8,128)(2,1)}, bf16[256,1536]{1,0:T(8,128)(2,1)}, u32[]{:S(2)}, u32[]{:S(2)}) collective-permute-start(bf16[256,1536]{1,0:T(8,128)(2,1)} %get-tuple-element.474), channel_id=1, source_target_pairs={{0,16},{8,24},{16,0},{24,8},{1,17},{9,25},{17,1},{25,9},{2,18},{10... | collective-permute-start | bytes 2359304 | tf_op jit(solution)/shard_map/cond/branch_1_fun/ppermute | solution.py:911
  61.1 24.6 %collective-permute-start.7 = (bf16[512,1024]{1,0:T(8,128)(2,1)}, bf16[512,1024]{1,0:T(8,128)(2,1)}, u32[]{:S(2)}, u32[]{:S(2)}) collective-permute-start(bf16[512,1024]{1,0:T(8,128)(2,1)} %get-tuple-element.489), channel_id=1, source_target_pairs={{0,1},{1,0},{2,3},{3,2},{4,5},{5,4},{6,7},{7,6},{8,9},{9,8},{10,11... | collective-permute-start | bytes 3145736 | tf_op jit(solution)/shard_map/cond/branch_1_fun/ppermute | solution.py:905
  62.2 19.8 %collective-permute-start.9 = (bf16[256,1536]{1,0:T(8,128)(2,1)}, bf16[256,1536]{1,0:T(8,128)(2,1)}, u32[]{:S(2)}, u32[]{:S(2)}) collective-permute-start(bf16[256,1536]{1,0:T(8,128)(2,1)} %get-tuple-element.491), channel_id=1, source_target_pairs={{0,16},{8,24},{16,0},{24,8},{1,17},{9,25},{17,1},{25,9},{2,18},{10... | collective-permute-start | bytes 2359304 | tf_op jit(solution)/shard_map/cond/branch_1_fun/ppermute | solution.py:911
  62.7 20.6 %collective-permute-start.5 = (bf16[256,1536]{1,0:T(8,128)(2,1)S(1)}, bf16[256,1536]{1,0:T(8,128)(2,1)}, u32[]{:S(2)}, u32[]{:S(2)}) collective-permute-start(bf16[256,1536]{1,0:T(8,128)(2,1)S(1)} %get-tuple-element.478.refs_0_), channel_id=1, source_target_pairs={{0,2},{1,3},{2,4},{3,5},{4,6},{5,7},{6,0},{7,1},{8,14},{9,15},{10,... | collective-permute-start | bytes 2359304 | tf_op jit(solution)/shard_map/cond/branch_1_fun/ppermute | solution.py:923
  85.9 23.7 %collective-permute-start.11 = (bf16[512,1024]{1,0:T(8,128)(2,1)}, bf16[512,1024]{1,0:T(8,128)(2,1)}, u32[]{:S(2)}, u32[]{:S(2)}) collective-permute-start(bf16[512,1024]{1,0:T(8,128)(2,1)} %get-tuple-element.510), channel_id=1, source_target_pairs={{0,1},{1,0},{2,3},{3,2},{4,5},{5,4},{6,7},{7,6},{8,9},{9,8},{10,11... | collective-permute-start | bytes 3145736 | tf_op jit(solution)/shard_map/cond/branch_1_fun/ppermute | solution.py:905
  86.5 23.1 %collective-permute-start.12 = (bf16[512,1024]{1,0:T(8,128)(2,1)}, bf16[512,1024]{1,0:T(8,128)(2,1)}, u32[]{:S(2)}, u32[]{:S(2)}) collective-permute-start(bf16[512,1024]{1,0:T(8,128)(2,1)} %get-tuple-element.511), channel_id=1, source_target_pairs={{0,8},{8,0},{16,24},{24,16},{1,9},{9,1},{17,25},{25,17},{2,10},{10... | collective-permute-start | bytes 3145736 | tf_op jit(solution)/shard_map/cond/branch_1_fun/ppermute | solution.py:905
  86.5 22.7 %collective-permute-start.10 = (bf16[256,1536]{1,0:T(8,128)(2,1)}, bf16[256,1536]{1,0:T(8,128)(2,1)}, u32[]{:S(2)}, u32[]{:S(2)}) collective-permute-start(bf16[256,1536]{1,0:T(8,128)(2,1)} %get-tuple-element.492), channel_id=1, source_target_pairs={{0,2},{1,3},{2,4},{3,5},{4,6},{5,7},{6,0},{7,1},{8,14},{9,15},{10,... | collective-permute-start | bytes 2359304 | tf_op jit(solution)/shard_map/cond/branch_1_fun/ppermute | solution.py:923
  88.0 21.3 %collective-permute-start.13 = (bf16[256,1536]{1,0:T(8,128)(2,1)}, bf16[256,1536]{1,0:T(8,128)(2,1)}, u32[]{:S(2)}, u32[]{:S(2)}) collective-permute-start(bf16[256,1536]{1,0:T(8,128)(2,1)} %get-tuple-element.512), channel_id=1, source_target_pairs={{0,8},{8,0},{16,24},{24,16},{1,9},{9,1},{17,25},{25,17},{2,10},{10... | collective-permute-start | bytes 2359304 | tf_op jit(solution)/shard_map/cond/branch_1_fun/ppermute | solution.py:905
  109.6 23.6 %collective-permute-start.16 = (bf16[16,80,2048]{2,1,0:T(8,128)(2,1)}, bf16[16,80,2048]{2,1,0:T(8,128)(2,1)}, u32[]{:S(2)}, u32[]{:S(2)}) collective-permute-start(bf16[16,80,2048]{2,1,0:T(8,128)(2,1)} %get-tuple-element.535), channel_id=1, source_target_pairs={{0,8},{8,0},{16,24},{24,16},{1,9},{9,1},{17,25},{25,17},{2,10},{10... | collective-permute-start | bytes 15728648 | tf_op jit(solution)/shard_map/cond/branch_1_fun/ppermute | solution.py:905
  109.9 28.0 %collective-permute-start.17 = (bf16[512,1024]{1,0:T(8,128)(2,1)}, bf16[512,1024]{1,0:T(8,128)(2,1)}, u32[]{:S(2)}, u32[]{:S(2)}) collective-permute-start(bf16[512,1024]{1,0:T(8,128)(2,1)} %get-tuple-element.540), channel_id=1, source_target_pairs={{0,1},{1,0},{2,3},{3,2},{4,5},{5,4},{6,7},{7,6},{8,9},{9,8},{10,11... | collective-permute-start | bytes 3145736 | tf_op jit(solution)/shard_map/cond/branch_1_fun/ppermute | solution.py:905
  111.4 26.6 %collective-permute-start.18 = (bf16[512,1024]{1,0:T(8,128)(2,1)}, bf16[512,1024]{1,0:T(8,128)(2,1)}, u32[]{:S(2)}, u32[]{:S(2)}) collective-permute-start(bf16[512,1024]{1,0:T(8,128)(2,1)} %get-tuple-element.541), channel_id=1, source_target_pairs={{0,8},{8,0},{16,24},{24,16},{1,9},{9,1},{17,25},{25,17},{2,10},{10... | collective-permute-start | bytes 3145736 | tf_op jit(solution)/shard_map/cond/branch_1_fun/ppermute | solution.py:905
  111.4 26.5 %collective-permute-start.15 = (bf16[256,1536]{1,0:T(8,128)(2,1)}, bf16[256,1536]{1,0:T(8,128)(2,1)}, u32[]{:S(2)}, u32[]{:S(2)}) collective-permute-start(bf16[256,1536]{1,0:T(8,128)(2,1)} %get-tuple-element.514.refs_1_), channel_id=1, source_target_pairs={{0,2},{1,3},{2,4},{3,5},{4,6},{5,7},{6,0},{7,1},{8,14},{9,15},{10,... | collective-permute-start | bytes 2359304 | tf_op jit(solution)/shard_map/cond/branch_1_fun/ppermute | solution.py:923
  155.4 21.6 %collective-permute-start.19 = (bf16[256,1664]{1,0:T(8,128)(2,1)}, bf16[256,1664]{1,0:T(8,128)(2,1)}, u32[]{:S(2)}, u32[]{:S(2)}) collective-permute-start(bf16[256,1664]{1,0:T(8,128)(2,1)} %get-tuple-element.544), channel_id=1, source_target_pairs={{0,2},{1,3},{2,4},{3,5},{4,6},{5,7},{6,0},{7,1},{8,14},{9,15},{10,... | collective-permute-start | bytes 2555912 | tf_op jit(solution)/shard_map/cond/branch_1_fun/ppermute | solution.py:923
  155.5 52.2 %collective-permute-start.21 = (bf16[1,160,2048]{2,1,0:T(8,128)(2,1)}, bf16[1,160,2048]{2,1,0:T(8,128)(2,1)}, u32[]{:S(2)}, u32[]{:S(2)}) collective-permute-start(bf16[1,160,2048]{2,1,0:T(8,128)(2,1)} %get-tuple-element.579), channel_id=1, source_target_pairs={{0,16},{8,24},{16,0},{24,8},{1,17},{9,25},{17,1},{25,9},{2,18},{10... | collective-permute-start | bytes 1966088 | tf_op jit(solution)/shard_map/cond/branch_1_fun/ppermute | solution.py:911
  156.0 51.7 %collective-permute-start.22 = (bf16[1,160,2048]{2,1,0:T(8,128)(2,1)}, bf16[1,160,2048]{2,1,0:T(8,128)(2,1)}, u32[]{:S(2)}, u32[]{:S(2)}) collective-permute-start(bf16[1,160,2048]{2,1,0:T(8,128)(2,1)} %get-tuple-element.580), channel_id=1, source_target_pairs={{0,16},{8,24},{16,0},{24,8},{1,17},{9,25},{17,1},{25,9},{2,18},{10... | collective-permute-start | bytes 1966088 | tf_op jit(solution)/shard_map/cond/branch_1_fun/ppermute | solution.py:911
  157.5 50.2 %collective-permute-start.23 = (bf16[1,160,2048]{2,1,0:T(8,128)(2,1)}, bf16[1,160,2048]{2,1,0:T(8,128)(2,1)}, u32[]{:S(2)}, u32[]{:S(2)}) collective-permute-start(bf16[1,160,2048]{2,1,0:T(8,128)(2,1)} %get-tuple-element.581), channel_id=1, source_target_pairs={{0,16},{8,24},{16,0},{24,8},{1,17},{9,25},{17,1},{25,9},{2,18},{10... | collective-permute-start | bytes 1966088 | tf_op jit(solution)/shard_map/cond/branch_1_fun/ppermute | solution.py:911
  210.6 25.6 %collective-permute-start.29 = (bf16[256,1536]{1,0:T(8,128)(2,1)}, bf16[256,1536]{1,0:T(8,128)(2,1)}, u32[]{:S(2)}, u32[]{:S(2)}) collective-permute-start(bf16[256,1536]{1,0:T(8,128)(2,1)} %add_convert_fusion), channel_id=1, source_target_pairs={{0,6},{1,7},{2,0},{3,1},{4,2},{5,3},{6,4},{7,5},{8,10},{9,11},{10,... | collective-permute-start | bytes 2359304 | tf_op jit(solution)/shard_map/cond/branch_1_fun/ppermute | solution.py:923
  236.2 22.5 %collective-permute-start.33 = (bf16[6,128,3072]{2,1,0:T(8,128)(2,1)}, bf16[6,128,3072]{2,1,0:T(8,128)(2,1)}, u32[]{:S(2)}, u32[]{:S(2)}) collective-permute-start(bf16[6,128,3072]{2,1,0:T(8,128)(2,1)} %get-tuple-element.599), channel_id=1, source_target_pairs={{0,8},{8,0},{16,24},{24,16},{1,9},{9,1},{17,25},{25,17},{2,10},{10... | collective-permute-start | bytes 14155784 | tf_op jit(solution)/shard_map/cond/branch_1_fun/ppermute | solution.py:905
  239.1 22.7 %collective-permute-start.32 = (bf16[256,1536]{1,0:T(8,128)(2,1)}, bf16[256,1536]{1,0:T(8,128)(2,1)}, u32[]{:S(2)}, u32[]{:S(2)}) collective-permute-start(bf16[256,1536]{1,0:T(8,128)(2,1)} %add_convert_fusion.1), channel_id=1, source_target_pairs={{0,6},{1,7},{2,0},{3,1},{4,2},{5,3},{6,4},{7,5},{8,10},{9,11},{10,... | collective-permute-start | bytes 2359304 | tf_op jit(solution)/shard_map/cond/branch_1_fun/ppermute | solution.py:923
  242.1 19.7 %collective-permute-start.34 = (bf16[2,80,2048]{2,1,0:T(8,128)(2,1)}, bf16[2,80,2048]{2,1,0:T(8,128)(2,1)}, u32[]{:S(2)}, u32[]{:S(2)}) collective-permute-start(bf16[2,80,2048]{2,1,0:T(8,128)(2,1)} %branch_1_fun.46), channel_id=1, source_target_pairs={{0,1},{1,0},{2,3},{3,2},{4,5},{5,4},{6,7},{7,6},{8,9},{9,8},{10,11... | collective-permute-start | bytes 1966088 | tf_op jit(solution)/shard_map/cond/branch_1_fun/ppermute | solution.py:905
  262.0 33.7 %collective-permute-start.36 = (bf16[6,128,3072]{2,1,0:T(8,128)(2,1)}, bf16[6,128,3072]{2,1,0:T(8,128)(2,1)}, u32[]{:S(2)}, u32[]{:S(2)}) collective-permute-start(bf16[6,128,3072]{2,1,0:T(8,128)(2,1)} %get-tuple-element.626), channel_id=1, source_target_pairs={{0,8},{8,0},{16,24},{24,16},{1,9},{9,1},{17,25},{25,17},{2,10},{10... | collective-permute-start | bytes 14155784 | tf_op jit(solution)/shard_map/cond/branch_1_fun/ppermute | solution.py:905
  262.3 33.4 %collective-permute-start.37 = (bf16[6,128,768]{2,1,0:T(8,128)(2,1)}, bf16[6,128,768]{2,1,0:T(8,128)(2,1)}, u32[]{:S(2)}, u32[]{:S(2)}) collective-permute-start(bf16[6,128,768]{2,1,0:T(8,128)(2,1)} %get-tuple-element.627), channel_id=1, source_target_pairs={{0,1},{1,0},{2,3},{3,2},{4,5},{5,4},{6,7},{7,6},{8,9},{9,8},{10,11... | collective-permute-start | bytes 3538952 | tf_op jit(solution)/shard_map/cond/branch_1_fun/ppermute | solution.py:905
  266.6 20.4 %collective-permute-start.35 = (bf16[256,1536]{1,0:T(8,128)(2,1)}, bf16[256,1536]{1,0:T(8,128)(2,1)S(1)}, u32[]{:S(2)}, u32[]{:S(2)}) collective-permute-start(bf16[256,1536]{1,0:T(8,128)(2,1)} %add_convert_fusion.3), channel_id=1, source_target_pairs={{0,6},{1,7},{2,0},{3,1},{4,2},{5,3},{6,4},{7,5},{8,10},{9,11},{10,... | collective-permute-start | bytes 2359304 | tf_op jit(solution)/shard_map/cond/branch_1_fun/ppermute | solution.py:923
  296.7 29.1 %collective-permute-start.27 = (bf16[6,128,768]{2,1,0:T(8,128)(2,1)}, bf16[6,128,768]{2,1,0:T(8,128)(2,1)}, u32[]{:S(2)}, u32[]{:S(2)}) collective-permute-start(bf16[6,128,768]{2,1,0:T(8,128)(2,1)} %get-tuple-element.658), channel_id=1, source_target_pairs={{0,1},{1,0},{2,3},{3,2},{4,5},{5,4},{6,7},{7,6},{8,9},{9,8},{10,11... | collective-permute-start | bytes 3538952 | tf_op jit(solution)/shard_map/cond/branch_1_fun/ppermute | solution.py:905
  297.2 28.5 %collective-permute-start.26 = (bf16[256,1536]{1,0:T(8,128)(2,1)}, bf16[256,1536]{1,0:T(8,128)(2,1)}, u32[]{:S(2)}, u32[]{:S(2)}) collective-permute-start(bf16[256,1536]{1,0:T(8,128)(2,1)} %get-tuple-element.657), channel_id=1, source_target_pairs={{0,6},{1,7},{2,0},{3,1},{4,2},{5,3},{6,4},{7,5},{8,10},{9,11},{10,... | collective-permute-start | bytes 2359304 | tf_op jit(solution)/shard_map/cond/branch_1_fun/ppermute | solution.py:923
  300.3 25.5 %collective-permute-start.25 = (bf16[256,1536]{1,0:T(8,128)(2,1)}, bf16[256,1536]{1,0:T(8,128)(2,1)}, u32[]{:S(2)}, u32[]{:S(2)}) collective-permute-start(bf16[256,1536]{1,0:T(8,128)(2,1)} %get-tuple-element.1311), channel_id=1, source_target_pairs={{0,16},{8,24},{16,0},{24,8},{1,17},{9,25},{17,1},{25,9},{2,18},{10... | collective-permute-start | bytes 2359304 | tf_op jit(solution)/shard_map/cond/branch_1_fun/ppermute | solution.py:911
  300.8 25.0 %collective-permute-start.24 = (bf16[256,1536]{1,0:T(8,128)(2,1)}, bf16[256,1536]{1,0:T(8,128)(2,1)}, u32[]{:S(2)}, u32[]{:S(2)}) collective-permute-start(bf16[256,1536]{1,0:T(8,128)(2,1)} %get-tuple-element.1311), channel_id=1, source_target_pairs={{0,8},{8,0},{16,24},{24,16},{1,9},{9,1},{17,25},{25,17},{2,10},{10... | collective-permute-start | bytes 2359304 | tf_op jit(solution)/shard_map/cond/branch_1_fun/ppermute | solution.py:905
  300.8 25.0 %collective-permute-start.28 = (bf16[80,2048]{1,0:T(8,128)(2,1)}, bf16[80,2048]{1,0:T(8,128)(2,1)}, u32[]{:S(2)}, u32[]{:S(2)}) collective-permute-start(bf16[80,2048]{1,0:T(8,128)(2,1)} %get-tuple-element.659), channel_id=1, source_target_pairs={{0,2},{1,3},{2,4},{3,5},{4,6},{5,7},{6,0},{7,1},{8,10},{9,11},{10,... | collective-permute-start | bytes 983048 | tf_op jit(solution)/shard_map/cond/branch_1_fun/ppermute | solution.py:911
  329.2 20.7 %collective-permute-start.42 = (bf16[256,1536]{1,0:T(8,128)(2,1)}, bf16[256,1536]{1,0:T(8,128)(2,1)}, u32[]{:S(2)}, u32[]{:S(2)}) collective-permute-start(bf16[256,1536]{1,0:T(8,128)(2,1)} %add_convert_fusion.5), channel_id=1, source_target_pairs={{0,6},{1,7},{2,0},{3,1},{4,2},{5,3},{6,4},{7,5},{8,10},{9,11},{10,... | collective-permute-start | bytes 2359304 | tf_op jit(solution)/shard_map/cond/branch_1_fun/ppermute | solution.py:923
  329.2 33.3 %collective-permute-start.43 = (bf16[6,128,768]{2,1,0:T(8,128)(2,1)}, bf16[6,128,768]{2,1,0:T(8,128)(2,1)}, u32[]{:S(2)}, u32[]{:S(2)}) collective-permute-start(bf16[6,128,768]{2,1,0:T(8,128)(2,1)} %get-tuple-element.680), channel_id=1, source_target_pairs={{0,1},{1,0},{2,3},{3,2},{4,5},{5,4},{6,7},{7,6},{8,9},{9,8},{10,11... | collective-permute-start | bytes 3538952 | tf_op jit(solution)/shard_map/cond/branch_1_fun/ppermute | solution.py:905
  330.7 31.8 %collective-permute-start.40 = (bf16[256,1536]{1,0:T(8,128)(2,1)S(1)}, bf16[256,1536]{1,0:T(8,128)(2,1)}, u32[]{:S(2)}, u32[]{:S(2)}) collective-permute-start(bf16[256,1536]{1,0:T(8,128)(2,1)S(1)} %get-tuple-element.662), channel_id=1, source_target_pairs={{0,16},{8,24},{16,0},{24,8},{1,17},{9,25},{17,1},{25,9},{2,18},{10... | collective-permute-start | bytes 2359304 | tf_op jit(solution)/shard_map/cond/branch_1_fun/ppermute | solution.py:911
  366.5 27.0 %collective-permute-start.44 = (bf16[512,1536]{1,0:T(8,128)(2,1)}, bf16[512,1536]{1,0:T(8,128)(2,1)}, u32[]{:S(2)}, u32[]{:S(2)}) collective-permute-start(bf16[512,1536]{1,0:T(8,128)(2,1)} %pad_maximum_fusion.3), channel_id=1, source_target_pairs={{0,8},{8,0},{16,24},{24,16},{1,9},{9,1},{17,25},{25,17},{2,10},{10... | collective-permute-start | bytes 4718600 | tf_op jit(solution)/shard_map/cond/branch_1_fun/ppermute | solution.py:905
  366.5 33.8 %collective-permute-start.48 = (bf16[6,128,768]{2,1,0:T(8,128)(2,1)}, bf16[6,128,768]{2,1,0:T(8,128)(2,1)}, u32[]{:S(2)}, u32[]{:S(2)}) collective-permute-start(bf16[6,128,768]{2,1,0:T(8,128)(2,1)} %get-tuple-element.697), channel_id=1, source_target_pairs={{0,1},{1,0},{2,3},{3,2},{4,5},{5,4},{6,7},{7,6},{8,9},{9,8},{10,11... | collective-permute-start | bytes 3538952 | tf_op jit(solution)/shard_map/cond/branch_1_fun/ppermute | solution.py:905
  367.0 34.7 %collective-permute-start.49 = (bf16[6,128,768]{2,1,0:T(8,128)(2,1)}, bf16[6,128,768]{2,1,0:T(8,128)(2,1)}, u32[]{:S(2)}, u32[]{:S(2)}) collective-permute-start(bf16[6,128,768]{2,1,0:T(8,128)(2,1)} %get-tuple-element.698), channel_id=1, source_target_pairs={{0,16},{8,24},{16,0},{24,8},{1,17},{9,25},{17,1},{25,9},{2,18},{10... | collective-permute-start | bytes 3538952 | tf_op jit(solution)/shard_map/cond/branch_1_fun/ppermute | solution.py:911
  379.6 20.7 %collective-permute-start.47 = (bf16[256,1536]{1,0:T(8,128)(2,1)}, bf16[256,1536]{1,0:T(8,128)(2,1)}, u32[]{:S(2)}, u32[]{:S(2)}) collective-permute-start(bf16[256,1536]{1,0:T(8,128)(2,1)} %get-tuple-element.696), channel_id=1, source_target_pairs={{0,6},{1,7},{2,0},{3,1},{4,2},{5,3},{6,4},{7,5},{8,10},{9,11},{10,... | collective-permute-start | bytes 2359304 | tf_op jit(solution)/shard_map/cond/branch_1_fun/ppermute | solution.py:923
  405.3 35.0 %collective-permute-start.50 = (bf16[4,48,4096]{2,1,0:T(8,128)(2,1)}, bf16[4,48,4096]{2,1,0:T(8,128)(2,1)}, u32[]{:S(2)}, u32[]{:S(2)}) collective-permute-start(bf16[4,48,4096]{2,1,0:T(8,128)(2,1)} %get-tuple-element.1094), channel_id=1, source_target_pairs={{0,1},{1,0},{2,3},{3,2},{4,5},{5,4},{6,7},{7,6},{8,9},{9,8},{10,11... | collective-permute-start | bytes 4718600 | tf_op jit(solution)/shard_map/cond/branch_1_fun/ppermute | solution.py:905
  409.6 30.7 %collective-permute-start.51 = (bf16[6,128,768]{2,1,0:T(8,128)(2,1)}, bf16[6,128,768]{2,1,0:T(8,128)(2,1)}, u32[]{:S(2)}, u32[]{:S(2)}) collective-permute-start(bf16[6,128,768]{2,1,0:T(8,128)(2,1)} %branch_1_fun.56), channel_id=1, source_target_pairs={{0,16},{8,24},{16,0},{24,8},{1,17},{9,25},{17,1},{25,9},{2,18},{10... | collective-permute-start | bytes 3538952 | tf_op jit(solution)/shard_map/cond/branch_1_fun/ppermute | solution.py:911
  411.0 29.3 %all-to-all-start = ((f32[32,2,48]{2,1,0:T(2,128)}), f32[32,2,48]{2,1,0:T(2,128)}, u32[]{:S(2)}, u32[]{:S(2)}) async-start(f32[32,2,48]{2,1,0:T(2,128)} %pad_maximum_fusion.6), calls=%async_computation | async-start | bytes 65536 | tf_op jit(solution)/shard_map/cond/branch_1_fun/all_to_all | solution.py:1343
  414.2 26.1 %collective-permute-start.52 = (bf16[80,2048]{1,0:T(8,128)(2,1)}, bf16[80,2048]{1,0:T(8,128)(2,1)}, u32[]{:S(2)}, u32[]{:S(2)}) collective-permute-start(bf16[80,2048]{1,0:T(8,128)(2,1)} %get-tuple-element.708), channel_id=1, source_target_pairs={{0,4},{1,5},{2,6},{3,7},{4,0},{5,1},{6,2},{7,3},{8,12},{9,13},{10,... | collective-permute-start | bytes 983048 | tf_op jit(solution)/shard_map/cond/branch_1_fun/ppermute | solution.py:911
  416.9 23.4 %collective-permute-start.53 = (bf16[80,2048]{1,0:T(8,128)(2,1)}, bf16[80,2048]{1,0:T(8,128)(2,1)}, u32[]{:S(2)}, u32[]{:S(2)}) collective-permute-start(bf16[80,2048]{1,0:T(8,128)(2,1)} %get-tuple-element.709), channel_id=1, source_target_pairs={{0,6},{1,7},{2,0},{3,1},{4,2},{5,3},{6,4},{7,5},{8,14},{9,15},{10,... | collective-permute-start | bytes 983048 | tf_op jit(solution)/shard_map/cond/branch_1_fun/ppermute | solution.py:911
  444.0 21.7 %collective-permute-start.54 = (bf16[48,4096]{1,0:T(8,128)(2,1)}, bf16[48,4096]{1,0:T(8,128)(2,1)S(1)}, u32[]{:S(2)}, u32[]{:S(2)}) collective-permute-start(bf16[48,4096]{1,0:T(8,128)(2,1)} %bitcast.99), channel_id=1, source_target_pairs={{0,2},{1,3},{2,4},{3,5},{4,6},{5,7},{6,0},{7,1},{8,10},{9,11},{10,... | collective-permute-start | bytes 1179656 | tf_op jit(solution)/shard_map/cond/branch_1_fun/ppermute | solution.py:911
  444.0 30.0 %collective-permute-start.55 = (bf16[48,4096]{1,0:T(8,128)(2,1)}, bf16[48,4096]{1,0:T(8,128)(2,1)S(1)}, u32[]{:S(2)}, u32[]{:S(2)}) collective-permute-start(bf16[48,4096]{1,0:T(8,128)(2,1)} %bitcast.98), channel_id=1, source_target_pairs={{0,4},{1,5},{2,6},{3,7},{4,0},{5,1},{6,2},{7,3},{8,12},{9,13},{10,... | collective-permute-start | bytes 1179656 | tf_op jit(solution)/shard_map/cond/branch_1_fun/ppermute | solution.py:911
  447.4 26.6 %collective-permute-start.56 = (bf16[48,4096]{1,0:T(8,128)(2,1)}, bf16[48,4096]{1,0:T(8,128)(2,1)S(1)}, u32[]{:S(2)}, u32[]{:S(2)}) collective-permute-start(bf16[48,4096]{1,0:T(8,128)(2,1)} %bitcast.97), channel_id=1, source_target_pairs={{0,6},{1,7},{2,0},{3,1},{4,2},{5,3},{6,4},{7,5},{8,14},{9,15},{10,... | collective-permute-start | bytes 1179656 | tf_op jit(solution)/shard_map/cond/branch_1_fun/ppermute | solution.py:911
  (44 other events, 565.9 us)

commit v7 on v6

--- a/solution.py
+++ b/solution.py
@@ -391,7 +391,8 @@
         dgu_ref[part, :chunk] = dg
         dgu_ref[part, chunk:] = du
         out_term = dot(hidden, wd_ref[...])
-        grad_term = dot_nt(dg, wg_ref[...]) + dot_nt(du, wu_ref[...])
+        both = jnp.concatenate([wg_ref[...], wu_ref[...]], axis=1)
+        grad_term = dot_nt(jnp.concatenate([dg, du], axis=1), both)
 
         @pl.when(step == 0)
         def _():
@@ -486,11 +487,10 @@
         at_hidden, at_gate, at_up = places(t, n)
         gate_cut, up_cut = columns(n)
         expert = (2 * pos[2] + 1 - pos[3]) * sets + lax.rem(pos[1] + t, 2)
-        gate = up = 0.0
-        for k in range(bands):
-            part = x_ref[:, k * band : (k + 1) * band]
-            gate = gate + dot(part, weights[t][k][:, gate_cut])
-            up = up + dot(part, weights[t][k][:, up_cut])
+        joined = lambda cut: jnp.concatenate([weights[t][k][:, cut] for k in range(bands)], axis=0)
+        x = x_ref[...]
+        gate = dot(x, joined(gate_cut))
+        up = dot(x, joined(up_cut))
         slope = dot_nt(c_ref[:, :width], weights[t][bands + n][...])
         sigmoid = 1.0 / (1.0 + jnp.exp(-gate))
         act = gate * sigmoid
@@ -503,13 +503,13 @@
     def results(k):
         out = grad = 0.0
         for t in range(sets):
-            for n in range(per):
-                at_hidden, at_gate, at_up = places(t, n)
-                gate_cut, up_cut = columns(n)
-                down = weights[t][bands + n][:, k * band : (k + 1) * band]
-                out = out + dot(hid_ref[:, at_hidden], down)
-                grad = grad + dot_nt(dgu_ref[:, at_gate], weights[t][k][:, gate_cut])
-                grad = grad + dot_nt(dgu_ref[:, at_up], weights[t][k][:, up_cut])
+            inner = per * chunk
+            first = lax.rem(pos[1] + t, 2) * inner
+            own = lambda ref, by: ref[:, pl.ds(pl.multiple_of(by * first, by * inner), by * inner)]
+            down = [weights[t][bands + n][:, k * band : (k + 1) * band] for n in range(per)]
+            both = [weights[t][k][:, cut] for n in range(per) for cut in columns(n)]
+            out = out + dot(own(hid_ref, 1), jnp.concatenate(down, axis=0))
+            grad = grad + dot_nt(own(dgu_ref, 2), jnp.concatenate(both, axis=1))
         for p in range(len(out_refs)):
             out_refs[p][...] = out[p * rows : (p + 1) * rows].astype(bf16)
             grad_refs[p][...] = grad[p * rows : (p + 1) * rows].astype(bf16)
@@ -628,10 +628,9 @@
 
 
 def rows_product_kernel(blocks, pos, *refs):
-    total = dot_tn(refs[0][...], refs[blocks][...])
-    for b in range(1, blocks):
-        total = total + dot_tn(refs[b][...], refs[blocks + b][...])
-    refs[-1][...] = total.astype(bf16)
+    left = jnp.concatenate([ref[...] for ref in refs[:blocks]], axis=0)
+    right = jnp.concatenate([ref[...] for ref in refs[blocks : 2 * blocks]], axis=0)
+    refs[-1][...] = dot_tn(left, right).astype(bf16)
 
 
 def rows_product(pos, lefts, rights, tile=512):

time: 485 us -> 482 us (level)
  the two profiles are of different devices: /device:TPU:0 before, /device:TPU:8 now
where the time goes in v7:
time: 482 us; the launch traced here: 477 us
  Pallas kernels  254 us (53%)
  waiting for transfers between devices  84.1 us (17%)
  starting transfers between devices  68.5 us (14%)
  other arithmetic  35 us (7%)
  local copies, waits for them, and re-layouts  18.6 us (4%)
  loops' own time  11.1 us (2%)
  matrix products  4.87 us (1%)
    pallas_call x4, Pallas kernels, experts(): pl.pallas_call(functools.partial(experts_kernel, count, per, gated, extra...  56.2 us
    ppermute x19, waiting for transfers between devices, shift_outer(): return lax.ppermute(value, axis, perm)  48.1 us
    pallas_call x10, Pallas kernels, sums(): pl.pallas_call(functools.partial(sums_kernel, [len(terms) for _, _, terms...  42.5 us
    pallas_call x2, Pallas kernels, others(): pl.pallas_call(functools.partial(others_kernel, sets, per, len(bands), ex...  37.1 us
    pallas_call x2, Pallas kernels, expert_halves(): pl.pallas_call(functools.partial(expert_halves_kernel, n_ctx, tiles), gri...  32.2 us
    ppermute x12, starting transfers between devices, ring_step(): return lax.ppermute(value, BOTH, perm)  26.9 us
    ppermute x19, starting transfers between devices, shift_outer(): return lax.ppermute(value, axis, perm)  21.2 us
    convert_element_type x8, other arithmetic, row_sum(): return total.astype(kind)  18.8 us
  transfers between devices with their start and end apart: 63, of which 17 were waited for; matrix products, arithmetic and copies ran while one was open for 9% of the time, Pallas kernels for 51%

profile of v7, /device:TPU:8, one launch (start us, length us, event | category | flops | bytes accessed | tf_op | source)
XLA Modules:
  0.0 477.3 jit_solution(16109452247711444137)
XLA Ops:
  6.0 28.7 %conditional.14 = (bf16[256,1536]{1,0:T(8,128)(2,1)}, bf16[256,1024]{1,0:T(8,128)(2,1)}, bf16[256,1024]{1,0:T(8,128)(2,1)}, bf16[256,1024]{1,0:T(8,128)(2,1)}, b...) conditional(s32[]{:T(128)} %convert_element_type.130, ...), branch_computations={%region_3.4_spmd, %region_4.5_spmd} | conditional | flops 1415970816 | bytes 48771484 | solution.py:1130
  6.6 5.1 %branch_1_fun.31 = (bf16[256,1536]{1,0:T(8,128)(2,1)}, bf16[256,1024]{1,0:T(8,128)(2,1)}) custom-call(bf16[256,1536]{1,0:T(8,128)(2,1)} %get-tuple-element.448.x_ref, f32[1,1536]{1,0:T(1,128)} %reshape.111.gain_ref, bf16[1536,512]{1,0:T(8,128)(2,1)} %get-tuple-element.450.wk_ref, bf16[1536,512]{1,0:T(8,128)(2,1)} %get-tuple-element.451.wv_ref), custom_call_target="tpu_custom_call" | custom-call | flops 201326592 | bytes 1310720 | tf_op jit(solution)/shard_map/cond/branch_1_fun/pallas_call | solution.py:66
  21.9 4.5 collective-permute-done.57
  27.5 4.9 %convolution_convert_fusion = bf16[256,1536]{1,0:T(8,128)(2,1)} fusion(bf16[256,1536]{1,0:T(8,128)(2,1)} %get-tuple-element.1108, bf16[1536,1536]{1,0:T(8,128)(2,1)} %get-tuple-element.454), kind=kOutput, calls=%fused_computation | convolution fusion | flops 1208352768 | bytes 6291456 | tf_op jit(solution)/shard_map/cond/branch_1_fun/dot_general | solution.py:26
  34.7 24.2 %conditional.15 = (bf16[256,1536]{1,0:T(8,128)(2,1)}, f32[4,1,768]{2,1,0:T(1,128)S(1)}, f32[256,1536]{1,0:T(8,128)}, bf16[256,1536]{1,0:T(8,128)(2,1)S(1)}, bf16...) conditional(s32[]{:T(128)} %convert_element_type.130, ...), branch_computations={%region_5.6_spmd, %region_6.7_spmd} | conditional | flops 1107296256 | bytes 22294828 | solution.py:1130
  39.9 9.5 %branch_1_fun.32 = (bf16[256,1536]{1,0:T(8,128)(2,1)}, f32[4,1,768]{2,1,0:T(1,128)S(1)}) custom-call(s32[4]{0:T(128)S(1)} %get-tuple-element.460.pos, s32[8]{0:T(128)S(1)} %get-tuple-element.461.spans, bf16[256,1536]{1,0:T(8,128)(2,1)} %get-tuple-element.462.q_ref, bf16[256,1024]{1,0:T(8,128)(2,1)} %get-tuple-element.463.refs_0_, ...), custom_call_target="tpu_custom_call" | custom-call | flops 805306368 | bytes 1048576 | tf_op jit(solution)/shard_map/cond/branch_1_fun/pallas_call | solution.py:128
  49.4 5.6 %branch_1_fun.33 = (f32[256,1536]{1,0:T(8,128)}, bf16[256,1536]{1,0:T(8,128)(2,1)S(1)}) custom-call(bf16[256,1536]{1,0:T(8,128)(2,1)S(1)} %copy-done.3, bf16[256,1536]{1,0:T(8,128)(2,1)} %get-tuple-element.1129.att_ref, bf16[1536,1536]{1,0:T(8,128)(2,1)} %get-tuple-element.470.w_ref, f32[1,1536]{1,0:T(1,128)} %reshape.112.gain_ref), custom_call_target="tpu_custom_call" | custom-call | flops 301989888 | bytes 2097152 | tf_op jit(solution)/shard_map/cond/branch_1_fun/pallas_call | solution.py:228
  58.9 25.2 %conditional.16 = (bf16[256,1536]{1,0:T(8,128)(2,1)}, f32[256,1536]{1,0:T(8,128)}, f32[256,1536]{1,0:T(8,128)}, bf16[256,1024]{1,0:T(8,128)(2,1)S(1)}, bf16[256,...) conditional(s32[]{:T(128)} %convert_element_type.130, ...), branch_computations={%region_7.8_spmd, %region_8.9_spmd} | conditional | flops 2617245696 | bytes 19923216 | solution.py:1130
  62.1 11.3 %branch_1_fun.34 = (f32[256,1536]{1,0:T(8,128)}, f32[256,1536]{1,0:T(8,128)}, bf16[256,1024]{1,0:T(8,128)(2,1)S(1)}, bf16[256,2048]{1,0:T(8,128)(2,1)S(1)}) custom-call(s32[4]{0:T(128)S(1)} %get-tuple-element.479.pos, bf16[256,1536]{1,0:T(8,128)(2,1)S(1)} %get-tuple-element.478.refs_0_, bf16[256,1536]{1,0:T(8,128)(2,1)S(1)} %get-tuple-element.480.refs_1_, ...), custom_call_target="tpu_custom_call" | custom-call | flops 2617245696 | bytes 3145728 | tf_op jit(solution)/shard_map/cond/branch_1_fun/pallas_call | solution.py:450
  73.4 6.4 %collective-permute-done.9 = bf16[256,1536]{1,0:T(8,128)(2,1)} collective-permute-done((bf16[256,1536]{1,0:T(8,128)(2,1)}, bf16[256,1536]{1,0:T(8,128)(2,1)}, u32[]{:S(2)}, u32[]{:S(2)}) %collective-permute-start.9) | collective-permute-done | bytes 786464 | tf_op jit(solution)/shard_map/cond/branch_1_fun/ppermute | solution.py:910
  84.1 24.5 %conditional.17 = (bf16[256,1536]{1,0:T(8,128)(2,1)}, bf16[256,1536]{1,0:T(8,128)(2,1)}, bf16[256,1536]{1,0:T(8,128)(2,1)}, bf16[1024,1536]{1,0:T(8,128)(2,1)}, ...) conditional(s32[]{:T(128)} %convert_element_type.130, ...), branch_computations={%region_9.10_spmd, %region_10.11_spmd} | conditional | flops 3825205248 | bytes 29360258 | solution.py:1130
  87.0 7.1 %branch_1_fun.36 = (bf16[16,80,2048]{2,1,0:T(8,128)(2,1)}, bf16[16,80,2048]{2,1,0:T(8,128)(2,1)}) custom-call(s32[4]{0:T(128)S(1)} %get-tuple-element.493.pos, bf16[256,1536]{1,0:T(8,128)(2,1)S(1)} %get-tuple-element.494.refs_0_, bf16[256,2048]{1,0:T(8,128)(2,1)S(1)} %get-tuple-element.505.refs_1_, bf16[256,1024]{1,0:T(8,128)(2,1)S(1)} %get-tuple-element.506.refs_2_, ...), custom_call_target="tpu_custom_call" | custom-call | flops 1207959552 | bytes 2097152 | tf_op jit(solution)/shard_map/cond/branch_1_fun/pallas_call | solution.py:613
  94.1 12.0 %branch_1_fun.35 = (bf16[256,1536]{1,0:T(8,128)(2,1)}, bf16[256,1536]{1,0:T(8,128)(2,1)}, bf16[1024,1536]{1,0:T(8,128)(2,1)}, bf16[1024,1664]{1,0:T(8,128)(2,1)S...) custom-call(s32[4]{0:T(128)S(1)} %get-tuple-element.493.pos, bf16[256,1536]{1,0:T(8,128)(2,1)} %copy-done.6, ...), custom_call_target="tpu_custom_call" | custom-call | flops 2617245696 | bytes 3145728 | tf_op jit(solution)/shard_map/cond/branch_1_fun/pallas_call | solution.py:450
  108.6 37.1 %conditional.18 = (bf16[256,1536]{1,0:T(8,128)(2,1)}, bf16[256,1536]{1,0:T(8,128)(2,1)}, bf16[256,1536]{1,0:T(8,128)(2,1)}, bf16[256,1536]{1,0:T(8,128)(2,1)}, b...) conditional(s32[]{:T(128)} %convert_element_type.130, ...), branch_computations={%region_11.12_spmd, %region_12.13_spmd} | conditional | flops 5234491392 | bytes 37749024 | solution.py:1130
  111.0 20.8 %branch_1_fun.37 = (bf16[256,1536]{1,0:T(8,128)(2,1)}, bf16[256,1536]{1,0:T(8,128)(2,1)}, bf16[256,1536]{1,0:T(8,128)(2,1)}, bf16[256,1536]{1,0:T(8,128)(2,1)}, ...) custom-call(s32[4]{0:T(128)S(1)} %get-tuple-element.515.pos, ...), custom_call_target="tpu_custom_call", output_to_operand_aliasing={{4}: (8, {}), {5}: (9, {}), {6}: (10, {}), {7}: (11, {})} | custom-call | flops 5234491392 | bytes 3145728 | tf_op jit(solution)/shard_map/cond/branch_1_fun/pallas_call | solution.py:450
  131.8 4.7 branch_1_fun.38
  145.7 53.8 %conditional.19 = (bf16[256,1536]{1,0:T(8,128)(2,1)}, bf16[256,1536]{1,0:T(8,128)(2,1)}, bf16[1024,1536]{1,0:T(8,128)(2,1)}, bf16[1024,1664]{1,0:T(8,128)(2,1)S(...) conditional(s32[]{:T(128)} %convert_element_type.130, ...), branch_computations={%region_13.14_spmd, %region_14.15_spmd} | conditional | flops 13086228480 | bytes 28967102 | solution.py:1130
  149.9 18.5 %branch_1_fun.40 = (bf16[256,1536]{1,0:T(8,128)(2,1)}, bf16[256,1536]{1,0:T(8,128)(2,1)}, bf16[256,1536]{1,0:T(8,128)(2,1)}, bf16[256,1536]{1,0:T(8,128)(2,1)}, ...) custom-call(s32[4]{0:T(128)S(1)} %get-tuple-element.542.pos, bf16[1024,1536]{1,0:T(8,128)(2,1)} %get-tuple-element.548.refs_5_.x_ref, ...), custom_call_target="tpu_custom_call" | custom-call | flops 5234491392 | bytes 3145728 | tf_op jit(solution)/shard_map/cond/branch_1_fun/pallas_call | solution.py:541
  168.3 12.0 %branch_1_fun.39 = (bf16[256,1536]{1,0:T(8,128)(2,1)}, bf16[256,1536]{1,0:T(8,128)(2,1)}, bf16[1024,1536]{1,0:T(8,128)(2,1)}, bf16[1024,1664]{1,0:T(8,128)(2,1)S...) custom-call(s32[4]{0:T(128)S(1)} %get-tuple-element.542.pos, ...), custom_call_target="tpu_custom_call", output_to_operand_aliasing={{2}: (6, {}), {3}: (7, {}), {4}: (8, {}), {5}: (9, {})} | custom-call | flops 2617245696 | bytes 3145728 | tf_op jit(solution)/shard_map/cond/branch_1_fun/pallas_call | solution.py:450
  180.4 18.6 %branch_1_fun.41 = (bf16[256,1536]{1,0:T(8,128)(2,1)}, bf16[256,1536]{1,0:T(8,128)(2,1)}, bf16[256,1536]{1,0:T(8,128)(2,1)}, bf16[256,1536]{1,0:T(8,128)(2,1)}, ...) custom-call(s32[4]{0:T(128)S(1)} %get-tuple-element.542.pos, ...), custom_call_target="tpu_custom_call", output_to_operand_aliasing={{4}: (13, {}), {5}: (14, {})} | custom-call | flops 5234491392 | bytes 3145728 | tf_op jit(solution)/shard_map/cond/branch_1_fun/pallas_call | solution.py:541
  199.5 25.6 %conditional.20 = (bf16[256,1536]{1,0:T(8,128)(2,1)}, bf16[6,128,3072]{2,1,0:T(8,128)(2,1)}, bf16[6,128,3072]{2,1,0:T(8,128)(2,1)}, bf16[2,80,2048]{2,1,0:T(8,128)(2,1)}, bf16[1,160,2048]{2,1,0:T(8,128)(2,1)}) conditional(s32[]{:T(128)} %convert_element_type.130, () %tuple.143, (bf16[256,1536]{1,0:T(8,128)(2,1)}, bf16[256,1536]{1,0:T(8,128)(2,1)}, ...), branch_computations={%region_15.16_spmd, %region_16.17_spmd} | conditional | flops 4833411072 | bytes 17039520 | solution.py:1130
  208.9 16.1 %branch_1_fun.42 = (bf16[6,128,3072]{2,1,0:T(8,128)(2,1)}, bf16[6,128,3072]{2,1,0:T(8,128)(2,1)}) custom-call(s32[4]{0:T(128)S(1)} %get-tuple-element.584.pos, bf16[1024,1536]{1,0:T(8,128)(2,1)} %get-tuple-element.585.refs_0_.refs_1_.refs_2_.refs_3_, bf16[1024,1536]{1,0:T(8,128)(2,1)} %get-tuple-element.585.refs_0_.refs_1_.refs_2_.refs_3_, ...), custom_call_target="tpu_custom_call" | custom-call | flops 4831838208 | bytes 4194304 | tf_op jit(solution)/shard_map/cond/branch_1_fun/pallas_call | solution.py:716
  225.1 29.5 %conditional.21 = (bf16[256,1536]{1,0:T(8,128)(2,1)}, bf16[6,128,3072]{2,1,0:T(8,128)(2,1)}, bf16[6,128,3072]{2,1,0:T(8,128)(2,1)}, bf16[6,128,3072]{2,1,0:T(8,1...) conditional(s32[]{:T(128)} %convert_element_type.130, () %tuple.142, ...), branch_computations={%region_17.18_spmd, %region_18.19_spmd} | conditional | flops 4834197504 | bytes 36176040 | solution.py:1130
  235.4 16.0 %branch_1_fun.44 = (bf16[6,128,3072]{2,1,0:T(8,128)(2,1)}, bf16[6,128,3072]{2,1,0:T(8,128)(2,1)}) custom-call(s32[4]{0:T(128)S(1)} %get-tuple-element.600.pos, bf16[1024,1536]{1,0:T(8,128)(2,1)} %get-tuple-element.601.refs_0_.refs_1_.refs_2_.refs_3_, bf16[1024,1536]{1,0:T(8,128)(2,1)} %get-tuple-element.601.refs_0_.refs_1_.refs_2_.refs_3_, ...), custom_call_target="tpu_custom_call" | custom-call | flops 4831838208 | bytes 4194304 | tf_op jit(solution)/shard_map/cond/branch_1_fun/pallas_call | solution.py:716
  254.5 33.7 %conditional.22 = (f32[256,1536]{1,0:T(8,128)}, bf16[256,1536]{1,0:T(8,128)(2,1)}, f32[1,1536]{1,0:T(1,128)S(1)}, bf16[256,1536]{1,0:T(8,128)(2,1)}, bf16[6,128,...) conditional(s32[]{:T(128)} %convert_element_type.130, ...), branch_computations={%region_19.20_spmd, %region_20.21_spmd} | conditional | flops 305922048 | bytes 55850036 | solution.py:1130
  259.9 5.2 %branch_1_fun.48 = (bf16[6,128,768]{2,1,0:T(8,128)(2,1)}, bf16[6,128,768]{2,1,0:T(8,128)(2,1)}, bf16[6,128,768]{2,1,0:T(8,128)(2,1)}) custom-call(s32[4]{0:T(128)S(1)} %get-tuple-element.628.pos, bf16[6,128,3072]{2,1,0:T(8,128)(2,1)} %get-tuple-element.629.refs_0_.refs_2_.refs_4_, bf16[6,128,3072]{2,1,0:T(8,128)(2,1)} %get-tuple-element.630.refs_1_.refs_3_.refs_5_, ...), custom_call_target="tpu_custom_call" | custom-call | bytes 2097152 | tf_op jit(solution)/shard_map/cond/branch_1_fun/pallas_call | solution.py:757
  265.1 6.3 %branch_1_fun.49 = bf16[4,80,2048]{2,1,0:T(8,128)(2,1)} custom-call(s32[4]{0:T(128)S(1)} %get-tuple-element.628.pos, bf16[8,160,2048]{2,1,0:T(8,128)(2,1)} %bitcast.17.refs_0_, bf16[8,160,2048]{2,1,0:T(8,128)(2,1)} %bitcast.18.refs_1_, bf16[1,160,2048]{2,1,0:T(8,128)(2,1)} %get-tuple-element.636.refs_2_, bf16[1,160,2048]{2,1,0:T(8,128)(2,1)} %get-tuple-element.637.refs_3_, ...), custom_call_target="tpu_custom_call" | custom-call | bytes 2097152 | tf_op jit(solution)/shard_map/cond/branch_1_fun/pallas_call | solution.py:757
  280.2 7.8 %branch_1_fun.47 = (f32[256,1536]{1,0:T(8,128)}, bf16[256,1536]{1,0:T(8,128)(2,1)}, f32[1,1536]{1,0:T(1,128)S(1)}, bf16[256,1536]{1,0:T(8,128)(2,1)}) custom-call(f32[256,1536]{1,0:T(8,128)} %get-tuple-element.612.refs_0_, bf16[256,1536]{1,0:T(8,128)(2,1)} %get-tuple-element.613.refs_1_, bf16[256,1536]{1,0:T(8,128)(2,1)} %get-tuple-element.614.refs_2_, ...), custom_call_target="tpu_custom_call" | custom-call | flops 301989888 | bytes 4194304 | tf_op jit(solution)/shard_map/cond/branch_1_fun/pallas_call | solution.py:273
  289.0 26.0 %conditional.23 = (bf16[256,1536]{1,0:T(8,128)(2,1)S(1)}, bf16[256,1536]{1,0:T(8,128)(2,1)}, bf16[256,1536]{1,0:T(8,128)(2,1)}, bf16[256,1536]{1,0:T(8,128)(2,1)...) conditional(s32[]{:T(128)} %convert_element_type.130, ...), branch_computations={%region_21.22_spmd, %region_22.23_spmd} | conditional | flops 2013265920 | bytes 19136940 | solution.py:1130
  293.2 14.7 %branch_1_fun.50 = (bf16[256,1536]{1,0:T(8,128)(2,1)S(1)}, bf16[512,1024]{1,0:T(8,128)(2,1)S(1)}, bf16[512,1024]{1,0:T(8,128)(2,1)}) custom-call(s32[4]{0:T(128)S(1)} %get-tuple-element.645.pos, s32[8]{0:T(128)} %copy-done.24, bf16[256,1536]{1,0:T(8,128)(2,1)} %get-tuple-element.647.q_ref, bf16[256,1536]{1,0:T(8,128)(2,1)} %get-tuple-element.648.grad_ref, ...), custom_call_target="tpu_custom_call" | custom-call | flops 2013265920 | bytes 2097152 | tf_op jit(solution)/shard_map/cond/branch_1_fun/pallas_call | solution.py:190
  307.9 7.1 %collective-permute-done.28 = bf16[80,2048]{1,0:T(8,128)(2,1)} collective-permute-done((bf16[80,2048]{1,0:T(8,128)(2,1)}, bf16[80,2048]{1,0:T(8,128)(2,1)}, u32[]{:S(2)}, u32[]{:S(2)}) %collective-permute-start.28) | collective-permute-done | bytes 327712 | tf_op jit(solution)/shard_map/cond/branch_1_fun/ppermute | solution.py:910
  315.0 36.7 %conditional.24 = (bf16[256,1024]{1,0:T(8,128)(2,1)S(1)}, bf16[256,1536]{1,0:T(8,128)(2,1)}, bf16[8,48,1536]{2,1,0:T(8,128)(2,1)S(1)}, bf16[6,128,768]{2,1,0:T(8...) conditional(s32[]{:T(128)} %convert_element_type.130, () %tuple.127, ...), branch_computations={%region_23.24_spmd, %region_24.25_spmd} | conditional | flops 611319808 | bytes 39846232 | solution.py:1130
  328.7 4.6 branch_1_fun.51
  343.0 7.4 %collective-permute-done.39 = bf16[256,1024]{1,0:T(8,128)(2,1)S(1)} collective-permute-done((bf16[256,1024]{1,0:T(8,128)(2,1)S(1)}, bf16[256,1024]{1,0:T(8,128)(2,1)S(1)}, u32[]{:S(2)}, u32[]{:S(2)}) %collective-permute-start.39) | collective-permute-done | bytes 524320 | tf_op jit(solution)/shard_map/cond/branch_1_fun/ppermute | solution.py:910
  352.7 38.6 %conditional.25 = (bf16[8,48,1536]{2,1,0:T(8,128)(2,1)}, bf16[8,48,1024]{2,1,0:T(8,128)(2,1)}, f32[1,1536]{1,0:T(1,128)S(1)}, bf16[256,1536]{1,0:T(8,128)(2,1)},...) conditional(s32[]{:T(128)} %convert_element_type.130, () %tuple.149, ...), branch_computations={%region_25.26_spmd, %region_26.27_spmd} | conditional | flops 1515192320 | bytes 38285636 | solution.py:1130
  358.6 5.3 %collective-permute-done.45.refs_6_ = bf16[256,1024]{1,0:T(8,128)(2,1)S(1)} collective-permute-done((bf16[256,1024]{1,0:T(8,128)(2,1)S(1)}, bf16[256,1024]{1,0:T(8,128)(2,1)S(1)}, u32[]{:S(2)}, u32[]{:S(2)}) %collective-permute-start.45) | collective-permute-done | bytes 524320 | tf_op jit(solution)/shard_map/cond/branch_1_fun/ppermute | solution.py:910
  365.0 7.3 %collective-permute-start.47 = (bf16[256,1536]{1,0:T(8,128)(2,1)}, bf16[256,1536]{1,0:T(8,128)(2,1)}, u32[]{:S(2)}, u32[]{:S(2)}) collective-permute-start(bf16[256,1536]{1,0:T(8,128)(2,1)} %get-tuple-element.696), channel_id=1, source_target_pairs={{0,6},{1,7},{2,0},{3,1},{4,2},{5,3},{6,4},{7,5},{8,10},{9,11},{10,... | collective-permute-start | bytes 2359304 | tf_op jit(solution)/shard_map/cond/branch_1_fun/ppermute | solution.py:922
  372.9 9.3 %branch_1_fun.55 = (f32[256,1536]{1,0:T(8,128)}, f32[1,1536]{1,0:T(1,128)S(1)}) custom-call(bf16[256,1536]{1,0:T(8,128)(2,1)S(1)} %get-tuple-element.686.refs_4_.dq_ref, bf16[256,1024]{1,0:T(8,128)(2,1)S(1)} %get-tuple-element.688.refs_4_.dkv_ref, bf16[1536,1536]{1,0:T(8,128)(2,1)} %get-tuple-element.689.wq_ref, ...), custom_call_target="tpu_custom_call" | custom-call | flops 503316480 | bytes 3670016 | tf_op jit(solution)/shard_map/cond/branch_1_fun/pallas_call | solution.py:324
  386.1 5.2 %branch_1_fun.53 = bf16[384,1536]{1,0:T(8,128)(2,1)} custom-call(s32[4]{0:T(128)S(1)} %get-tuple-element.681.pos, bf16[256,1536]{1,0:T(8,128)(2,1)} %get-tuple-element.682.refs_0_, bf16[256,1536]{1,0:T(8,128)(2,1)} %get-tuple-element.683.refs_1_, bf16[256,1536]{1,0:T(8,128)(2,1)} %get-tuple-element.684.refs_2_, ...), custom_call_target="tpu_custom_call" | custom-call | flops 603979776 | bytes 1048576 | tf_op jit(solution)/shard_map/cond/branch_1_fun/pallas_call | solution.py:656
  391.4 39.9 %conditional.26 = (bf16[4,48,4096]{2,1,0:T(8,128)(2,1)S(1)}, bf16[4,48,4096]{2,1,0:T(8,128)(2,1)}, bf16[6,128,768]{2,1,0:T(8,128)(2,1)}, bf16[80,2048]{1,0:T(8,1...) conditional(s32[]{:T(128)} %convert_element_type.130, ...), branch_computations={%region_27.28_spmd, %region_28.29_spmd} | conditional | flops 12586004 | bytes 34755032 | solution.py:1130
  400.6 5.9 %all-to-all-start = ((f32[32,2,48]{2,1,0:T(2,128)}), f32[32,2,48]{2,1,0:T(2,128)}, u32[]{:S(2)}, u32[]{:S(2)}) async-start(f32[32,2,48]{2,1,0:T(2,128)} %pad_maximum_fusion.6), calls=%async_computation | async-start | bytes 65536 | tf_op jit(solution)/shard_map/cond/branch_1_fun/all_to_all | solution.py:1342
  413.1 17.9 %all-to-all-done = f32[32,2,48]{2,1,0:T(2,128)} async-done(((f32[32,2,48]{2,1,0:T(2,128)}), f32[32,2,48]{2,1,0:T(2,128)}, u32[]{:S(2)}, u32[]{:S(2)}) %all-to-all-start) | async-done | bytes 12320 | tf_op jit(solution)/shard_map/cond/branch_1_fun/all_to_all | solution.py:1342
  431.3 45.2 %conditional.27 = (f32[2,48]{1,0:T(2,128)}, f32[48,1024]{1,0:T(8,128)}, f32[48,1024]{1,0:T(8,128)}, f32[32,1536]{1,0:T(8,128)}, f32[48,1536]{1,0:T(8,128)}, /*in...) conditional(s32[]{:T(128)} %convert_element_type.130, ...), branch_computations={%region_29.30_spmd, %region_30.32_spmd} | conditional | flops 2976 | bytes 16270620 | solution.py:1130
  434.8 4.3 collective-permute-start.55
  443.0 6.2 %branch_1_fun.60 = (bf16[3,128,768]{2,1,0:T(8,128)(2,1)}, bf16[3,128,768]{2,1,0:T(8,128)(2,1)}, bf16[3,128,768]{2,1,0:T(8,128)(2,1)}, bf16[3,128,768]{2,1,0:T(8,128)(2,1)}) custom-call(s32[4]{0:T(128)S(1)} %get-tuple-element.725.pos, bf16[6,128,3072]{2,1,0:T(8,128)(2,1)} %get-tuple-element.736.refs_0_.refs_4_.refs_8_.refs_12_, ...), custom_call_target="tpu_custom_call" | custom-call | bytes 2097152 | tf_op jit(solution)/shard_map/cond/branch_1_fun/pallas_call | solution.py:757
  449.3 8.8 %branch_1_fun.61 = (f32[2,384,512]{2,1,0:T(8,128)}, f32[2,384,512]{2,1,0:T(8,128)}, f32[2,512,384]{2,1,0:T(8,128)}) custom-call(bf16[384,768]{1,0:T(8,128)(2,1)} %bitcast.92, bf16[384,768]{1,0:T(8,128)(2,1)} %bitcast.93, bf16[384,768]{1,0:T(8,128)(2,1)} %bitcast.94, bf16[384,768]{1,0:T(8,128)(2,1)} %bitcast.95), custom_call_target="tpu_custom_call" | custom-call | bytes 2097152 | tf_op jit(solution)/shard_map/cond/branch_1_fun/pallas_call | solution.py:817
  458.0 11.1 %collective-permute-done.55.refs_2_ = bf16[48,4096]{1,0:T(8,128)(2,1)S(1)} collective-permute-done((bf16[48,4096]{1,0:T(8,128)(2,1)}, bf16[48,4096]{1,0:T(8,128)(2,1)S(1)}, u32[]{:S(2)}, u32[]{:S(2)}) %collective-permute-start.55) | collective-permute-done | bytes 393248 | tf_op jit(solution)/shard_map/cond/branch_1_fun/ppermute | solution.py:910
  469.2 4.2 collective-permute-done.56.refs_3_
  (227 shorter events, 153.6 us)
Async XLA Ops:
  11.7 20.6 %collective-permute-start.58 = (bf16[256,1024]{1,0:T(8,128)(2,1)}, bf16[256,1024]{1,0:T(8,128)(2,1)}, u32[]{:S(2)}, u32[]{:S(2)}) collective-permute-start(bf16[256,1024]{1,0:T(8,128)(2,1)} %get-tuple-element.1109), channel_id=1, source_target_pairs={{0,8},{8,0},{16,24},{24,16},{1,9},{9,1},{17,25},{25,17},{2,10},{10... | collective-permute-start | bytes 1572872 | tf_op jit(solution)/shard_map/cond/branch_1_fun/ppermute | solution.py:904
  13.3 21.4 %collective-permute-start.60 = (bf16[256,1664]{1,0:T(8,128)(2,1)}, bf16[256,1664]{1,0:T(8,128)(2,1)}, u32[]{:S(2)}, u32[]{:S(2)}) collective-permute-start(bf16[256,1664]{1,0:T(8,128)(2,1)} %get-tuple-element.455), channel_id=1, source_target_pairs={{0,2},{1,3},{2,4},{3,5},{4,6},{5,7},{6,0},{7,1},{8,14},{9,15},{10,... | collective-permute-start | bytes 2555912 | tf_op jit(solution)/shard_map/cond/branch_1_fun/ppermute | solution.py:922
  34.7 24.1 %collective-permute-start.2 = (bf16[256,1664]{1,0:T(8,128)(2,1)}, bf16[256,1664]{1,0:T(8,128)(2,1)}, u32[]{:S(2)}, u32[]{:S(2)}) collective-permute-start(bf16[256,1664]{1,0:T(8,128)(2,1)} %get-tuple-element.475), channel_id=1, source_target_pairs={{0,2},{1,3},{2,4},{3,5},{4,6},{5,7},{6,0},{7,1},{8,14},{9,15},{10,... | collective-permute-start | bytes 2555912 | tf_op jit(solution)/shard_map/cond/branch_1_fun/ppermute | solution.py:922
  37.1 19.7 %collective-permute-start.3 = (bf16[256,1536]{1,0:T(8,128)(2,1)}, bf16[256,1536]{1,0:T(8,128)(2,1)}, u32[]{:S(2)}, u32[]{:S(2)}) collective-permute-start(bf16[256,1536]{1,0:T(8,128)(2,1)} %get-tuple-element.476), channel_id=1, source_target_pairs={{0,1},{1,0},{2,3},{3,2},{4,5},{5,4},{6,7},{7,6},{8,9},{9,8},{10,11... | collective-permute-start | bytes 2359304 | tf_op jit(solution)/shard_map/cond/branch_1_fun/ppermute | solution.py:904
  38.6 20.3 %collective-permute-start.1 = (bf16[256,1536]{1,0:T(8,128)(2,1)}, bf16[256,1536]{1,0:T(8,128)(2,1)}, u32[]{:S(2)}, u32[]{:S(2)}) collective-permute-start(bf16[256,1536]{1,0:T(8,128)(2,1)} %get-tuple-element.474), channel_id=1, source_target_pairs={{0,16},{8,24},{16,0},{24,8},{1,17},{9,25},{17,1},{25,9},{2,18},{10... | collective-permute-start | bytes 2359304 | tf_op jit(solution)/shard_map/cond/branch_1_fun/ppermute | solution.py:910
  39.1 19.8 %collective-permute-start = (bf16[256,1536]{1,0:T(8,128)(2,1)}, bf16[256,1536]{1,0:T(8,128)(2,1)}, u32[]{:S(2)}, u32[]{:S(2)}) collective-permute-start(bf16[256,1536]{1,0:T(8,128)(2,1)} %get-tuple-element.474), channel_id=1, source_target_pairs={{0,8},{8,0},{16,24},{24,16},{1,9},{9,1},{17,25},{25,17},{2,10},{10... | collective-permute-start | bytes 2359304 | tf_op jit(solution)/shard_map/cond/branch_1_fun/ppermute | solution.py:904
  58.9 25.2 %collective-permute-start.7 = (bf16[512,1024]{1,0:T(8,128)(2,1)}, bf16[512,1024]{1,0:T(8,128)(2,1)}, u32[]{:S(2)}, u32[]{:S(2)}) collective-permute-start(bf16[512,1024]{1,0:T(8,128)(2,1)} %get-tuple-element.489), channel_id=1, source_target_pairs={{0,1},{1,0},{2,3},{3,2},{4,5},{5,4},{6,7},{7,6},{8,9},{9,8},{10,11... | collective-permute-start | bytes 3145736 | tf_op jit(solution)/shard_map/cond/branch_1_fun/ppermute | solution.py:904
  60.0 19.8 %collective-permute-start.9 = (bf16[256,1536]{1,0:T(8,128)(2,1)}, bf16[256,1536]{1,0:T(8,128)(2,1)}, u32[]{:S(2)}, u32[]{:S(2)}) collective-permute-start(bf16[256,1536]{1,0:T(8,128)(2,1)} %get-tuple-element.491), channel_id=1, source_target_pairs={{0,16},{8,24},{16,0},{24,8},{1,17},{9,25},{17,1},{25,9},{2,18},{10... | collective-permute-start | bytes 2359304 | tf_op jit(solution)/shard_map/cond/branch_1_fun/ppermute | solution.py:910
  60.5 19.9 %collective-permute-start.5 = (bf16[256,1536]{1,0:T(8,128)(2,1)S(1)}, bf16[256,1536]{1,0:T(8,128)(2,1)}, u32[]{:S(2)}, u32[]{:S(2)}) collective-permute-start(bf16[256,1536]{1,0:T(8,128)(2,1)S(1)} %get-tuple-element.478.refs_0_), channel_id=1, source_target_pairs={{0,2},{1,3},{2,4},{3,5},{4,6},{5,7},{6,0},{7,1},{8,14},{9,15},{10,... | collective-permute-start | bytes 2359304 | tf_op jit(solution)/shard_map/cond/branch_1_fun/ppermute | solution.py:922
  84.3 24.3 %collective-permute-start.11 = (bf16[512,1024]{1,0:T(8,128)(2,1)}, bf16[512,1024]{1,0:T(8,128)(2,1)}, u32[]{:S(2)}, u32[]{:S(2)}) collective-permute-start(bf16[512,1024]{1,0:T(8,128)(2,1)} %get-tuple-element.510), channel_id=1, source_target_pairs={{0,1},{1,0},{2,3},{3,2},{4,5},{5,4},{6,7},{7,6},{8,9},{9,8},{10,11... | collective-permute-start | bytes 3145736 | tf_op jit(solution)/shard_map/cond/branch_1_fun/ppermute | solution.py:904
  85.0 23.7 %collective-permute-start.12 = (bf16[512,1024]{1,0:T(8,128)(2,1)}, bf16[512,1024]{1,0:T(8,128)(2,1)}, u32[]{:S(2)}, u32[]{:S(2)}) collective-permute-start(bf16[512,1024]{1,0:T(8,128)(2,1)} %get-tuple-element.511), channel_id=1, source_target_pairs={{0,8},{8,0},{16,24},{24,16},{1,9},{9,1},{17,25},{25,17},{2,10},{10... | collective-permute-start | bytes 3145736 | tf_op jit(solution)/shard_map/cond/branch_1_fun/ppermute | solution.py:904
  85.0 21.2 %collective-permute-start.10 = (bf16[256,1536]{1,0:T(8,128)(2,1)}, bf16[256,1536]{1,0:T(8,128)(2,1)}, u32[]{:S(2)}, u32[]{:S(2)}) collective-permute-start(bf16[256,1536]{1,0:T(8,128)(2,1)} %get-tuple-element.492), channel_id=1, source_target_pairs={{0,2},{1,3},{2,4},{3,5},{4,6},{5,7},{6,0},{7,1},{8,14},{9,15},{10,... | collective-permute-start | bytes 2359304 | tf_op jit(solution)/shard_map/cond/branch_1_fun/ppermute | solution.py:922
  86.5 19.6 %collective-permute-start.14 = (bf16[256,1536]{1,0:T(8,128)(2,1)}, bf16[256,1536]{1,0:T(8,128)(2,1)}, u32[]{:S(2)}, u32[]{:S(2)}) collective-permute-start(bf16[256,1536]{1,0:T(8,128)(2,1)} %get-tuple-element.513), channel_id=1, source_target_pairs={{0,8},{8,0},{16,24},{24,16},{1,9},{9,1},{17,25},{25,17},{2,10},{10... | collective-permute-start | bytes 2359304 | tf_op jit(solution)/shard_map/cond/branch_1_fun/ppermute | solution.py:904
  108.6 23.2 %collective-permute-start.16 = (bf16[16,80,2048]{2,1,0:T(8,128)(2,1)}, bf16[16,80,2048]{2,1,0:T(8,128)(2,1)}, u32[]{:S(2)}, u32[]{:S(2)}) collective-permute-start(bf16[16,80,2048]{2,1,0:T(8,128)(2,1)} %get-tuple-element.535), channel_id=1, source_target_pairs={{0,8},{8,0},{16,24},{24,16},{1,9},{9,1},{17,25},{25,17},{2,10},{10... | collective-permute-start | bytes 15728648 | tf_op jit(solution)/shard_map/cond/branch_1_fun/ppermute | solution.py:904
  108.6 27.8 %collective-permute-start.17 = (bf16[512,1024]{1,0:T(8,128)(2,1)}, bf16[512,1024]{1,0:T(8,128)(2,1)}, u32[]{:S(2)}, u32[]{:S(2)}) collective-permute-start(bf16[512,1024]{1,0:T(8,128)(2,1)} %get-tuple-element.540), channel_id=1, source_target_pairs={{0,1},{1,0},{2,3},{3,2},{4,5},{5,4},{6,7},{7,6},{8,9},{9,8},{10,11... | collective-permute-start | bytes 3145736 | tf_op jit(solution)/shard_map/cond/branch_1_fun/ppermute | solution.py:904
  109.2 27.3 %collective-permute-start.18 = (bf16[512,1024]{1,0:T(8,128)(2,1)}, bf16[512,1024]{1,0:T(8,128)(2,1)}, u32[]{:S(2)}, u32[]{:S(2)}) collective-permute-start(bf16[512,1024]{1,0:T(8,128)(2,1)} %get-tuple-element.541), channel_id=1, source_target_pairs={{0,8},{8,0},{16,24},{24,16},{1,9},{9,1},{17,25},{25,17},{2,10},{10... | collective-permute-start | bytes 3145736 | tf_op jit(solution)/shard_map/cond/branch_1_fun/ppermute | solution.py:904
  109.4 27.1 %collective-permute-start.15 = (bf16[256,1536]{1,0:T(8,128)(2,1)}, bf16[256,1536]{1,0:T(8,128)(2,1)}, u32[]{:S(2)}, u32[]{:S(2)}) collective-permute-start(bf16[256,1536]{1,0:T(8,128)(2,1)} %get-tuple-element.514.refs_1_), channel_id=1, source_target_pairs={{0,2},{1,3},{2,4},{3,5},{4,6},{5,7},{6,0},{7,1},{8,14},{9,15},{10,... | collective-permute-start | bytes 2359304 | tf_op jit(solution)/shard_map/cond/branch_1_fun/ppermute | solution.py:922
  145.8 22.5 %collective-permute-start.19 = (bf16[256,1664]{1,0:T(8,128)(2,1)}, bf16[256,1664]{1,0:T(8,128)(2,1)}, u32[]{:S(2)}, u32[]{:S(2)}) collective-permute-start(bf16[256,1664]{1,0:T(8,128)(2,1)} %get-tuple-element.544), channel_id=1, source_target_pairs={{0,2},{1,3},{2,4},{3,5},{4,6},{5,7},{6,0},{7,1},{8,14},{9,15},{10,... | collective-permute-start | bytes 2555912 | tf_op jit(solution)/shard_map/cond/branch_1_fun/ppermute | solution.py:922
  147.3 51.7 %collective-permute-start.21 = (bf16[1,160,2048]{2,1,0:T(8,128)(2,1)}, bf16[1,160,2048]{2,1,0:T(8,128)(2,1)}, u32[]{:S(2)}, u32[]{:S(2)}) collective-permute-start(bf16[1,160,2048]{2,1,0:T(8,128)(2,1)} %get-tuple-element.579), channel_id=1, source_target_pairs={{0,16},{8,24},{16,0},{24,8},{1,17},{9,25},{17,1},{25,9},{2,18},{10... | collective-permute-start | bytes 1966088 | tf_op jit(solution)/shard_map/cond/branch_1_fun/ppermute | solution.py:910
  147.8 51.2 %collective-permute-start.22 = (bf16[1,160,2048]{2,1,0:T(8,128)(2,1)}, bf16[1,160,2048]{2,1,0:T(8,128)(2,1)}, u32[]{:S(2)}, u32[]{:S(2)}) collective-permute-start(bf16[1,160,2048]{2,1,0:T(8,128)(2,1)} %get-tuple-element.580), channel_id=1, source_target_pairs={{0,16},{8,24},{16,0},{24,8},{1,17},{9,25},{17,1},{25,9},{2,18},{10... | collective-permute-start | bytes 1966088 | tf_op jit(solution)/shard_map/cond/branch_1_fun/ppermute | solution.py:910
  149.4 49.7 %collective-permute-start.23 = (bf16[1,160,2048]{2,1,0:T(8,128)(2,1)}, bf16[1,160,2048]{2,1,0:T(8,128)(2,1)}, u32[]{:S(2)}, u32[]{:S(2)}) collective-permute-start(bf16[1,160,2048]{2,1,0:T(8,128)(2,1)} %get-tuple-element.581), channel_id=1, source_target_pairs={{0,16},{8,24},{16,0},{24,8},{1,17},{9,25},{17,1},{25,9},{2,18},{10... | collective-permute-start | bytes 1966088 | tf_op jit(solution)/shard_map/cond/branch_1_fun/ppermute | solution.py:910
  202.0 23.1 %collective-permute-start.29 = (bf16[256,1536]{1,0:T(8,128)(2,1)}, bf16[256,1536]{1,0:T(8,128)(2,1)}, u32[]{:S(2)}, u32[]{:S(2)}) collective-permute-start(bf16[256,1536]{1,0:T(8,128)(2,1)} %add_convert_fusion), channel_id=1, source_target_pairs={{0,6},{1,7},{2,0},{3,1},{4,2},{5,3},{6,4},{7,5},{8,10},{9,11},{10,... | collective-permute-start | bytes 2359304 | tf_op jit(solution)/shard_map/cond/branch_1_fun/ppermute | solution.py:922
  225.1 26.3 %collective-permute-start.33 = (bf16[6,128,3072]{2,1,0:T(8,128)(2,1)}, bf16[6,128,3072]{2,1,0:T(8,128)(2,1)}, u32[]{:S(2)}, u32[]{:S(2)}) collective-permute-start(bf16[6,128,3072]{2,1,0:T(8,128)(2,1)} %get-tuple-element.599), channel_id=1, source_target_pairs={{0,8},{8,0},{16,24},{24,16},{1,9},{9,1},{17,25},{25,17},{2,10},{10... | collective-permute-start | bytes 14155784 | tf_op jit(solution)/shard_map/cond/branch_1_fun/ppermute | solution.py:904
  228.0 26.6 %collective-permute-start.32 = (bf16[256,1536]{1,0:T(8,128)(2,1)}, bf16[256,1536]{1,0:T(8,128)(2,1)}, u32[]{:S(2)}, u32[]{:S(2)}) collective-permute-start(bf16[256,1536]{1,0:T(8,128)(2,1)} %add_convert_fusion.1), channel_id=1, source_target_pairs={{0,6},{1,7},{2,0},{3,1},{4,2},{5,3},{6,4},{7,5},{8,10},{9,11},{10,... | collective-permute-start | bytes 2359304 | tf_op jit(solution)/shard_map/cond/branch_1_fun/ppermute | solution.py:922
  234.8 19.7 %collective-permute-start.34 = (bf16[2,80,2048]{2,1,0:T(8,128)(2,1)}, bf16[2,80,2048]{2,1,0:T(8,128)(2,1)}, u32[]{:S(2)}, u32[]{:S(2)}) collective-permute-start(bf16[2,80,2048]{2,1,0:T(8,128)(2,1)} %branch_1_fun.46), channel_id=1, source_target_pairs={{0,1},{1,0},{2,3},{3,2},{4,5},{5,4},{6,7},{7,6},{8,9},{9,8},{10,11... | collective-permute-start | bytes 1966088 | tf_op jit(solution)/shard_map/cond/branch_1_fun/ppermute | solution.py:904
  254.7 33.3 %collective-permute-start.36 = (bf16[6,128,3072]{2,1,0:T(8,128)(2,1)}, bf16[6,128,3072]{2,1,0:T(8,128)(2,1)}, u32[]{:S(2)}, u32[]{:S(2)}) collective-permute-start(bf16[6,128,3072]{2,1,0:T(8,128)(2,1)} %get-tuple-element.626), channel_id=1, source_target_pairs={{0,8},{8,0},{16,24},{24,16},{1,9},{9,1},{17,25},{25,17},{2,10},{10... | collective-permute-start | bytes 14155784 | tf_op jit(solution)/shard_map/cond/branch_1_fun/ppermute | solution.py:904
  254.8 33.2 %collective-permute-start.37 = (bf16[6,128,768]{2,1,0:T(8,128)(2,1)}, bf16[6,128,768]{2,1,0:T(8,128)(2,1)}, u32[]{:S(2)}, u32[]{:S(2)}) collective-permute-start(bf16[6,128,768]{2,1,0:T(8,128)(2,1)} %get-tuple-element.627), channel_id=1, source_target_pairs={{0,1},{1,0},{2,3},{3,2},{4,5},{5,4},{6,7},{7,6},{8,9},{9,8},{10,11... | collective-permute-start | bytes 3538952 | tf_op jit(solution)/shard_map/cond/branch_1_fun/ppermute | solution.py:904
  259.1 20.1 %collective-permute-start.35 = (bf16[256,1536]{1,0:T(8,128)(2,1)}, bf16[256,1536]{1,0:T(8,128)(2,1)S(1)}, u32[]{:S(2)}, u32[]{:S(2)}) collective-permute-start(bf16[256,1536]{1,0:T(8,128)(2,1)} %add_convert_fusion.3), channel_id=1, source_target_pairs={{0,6},{1,7},{2,0},{3,1},{4,2},{5,3},{6,4},{7,5},{8,10},{9,11},{10,... | collective-permute-start | bytes 2359304 | tf_op jit(solution)/shard_map/cond/branch_1_fun/ppermute | solution.py:922
  289.0 26.0 %collective-permute-start.27 = (bf16[6,128,768]{2,1,0:T(8,128)(2,1)}, bf16[6,128,768]{2,1,0:T(8,128)(2,1)}, u32[]{:S(2)}, u32[]{:S(2)}) collective-permute-start(bf16[6,128,768]{2,1,0:T(8,128)(2,1)} %get-tuple-element.658), channel_id=1, source_target_pairs={{0,1},{1,0},{2,3},{3,2},{4,5},{5,4},{6,7},{7,6},{8,9},{9,8},{10,11... | collective-permute-start | bytes 3538952 | tf_op jit(solution)/shard_map/cond/branch_1_fun/ppermute | solution.py:904
  289.5 25.4 %collective-permute-start.26 = (bf16[256,1536]{1,0:T(8,128)(2,1)}, bf16[256,1536]{1,0:T(8,128)(2,1)}, u32[]{:S(2)}, u32[]{:S(2)}) collective-permute-start(bf16[256,1536]{1,0:T(8,128)(2,1)} %get-tuple-element.657), channel_id=1, source_target_pairs={{0,6},{1,7},{2,0},{3,1},{4,2},{5,3},{6,4},{7,5},{8,10},{9,11},{10,... | collective-permute-start | bytes 2359304 | tf_op jit(solution)/shard_map/cond/branch_1_fun/ppermute | solution.py:922
  290.0 25.0 %collective-permute-start.25 = (bf16[256,1536]{1,0:T(8,128)(2,1)}, bf16[256,1536]{1,0:T(8,128)(2,1)}, u32[]{:S(2)}, u32[]{:S(2)}) collective-permute-start(bf16[256,1536]{1,0:T(8,128)(2,1)} %get-tuple-element.1311), channel_id=1, source_target_pairs={{0,16},{8,24},{16,0},{24,8},{1,17},{9,25},{17,1},{25,9},{2,18},{10... | collective-permute-start | bytes 2359304 | tf_op jit(solution)/shard_map/cond/branch_1_fun/ppermute | solution.py:910
  290.4 24.5 %collective-permute-start.24 = (bf16[256,1536]{1,0:T(8,128)(2,1)}, bf16[256,1536]{1,0:T(8,128)(2,1)}, u32[]{:S(2)}, u32[]{:S(2)}) collective-permute-start(bf16[256,1536]{1,0:T(8,128)(2,1)} %get-tuple-element.1311), channel_id=1, source_target_pairs={{0,8},{8,0},{16,24},{24,16},{1,9},{9,1},{17,25},{25,17},{2,10},{10... | collective-permute-start | bytes 2359304 | tf_op jit(solution)/shard_map/cond/branch_1_fun/ppermute | solution.py:904
  290.5 24.5 %collective-permute-start.28 = (bf16[80,2048]{1,0:T(8,128)(2,1)}, bf16[80,2048]{1,0:T(8,128)(2,1)}, u32[]{:S(2)}, u32[]{:S(2)}) collective-permute-start(bf16[80,2048]{1,0:T(8,128)(2,1)} %get-tuple-element.659), channel_id=1, source_target_pairs={{0,2},{1,3},{2,4},{3,5},{4,6},{5,7},{6,0},{7,1},{8,10},{9,11},{10,... | collective-permute-start | bytes 983048 | tf_op jit(solution)/shard_map/cond/branch_1_fun/ppermute | solution.py:910
  318.4 21.8 %collective-permute-start.42 = (bf16[256,1536]{1,0:T(8,128)(2,1)}, bf16[256,1536]{1,0:T(8,128)(2,1)}, u32[]{:S(2)}, u32[]{:S(2)}) collective-permute-start(bf16[256,1536]{1,0:T(8,128)(2,1)} %add_convert_fusion.5), channel_id=1, source_target_pairs={{0,6},{1,7},{2,0},{3,1},{4,2},{5,3},{6,4},{7,5},{8,10},{9,11},{10,... | collective-permute-start | bytes 2359304 | tf_op jit(solution)/shard_map/cond/branch_1_fun/ppermute | solution.py:922
  321.9 29.8 %collective-permute-start.43 = (bf16[6,128,768]{2,1,0:T(8,128)(2,1)}, bf16[6,128,768]{2,1,0:T(8,128)(2,1)}, u32[]{:S(2)}, u32[]{:S(2)}) collective-permute-start(bf16[6,128,768]{2,1,0:T(8,128)(2,1)} %get-tuple-element.680), channel_id=1, source_target_pairs={{0,1},{1,0},{2,3},{3,2},{4,5},{5,4},{6,7},{7,6},{8,9},{9,8},{10,11... | collective-permute-start | bytes 3538952 | tf_op jit(solution)/shard_map/cond/branch_1_fun/ppermute | solution.py:904
  323.4 28.3 %collective-permute-start.40 = (bf16[256,1536]{1,0:T(8,128)(2,1)S(1)}, bf16[256,1536]{1,0:T(8,128)(2,1)}, u32[]{:S(2)}, u32[]{:S(2)}) collective-permute-start(bf16[256,1536]{1,0:T(8,128)(2,1)S(1)} %get-tuple-element.662), channel_id=1, source_target_pairs={{0,16},{8,24},{16,0},{24,8},{1,17},{9,25},{17,1},{25,9},{2,18},{10... | collective-permute-start | bytes 2359304 | tf_op jit(solution)/shard_map/cond/branch_1_fun/ppermute | solution.py:910
  355.6 30.5 %collective-permute-start.44 = (bf16[512,1536]{1,0:T(8,128)(2,1)}, bf16[512,1536]{1,0:T(8,128)(2,1)}, u32[]{:S(2)}, u32[]{:S(2)}) collective-permute-start(bf16[512,1536]{1,0:T(8,128)(2,1)} %pad_maximum_fusion.3), channel_id=1, source_target_pairs={{0,8},{8,0},{16,24},{24,16},{1,9},{9,1},{17,25},{25,17},{2,10},{10... | collective-permute-start | bytes 4718600 | tf_op jit(solution)/shard_map/cond/branch_1_fun/ppermute | solution.py:904
  355.6 35.7 %collective-permute-start.48 = (bf16[6,128,768]{2,1,0:T(8,128)(2,1)}, bf16[6,128,768]{2,1,0:T(8,128)(2,1)}, u32[]{:S(2)}, u32[]{:S(2)}) collective-permute-start(bf16[6,128,768]{2,1,0:T(8,128)(2,1)} %get-tuple-element.697), channel_id=1, source_target_pairs={{0,1},{1,0},{2,3},{3,2},{4,5},{5,4},{6,7},{7,6},{8,9},{9,8},{10,11... | collective-permute-start | bytes 3538952 | tf_op jit(solution)/shard_map/cond/branch_1_fun/ppermute | solution.py:904
  357.0 34.3 %collective-permute-start.49 = (bf16[6,128,768]{2,1,0:T(8,128)(2,1)}, bf16[6,128,768]{2,1,0:T(8,128)(2,1)}, u32[]{:S(2)}, u32[]{:S(2)}) collective-permute-start(bf16[6,128,768]{2,1,0:T(8,128)(2,1)} %get-tuple-element.698), channel_id=1, source_target_pairs={{0,16},{8,24},{16,0},{24,8},{1,17},{9,25},{17,1},{25,9},{2,18},{10... | collective-permute-start | bytes 3538952 | tf_op jit(solution)/shard_map/cond/branch_1_fun/ppermute | solution.py:910
  365.0 26.3 %collective-permute-start.47 = (bf16[256,1536]{1,0:T(8,128)(2,1)}, bf16[256,1536]{1,0:T(8,128)(2,1)}, u32[]{:S(2)}, u32[]{:S(2)}) collective-permute-start(bf16[256,1536]{1,0:T(8,128)(2,1)} %get-tuple-element.696), channel_id=1, source_target_pairs={{0,6},{1,7},{2,0},{3,1},{4,2},{5,3},{6,4},{7,5},{8,10},{9,11},{10,... | collective-permute-start | bytes 2359304 | tf_op jit(solution)/shard_map/cond/branch_1_fun/ppermute | solution.py:922
  394.9 36.1 %collective-permute-start.50 = (bf16[4,48,4096]{2,1,0:T(8,128)(2,1)}, bf16[4,48,4096]{2,1,0:T(8,128)(2,1)}, u32[]{:S(2)}, u32[]{:S(2)}) collective-permute-start(bf16[4,48,4096]{2,1,0:T(8,128)(2,1)} %get-tuple-element.1094), channel_id=1, source_target_pairs={{0,1},{1,0},{2,3},{3,2},{4,5},{5,4},{6,7},{7,6},{8,9},{9,8},{10,11... | collective-permute-start | bytes 4718600 | tf_op jit(solution)/shard_map/cond/branch_1_fun/ppermute | solution.py:904
  399.2 31.8 %collective-permute-start.51 = (bf16[6,128,768]{2,1,0:T(8,128)(2,1)}, bf16[6,128,768]{2,1,0:T(8,128)(2,1)}, u32[]{:S(2)}, u32[]{:S(2)}) collective-permute-start(bf16[6,128,768]{2,1,0:T(8,128)(2,1)} %branch_1_fun.56), channel_id=1, source_target_pairs={{0,16},{8,24},{16,0},{24,8},{1,17},{9,25},{17,1},{25,9},{2,18},{10... | collective-permute-start | bytes 3538952 | tf_op jit(solution)/shard_map/cond/branch_1_fun/ppermute | solution.py:910
  400.6 30.3 %all-to-all-start = ((f32[32,2,48]{2,1,0:T(2,128)}), f32[32,2,48]{2,1,0:T(2,128)}, u32[]{:S(2)}, u32[]{:S(2)}) async-start(f32[32,2,48]{2,1,0:T(2,128)} %pad_maximum_fusion.6), calls=%async_computation | async-start | bytes 65536 | tf_op jit(solution)/shard_map/cond/branch_1_fun/all_to_all | solution.py:1342
  406.5 24.4 %collective-permute-start.52 = (bf16[80,2048]{1,0:T(8,128)(2,1)}, bf16[80,2048]{1,0:T(8,128)(2,1)}, u32[]{:S(2)}, u32[]{:S(2)}) collective-permute-start(bf16[80,2048]{1,0:T(8,128)(2,1)} %get-tuple-element.708), channel_id=1, source_target_pairs={{0,4},{1,5},{2,6},{3,7},{4,0},{5,1},{6,2},{7,3},{8,12},{9,13},{10,... | collective-permute-start | bytes 983048 | tf_op jit(solution)/shard_map/cond/branch_1_fun/ppermute | solution.py:910
  409.1 22.0 %collective-permute-start.53 = (bf16[80,2048]{1,0:T(8,128)(2,1)}, bf16[80,2048]{1,0:T(8,128)(2,1)}, u32[]{:S(2)}, u32[]{:S(2)}) collective-permute-start(bf16[80,2048]{1,0:T(8,128)(2,1)} %get-tuple-element.709), channel_id=1, source_target_pairs={{0,6},{1,7},{2,0},{3,1},{4,2},{5,3},{6,4},{7,5},{8,14},{9,15},{10,... | collective-permute-start | bytes 983048 | tf_op jit(solution)/shard_map/cond/branch_1_fun/ppermute | solution.py:910
  434.7 23.3 %collective-permute-start.54 = (bf16[48,4096]{1,0:T(8,128)(2,1)}, bf16[48,4096]{1,0:T(8,128)(2,1)S(1)}, u32[]{:S(2)}, u32[]{:S(2)}) collective-permute-start(bf16[48,4096]{1,0:T(8,128)(2,1)} %bitcast.99), channel_id=1, source_target_pairs={{0,2},{1,3},{2,4},{3,5},{4,6},{5,7},{6,0},{7,1},{8,10},{9,11},{10,... | collective-permute-start | bytes 1179656 | tf_op jit(solution)/shard_map/cond/branch_1_fun/ppermute | solution.py:910
  434.8 34.4 %collective-permute-start.55 = (bf16[48,4096]{1,0:T(8,128)(2,1)}, bf16[48,4096]{1,0:T(8,128)(2,1)S(1)}, u32[]{:S(2)}, u32[]{:S(2)}) collective-permute-start(bf16[48,4096]{1,0:T(8,128)(2,1)} %bitcast.98), channel_id=1, source_target_pairs={{0,4},{1,5},{2,6},{3,7},{4,0},{5,1},{6,2},{7,3},{8,12},{9,13},{10,... | collective-permute-start | bytes 1179656 | tf_op jit(solution)/shard_map/cond/branch_1_fun/ppermute | solution.py:910
  439.0 34.3 %collective-permute-start.56 = (bf16[48,4096]{1,0:T(8,128)(2,1)}, bf16[48,4096]{1,0:T(8,128)(2,1)S(1)}, u32[]{:S(2)}, u32[]{:S(2)}) collective-permute-start(bf16[48,4096]{1,0:T(8,128)(2,1)} %bitcast.97), channel_id=1, source_target_pairs={{0,6},{1,7},{2,0},{3,1},{4,2},{5,3},{6,4},{7,5},{8,14},{9,15},{10,... | collective-permute-start | bytes 1179656 | tf_op jit(solution)/shard_map/cond/branch_1_fun/ppermute | solution.py:910
  (44 other events, 586.3 us)
